TPU v7x, 32 devices: a whole 2x2x4 slice. The times are simulated.
32 devices in a mesh: rep: 2 (over core), fsdp: 16 (over z, y, x).
Axes of the slice: x: 2, y: 2, z: 4, core: 2. Of those that a mesh axis runs over, the one named last changes fastest.
Arguments:
- tokens: bfloat16 [20480, 1536], P(('rep', 'fsdp')), may hold values from -6 to 6
- lengths: int32 [32, 4], P(('rep', 'fsdp')), may hold values from 1 to 480, 640 in all within a row
- attn_gain: bfloat16 [1536], P('fsdp'), may hold values from 0.099609375 to 1.8984375
- w_query: bfloat16 [1536, 1536], P('fsdp'), may hold values from -0.15625 to 0.15625
- w_key: bfloat16 [1536, 768], P('fsdp'), may hold values from -0.15625 to 0.15625
- w_value: bfloat16 [1536, 768], P('fsdp'), may hold values from -0.15625 to 0.15625
- w_out: bfloat16 [1536, 1536], P('fsdp'), may hold values from -0.625 to 0.625
- ffn_gain: bfloat16 [1536], P('fsdp'), may hold values from 0.099609375 to 1.8984375
- w_gate: bfloat16 [1536, 4096], P('fsdp'), may hold values from -0.15625 to 0.15625
- w_up: bfloat16 [1536, 4096], P('fsdp'), may hold values from -0.15625 to 0.15625
- w_down: bfloat16 [4096, 1536], P('fsdp'), may hold values from -0.09375 to 0.09375
- cotangent: bfloat16 [20480, 1536], P(('rep', 'fsdp')), may hold values from -6 to 6
Outputs:
- output: bfloat16 [20480, 1536], P(('rep', 'fsdp'))
- grad_tokens: float32 [20480, 1536], P(('rep', 'fsdp'))
- grad_attn_gain: float32 [1536], P('fsdp')
- grad_query: float32 [1536, 1536], P('fsdp')
- grad_key: float32 [1536, 768], P('fsdp')
- grad_value: float32 [1536, 768], P('fsdp')
- grad_out: float32 [1536, 1536], P('fsdp')
- grad_ffn_gain: float32 [1536], P('fsdp')
- grad_gate: float32 [1536, 4096], P('fsdp')
- grad_up: float32 [1536, 4096], P('fsdp')
- grad_down: float32 [4096, 1536], P('fsdp')
Inputs may be any that keep to these rules, and one draw needn't show every extreme that they name: Each row holds the lengths of the 4 documents on one device, summing to 640; the longest in each row is exactly 480.
All inputs are finite; a program needn't handle non-finite values.
Results may differ from a plain program's by a relative error of at most 0.015.
Values may be sent and summed in bfloat16 or wider, within the bound.
No kernel may reach another device: no remote copies, remote signals or barrier semaphores. Data moves between devices by JAX's collectives and lax.ppermute only.
A program may use at most 320 MiB of HBM per device.

v0:
```python
import jax
import jax.numpy as jnp
from jax import lax
from jax.sharding import PartitionSpec as P

H = 16
KV = 8
HD = 96


epsilon = 1e-05
rope_base = 100000.0
masked_score = -1e30


def layout(length_row, count):
    ends = jnp.cumsum(length_row)
    slots = jnp.arange(count, dtype=jnp.int32)
    passed = (slots[:, None] >= ends[None, :]).astype(jnp.int32)
    segment = jnp.sum(passed, axis=1)
    position = slots - jnp.sum(passed * length_row[None, :], axis=1)
    allowed = (segment[:, None] == segment[None, :]) & (slots[None, :] <= slots[:, None])
    return (position, allowed)


def rotation(position):
    half_size = HD // 2
    frequency = rope_base ** (-jnp.arange(half_size, dtype=jnp.float32) * 2.0 / HD)
    angle = position.astype(jnp.float32)[:, None] * frequency[None, :]
    cosine = jnp.concatenate([jnp.cos(angle), jnp.cos(angle)], axis=-1)[:, None, :]
    sine = jnp.concatenate([jnp.sin(angle), jnp.sin(angle)], axis=-1)[:, None, :]
    return (cosine, sine)


def rotate(field, cosine, sine, heads):
    half_size = HD // 2
    shaped = field.reshape(field.shape[0], heads, HD)
    turned = jnp.concatenate([-shaped[..., half_size:], shaped[..., :half_size]], axis=-1)
    return (shaped * cosine + turned * sine).reshape(field.shape)


def unrotate(grad, cosine, sine, heads):
    half_size = HD // 2
    shaped = grad.reshape(grad.shape[0], heads, HD)
    along = shaped * sine
    turned = jnp.concatenate([along[..., half_size:], -along[..., :half_size]], axis=-1)
    return (shaped * cosine + turned).reshape(grad.shape)


def normalize(hidden, gain):
    scale = lax.rsqrt(jnp.mean(hidden * hidden, axis=-1, keepdims=True) + epsilon)
    return (hidden * scale * gain, scale)


def norm_back(hidden, scale, gain, incoming):
    weighted = incoming * gain
    inner = jnp.mean(weighted * hidden, axis=-1, keepdims=True)
    return (
        scale * weighted - hidden * scale**3 * inner,
        jnp.sum(incoming * hidden * scale, axis=0),
    )


def project(left, weight):
    return jnp.dot(left, weight, preferred_element_type=jnp.float32)


def against(left, weight):
    return lax.dot_general(
        left, weight, (((1,), (1,)), ((), ())), preferred_element_type=jnp.float32
    )


def weight_grad(left, right):
    return lax.dot_general(
        left, right, (((0,), (0,)), ((), ())), preferred_element_type=jnp.float32
    )


def scores_of(queries, keys, allowed):
    raw = jnp.einsum("qgrd,kgd->grqk", queries, keys, preferred_element_type=jnp.float32)
    return jnp.where(allowed[None, None], raw * HD ** (-0.5), masked_score)


def reduce_ffn(grad_gain, grad_gate, grad_up, grad_down):
    owned = (
        lax.psum_scatter(grad_gain, "fsdp", scatter_dimension=0, tiled=True),
        lax.psum_scatter(grad_gate, "fsdp", scatter_dimension=0, tiled=True),
        lax.psum_scatter(grad_up, "fsdp", scatter_dimension=0, tiled=True),
        lax.psum_scatter(grad_down, "fsdp", scatter_dimension=0, tiled=True),
    )
    return (
        lax.psum(owned[0].astype(jnp.bfloat16), "rep").astype(jnp.float32),
        lax.psum(owned[1].astype(jnp.bfloat16), "rep").astype(jnp.float32),
        lax.psum(owned[2].astype(jnp.bfloat16), "rep").astype(jnp.float32),
        lax.psum(owned[3].astype(jnp.bfloat16), "rep").astype(jnp.float32),
    )


def reduce_attn(grad_gain, grad_query, grad_key, grad_value, grad_out):
    owned = (
        lax.psum_scatter(grad_gain, "fsdp", scatter_dimension=0, tiled=True),
        lax.psum_scatter(grad_query, "fsdp", scatter_dimension=0, tiled=True),
        lax.psum_scatter(grad_key, "fsdp", scatter_dimension=0, tiled=True),
        lax.psum_scatter(grad_value, "fsdp", scatter_dimension=0, tiled=True),
        lax.psum_scatter(grad_out, "fsdp", scatter_dimension=0, tiled=True),
    )
    return (
        lax.psum(owned[0].astype(jnp.bfloat16), "rep").astype(jnp.float32),
        lax.psum(owned[1].astype(jnp.bfloat16), "rep").astype(jnp.float32),
        lax.psum(owned[2].astype(jnp.bfloat16), "rep").astype(jnp.float32),
        lax.psum(owned[3].astype(jnp.bfloat16), "rep").astype(jnp.float32),
        lax.psum(owned[4].astype(jnp.bfloat16), "rep").astype(jnp.float32),
    )


def on_device(
    tokens,
    lengths,
    attn_gain,
    w_query,
    w_key,
    w_value,
    w_out,
    ffn_gain,
    w_gate,
    w_up,
    w_down,
    cotangent,
):
    count = tokens.shape[0]
    groups = H // KV
    position, allowed = layout(lengths[0], count)
    cosine, sine = rotation(position)
    attn_full = (
        lax.all_gather(attn_gain, "fsdp", axis=0, tiled=True),
        lax.all_gather(w_query, "fsdp", axis=0, tiled=True),
        lax.all_gather(w_key, "fsdp", axis=0, tiled=True),
        lax.all_gather(w_value, "fsdp", axis=0, tiled=True),
        lax.all_gather(w_out, "fsdp", axis=0, tiled=True),
    )
    ffn_full = (
        lax.all_gather(ffn_gain, "fsdp", axis=0, tiled=True),
        lax.all_gather(w_gate, "fsdp", axis=0, tiled=True),
        lax.all_gather(w_up, "fsdp", axis=0, tiled=True),
        lax.all_gather(w_down, "fsdp", axis=0, tiled=True),
    )
    gain_one = attn_full[0].astype(jnp.float32)
    gain_two = ffn_full[0].astype(jnp.float32)
    hidden = tokens.astype(jnp.float32)
    normed, scale_one = normalize(hidden, gain_one)
    normed_low = normed.astype(jnp.bfloat16)
    queries = (
        rotate(project(normed_low, attn_full[1]), cosine, sine, H)
        .astype(jnp.bfloat16)
        .reshape(count, KV, groups, HD)
    )
    keys = (
        rotate(project(normed_low, attn_full[2]), cosine, sine, KV)
        .astype(jnp.bfloat16)
        .reshape(count, KV, HD)
    )
    values = project(normed_low, attn_full[3]).astype(jnp.bfloat16).reshape(count, KV, HD)
    scores = scores_of(queries, keys, allowed)
    top = jnp.max(scores, axis=-1, keepdims=True)
    total = jnp.log(jnp.sum(jnp.exp(scores - top), axis=-1, keepdims=True)) + top
    probs_low = jnp.exp(scores - total).astype(jnp.bfloat16)
    attended = jnp.einsum("grqk,kgd->qgrd", probs_low, values, preferred_element_type=jnp.float32)
    attended_low = attended.reshape(count, H * HD).astype(jnp.bfloat16)
    middle = hidden + project(attended_low, attn_full[4])
    normed_two, scale_two = normalize(middle, gain_two)
    normed_two_low = normed_two.astype(jnp.bfloat16)
    gate = project(normed_two_low, ffn_full[1])
    upward = project(normed_two_low, ffn_full[2])
    inner_low = (jax.nn.silu(gate) * upward).astype(jnp.bfloat16)
    output = (middle + project(inner_low, ffn_full[3])).astype(jnp.bfloat16)
    ffn_back = (
        lax.all_gather(ffn_gain, "fsdp", axis=0, tiled=True),
        lax.all_gather(w_gate, "fsdp", axis=0, tiled=True),
        lax.all_gather(w_up, "fsdp", axis=0, tiled=True),
        lax.all_gather(w_down, "fsdp", axis=0, tiled=True),
    )
    attn_back = (
        lax.all_gather(attn_gain, "fsdp", axis=0, tiled=True),
        lax.all_gather(w_query, "fsdp", axis=0, tiled=True),
        lax.all_gather(w_key, "fsdp", axis=0, tiled=True),
        lax.all_gather(w_value, "fsdp", axis=0, tiled=True),
        lax.all_gather(w_out, "fsdp", axis=0, tiled=True),
    )
    grad_down = weight_grad(inner_low, cotangent)
    grad_inner = against(cotangent, ffn_back[3])
    sigma = jax.nn.sigmoid(gate)
    grad_gate_low = (grad_inner * upward * sigma * (1.0 + gate * (1.0 - sigma))).astype(
        jnp.bfloat16
    )
    grad_up_low = (grad_inner * gate * sigma).astype(jnp.bfloat16)
    grad_gate = weight_grad(normed_two_low, grad_gate_low)
    grad_up = weight_grad(normed_two_low, grad_up_low)
    grad_normed_two = against(grad_gate_low, ffn_back[1]) + against(grad_up_low, ffn_back[2])
    middle_part, grad_ffn_gain = norm_back(middle, scale_two, gain_two, grad_normed_two)
    grad_middle = cotangent.astype(jnp.float32) + middle_part
    ffn_owned = reduce_ffn(grad_ffn_gain, grad_gate, grad_up, grad_down)
    grad_branch = grad_middle.astype(jnp.bfloat16)
    grad_out = weight_grad(attended_low, grad_branch)
    grad_attended = (
        against(grad_branch, attn_back[4]).astype(jnp.bfloat16).reshape(count, KV, groups, HD)
    )
    again_scores = scores_of(queries, keys, allowed)
    probs = jnp.exp(again_scores - total)
    again_low = probs.astype(jnp.bfloat16)
    grad_values = jnp.einsum(
        "grqk,qgrd->kgd", again_low, grad_attended, preferred_element_type=jnp.float32
    )
    grad_probs = jnp.einsum(
        "qgrd,kgd->grqk", grad_attended, values, preferred_element_type=jnp.float32
    )
    delta = jnp.sum(probs * grad_probs, axis=-1, keepdims=True)
    grad_raw = (probs * (grad_probs - delta) * HD ** (-0.5)).astype(jnp.bfloat16)
    grad_queries = jnp.einsum(
        "grqk,kgd->qgrd", grad_raw, keys, preferred_element_type=jnp.float32
    ).reshape(count, H * HD)
    grad_keys = jnp.einsum(
        "grqk,qgrd->kgd", grad_raw, queries, preferred_element_type=jnp.float32
    ).reshape(count, KV * HD)
    grad_queries = unrotate(grad_queries, cosine, sine, H).astype(jnp.bfloat16)
    grad_keys = unrotate(grad_keys, cosine, sine, KV).astype(jnp.bfloat16)
    grad_values = grad_values.reshape(count, KV * HD).astype(jnp.bfloat16)
    grad_query = weight_grad(normed_low, grad_queries)
    grad_key = weight_grad(normed_low, grad_keys)
    grad_value = weight_grad(normed_low, grad_values)
    grad_normed = (
        against(grad_queries, attn_back[1])
        + against(grad_keys, attn_back[2])
        + against(grad_values, attn_back[3])
    )
    hidden_part, grad_attn_gain = norm_back(hidden, scale_one, gain_one, grad_normed)
    grad_tokens = grad_middle + hidden_part
    attn_owned = reduce_attn(grad_attn_gain, grad_query, grad_key, grad_value, grad_out)
    return (
        output,
        grad_tokens,
        attn_owned[0],
        attn_owned[1],
        attn_owned[2],
        attn_owned[3],
        attn_owned[4],
        ffn_owned[0],
        ffn_owned[1],
        ffn_owned[2],
        ffn_owned[3],
    )


def solution(mesh):
    in_specs = (
        P(("rep", "fsdp"), None),
        P(("rep", "fsdp"), None),
        P("fsdp"),
        P("fsdp", None),
        P("fsdp", None),
        P("fsdp", None),
        P("fsdp", None),
        P("fsdp"),
        P("fsdp", None),
        P("fsdp", None),
        P("fsdp", None),
        P(("rep", "fsdp"), None),
    )
    out_specs = (
        P(("rep", "fsdp"), None),
        P(("rep", "fsdp"), None),
        P("fsdp"),
        P("fsdp", None),
        P("fsdp", None),
        P("fsdp", None),
        P("fsdp", None),
        P("fsdp"),
        P("fsdp", None),
        P("fsdp", None),
        P("fsdp", None),
    )
    return jax.shard_map(
        on_device, mesh=mesh, in_specs=in_specs, out_specs=out_specs, check_vma=False
    )
```

profile of v0, /device:TPU:0, one launch (start us, length us, event | category | flops | bytes accessed | tf_op | source)
XLA Modules:
  0.0 2627.5 jit_solution(11488330716217102350)
XLA Ops:
  15.6 44.3 %all-reduce.5 = (bf16[1536]{0:T(1024)(128)(2,1)S(1)}, bf16[1536]{0:T(1024)(128)(2,1)S(1)}) all-reduce(bf16[1536]{0:T(1024)(128)(2,1)S(1)} %dynamic-update-slice, bf16[1536]{0:T(1024)(128)(2,1)S(1)} %dynamic-update-slice.1), channel_id=1, replica_groups=mesh['rep'=2,'fsdp'=16] {'fsdp'}, use_global_device_ids=true, to_apply=%add | all-reduce | flops 3072 | bytes 12288
  82.7 57.3 %all-gather.10.cloned.1.call-done = bf16[1536,768]{1,0:T(8,128)(2,1)} async-done(((bf16[96,768]{1,0:T(8,128)(2,1)}), bf16[1536,768]{1,0:T(8,128)(2,1)}) %all-gather.10.cloned.1.call-update) | async-done | bytes 2359312 | tf_op jit(solution)/shard_map/all_gather | solution.py:138
  159.1 63.0 %all-gather.12.cloned.1.call-done = bf16[1536,1536]{1,0:T(8,128)(2,1)} async-done(((bf16[96,1536]{1,0:T(8,128)(2,1)}), bf16[1536,1536]{1,0:T(8,128)(2,1)}) %all-gather.12.cloned.1.call-update) | async-done | bytes 4718608 | tf_op jit(solution)/shard_map/all_gather | solution.py:137
  222.2 7.5 fusion.47
  245.5 6.7 add_convert_fusion.1
  256.4 14.6 fusion.5
  271.0 12.1 exponential_reduce_fusion
  283.2 13.0 convolution_convert_fusion.1
  296.2 7.7 all-gather.14.cloned.1.call-done
  313.7 143.5 %all-gather.18.cloned.1.call-done = bf16[1536,4096]{1,0:T(8,128)(2,1)} async-done(((bf16[96,4096]{1,0:T(8,128)(2,1)}), bf16[1536,4096]{1,0:T(8,128)(2,1)}) %all-gather.18.cloned.1.call-update) | async-done | bytes 12582928 | tf_op jit(solution)/shard_map/all_gather | solution.py:145
  457.2 14.5 fusion.56
  471.7 138.4 %all-gather.16.cloned.1.call-done = bf16[1536,4096]{1,0:T(8,128)(2,1)} async-done(((bf16[96,4096]{1,0:T(8,128)(2,1)}), bf16[1536,4096]{1,0:T(8,128)(2,1)}) %all-gather.16.cloned.1.call-update) | async-done | bytes 12582928 | tf_op jit(solution)/shard_map/all_gather | solution.py:144
  610.1 14.2 fusion.55
  624.3 138.8 %all-gather.20.cloned.1.call-done = bf16[4096,1536]{1,0:T(8,128)(2,1)} async-done(((bf16[256,1536]{1,0:T(8,128)(2,1)}), bf16[4096,1536]{1,0:T(8,128)(2,1)}) %all-gather.20.cloned.1.call-update) | async-done | bytes 12582928 | tf_op jit(solution)/shard_map/all_gather | solution.py:146
  763.1 23.4 multiply_convert_fusion
  786.6 14.4 fusion.57
  801.0 15.8 multiply_reduce_fusion
  831.2 15.5 bitcast_convert_fusion
  853.3 13.9 fusion.58
  867.2 40.4 %bitcast_multiply_fusion.8 = (f32[640,8,96]{0,2,1:T(8,128)}, f32[8,96,640,1]{2,1,3,0:T(8,128)}) fusion(f32[640,96]{0,1:T(8,128)} %copy-done.11, bf16[640,8,2,96]{0,3,2,1:T(8,128)(2,1)} %bitcast.157, f32[8,640,640,2]{2,1,3,0:T(8,128)} %fusion.58, f32[8,640,640,2]{2,1,3,0:T(8,128)} %get-tuple-element.50, f32[8,2,640]{2,1,0:T(2,128)S(1)} %bitcast.179, ...), kind=kOutput, calls=%fused_computation.55 | convolution fusion | flops 1330883200 | bytes 59023360 | tf_op jit(solution)/shard_map/grqk,qgrd->kgd/dot_general | solution.py:222
  915.6 10.3 fusion.22
  926.0 38.0 %fusion.8 = f32[8,96,2,640]{3,1,2,0:T(8,128)} fusion(bf16[640,8,96,1]{0,2,3,1:T(8,128)(2,1)} %bitcast.166, f32[8,640,640,2]{2,1,3,0:T(8,128)} %fusion.58, f32[8,640,640,2]{2,1,3,0:T(8,128)} %get-tuple-element.50, f32[8,2,640]{2,1,0:T(2,128)S(1)} %bitcast.180, pred[640,640]{0,1:T(8,128)(4,1)S(1)} %fusion.21), kind=kOutput, calls=%fused_computation.23 | convolution fusion | flops 1330391680 | bytes 57794560 | tf_op jit(solution)/shard_map/grqk,kgd->qgrd/dot_general | solution.py:219
  977.4 18.1 fusion.63
  995.6 17.6 fusion.62
  1013.2 18.0 fusion.61
  1046.4 75.1 %all-reduce.4 = (bf16[1536]{0:T(1024)(128)(2,1)S(1)}, bf16[1536]{0:T(1024)(128)(2,1)S(1)}) all-reduce(f32[1536]{0:T(1024)S(1)} %get-tuple-element.13, f32[1536]{0:T(1024)S(1)} %copy-done.29), channel_id=2, replica_groups=mesh['rep'=2,'fsdp'=16] {'fsdp'}, use_global_device_ids=true, to_apply=%region_11.12.clone | all-reduce | flops 3072 | bytes 18432
  1132.6 173.8 %reduce-scatter.14.cloned.1.call-done = f32[96,1536]{1,0:T(8,128)} async-done(((f32[1536,1536]{1,0:T(8,128)}), f32[96,1536]{1,0:T(8,128)}) %reduce-scatter.14.cloned.1.call-update) | async-done | bytes 589840 | tf_op jit(solution)/shard_map/reduce_scatter | solution.py:106
  1308.2 174.6 %reduce-scatter.8.cloned.1.call-done = f32[96,1536]{1,0:T(8,128)} async-done(((f32[1536,1536]{1,0:T(8,128)}), f32[96,1536]{1,0:T(8,128)}) %reduce-scatter.8.cloned.1.call-update) | async-done | bytes 589840 | tf_op jit(solution)/shard_map/reduce_scatter | solution.py:103
  1484.6 364.3 %reduce-scatter.20.cloned.1.call-done = f32[256,1536]{1,0:T(8,128)} async-done(((f32[4096,1536]{1,0:T(8,128)}), f32[256,1536]{1,0:T(8,128)}) %reduce-scatter.20.cloned.1.call-update) | async-done | bytes 1572880 | tf_op jit(solution)/shard_map/reduce_scatter | solution.py:90
  1851.3 364.1 %reduce-scatter.18.cloned.1.call-done = f32[96,4096]{1,0:T(8,128)} async-done(((f32[1536,4096]{1,0:T(8,128)}), f32[96,4096]{1,0:T(8,128)}) %reduce-scatter.18.cloned.1.call-update) | async-done | bytes 1572880 | tf_op jit(solution)/shard_map/reduce_scatter | solution.py:89
  2217.8 363.9 %reduce-scatter.16.cloned.1.call-done = f32[96,4096]{1,0:T(8,128)} async-done(((f32[1536,4096]{1,0:T(8,128)}), f32[96,4096]{1,0:T(8,128)}) %reduce-scatter.16.cloned.1.call-update) | async-done | bytes 1572880 | tf_op jit(solution)/shard_map/reduce_scatter | solution.py:88
  2590.5 14.6 add_convert_fusion
  (175 shorter events, 179.5 us)
Async XLA Ops:
  7.2 68.9 %all-gather.8.cloned.1.call-start = ((), (), s32[]{:S(2)}) async-start(), calls=%async_computation.7 | async-start | bytes 2506752 | tf_op jit(solution)/shard_map/all_gather | solution.py:139
  7.9 132.1 %all-gather.10.cloned.1.call-start = ((), (), s32[]{:S(2)}) async-start(), calls=%async_computation.8 | async-start | bytes 2506752 | tf_op jit(solution)/shard_map/all_gather | solution.py:138
  8.7 213.5 %all-gather.12.cloned.1.call-start = ((), (), s32[]{:S(2)}) async-start(), calls=%async_computation.9 | async-start | bytes 5013504 | tf_op jit(solution)/shard_map/all_gather | solution.py:137
  9.4 294.5 %all-gather.14.cloned.1.call-start = ((), (), s32[]{:S(2)}) async-start(), calls=%async_computation.10 | async-start | bytes 5013504 | tf_op jit(solution)/shard_map/all_gather | solution.py:140
  10.0 447.3 %all-gather.18.cloned.1.call-start = ((), (), s32[]{:S(2)}) async-start(), calls=%async_computation.12 | async-start | bytes 13369344 | tf_op jit(solution)/shard_map/all_gather | solution.py:145
  10.6 599.5 %all-gather.16.cloned.1.call-start = ((), (), s32[]{:S(2)}) async-start(), calls=%async_computation.11 | async-start | bytes 13369344 | tf_op jit(solution)/shard_map/all_gather | solution.py:144
  11.1 752.0 %all-gather.20.cloned.1.call-start = ((), (), s32[]{:S(2)}) async-start(), calls=%async_computation.13 | async-start | bytes 13369344 | tf_op jit(solution)/shard_map/all_gather | solution.py:146
  11.9 1113.6 %reduce-scatter.12.cloned.1.call-start = ((), (), s32[]{:S(2)}) async-start(), calls=%async_computation.16 | async-start | bytes 5013504 | tf_op jit(solution)/shard_map/reduce_scatter | solution.py:105
  59.9 162.2 %copy-start.24 = (f32[1536]{0:T(1024)}, f32[1536]{0:T(1024)S(1)}, u32[]{:S(2)}) copy-start(f32[1536]{0:T(1024)S(1)} %convert_element_type.144) | copy-start | bytes 18436
  66.4 5.7 copy-start.3
  72.2 77.0 %copy-start.11 = (f32[640,96]{0,1:T(8,128)}, f32[640,96]{0,1:T(8,128)S(1)}, u32[]{:S(2)}) copy-start(f32[640,96]{0,1:T(8,128)S(1)} %pad_maximum_fusion.2) | copy-start | bytes 737284
  73.2 148.9 %copy-start.26 = (f32[640]{0:T(1024)}, f32[640]{0:T(1024)S(1)}, u32[]{:S(2)}) copy-start(f32[640]{0:T(1024)S(1)} %get-tuple-element.44) | copy-start | bytes 7684
  159.1 97.2 %copy-start.8 = (bf16[640,768]{0,1:T(8,128)(2,1)}, bf16[640,768]{0,1:T(8,128)(2,1)S(1)}, u32[]{:S(2)}) copy-start(bf16[640,768]{0,1:T(8,128)(2,1)S(1)} %copy.75) | copy-start | bytes 2949124
  271.0 12.2 copy-start.9
  786.6 14.4 copy-start.1
  786.6 35.9 %slice-start = ((s8[4718592]{0:T(1024)(128)(4,1)}), s8[4194304]{0:T(1024)(128)(4,1)S(1)}, s32[]{:S(2)}) async-start(s8[4718592]{0:T(1024)(128)(4,1)} %bitcast.163), calls=%async_computation.22 | async-start | bytes 8388608
  801.0 21.5 slice-start.1
  831.1 16.5 copy-start.25
  831.2 16.5 copy-start.27
  852.1 278.9 %reduce-scatter.10.cloned.1.call-start = ((), (), s32[]{:S(2)}) async-start(), calls=%async_computation.15 | async-start | bytes 5013504 | tf_op jit(solution)/shard_map/reduce_scatter | solution.py:104
  915.6 390.8 %reduce-scatter.14.cloned.1.call-start = ((), (), s32[]{:S(2)}) async-start(), calls=%async_computation.17 | async-start | bytes 10027008 | tf_op jit(solution)/shard_map/reduce_scatter | solution.py:106
  926.0 38.0 %copy-start.13 = (f32[640,96]{0,1:T(8,128)S(1)}, f32[640,96]{0,1:T(8,128)}, u32[]{:S(2)}) copy-start(f32[640,96]{0,1:T(8,128)} %copy-done.11) | copy-start | bytes 737284
  926.0 556.8 %reduce-scatter.8.cloned.1.call-start = ((), (), s32[]{:S(2)}) async-start(), calls=%async_computation.14 | async-start | bytes 10027008 | tf_op jit(solution)/shard_map/reduce_scatter | solution.py:103
  977.4 871.5 %reduce-scatter.20.cloned.1.call-start = ((), (), s32[]{:S(2)}) async-start(), calls=%async_computation.20 | async-start | bytes 26738688 | tf_op jit(solution)/shard_map/reduce_scatter | solution.py:90
  995.5 1219.8 %reduce-scatter.18.cloned.1.call-start = ((), (), s32[]{:S(2)}) async-start(), calls=%async_computation.19 | async-start | bytes 26738688 | tf_op jit(solution)/shard_map/reduce_scatter | solution.py:89
  1013.2 1568.5 %reduce-scatter.16.cloned.1.call-start = ((), (), s32[]{:S(2)}) async-start(), calls=%async_computation.18 | async-start | bytes 26738688 | tf_op jit(solution)/shard_map/reduce_scatter | solution.py:88
  1031.2 1577.2 %all-reduce.10.cloned.1.call-start = ((), (), s32[]{:S(2)}) async-start(), calls=%async_computation.21 | async-start | bytes 6488064 | tf_op jit(solution)/shard_map/psum | solution.py:110
  1036.0 5.5 copy-start.14
  1851.3 732.8 %copy-start.28 = (f32[640]{0:T(1024)S(1)}, f32[640]{0:T(1024)}, u32[]{:S(2)}) copy-start(f32[640]{0:T(1024)} %get-tuple-element.43) | copy-start | bytes 7684
  2584.1 6.4 copy-start.2
  2608.4 9.5 copy-start.23
  2608.4 10.8 copy-start.22
  (15 other events, 36.4 us)
Sparse Core Ops, SparseCore 0:
  10.8 65.2 all-gather.7
  78.9 61.0 all-gather.9
  142.9 79.2 all-gather.11
  224.8 79.0 all-gather.13
  306.6 150.6 all-gather.17
  459.9 150.1 all-gather.15
  612.9 150.1 all-gather.19
  852.2 135.8 reduce-scatter.11
  994.1 136.8 reduce-scatter.9
  1136.5 169.8 reduce-scatter.13
  1313.0 169.7 reduce-scatter.7
  1488.4 360.4 reduce-scatter.19
  1854.7 360.6 reduce-scatter.17
  2221.0 360.6 reduce-scatter.15
  2585.6 22.7 all-reduce.9
where the time goes:
time: 2640 us; the launch traced here: 2630 us
  waiting for transfers between devices  2000 us (76%)
  matrix products  353 us (13%)
  blocking collectives  122 us (5%)
  other arithmetic  78.9 us (3%)
  local copies, waits for them, and re-layouts  52.9 us (2%)
    reduce_scatter x1, waiting for transfers between devices, reduce_ffn(): lax.psum_scatter(grad_down, 'fsdp', scatter_dimension=0, tiled=True)  364 us
    reduce_scatter x1, waiting for transfers between devices, reduce_ffn(): lax.psum_scatter(grad_up, 'fsdp', scatter_dimension=0, tiled=True)  364 us
    reduce_scatter x1, waiting for transfers between devices, reduce_ffn(): lax.psum_scatter(grad_gate, 'fsdp', scatter_dimension=0, tiled=True)  364 us
    reduce_scatter x1, waiting for transfers between devices, reduce_attn(): lax.psum_scatter(grad_query, 'fsdp', scatter_dimension=0, tiled=True)  175 us
    reduce_scatter x1, waiting for transfers between devices, reduce_attn(): lax.psum_scatter(grad_out, 'fsdp', scatter_dimension=0, tiled=True)  174 us
    all_gather x1, waiting for transfers between devices, on_device(): lax.all_gather(w_up, 'fsdp', axis=0, tiled=True)  144 us
    all_gather x1, waiting for transfers between devices, on_device(): lax.all_gather(w_down, 'fsdp', axis=0, tiled=True)  139 us
    all_gather x1, waiting for transfers between devices, on_device(): lax.all_gather(w_gate, 'fsdp', axis=0, tiled=True)  138 us
  transfers between devices with their start and end apart: 15, of which 14 were waited for; matrix products, arithmetic and copies ran while one was open for 14% of the time, Pallas kernels for 0%

commit v1 on v0

v1 whole, which is shorter than its diff:
```python
import functools
import math

import jax
import jax.numpy as jnp
from jax import lax
from jax.experimental import pallas as pl
from jax.experimental.pallas import tpu as pltpu
from jax.sharding import PartitionSpec as P

H = 16
KV = 8
HD = 96
LANES = 128
BLOCKS = 16
TILE = 128
SLAB = 512
CHUNKS = 2

epsilon = 1e-05
rope_base = 100000.0
masked_score = -1e30
low = jnp.bfloat16
wide = jnp.float32


class Routes:
    def __init__(self, count):
        self.count = count
        self.direct = count == BLOCKS
        self.fold = count // BLOCKS

    def place(self):
        zero = jnp.int32(0)
        if not self.direct:
            return zero, zero, zero
        index = lax.axis_index("fsdp")
        return index // 4, (index // 2) % 2, index % 2

    def hop(self, array, step):
        pairs = []
        for source in range(BLOCKS):
            z, y, x = source // 4, (source // 2) % 2, source % 2
            z, y, x = (z + step[0]) % 4, (y + step[1]) % 2, (x + step[2]) % 2
            pairs.append((source, (z * 2 + y) * 2 + x))
        return lax.ppermute(array, "fsdp", pairs)

    def regroup(self, blocks, slabs):
        parts, start = [], 0
        for rows in slabs:
            part = blocks[:, start : start + rows]
            parts.append(part.reshape(BLOCKS, self.fold * rows, part.shape[2]))
            start += rows
        return jnp.concatenate(parts, axis=1)

    def ungroup(self, blocks, slabs):
        parts, start = [], 0
        for rows in slabs:
            part = blocks[:, start : start + self.fold * rows]
            parts.append(part.reshape(self.count, rows, part.shape[2]))
            start += self.fold * rows
        return jnp.concatenate(parts, axis=1)

    def gather(self, shard, slabs):
        if not self.direct:
            blocks = self.regroup(lax.all_gather(shard, "fsdp", axis=0), slabs)
            blocks = blocks.reshape(4, 2, 2, *blocks.shape[1:])
            half = blocks.shape[3] // 2
            return (
                blocks[:, 0, 0],
                blocks[:, 0, 1],
                blocks[:, 1, 0],
                blocks[:, 1, 1, :half],
                blocks[:, 1, 1, half:],
            )
        half = shard.shape[0] // 2
        line = jnp.stack([shard] + [self.hop(shard, (-k, 0, 0)) for k in (1, 2, 3)])
        from_x = self.hop(line, (0, 0, 1))
        from_y = self.hop(line, (0, 1, 0))
        far_a = self.hop(from_x[:, :half], (0, 1, 0))
        far_b = self.hop(from_y[:, half:], (0, 0, 1))
        return line, from_x, from_y, far_a, far_b

    def scatter(self, pieces, slabs):
        to_x, to_y, late_x, late_y, own = pieces
        if not self.direct:
            far = jnp.concatenate([to_x[0], to_y[0]], axis=1)
            near_x = jnp.concatenate([to_x[1], late_x], axis=1)
            near_y = jnp.concatenate([late_y, to_y[1]], axis=1)
            blocks = jnp.stack([jnp.stack([own, near_x], 1), jnp.stack([near_y, far], 1)], 1)
            blocks = self.ungroup(blocks.reshape(BLOCKS, *own.shape[1:]), slabs)
            return lax.psum_scatter(blocks, "fsdp", scatter_dimension=0, tiled=True)[0].astype(wide)
        half = own.shape[1] // 2
        got_x = self.hop(to_x, (0, 0, 1))
        got_y = self.hop(to_y, (0, 1, 0))
        more_x = self.hop(late_x + got_y[0], (0, 0, 1))
        more_y = self.hop(late_y + got_x[0], (0, 1, 0))

        def summed(k):
            upper = own[k, :half].astype(wide) + got_x[1, k].astype(wide) + more_y[k].astype(wide)
            lower = own[k, half:].astype(wide) + got_y[1, k].astype(wide) + more_x[k].astype(wide)
            return jnp.concatenate([upper, lower], axis=0)

        total = summed(0)
        for k in (1, 2, 3):
            total = total + self.hop(summed(k).astype(own.dtype), (k, 0, 0)).astype(wide)
        return total


def swap(array):
    return lax.ppermute(array, "rep", [(0, 1), (1, 0)])


def block_index(place_ref, k, dy, dx):
    z, y, x = place_ref[0], place_ref[1], place_ref[2]
    return (lax.rem(z + k, 4) * 2 + (y + dy - 2 * y * dy)) * 2 + (x + dx - 2 * x * dx)


def piece_rows(pieces, k, dy, dx, row, rows, half):
    line, from_x, from_y, far_a, far_b = pieces
    if (dy, dx) == (0, 0):
        return line.at[k, pl.ds(row, rows)]
    if (dy, dx) == (0, 1):
        return from_x.at[k, pl.ds(row, rows)]
    if (dy, dx) == (1, 0):
        return from_y.at[k, pl.ds(row, rows)]
    if row < half:
        return far_a.at[k, pl.ds(row, rows)]
    return far_b.at[k, pl.ds(row - half, rows)]


def grad_rows(outs, k, dy, dx, row, rows, half):
    to_x, to_y, late_x, late_y, own = outs
    first = row < half
    at = pl.ds(row if first else row - half, rows)
    if (dy, dx) == (0, 0):
        return own.at[k, pl.ds(row, rows)]
    if (dy, dx) == (0, 1):
        return to_x.at[1, k, at] if first else late_x.at[k, at]
    if (dy, dx) == (1, 0):
        return late_y.at[k, at] if first else to_y.at[1, k, at]
    return to_x.at[0, k, at] if first else to_y.at[0, k, at]


class Slab:
    def __init__(self, matrix, row, rows, stride, offset, column, width):
        self.matrix, self.row, self.rows = matrix, row, rows
        self.stride, self.offset = stride, offset
        self.column, self.width = column, width

    def of(self, refs, block):
        rows = pl.ds(pl.multiple_of(block * self.stride + self.offset, 16), self.rows)
        return refs[self.matrix].at[rows, pl.ds(self.column, self.width)]


def all_blocks():
    for k in range(4):
        for dy in range(2):
            for dx in range(2):
                yield k, dy, dx


def assemble_kernel(slabs, half, pads, matrices, place_ref, *refs):
    pieces = refs[:5]
    outs = refs[5 : 5 + matrices]
    sems = refs[5 + matrices]
    if pads:
        zeros = jnp.zeros((LANES - HD, outs[0].shape[1]), low)
        for block in range(BLOCKS):
            outs[0][pl.ds(block * LANES + HD, LANES - HD), :] = zeros
    for k, dy, dx in all_blocks():
        block = block_index(place_ref, k, dy, dx)
        for slab in slabs:
            source = piece_rows(pieces, k, dy, dx, slab.row, slab.rows, half)
            pltpu.make_async_copy(source, slab.of(outs, block), sems.at[slab.matrix]).start()
    for index, out in enumerate(outs):
        if pads:
            out = out.at[pl.ds(0, BLOCKS * HD)]
        pltpu.make_async_copy(out, out, sems.at[index]).wait()


def assemble(place, pieces, slabs, shapes, pads=False):
    half = pieces[0].shape[1] // 2
    any_space = pl.BlockSpec(memory_space=pl.ANY)
    whole = [pl.BlockSpec(shape, lambda i, place: (0, 0)) for shape in shapes]
    size = sum(math.prod(shape) for shape in shapes)
    return pl.pallas_call(
        functools.partial(assemble_kernel, slabs, half, pads, len(shapes)),
        grid_spec=pltpu.PrefetchScalarGridSpec(
            num_scalar_prefetch=1,
            grid=(1,),
            in_specs=[any_space] * 5,
            out_specs=whole,
            scratch_shapes=[pltpu.SemaphoreType.DMA((len(shapes),))],
        ),
        out_shape=[jax.ShapeDtypeStruct(shape, low) for shape in shapes],
        compiler_params=pltpu.CompilerParams(vmem_limit_bytes=48 * 2**20),
        cost_estimate=pl.CostEstimate(flops=0, bytes_accessed=4 * size, transcendentals=0),
        name="assemble",
    )(place, *pieces)


def cut_kernel(slabs, half, matrices, place_ref, *refs):
    sources = refs[:matrices]
    outs = refs[matrices : matrices + 5]
    sems = refs[matrices + 5]
    for k, dy, dx in all_blocks():
        block = block_index(place_ref, k, dy, dx)
        for slab in slabs:
            target = grad_rows(outs, k, dy, dx, slab.row, slab.rows, half)
            which = {(0, 0): 4, (0, 1): 0 if slab.row < half else 2}.get((dy, dx))
            if which is None:
                if (dy, dx) == (1, 0):
                    which = 3 if slab.row < half else 1
                else:
                    which = 0 if slab.row < half else 1
            pltpu.make_async_copy(slab.of(sources, block), target, sems.at[which]).start()
    for index, out in enumerate(outs):
        pltpu.make_async_copy(out, out, sems.at[index]).wait()


def cut(place, grads, slabs, rows, width):
    half = rows // 2
    any_space = pl.BlockSpec(memory_space=pl.ANY)
    shapes = [(2, 4, half, width)] * 2 + [(4, half, width)] * 2 + [(4, rows, width)]
    size = sum(math.prod(shape) for shape in shapes)
    return pl.pallas_call(
        functools.partial(cut_kernel, slabs, half, len(grads)),
        grid_spec=pltpu.PrefetchScalarGridSpec(
            num_scalar_prefetch=1,
            grid=(1,),
            in_specs=[pl.BlockSpec(g.shape, lambda i, place: (0, 0)) for g in grads],
            out_specs=[any_space] * 5,
            scratch_shapes=[pltpu.SemaphoreType.DMA((5,))],
        ),
        out_shape=[jax.ShapeDtypeStruct(shape, low) for shape in shapes],
        compiler_params=pltpu.CompilerParams(vmem_limit_bytes=48 * 2**20),
        cost_estimate=pl.CostEstimate(flops=0, bytes_accessed=4 * size, transcendentals=0),
        name="cut",
    )(place, *grads)


def turn_table(position):
    half_size = HD // 2
    frequency = rope_base ** (-jnp.arange(half_size, dtype=wide) * 2.0 / HD)
    angle = position.astype(wide)[:, None] * frequency[None, :]
    gap = jnp.zeros((position.shape[0], LANES // 2 - half_size), wide)
    cosine, sine = jnp.cos(angle), jnp.sin(angle)
    return (
        jnp.concatenate([cosine, gap, cosine, gap], axis=1),
        jnp.concatenate([-sine, gap, sine, gap], axis=1),
    )


def qkv_kernel(x_ref, w_ref, cos_ref, sin_ref, q_ref, k_ref, v_ref):
    half = HD // 2
    gap = jnp.zeros((x_ref.shape[0], LANES // 2 - half), wide)
    heads = q_ref.shape[1] // LANES
    groups = k_ref.shape[1] // LANES
    step = 4
    for first in range(0, heads + 2 * groups, step):
        part = jnp.dot(
            x_ref[...], w_ref[:, first * HD : (first + step) * HD], preferred_element_type=wide
        )
        for index in range(first, first + step):
            at = (index - first) * HD
            if index >= heads + groups:
                column = (index - heads - groups) * LANES
                padded = jnp.concatenate([part[:, at : at + HD], gap, gap], axis=1)
                v_ref[:, column : column + LANES] = padded.astype(low)
                continue
            padded = jnp.concatenate(
                [part[:, at : at + half], gap, part[:, at + half : at + HD], gap], axis=1
            )
            turned = pltpu.roll(padded, LANES // 2, 1)
            padded = (padded * cos_ref[...] + turned * sin_ref[...]).astype(low)
            if index < heads:
                q_ref[:, index * LANES : (index + 1) * LANES] = padded
            else:
                column = (index - heads) * LANES
                k_ref[:, column : column + LANES] = padded


def project_qkv(x, weight, cosine, sine):
    count, depth = x.shape
    tile = 256
    heads, groups = H // 2, KV // 2
    row = lambda width: pl.BlockSpec((tile, width), lambda i: (i, 0))
    return pl.pallas_call(
        qkv_kernel,
        grid=(count // tile,),
        in_specs=[
            row(depth),
            pl.BlockSpec(weight.shape, lambda i: (0, 0)),
            row(LANES),
            row(LANES),
        ],
        out_specs=[row(heads * LANES), row(groups * LANES), row(groups * LANES)],
        out_shape=[
            jax.ShapeDtypeStruct((count, heads * LANES), low),
            jax.ShapeDtypeStruct((count, groups * LANES), low),
            jax.ShapeDtypeStruct((count, groups * LANES), low),
        ],
        compiler_params=pltpu.CompilerParams(vmem_limit_bytes=48 * 2**20),
        cost_estimate=pl.CostEstimate(
            flops=2 * count * depth * weight.shape[1],
            bytes_accessed=2 * (2 * count * depth + weight.size),
            transcendentals=0,
        ),
        name="project_qkv",
    )(x, weight, cosine, sine)


def fill_bias(bias_ref, column_ref, row_ref):
    size = bias_ref.shape[0]
    for start in range(0, size, TILE):
        shape = (TILE, size)
        slots = lax.broadcasted_iota(jnp.int32, shape, 0) + start
        keys = lax.broadcasted_iota(jnp.int32, shape, 1)
        same = column_ref[start : start + TILE, :] == row_ref[0]
        allowed = same & (keys <= slots)
        bias_ref[start : start + TILE, :] = jnp.where(allowed, 0.0, masked_score)


def across(left, right):
    return lax.dot_general(left, right, (((1,), (1,)), ((), ())), preferred_element_type=wide)


def down(left, right):
    return lax.dot_general(left, right, (((0,), (0,)), ((), ())), preferred_element_type=wide)


def attend_kernel(q_ref, k_ref, v_ref, column_ref, row_ref, out_ref, total_ref, bias_ref):
    group = pl.program_id(1)
    size = q_ref.shape[0]

    @pl.when(group == 0)
    def _():
        fill_bias(bias_ref, column_ref, row_ref)
        total_ref[...] = jnp.zeros_like(total_ref)

    lane = lax.broadcasted_iota(jnp.int32, (TILE, LANES), 1)
    for start in range(0, size, TILE):
        stop = start + TILE
        for head in range(2):
            columns = slice(head * LANES, (head + 1) * LANES)
            raw = across(q_ref[start:stop, columns], k_ref[:stop, :])
            scores = raw * HD ** (-0.5) + bias_ref[start:stop, :stop]
            top = jnp.max(scores, axis=-1, keepdims=True)
            powers = jnp.exp(scores - top)
            amount = jnp.sum(powers, axis=-1, keepdims=True)
            probs = (powers * (1.0 / amount)).astype(low)
            mixed = jnp.dot(probs, v_ref[:stop, :], preferred_element_type=wide)
            out_ref[start:stop, columns] = mixed.astype(low)
            total = top + jnp.log(amount)
            total_ref[start:stop, :] = jnp.where(
                lane == 2 * group + head, total, total_ref[start:stop, :]
            )


def attention_specs(size):
    return dict(
        pair=pl.BlockSpec((size, 2 * LANES), lambda b, g: (b, g)),
        one=pl.BlockSpec((size, LANES), lambda b, g: (b, g)),
        shared=pl.BlockSpec((size, LANES), lambda b, g: (b, 0)),
        column=pl.BlockSpec((size, 1), lambda b, g: (b, 0)),
        row=pl.BlockSpec((1, 1, size), lambda b, g: (b, 0, 0)),
    )


def attend(q, k, v, segment):
    blocks, size = segment.shape
    count = blocks * size
    spec = attention_specs(size)
    work = q.shape[1] // LANES * blocks * size * size
    return pl.pallas_call(
        attend_kernel,
        grid=(blocks, k.shape[1] // LANES),
        in_specs=[spec["pair"], spec["one"], spec["one"], spec["column"], spec["row"]],
        out_specs=[spec["pair"], spec["shared"]],
        out_shape=[
            jax.ShapeDtypeStruct(q.shape, low),
            jax.ShapeDtypeStruct((count, LANES), wide),
        ],
        scratch_shapes=[pltpu.VMEM((size, size), wide)],
        compiler_params=pltpu.CompilerParams(vmem_limit_bytes=48 * 2**20),
        cost_estimate=pl.CostEstimate(
            flops=8 * work * LANES, bytes_accessed=4 * q.size, transcendentals=work
        ),
        name="attend",
    )(q, k, v, segment.reshape(count, 1), segment.reshape(blocks, 1, size))


def attend_back_kernel(
    q_ref,
    k_ref,
    v_ref,
    grad_ref,
    total_ref,
    column_ref,
    row_ref,
    cos_ref,
    sin_ref,
    dq_ref,
    dk_ref,
    dv_ref,
    bias_ref,
    dk_sum,
    dv_sum,
):
    group = pl.program_id(1)
    size = q_ref.shape[0]

    @pl.when(group == 0)
    def _():
        fill_bias(bias_ref, column_ref, row_ref)

    def turned_back(grad, rows):
        turned = pltpu.roll(grad, LANES // 2, 1)
        return (grad * cos_ref[rows, :] - turned * sin_ref[rows, :]).astype(low)

    dk_sum[...] = jnp.zeros_like(dk_sum)
    dv_sum[...] = jnp.zeros_like(dv_sum)
    lane = lax.broadcasted_iota(jnp.int32, (TILE, LANES), 1)
    for start in range(0, size, TILE):
        stop = start + TILE
        for head in range(2):
            columns = slice(head * LANES, (head + 1) * LANES)
            queries = q_ref[start:stop, columns]
            grads = grad_ref[start:stop, columns]
            total = jnp.sum(
                jnp.where(lane == 2 * group + head, total_ref[start:stop, :], 0.0),
                axis=-1,
                keepdims=True,
            )
            raw = across(queries, k_ref[:stop, :])
            probs = jnp.exp(raw * HD ** (-0.5) + bias_ref[start:stop, :stop] - total)
            dv_sum[:stop, :] += down(probs.astype(low), grads)
            grad_probs = across(grads, v_ref[:stop, :])
            weighted = probs * grad_probs
            delta = jnp.sum(weighted, axis=-1, keepdims=True)
            grad_raw = ((weighted - probs * delta) * HD ** (-0.5)).astype(low)
            dq = jnp.dot(grad_raw, k_ref[:stop, :], preferred_element_type=wide)
            dq_ref[start:stop, columns] = turned_back(dq, slice(start, stop))
            dk_sum[:stop, :] += down(grad_raw, queries)
    dv_ref[...] = dv_sum[...].astype(low)
    dk_ref[...] = turned_back(dk_sum[...], slice(None))


def attend_back(q, k, v, grad, total, segment, cosine, sine):
    blocks, size = segment.shape
    count = blocks * size
    spec = attention_specs(size)
    work = q.shape[1] // LANES * blocks * size * size
    return pl.pallas_call(
        attend_back_kernel,
        grid=(blocks, k.shape[1] // LANES),
        in_specs=[
            spec["pair"],
            spec["one"],
            spec["one"],
            spec["pair"],
            spec["shared"],
            spec["column"],
            spec["row"],
            spec["shared"],
            spec["shared"],
        ],
        out_specs=[spec["pair"], spec["one"], spec["one"]],
        out_shape=[
            jax.ShapeDtypeStruct(q.shape, low),
            jax.ShapeDtypeStruct(k.shape, low),
            jax.ShapeDtypeStruct(v.shape, low),
        ],
        scratch_shapes=[
            pltpu.VMEM((size, size), wide),
            pltpu.VMEM((size, LANES), wide),
            pltpu.VMEM((size, LANES), wide),
        ],
        compiler_params=pltpu.CompilerParams(vmem_limit_bytes=48 * 2**20),
        cost_estimate=pl.CostEstimate(
            flops=20 * work * LANES, bytes_accessed=10 * q.size, transcendentals=work
        ),
        name="attend_back",
    )(
        q,
        k,
        v,
        grad,
        total,
        segment.reshape(count, 1),
        segment.reshape(blocks, 1, size),
        cosine,
        sine,
    )


def squeeze_kernel(dq_ref, dk_ref, dv_ref, out_ref):
    half = HD // 2
    parts = []
    for ref in (dq_ref, dk_ref):
        for at in range(0, ref.shape[1], LANES):
            head = ref[:, at : at + LANES].astype(wide)
            parts.append(head[:, :half])
            parts.append(head[:, LANES // 2 : LANES // 2 + half])
    for at in range(0, dv_ref.shape[1], LANES):
        parts.append(dv_ref[:, at : at + LANES].astype(wide)[:, :HD])
    out_ref[...] = jnp.concatenate(parts, axis=1).astype(low)


def squeeze(dq, dk, dv):
    count = dq.shape[0]
    tile = 256
    width = (dq.shape[1] + dk.shape[1] + dv.shape[1]) // LANES * HD
    row = lambda columns: pl.BlockSpec((tile, columns), lambda i: (i, 0))
    return pl.pallas_call(
        squeeze_kernel,
        grid=(count // tile,),
        in_specs=[row(dq.shape[1]), row(dk.shape[1]), row(dv.shape[1])],
        out_specs=row(width),
        out_shape=jax.ShapeDtypeStruct((count, width), low),
        cost_estimate=pl.CostEstimate(
            flops=0, bytes_accessed=4 * count * width, transcendentals=0
        ),
        name="squeeze",
    )(dq, dk, dv)


def layout(length_row, count):
    ends = jnp.cumsum(length_row)
    slots = jnp.arange(count, dtype=jnp.int32)
    passed = (slots[:, None] >= ends[None, :]).astype(jnp.int32)
    segment = jnp.sum(passed, axis=1)
    position = slots - jnp.sum(passed * length_row[None, :], axis=1)
    return position, segment


def normalize(hidden, gain):
    scale = lax.rsqrt(jnp.mean(hidden * hidden, axis=-1, keepdims=True) + epsilon)
    return (hidden * scale * gain, scale)


def norm_back(hidden, scale, gain, incoming):
    weighted = incoming * gain
    inner = jnp.mean(weighted * hidden, axis=-1, keepdims=True)
    return (
        scale * weighted - hidden * scale**3 * inner,
        jnp.sum(incoming * hidden * scale, axis=0),
    )


def project(left, weight):
    return jnp.dot(left, weight, preferred_element_type=wide)


def in_order(core, mine, other, axis):
    return jnp.where(
        core == 0,
        jnp.concatenate([mine, other], axis=axis),
        jnp.concatenate([other, mine], axis=axis),
    )


def on_device(
    routes,
    tokens,
    lengths,
    attn_gain,
    w_query,
    w_key,
    w_value,
    w_out,
    ffn_gain,
    w_gate,
    w_up,
    w_down,
    cotangent,
):
    count, width = tokens.shape
    n = routes.count
    owned = attn_gain.shape[0]
    units = w_down.shape[0]
    core = lax.axis_index("rep")
    z, y, x = routes.place()
    place = jnp.stack([z, y, x]).astype(jnp.int32)
    half_width = width // 2
    block_rows = width // BLOCKS
    quarter = units // (2 * CHUNKS)

    qkv_shard = jnp.concatenate(
        [
            lax.dynamic_slice_in_dim(w, core * (w.shape[1] // 2), w.shape[1] // 2, axis=1)
            for w in (w_query, w_key, w_value)
        ],
        axis=1,
    )
    out_shard = lax.dynamic_slice_in_dim(w_out, core * half_width, half_width, axis=1)

    def units_of(weight, chunk):
        split = weight.reshape(weight.shape[0], n, 2 * CHUNKS, quarter)
        part = lax.dynamic_index_in_dim(split, CHUNKS * core + chunk, axis=2, keepdims=False)
        return part.reshape(weight.shape[0], n * quarter)

    def slabs_of(weight):
        return [weight[:, at : at + SLAB] for at in range(0, weight.shape[1], SLAB)]

    ffn_shards = []
    for chunk in range(CHUNKS):
        rows = lax.dynamic_slice_in_dim(w_down, (CHUNKS * core + chunk) * quarter, quarter, axis=0)
        ffn_shards.append(
            jnp.concatenate(
                slabs_of(units_of(w_gate, chunk)) + slabs_of(units_of(w_up, chunk)) + slabs_of(rows),
                axis=0,
            )
        )
    chunk_units = n * quarter
    gate_slabs = chunk_units // SLAB
    down_slabs = width // SLAB
    ffn_parts = [owned] * (2 * gate_slabs) + [quarter] * down_slabs
    ffn_plan, row = [], 0
    for matrix in range(2):
        for at in range(gate_slabs):
            ffn_plan.append(Slab(matrix, row, block_rows, block_rows, 0, at * SLAB, SLAB))
            row += block_rows
    block_units = chunk_units // BLOCKS
    for at in range(down_slabs):
        ffn_plan.append(Slab(2, row, block_units, block_units, 0, at * SLAB, SLAB))
        row += block_units
    ffn_rows = row
    ffn_shapes = [(width, chunk_units), (width, chunk_units), (chunk_units, width)]
    cut_half = block_rows // 2
    square_plan = [
        Slab(0, at, cut_half, block_rows, at, 0, width) for at in (0, cut_half)
    ]
    out_plan = [Slab(0, at, cut_half, LANES, at, 0, half_width) for at in (0, cut_half)]

    other_tokens = swap(tokens)
    both_cotangents = jnp.concatenate([cotangent, swap(cotangent)], axis=0)
    both_lengths = (lengths[0], swap(lengths)[0])
    laid = [layout(row, count) for row in both_lengths]
    segment = jnp.stack([item[1] for item in laid])
    cosine, sine = turn_table(jnp.concatenate([item[0] for item in laid]))

    small = jnp.zeros((8, LANES), wide)
    small = small.at[0, :owned].set(attn_gain.astype(wide))
    small = small.at[4, :owned].set(ffn_gain.astype(wide))
    if routes.direct:
        line, from_x, from_y, far_a, far_b = routes.gather(small, [8])
        far = jnp.concatenate([far_a, far_b], axis=1)
        blocks = jnp.stack([jnp.stack([line, from_x], 1), jnp.stack([from_y, far], 1)], 1)
        blocks = blocks[(jnp.arange(4) - z) % 4]
        blocks = blocks[:, jnp.arange(2) ^ y]
        blocks = blocks[:, :, jnp.arange(2) ^ x].reshape(BLOCKS, 8, LANES)
    else:
        blocks = lax.all_gather(small, "fsdp", axis=0)
    gain_one = blocks[:, 0, :owned].reshape(width)
    gain_two = blocks[:, 4, :owned].reshape(width)

    qkv_pieces = routes.gather(qkv_shard, [owned])
    out_pieces = routes.gather(out_shard, [owned])
    ffn_pieces = [routes.gather(shard, ffn_parts) for shard in ffn_shards]

    hidden = tokens.astype(wide)
    normed, scale_one = normalize(hidden, gain_one)
    other_normed, _ = normalize(other_tokens.astype(wide), gain_one)
    normed_low = jnp.concatenate([normed.astype(low), other_normed.astype(low)], axis=0)
    (qkv_full,) = assemble(place, qkv_pieces, square_plan, [(width, width)])
    queries, keys, values = project_qkv(normed_low, qkv_full, cosine, sine)
    attended, total = attend(queries, keys, values, segment)
    other_attended = swap(attended)
    (out_mine,) = assemble(place, out_pieces, out_plan, [(H * LANES, half_width)], pads=True)
    out_full = in_order(core, out_mine, swap(out_mine), 1)
    attended_own = in_order(core, attended[:count], other_attended[count:], 1)
    attended_other = in_order(core, attended[count:], other_attended[:count], 1)
    middle = hidden + project(attended_own, out_full)
    normed_two, scale_two = normalize(middle, gain_two)
    normed_two_own = normed_two.astype(low)
    normed_two_low = jnp.concatenate([normed_two_own, swap(normed_two_own)], axis=0)

    output_part, normed_part = None, None
    ffn_owned = []
    for chunk in range(CHUNKS):
        gate_w, up_w, down_w = assemble(place, ffn_pieces[chunk], ffn_plan, ffn_shapes)
        gate = project(normed_two_low, gate_w)
        upward = project(normed_two_low, up_w)
        sigma = jax.nn.sigmoid(gate)
        inner_low = (gate * sigma * upward).astype(low)
        grad_inner = across(both_cotangents, down_w)
        grad_gate_low = (grad_inner * upward * sigma * (1.0 + gate * (1.0 - sigma))).astype(low)
        grad_up_low = (grad_inner * gate * sigma).astype(low)
        grads = (
            down(normed_two_low, grad_gate_low).astype(low),
            down(normed_two_low, grad_up_low).astype(low),
            down(inner_low, both_cotangents).astype(low),
        )
        ffn_owned.append(
            routes.scatter(cut(place, grads, ffn_plan, ffn_rows, SLAB), ffn_parts)
        )
        out_term = project(inner_low, down_w)
        normed_term = across(grad_gate_low, gate_w) + across(grad_up_low, up_w)
        output_part = out_term if output_part is None else output_part + out_term
        normed_part = normed_term if normed_part is None else normed_part + normed_term
    output = (middle + output_part[:count] + swap(output_part[count:])).astype(low)
    grad_normed_two = normed_part[:count] + swap(normed_part[count:])

    middle_part, grad_ffn_gain = norm_back(middle, scale_two, gain_two, grad_normed_two)
    grad_middle = cotangent.astype(wide) + middle_part
    grad_branch = grad_middle.astype(low)

    branch_mine = lax.dynamic_slice_in_dim(grad_branch, core * half_width, half_width, axis=1)
    branch_sent = lax.dynamic_slice_in_dim(grad_branch, (1 - core) * half_width, half_width, axis=1)
    branch_columns = jnp.concatenate([branch_mine, swap(branch_sent)], axis=0)
    grad_out = down(jnp.concatenate([attended_own, attended_other], axis=0), branch_columns)
    out_owned = routes.scatter(
        cut(place, (grad_out.astype(low),), out_plan, block_rows, half_width), [owned]
    )
    grad_attended = across(grad_branch, out_full).astype(low)
    half_heads = H // 2 * LANES
    attended_mine = lax.dynamic_slice_in_dim(grad_attended, core * half_heads, half_heads, axis=1)
    attended_sent = lax.dynamic_slice_in_dim(
        grad_attended, (1 - core) * half_heads, half_heads, axis=1
    )
    grad_heads = jnp.concatenate([attended_mine, swap(attended_sent)], axis=0)
    grad_qkv = squeeze(
        *attend_back(queries, keys, values, grad_heads, total, segment, cosine, sine)
    )
    qkv_owned = routes.scatter(
        cut(place, (down(normed_low, grad_qkv).astype(low),), square_plan, block_rows, width),
        [owned],
    )
    normed_part = across(grad_qkv, qkv_full)
    grad_normed = normed_part[:count] + swap(normed_part[count:])
    hidden_part, grad_attn_gain = norm_back(hidden, scale_one, gain_one, grad_normed)
    grad_tokens = grad_middle + hidden_part

    gains = jnp.zeros((n, 8, LANES), wide)
    gains = gains.at[:, 0, :owned].set(grad_attn_gain.reshape(n, owned))
    gains = gains.at[:, 4, :owned].set(grad_ffn_gain.reshape(n, owned))
    gains = gains + swap(gains)
    if routes.direct:
        blocks = gains.reshape(4, 2, 2, 8, LANES)[(jnp.arange(4) + z) % 4]
        blocks = blocks[:, jnp.arange(2) ^ y][:, :, jnp.arange(2) ^ x]
        far, near_x, near_y = blocks[:, 1, 1], blocks[:, 0, 1], blocks[:, 1, 0]
        pieces = (
            jnp.stack([far[:, :4], near_x[:, :4]]),
            jnp.stack([far[:, 4:], near_y[:, 4:]]),
            near_x[:, 4:],
            near_y[:, :4],
            blocks[:, 0, 0],
        )
        gains = routes.scatter(pieces, [8])
    else:
        gains = lax.psum_scatter(gains, "fsdp", scatter_dimension=0, tiled=True)[0]

    def both(mine):
        other = swap(mine.astype(low)).astype(wide)
        return jnp.where(core == 0, mine, other), jnp.where(core == 0, other, mine)

    qkv_halves = both(qkv_owned)
    q_columns, k_columns = w_query.shape[1] // 2, w_key.shape[1] // 2
    at = 0
    attn_grads = []
    for columns in (q_columns, k_columns, k_columns):
        attn_grads.append(
            jnp.concatenate([item[:, at : at + columns] for item in qkv_halves], axis=1)
        )
        at += columns
    grad_out_rows = jnp.concatenate(both(out_owned), axis=1)
    ffn_halves = [both(item) for item in ffn_owned]
    quarters = [ffn_halves[chunk][part] for part in range(2) for chunk in range(CHUNKS)]
    span = owned * gate_slabs

    def matrix_rows(packed, start, rows, slabs):
        return jnp.concatenate(
            [packed[start + s * rows : start + (s + 1) * rows] for s in range(slabs)], axis=1
        )

    def unit_columns(start):
        parts = [
            matrix_rows(item, start, owned, gate_slabs).reshape(owned, n, quarter)
            for item in quarters
        ]
        return jnp.stack(parts, axis=2).reshape(owned, n * units)

    grad_gate = unit_columns(0)
    grad_up = unit_columns(span)
    grad_down = jnp.concatenate(
        [matrix_rows(item, 2 * span, quarter, down_slabs) for item in quarters], axis=0
    )
    return (
        output,
        grad_tokens,
        gains[0, :owned],
        attn_grads[0],
        attn_grads[1],
        attn_grads[2],
        grad_out_rows,
        gains[4, :owned],
        grad_gate,
        grad_up,
        grad_down,
    )


def solution(mesh):
    rows = P(("rep", "fsdp"), None)
    split = P("fsdp", None)
    gain = P("fsdp")
    return jax.shard_map(
        functools.partial(on_device, Routes(mesh.shape["fsdp"])),
        mesh=mesh,
        in_specs=(rows, rows, gain) + (split,) * 4 + (gain,) + (split,) * 3 + (rows,),
        out_specs=(rows, rows, gain) + (split,) * 4 + (gain,) + (split,) * 3,
        check_vma=False,
    )
```

time: 2640 us -> 1040 us (0.39)
  waiting for transfers between devices: 2000 us -> 391 us
  matrix products: 353 us -> 182 us
  Pallas kernels: 0 us -> 144 us
  blocking collectives: 122 us -> 0 us
  starting transfers between devices: 0.6 us -> 110 us
  local copies, waits for them, and re-layouts: 52.9 us -> 97.6 us
  other arithmetic: 78.9 us -> 107 us
    reduce_scatter x7 -> x0, waiting for transfers between devices: 1440 us -> none  [the longest x1 364 us: reduce_ffn(): lax.psum_scatter(grad_down, 'fsdp', scatter_dimension=0, tiled=True)]
    all_gather x7 -> x0, waiting for transfers between devices: 551 us -> none  [the longest x1 144 us: on_device(): lax.all_gather(w_up, 'fsdp', axis=0, tiled=True)]
    ppermute x0 -> x86, waiting for transfers between devices: none -> 391 us  [the longest x70 390 us: hop(): return lax.ppermute(array, 'fsdp', pairs)]
    dot_general x27 -> x23, matrix products: 353 us -> 182 us  [the longest x7 65.2 us: project(): return jnp.dot(left, weight, preferred_element_type=wide)]
    pallas_call x0 -> x12, Pallas kernels: none -> 144 us  [the longest x1 38 us: attend_back(): pl.pallas_call(attend_back_kernel, grid=(blocks, k.shape[1] // LANES), in...]
    unnamed x2 -> x0, blocking collectives: 119 us -> none
    ppermute x0 -> x86, starting transfers between devices: none -> 110 us  [the longest x70 109 us: hop(): return lax.ppermute(array, 'fsdp', pairs)]
    slice x0 -> x32, local copies, waits for them, and re-layouts: none -> 28.5 us  [the longest x5 5.83 us: gather(): far_b = self.hop(from_y[:, half:], (0, 0, 1))]
  transfers between devices with their start and end apart: 15 -> 86, of which waited for: 14 -> 31; matrix products, arithmetic and copies ran while one was open for 14% -> 27% of each run, Pallas kernels for 0% -> 14%
where the time goes in v1:
time: 1040 us; the launch traced here: 1030 us
  waiting for transfers between devices  391 us (38%)
  matrix products  182 us (18%)
  Pallas kernels  144 us (14%)
  starting transfers between devices  110 us (11%)
  other arithmetic  107 us (10%)
  local copies, waits for them, and re-layouts  97.6 us (9%)
    ppermute x70, waiting for transfers between devices, hop(): return lax.ppermute(array, 'fsdp', pairs)  390 us
    ppermute x70, starting transfers between devices, hop(): return lax.ppermute(array, 'fsdp', pairs)  109 us
    dot_general x7, matrix products, project(): return jnp.dot(left, weight, preferred_element_type=wide)  65.2 us
    dot_general x8, matrix products, across(): lax.dot_general(left, right, (((1,), (1,)), ((), ())), preferred_element_...  62.6 us
    dot_general x8, matrix products, down(): lax.dot_general(left, right, (((0,), (0,)), ((), ())), preferred_element_...  54.2 us
    pallas_call x1, Pallas kernels, attend_back(): pl.pallas_call(attend_back_kernel, grid=(blocks, k.shape[1] // LANES), in...  38 us
    unnamed x265, local copies, waits for them, and re-layouts  34.3 us
    pallas_call x1, Pallas kernels, attend(): pl.pallas_call(attend_kernel, grid=(blocks, k.shape[1] // LANES), in_spec...  31.6 us
  transfers between devices with their start and end apart: 86, of which 31 were waited for; matrix products, arithmetic and copies ran while one was open for 27% of the time, Pallas kernels for 14%

profile of v1, /device:TPU:0, one launch (start us, length us, event | category | flops | bytes accessed | tf_op | source)
XLA Modules:
  0.0 1033.9 jit_solution(10794133110387367725)
XLA Ops:
  43.8 10.8 %collective-permute-done.17 = bf16[96,768]{1,0:T(8,128)(2,1)S(1)} collective-permute-done((bf16[96,768]{1,0:T(8,128)(2,1)}, bf16[96,768]{1,0:T(8,128)(2,1)S(1)}, u32[]{:S(2)}, u32[]{:S(2)}) %collective-permute-start.17) | collective-permute-done | bytes 147488 | tf_op jit(solution)/shard_map/ppermute | solution.py:46
  55.8 21.1 %collective-permute-done.10 = bf16[96,1536]{1,0:T(8,128)(2,1)S(1)} collective-permute-done((bf16[96,1536]{1,0:T(8,128)(2,1)S(1)}, bf16[96,1536]{1,0:T(8,128)(2,1)S(1)}, u32[]{:S(2)}, u32[]{:S(2)}) %collective-permute-start.10) | collective-permute-done | bytes 294944 | tf_op jit(solution)/shard_map/ppermute | solution.py:46
  76.8 23.6 %collective-permute-done.9 = bf16[96,1536]{1,0:T(8,128)(2,1)S(1)} collective-permute-done((bf16[96,1536]{1,0:T(8,128)(2,1)S(1)}, bf16[96,1536]{1,0:T(8,128)(2,1)S(1)}, u32[]{:S(2)}, u32[]{:S(2)}) %collective-permute-start.9) | collective-permute-done | bytes 294944 | tf_op jit(solution)/shard_map/ppermute | solution.py:46
  112.0 9.5 collective-permute-done.33
  122.0 10.7 %collective-permute-done.28 = bf16[576,512]{1,0:T(8,128)(2,1)S(1)} collective-permute-done((bf16[576,512]{1,0:T(8,128)(2,1)}, bf16[576,512]{1,0:T(8,128)(2,1)S(1)}, u32[]{:S(2)}, u32[]{:S(2)}) %collective-permute-start.28) | collective-permute-done | bytes 589856 | tf_op jit(solution)/shard_map/ppermute | solution.py:46
  154.2 10.0 collective-permute-done.27
  194.2 40.0 %collective-permute-done.13.refs_3_ = bf16[4,48,1536]{2,1,0:T(8,128)(2,1)S(1)} collective-permute-done((bf16[4,48,1536]{2,1,0:T(8,128)(2,1)S(1)}, bf16[4,48,1536]{2,1,0:T(8,128)(2,1)S(1)}, u32[]{:S(2)}, u32[]{:S(2)}) %collective-permute-start.13) | collective-permute-done | bytes 589856 | tf_op jit(solution)/shard_map/ppermute | solution.py:46
  234.2 51.4 %collective-permute-done.14.refs_4_ = bf16[4,48,1536]{2,1,0:T(8,128)(2,1)S(1)} collective-permute-done((bf16[4,48,1536]{2,1,0:T(8,128)(2,1)S(1)}, bf16[4,48,1536]{2,1,0:T(8,128)(2,1)S(1)}, u32[]{:S(2)}, u32[]{:S(2)}) %collective-permute-start.14) | collective-permute-done | bytes 589856 | tf_op jit(solution)/shard_map/ppermute | solution.py:46
  293.3 14.1 %project_qkv.1 = (bf16[1280,1024]{1,0:T(8,128)(2,1)}, bf16[1280,512]{1,0:T(8,128)(2,1)S(1)}, bf16[1280,512]{1,0:T(8,128)(2,1)S(1)}) custom-call(bf16[1280,1536]{1,0:T(8,128)(2,1)} %pad_maximum_fusion.x_ref, bf16[1536,1536]{1,0:T(8,128)(2,1)} %assemble.4.w_ref, f32[1280,128]{1,0:T(8,128)S(1)} %copy-done.16, f32[1280,128]{1,0:T(8,128)S(1)} %copy-done.14), custom_call_target="tpu_custom_call" | custom-call | flops 6039797760 | bytes 12582912 | tf_op jit(solution)/shard_map/project_qkv/pallas_call | solution.py:289
  307.5 31.6 %attend.1 = (bf16[1280,1024]{1,0:T(8,128)(2,1)}, f32[1280,128]{1,0:T(8,128)S(1)}) custom-call(bf16[1280,1024]{1,0:T(8,128)(2,1)} %get-tuple-element.93.q_ref, bf16[1280,512]{1,0:T(8,128)(2,1)S(1)} %get-tuple-element.94.k_ref, bf16[1280,512]{1,0:T(8,128)(2,1)S(1)} %get-tuple-element.95.v_ref, s32[1280,1]{1,0:T(8,128)S(1)} %bitcast.706, ...), custom_call_target="tpu_custom_call" | custom-call | flops 6710886400 | bytes 5242880 | tf_op jit(solution)/shard_map/attend/pallas_call | solution.py:376
  350.0 19.6 %collective-permute-done.38.refs_3_ = bf16[4,288,512]{2,1,0:T(8,128)(2,1)S(1)} collective-permute-done((bf16[4,288,512]{2,1,0:T(8,128)(2,1)S(1)}, bf16[4,288,512]{2,1,0:T(8,128)(2,1)S(1)}, u32[]{:S(2)}, u32[]{:S(2)}) %collective-permute-start.38) | collective-permute-done | bytes 1179680 | tf_op jit(solution)/shard_map/ppermute | solution.py:46
  410.5 11.3 %multiply_reduce_fusion.2 = (f32[640]{0:T(1024)S(1)}, f32[640,1536]{1,0:T(8,128)S(1)}) fusion(bf16[2048,768]{1,0:T(8,128)(2,1)} %collective-permute-done.24, bf16[2048,768]{1,0:T(8,128)(2,1)} %assemble.5, pred[]{:T(512)S(6)} %eq.8, bf16[640,1024]{1,0:T(8,128)(2,1)S(1)} %get-tuple-element.214, bf16[640,1024]{1,0:T(8,128)(2,1)S(1)} %get-tuple-element.212, ...), kind=kOutput, calls=%fused_computation.55 | convolution fusion | flops 4070571520 | bytes 14813697 | tf_op jit(solution)/shard_map/dot_general | solution.py:553
  426.0 8.1 fusion.132
  450.0 11.0 %multiply_convert_fusion.1 = (bf16[1280,1024]{1,0:T(8,128)(2,1)}, bf16[1280,1024]{1,0:T(8,128)(2,1)}, bf16[1280,1024]{1,0:T(8,128)(2,1)S(1)}) fusion(f32[1280,1024]{1,0:T(8,128)S(1)} %bitcast.757, f32[1280,1024]{1,0:T(8,128)} %fusion.100, bf16[1536,1024]{1,0:T(8,128)(2,1)S(1)} %copy-done.97, bf16[640,1536]{1,0:T(8,128)(2,1)S(1)} %collective-permute-done.25, ...), kind=kOutput, calls=%fused_computation.23 | convolution fusion | flops 4055367680 | bytes 25427968 | tf_op jit(solution)/shard_map/dot_general | solution.py:553
  474.8 11.1 %multiply_convert_fusion.3 = (bf16[1280,1024]{1,0:T(8,128)(2,1)S(1)}, bf16[1280,1024]{1,0:T(8,128)(2,1)}, bf16[1280,1024]{1,0:T(8,128)(2,1)S(1)}) fusion(f32[1280,1024]{1,0:T(8,128)} %fusion.130, f32[1280,1024]{1,0:T(8,128)} %fusion.102, bf16[1536,1024]{1,0:T(8,128)(2,1)S(1)} %copy-done.99, bf16[640,1536]{1,0:T(8,128)(2,1)S(1)} %copy-done.102, ...), kind=kOutput, calls=%fused_computation.25 | convolution fusion | flops 4055367680 | bytes 25427968 | tf_op jit(solution)/shard_map/dot_general | solution.py:553
  492.4 8.6 convolution_add_fusion
  501.0 8.1 fusion
  570.8 10.1 fusion.129
  599.7 44.1 %collective-permute-done.72 = bf16[2,4,288,512]{3,2,1,0:T(8,128)(2,1)S(1)} collective-permute-done((bf16[2,4,288,512]{3,2,1,0:T(8,128)(2,1)}, bf16[2,4,288,512]{3,2,1,0:T(8,128)(2,1)S(1)}, u32[]{:S(2)}, u32[]{:S(2)}) %collective-permute-start.72) | collective-permute-done | bytes 2359328 | tf_op jit(solution)/shard_map/ppermute | solution.py:46
  647.7 24.0 %collective-permute-done.81 = bf16[4,288,512]{2,1,0:T(8,128)(2,1)S(1)} collective-permute-done((bf16[4,288,512]{2,1,0:T(8,128)(2,1)S(1)}, bf16[4,288,512]{2,1,0:T(8,128)(2,1)S(1)}, u32[]{:S(2)}, u32[]{:S(2)}) %collective-permute-start.81) | collective-permute-done | bytes 1179680 | tf_op jit(solution)/shard_map/ppermute | solution.py:46
  677.4 15.6 %collective-permute-start.84 = (bf16[576,512]{1,0:T(8,128)(2,1)}, bf16[576,512]{1,0:T(8,128)(2,1)}, u32[]{:S(2)}, u32[]{:S(2)}) collective-permute-start(bf16[576,512]{1,0:T(8,128)(2,1)} %pad_maximum_fusion.20), channel_id=1, source_target_pairs={{0,12},{1,13},{2,14},{3,15},{4,0},{5,1},{6,2},{7,3},{8,4},{9,5},{1... | collective-permute-start | bytes 1769480 | tf_op jit(solution)/shard_map/ppermute | solution.py:46
  695.0 11.0 %collective-permute-start.83 = (bf16[576,512]{1,0:T(8,128)(2,1)}, bf16[576,512]{1,0:T(8,128)(2,1)}, u32[]{:S(2)}, u32[]{:S(2)}) collective-permute-start(bf16[576,512]{1,0:T(8,128)(2,1)} %pad_maximum_fusion.19), channel_id=1, source_target_pairs={{0,8},{1,9},{2,10},{3,11},{4,12},{5,13},{6,14},{7,15},{8,0},{9,1},... | collective-permute-start | bytes 1769480 | tf_op jit(solution)/shard_map/ppermute | solution.py:46
  725.1 9.4 convolution_convert_fusion.7
  735.2 11.3 %collective-permute-done.83 = bf16[576,512]{1,0:T(8,128)(2,1)} collective-permute-done((bf16[576,512]{1,0:T(8,128)(2,1)}, bf16[576,512]{1,0:T(8,128)(2,1)}, u32[]{:S(2)}, u32[]{:S(2)}) %collective-permute-start.83) | collective-permute-done | bytes 589856 | tf_op jit(solution)/shard_map/ppermute | solution.py:46
  753.6 40.1 %collective-permute-done.75 = bf16[576,512]{1,0:T(8,128)(2,1)} collective-permute-done((bf16[576,512]{1,0:T(8,128)(2,1)}, bf16[576,512]{1,0:T(8,128)(2,1)}, u32[]{:S(2)}, u32[]{:S(2)}) %collective-permute-start.75) | collective-permute-done | bytes 589856 | tf_op jit(solution)/shard_map/ppermute | solution.py:46
  838.0 38.0 %attend_back.1 = (bf16[1280,1024]{1,0:T(8,128)(2,1)}, bf16[1280,512]{1,0:T(8,128)(2,1)S(1)}, bf16[1280,512]{1,0:T(8,128)(2,1)S(1)}) custom-call(bf16[1280,1024]{1,0:T(8,128)(2,1)} %get-tuple-element.93.q_ref, bf16[1280,512]{1,0:T(8,128)(2,1)} %copy-done.18, bf16[1280,512]{1,0:T(8,128)(2,1)} %copy-done.19, bf16[1280,1024]{1,0:T(8,128)(2,1)} %pad_maximum_fusion.2.grad_ref, ...), custom_call_target="tpu_custom_call" | custom-call | flops 16777216000 | bytes 13107200 | tf_op jit(solution)/shard_map/attend_back/pallas_call | solution.py:455
  884.9 10.7 %convolution_convert_fusion.refs_0_ = bf16[1536,1536]{1,0:T(8,128)(2,1)} fusion(bf16[1280,1536]{1,0:T(8,128)(2,1)} %squeeze.126, bf16[640,1536]{1,0:T(8,128)(2,1)} %copy-done.32, bf16[640,1536]{1,0:T(8,128)(2,1)} %copy-done.31), kind=kOutput, calls=%fused_computation.16 | convolution fusion | flops 6050021376 | bytes 12582912 | tf_op jit(solution)/shard_map/dot_general | solution.py:330
  895.6 9.1 cut.4
  910.7 9.5 fusion.134
  924.2 14.7 %collective-permute-done.63 = bf16[4,48,768]{2,1,0:T(8,128)(2,1)S(1)} collective-permute-done((bf16[4,48,768]{2,1,0:T(8,128)(2,1)S(1)}, bf16[4,48,768]{2,1,0:T(8,128)(2,1)S(1)}, u32[]{:S(2)}, u32[]{:S(2)}) %collective-permute-start.63) | collective-permute-done | bytes 294944 | tf_op jit(solution)/shard_map/ppermute | solution.py:46
  953.0 10.5 %collective-permute-done.56 = bf16[4,48,1536]{2,1,0:T(8,128)(2,1)S(1)} collective-permute-done((bf16[4,48,1536]{2,1,0:T(8,128)(2,1)S(1)}, bf16[4,48,1536]{2,1,0:T(8,128)(2,1)S(1)}, u32[]{:S(2)}, u32[]{:S(2)}) %collective-permute-start.56) | collective-permute-done | bytes 589856 | tf_op jit(solution)/shard_map/ppermute | solution.py:46
  982.2 14.4 %collective-permute-done.58 = bf16[96,1536]{1,0:T(8,128)(2,1)} collective-permute-done((bf16[96,1536]{1,0:T(8,128)(2,1)}, bf16[96,1536]{1,0:T(8,128)(2,1)}, u32[]{:S(2)}, u32[]{:S(2)}) %collective-permute-start.58) | collective-permute-done | bytes 294944 | tf_op jit(solution)/shard_map/ppermute | solution.py:46
  (627 shorter events, 458.2 us)
Async XLA Ops:
  37.6 69.8 %collective-permute-start.35 = (bf16[576,512]{1,0:T(8,128)(2,1)}, bf16[576,512]{1,0:T(8,128)(2,1)S(1)}, u32[]{:S(2)}, u32[]{:S(2)}) collective-permute-start(bf16[576,512]{1,0:T(8,128)(2,1)} %dynamic-slice_dynamic-update-slice_fusion), channel_id=1, source_target_pairs={{0,4},{1,5},{2,6},{3,7},{4,8},{5,9},{6,10},{7,11},{8,12},{9,13},{1... | collective-permute-start | bytes 1769480 | tf_op jit(solution)/shard_map/ppermute | solution.py:46
  38.8 69.1 %collective-permute-start.34 = (bf16[576,512]{1,0:T(8,128)(2,1)}, bf16[576,512]{1,0:T(8,128)(2,1)S(1)}, u32[]{:S(2)}, u32[]{:S(2)}) collective-permute-start(bf16[576,512]{1,0:T(8,128)(2,1)} %dynamic-slice_dynamic-update-slice_fusion), channel_id=1, source_target_pairs={{0,8},{1,9},{2,10},{3,11},{4,12},{5,13},{6,14},{7,15},{8,0},{9,1},... | collective-permute-start | bytes 1769480 | tf_op jit(solution)/shard_map/ppermute | solution.py:46
  43.0 57.5 %collective-permute-start.9 = (bf16[96,1536]{1,0:T(8,128)(2,1)S(1)}, bf16[96,1536]{1,0:T(8,128)(2,1)S(1)}, u32[]{:S(2)}, u32[]{:S(2)}) collective-permute-start(bf16[96,1536]{1,0:T(8,128)(2,1)S(1)} %get-tuple-element.278), channel_id=1, source_target_pairs={{0,8},{1,9},{2,10},{3,11},{4,12},{5,13},{6,14},{7,15},{8,0},{9,1},... | collective-permute-start | bytes 884744 | tf_op jit(solution)/shard_map/ppermute | solution.py:46
  54.7 52.6 %collective-permute-start.8 = (bf16[96,1536]{1,0:T(8,128)(2,1)S(1)}, bf16[96,1536]{1,0:T(8,128)(2,1)S(1)}, u32[]{:S(2)}, u32[]{:S(2)}) collective-permute-start(bf16[96,1536]{1,0:T(8,128)(2,1)S(1)} %get-tuple-element.278), channel_id=1, source_target_pairs={{0,12},{1,13},{2,14},{3,15},{4,0},{5,1},{6,2},{7,3},{8,4},{9,5},{1... | collective-permute-start | bytes 884744 | tf_op jit(solution)/shard_map/ppermute | solution.py:46
  76.8 106.8 %collective-permute-start.7 = (bf16[640,1536]{1,0:T(8,128)(2,1)}, bf16[640,1536]{1,0:T(8,128)(2,1)}, u32[]{:S(2)}, u32[]{:S(2)}) collective-permute-start(bf16[640,1536]{1,0:T(8,128)(2,1)} %param.20), channel_id=1, source_target_pairs={{0,16},{16,0},{1,17},{17,1},{2,18},{18,2},{3,19},{19,3},{4,20},{20... | collective-permute-start | bytes 5898248 | tf_op jit(solution)/shard_map/ppermute | solution.py:111
  121.4 59.2 %collective-permute-start.11 = (bf16[4,96,1536]{2,1,0:T(8,128)(2,1)S(1)}, bf16[4,96,1536]{2,1,0:T(8,128)(2,1)}, u32[]{:S(2)}, u32[]{:S(2)}) collective-permute-start(bf16[4,96,1536]{2,1,0:T(8,128)(2,1)S(1)} %pad_maximum_fusion.7.refs_0_), channel_id=1, source_target_pairs={{0,1},{1,0},{2,3},{3,2},{4,5},{5,4},{6,7},{7,6},{8,9},{9,8},{10,11... | collective-permute-start | bytes 3538952 | tf_op jit(solution)/shard_map/ppermute | solution.py:46
  132.6 49.2 %collective-permute-start.12 = (bf16[4,96,1536]{2,1,0:T(8,128)(2,1)S(1)}, bf16[4,96,1536]{2,1,0:T(8,128)(2,1)}, u32[]{:S(2)}, u32[]{:S(2)}) collective-permute-start(bf16[4,96,1536]{2,1,0:T(8,128)(2,1)S(1)} %pad_maximum_fusion.7.refs_0_), channel_id=1, source_target_pairs={{0,2},{1,3},{2,0},{3,1},{4,6},{5,7},{6,4},{7,5},{8,10},{9,11},{10,... | collective-permute-start | bytes 3538952 | tf_op jit(solution)/shard_map/ppermute | solution.py:46
  170.9 136.5 %collective-permute-start.36 = (bf16[4,576,512]{2,1,0:T(8,128)(2,1)S(1)}, bf16[4,576,512]{2,1,0:T(8,128)(2,1)}, u32[]{:S(2)}, u32[]{:S(2)}) collective-permute-start(bf16[4,576,512]{2,1,0:T(8,128)(2,1)S(1)} %pad_maximum_fusion.4.refs_0_), channel_id=1, source_target_pairs={{0,1},{1,0},{2,3},{3,2},{4,5},{5,4},{6,7},{7,6},{8,9},{9,8},{10,11... | collective-permute-start | bytes 7077896 | tf_op jit(solution)/shard_map/ppermute | solution.py:46
  173.6 165.5 %collective-permute-start.37 = (bf16[4,576,512]{2,1,0:T(8,128)(2,1)S(1)}, bf16[4,576,512]{2,1,0:T(8,128)(2,1)}, u32[]{:S(2)}, u32[]{:S(2)}) collective-permute-start(bf16[4,576,512]{2,1,0:T(8,128)(2,1)S(1)} %pad_maximum_fusion.4.refs_0_), channel_id=1, source_target_pairs={{0,2},{1,3},{2,0},{3,1},{4,6},{5,7},{6,4},{7,5},{8,10},{9,11},{10,... | collective-permute-start | bytes 7077896 | tf_op jit(solution)/shard_map/ppermute | solution.py:46
  180.6 160.1 %collective-permute-start.29 = (bf16[4,576,512]{2,1,0:T(8,128)(2,1)S(1)}, bf16[4,576,512]{2,1,0:T(8,128)(2,1)}, u32[]{:S(2)}, u32[]{:S(2)}) collective-permute-start(bf16[4,576,512]{2,1,0:T(8,128)(2,1)S(1)} %pad_maximum_fusion.3.refs_0_), channel_id=1, source_target_pairs={{0,1},{1,0},{2,3},{3,2},{4,5},{5,4},{6,7},{7,6},{8,9},{9,8},{10,11... | collective-permute-start | bytes 7077896 | tf_op jit(solution)/shard_map/ppermute | solution.py:46
  181.8 52.4 %collective-permute-start.13 = (bf16[4,48,1536]{2,1,0:T(8,128)(2,1)S(1)}, bf16[4,48,1536]{2,1,0:T(8,128)(2,1)S(1)}, u32[]{:S(2)}, u32[]{:S(2)}) collective-permute-start(bf16[4,48,1536]{2,1,0:T(8,128)(2,1)S(1)} %slice.948), channel_id=1, source_target_pairs={{0,2},{1,3},{2,0},{3,1},{4,6},{5,7},{6,4},{7,5},{8,10},{9,11},{10,... | collective-permute-start | bytes 1769480 | tf_op jit(solution)/shard_map/ppermute | solution.py:46
  183.7 101.9 %collective-permute-start.14 = (bf16[4,48,1536]{2,1,0:T(8,128)(2,1)S(1)}, bf16[4,48,1536]{2,1,0:T(8,128)(2,1)S(1)}, u32[]{:S(2)}, u32[]{:S(2)}) collective-permute-start(bf16[4,48,1536]{2,1,0:T(8,128)(2,1)S(1)} %slice.949), channel_id=1, source_target_pairs={{0,1},{1,0},{2,3},{3,2},{4,5},{5,4},{6,7},{7,6},{8,9},{9,8},{10,11... | collective-permute-start | bytes 1769480 | tf_op jit(solution)/shard_map/ppermute | solution.py:46
  234.2 114.7 %collective-permute-start.41 = (bf16[640,1536]{1,0:T(8,128)(2,1)S(1)}, bf16[640,1536]{1,0:T(8,128)(2,1)S(1)}, u32[]{:S(2)}, u32[]{:S(2)}) collective-permute-start(bf16[640,1536]{1,0:T(8,128)(2,1)S(1)} %copy-done.28), channel_id=1, source_target_pairs={{0,16},{16,0},{1,17},{17,1},{2,18},{18,2},{3,19},{19,3},{4,20},{20... | collective-permute-start | bytes 5898248 | tf_op jit(solution)/shard_map/ppermute | solution.py:111
  285.6 60.9 %collective-permute-start.30 = (bf16[4,576,512]{2,1,0:T(8,128)(2,1)S(1)}, bf16[4,576,512]{2,1,0:T(8,128)(2,1)}, u32[]{:S(2)}, u32[]{:S(2)}) collective-permute-start(bf16[4,576,512]{2,1,0:T(8,128)(2,1)S(1)} %pad_maximum_fusion.3.refs_0_), channel_id=1, source_target_pairs={{0,2},{1,3},{2,0},{3,1},{4,6},{5,7},{6,4},{7,5},{8,10},{9,11},{10,... | collective-permute-start | bytes 7077896 | tf_op jit(solution)/shard_map/ppermute | solution.py:46
  307.4 103.1 %collective-permute-start.24 = (bf16[2048,768]{1,0:T(8,128)(2,1)}, bf16[2048,768]{1,0:T(8,128)(2,1)}, u32[]{:S(2)}, u32[]{:S(2)}) collective-permute-start(bf16[2048,768]{1,0:T(8,128)(2,1)} %assemble.5), channel_id=1, source_target_pairs={{0,16},{16,0},{1,17},{17,1},{2,18},{18,2},{3,19},{19,3},{4,20},{20... | collective-permute-start | bytes 9437192 | tf_op jit(solution)/shard_map/ppermute | solution.py:111
  339.1 68.4 %collective-permute-start.16 = (bf16[1280,1024]{1,0:T(8,128)(2,1)}, bf16[1280,1024]{1,0:T(8,128)(2,1)}, u32[]{:S(2)}, u32[]{:S(2)}) collective-permute-start(bf16[1280,1024]{1,0:T(8,128)(2,1)} %get-tuple-element.96), channel_id=1, source_target_pairs={{0,16},{16,0},{1,17},{17,1},{2,18},{18,2},{3,19},{19,3},{4,20},{20... | collective-permute-start | bytes 7864328 | tf_op jit(solution)/shard_map/ppermute | solution.py:111
  514.9 201.3 %collective-permute-start.42 = (f32[640,1536]{1,0:T(8,128)}, f32[640,1536]{1,0:T(8,128)S(1)}, u32[]{:S(2)}, u32[]{:S(2)}) collective-permute-start(f32[640,1536]{1,0:T(8,128)} %slice.969), channel_id=1, source_target_pairs={{0,16},{16,0},{1,17},{17,1},{2,18},{18,2},{3,19},{19,3},{4,20},{20... | collective-permute-start | bytes 11796488 | tf_op jit(solution)/shard_map/ppermute | solution.py:111
  540.5 54.5 %collective-permute-start.80 = (bf16[2,4,288,512]{3,2,1,0:T(8,128)(2,1)}, bf16[2,4,288,512]{3,2,1,0:T(8,128)(2,1)S(1)}, u32[]{:S(2)}, u32[]{:S(2)}) collective-permute-start(bf16[2,4,288,512]{3,2,1,0:T(8,128)(2,1)} %get-tuple-element.125), channel_id=1, source_target_pairs={{0,2},{1,3},{2,0},{3,1},{4,6},{5,7},{6,4},{7,5},{8,10},{9,11},{10,... | collective-permute-start | bytes 7077896 | tf_op jit(solution)/shard_map/ppermute | solution.py:46
  541.6 56.3 %collective-permute-start.78 = (bf16[2,4,288,512]{3,2,1,0:T(8,128)(2,1)S(1)}, bf16[2,4,288,512]{3,2,1,0:T(8,128)(2,1)}, u32[]{:S(2)}, u32[]{:S(2)}) collective-permute-start(bf16[2,4,288,512]{3,2,1,0:T(8,128)(2,1)S(1)} %get-tuple-element.123), channel_id=1, source_target_pairs={{0,1},{1,0},{2,3},{3,2},{4,5},{5,4},{6,7},{7,6},{8,9},{9,8},{10,11... | collective-permute-start | bytes 7077896 | tf_op jit(solution)/shard_map/ppermute | solution.py:46
  568.1 75.7 %collective-permute-start.72 = (bf16[2,4,288,512]{3,2,1,0:T(8,128)(2,1)}, bf16[2,4,288,512]{3,2,1,0:T(8,128)(2,1)S(1)}, u32[]{:S(2)}, u32[]{:S(2)}) collective-permute-start(bf16[2,4,288,512]{3,2,1,0:T(8,128)(2,1)} %get-tuple-element.120), channel_id=1, source_target_pairs={{0,2},{1,3},{2,0},{3,1},{4,6},{5,7},{6,4},{7,5},{8,10},{9,11},{10,... | collective-permute-start | bytes 7077896 | tf_op jit(solution)/shard_map/ppermute | solution.py:46
  569.1 78.0 %collective-permute-start.70 = (bf16[2,4,288,512]{3,2,1,0:T(8,128)(2,1)S(1)}, bf16[2,4,288,512]{3,2,1,0:T(8,128)(2,1)S(1)}, u32[]{:S(2)}, u32[]{:S(2)}) collective-permute-start(bf16[2,4,288,512]{3,2,1,0:T(8,128)(2,1)S(1)} %get-tuple-element.118), channel_id=1, source_target_pairs={{0,1},{1,0},{2,3},{3,2},{4,5},{5,4},{6,7},{7,6},{8,9},{9,8},{10,11... | collective-permute-start | bytes 7077896 | tf_op jit(solution)/shard_map/ppermute | solution.py:46
  594.9 122.9 %collective-permute-start.40 = (f32[640,1536]{1,0:T(8,128)}, f32[640,1536]{1,0:T(8,128)}, u32[]{:S(2)}, u32[]{:S(2)}) collective-permute-start(f32[640,1536]{1,0:T(8,128)} %slice.967), channel_id=1, source_target_pairs={{0,16},{16,0},{1,17},{17,1},{2,18},{18,2},{3,19},{19,3},{4,20},{20... | collective-permute-start | bytes 11796488 | tf_op jit(solution)/shard_map/ppermute | solution.py:111
  597.9 73.8 %collective-permute-start.81 = (bf16[4,288,512]{2,1,0:T(8,128)(2,1)S(1)}, bf16[4,288,512]{2,1,0:T(8,128)(2,1)S(1)}, u32[]{:S(2)}, u32[]{:S(2)}) collective-permute-start(bf16[4,288,512]{2,1,0:T(8,128)(2,1)S(1)} %fusion.25), channel_id=1, source_target_pairs={{0,1},{1,0},{2,3},{3,2},{4,5},{5,4},{6,7},{7,6},{8,9},{9,8},{10,11... | collective-permute-start | bytes 3538952 | tf_op jit(solution)/shard_map/ppermute | solution.py:46
  677.4 57.1 %collective-permute-start.84 = (bf16[576,512]{1,0:T(8,128)(2,1)}, bf16[576,512]{1,0:T(8,128)(2,1)}, u32[]{:S(2)}, u32[]{:S(2)}) collective-permute-start(bf16[576,512]{1,0:T(8,128)(2,1)} %pad_maximum_fusion.20), channel_id=1, source_target_pairs={{0,12},{1,13},{2,14},{3,15},{4,0},{5,1},{6,2},{7,3},{8,4},{9,5},{1... | collective-permute-start | bytes 1769480 | tf_op jit(solution)/shard_map/ppermute | solution.py:46
  695.0 51.5 %collective-permute-start.83 = (bf16[576,512]{1,0:T(8,128)(2,1)}, bf16[576,512]{1,0:T(8,128)(2,1)}, u32[]{:S(2)}, u32[]{:S(2)}) collective-permute-start(bf16[576,512]{1,0:T(8,128)(2,1)} %pad_maximum_fusion.19), channel_id=1, source_target_pairs={{0,8},{1,9},{2,10},{3,11},{4,12},{5,13},{6,14},{7,15},{8,0},{9,1},... | collective-permute-start | bytes 1769480 | tf_op jit(solution)/shard_map/ppermute | solution.py:46
  717.8 75.9 %collective-permute-start.75 = (bf16[576,512]{1,0:T(8,128)(2,1)}, bf16[576,512]{1,0:T(8,128)(2,1)}, u32[]{:S(2)}, u32[]{:S(2)}) collective-permute-start(bf16[576,512]{1,0:T(8,128)(2,1)} %pad_maximum_fusion.16), channel_id=1, source_target_pairs={{0,8},{1,9},{2,10},{3,11},{4,12},{5,13},{6,14},{7,15},{8,0},{9,1},... | collective-permute-start | bytes 1769480 | tf_op jit(solution)/shard_map/ppermute | solution.py:46
  734.5 59.2 %collective-permute-start.74 = (bf16[576,512]{1,0:T(8,128)(2,1)}, bf16[576,512]{1,0:T(8,128)(2,1)}, u32[]{:S(2)}, u32[]{:S(2)}) collective-permute-start(bf16[576,512]{1,0:T(8,128)(2,1)} %pad_maximum_fusion.15), channel_id=1, source_target_pairs={{0,4},{1,5},{2,6},{3,7},{4,8},{5,9},{6,10},{7,11},{8,12},{9,13},{1... | collective-permute-start | bytes 1769480 | tf_op jit(solution)/shard_map/ppermute | solution.py:46
  751.0 83.9 %collective-permute-start.43 = (bf16[640,1024]{1,0:T(8,128)(2,1)}, bf16[640,1024]{1,0:T(8,128)(2,1)}, u32[]{:S(2)}, u32[]{:S(2)}) collective-permute-start(bf16[640,1024]{1,0:T(8,128)(2,1)} %get-tuple-element.216), channel_id=1, source_target_pairs={{0,16},{16,0},{1,17},{17,1},{2,18},{18,2},{3,19},{19,3},{4,20},{20... | collective-permute-start | bytes 3932168 | tf_op jit(solution)/shard_map/ppermute | solution.py:111
  753.6 69.4 %collective-permute-start.61 = (bf16[640,768]{1,0:T(8,128)(2,1)}, bf16[640,768]{1,0:T(8,128)(2,1)}, u32[]{:S(2)}, u32[]{:S(2)}) collective-permute-start(bf16[640,768]{1,0:T(8,128)(2,1)} %get-tuple-element.218), channel_id=1, source_target_pairs={{0,16},{16,0},{1,17},{17,1},{2,18},{18,2},{3,19},{19,3},{4,20},{20... | collective-permute-start | bytes 2949128 | tf_op jit(solution)/shard_map/ppermute | solution.py:111
  833.5 72.2 %collective-permute-start.64 = (bf16[2,4,48,768]{3,2,1,0:T(8,128)(2,1)S(1)}, bf16[2,4,48,768]{3,2,1,0:T(8,128)(2,1)}, u32[]{:S(2)}, u32[]{:S(2)}) collective-permute-start(bf16[2,4,48,768]{3,2,1,0:T(8,128)(2,1)S(1)} %get-tuple-element.115), channel_id=1, source_target_pairs={{0,2},{1,3},{2,0},{3,1},{4,6},{5,7},{6,4},{7,5},{8,10},{9,11},{10,... | collective-permute-start | bytes 1769480 | tf_op jit(solution)/shard_map/ppermute | solution.py:46
  834.7 73.9 %collective-permute-start.62 = (bf16[2,4,48,768]{3,2,1,0:T(8,128)(2,1)S(1)}, bf16[2,4,48,768]{3,2,1,0:T(8,128)(2,1)}, u32[]{:S(2)}, u32[]{:S(2)}) collective-permute-start(bf16[2,4,48,768]{3,2,1,0:T(8,128)(2,1)S(1)} %get-tuple-element.113), channel_id=1, source_target_pairs={{0,1},{1,0},{2,3},{3,2},{4,5},{5,4},{6,7},{7,6},{8,9},{9,8},{10,11... | collective-permute-start | bytes 1769480 | tf_op jit(solution)/shard_map/ppermute | solution.py:46
  922.5 78.2 %collective-permute-start.44 = (f32[640,1536]{1,0:T(8,128)}, f32[640,1536]{1,0:T(8,128)}, u32[]{:S(2)}, u32[]{:S(2)}) collective-permute-start(f32[640,1536]{1,0:T(8,128)} %slice.971), channel_id=1, source_target_pairs={{0,16},{16,0},{1,17},{17,1},{2,18},{18,2},{3,19},{19,3},{4,20},{20... | collective-permute-start | bytes 11796488 | tf_op jit(solution)/shard_map/ppermute | solution.py:111
  (174 other events, 3373.2 us)

commit v2 on v0

v2 whole, which is shorter than its diff:
```python
import functools

import jax
import jax.numpy as jnp
from jax import lax
from jax.experimental import pallas as pl
from jax.experimental.pallas import tpu as pltpu
from jax.sharding import PartitionSpec as P

H = 16
KV = 8
HD = 96
HALF = HD // 2
LANES = 128
BLOCKS = 16
TILE = 128
SLAB = 512
CHUNKS = 2
COST_SCALE = 0.001

epsilon = 1e-05
rope_base = 100000.0
masked_score = -1e30
low = jnp.bfloat16
wide = jnp.float32


def whole(array, buffers=1):
    zeros = (0,) * array.ndim
    mode = pl.Buffered(buffers)
    return pl.BlockSpec(array.shape, lambda *at: zeros, pipeline_mode=mode)


def rows_of(tile, width, first=0):
    return pl.BlockSpec((tile, width), lambda i, place: (first + i, 0))


def shaped(shape, dtype):
    return jax.ShapeDtypeStruct(shape, dtype)


anywhere = pl.BlockSpec(memory_space=pl.ANY)


def run(kernel, name, place, grid, operands, outs, scratch=(), after=(), vmem=56, us=4):
    after = [item for item in after if isinstance(item, jax.Array)]
    count, extra = len(operands), len(after)

    def body(place_ref, *refs):
        kernel(place_ref, *refs[:count], *refs[count + extra :])

    return pl.pallas_call(
        body,
        grid_spec=pltpu.PrefetchScalarGridSpec(
            num_scalar_prefetch=1,
            grid=grid,
            in_specs=[spec for _, spec in operands] + [anywhere] * extra,
            out_specs=[spec for _, spec in outs],
            scratch_shapes=list(scratch),
        ),
        out_shape=[shape for shape, _ in outs],
        compiler_params=pltpu.CompilerParams(vmem_limit_bytes=vmem * 2**20),
        cost_estimate=pl.CostEstimate(
            flops=0, bytes_accessed=int(us * COST_SCALE * 3.3e6), transcendentals=0
        ),
        name=name,
    )(place, *[array for array, _ in operands], *after)


def across(left, right):
    return lax.dot_general(left, right, (((1,), (1,)), ((), ())), preferred_element_type=wide)


def down(left, right):
    return lax.dot_general(left, right, (((0,), (0,)), ((), ())), preferred_element_type=wide)


def project(left, right):
    return jnp.dot(left, right, preferred_element_type=wide)


class Slab:
    def __init__(self, matrix, row, rows, stride, offset, column, width=SLAB, lane=0):
        self.matrix, self.row, self.rows = matrix, row, rows
        self.stride, self.offset = stride, offset
        self.column, self.width, self.lane = column, width, lane

    def of(self, refs, block):
        rows = pl.ds(pl.multiple_of(block * self.stride + self.offset, 16), self.rows)
        return refs[self.matrix].at[rows, pl.ds(self.column, self.width)]

    def lanes(self):
        return pl.ds(self.lane, self.width)


FIRST_HALF, FFN_HALF, QKV_HALF, OUT_HALF = 224, 288, 160, 80


def square_plan(half):
    plan = []
    for slab in range(3):
        top, bottom = slab * 96, slab * 96 + 96
        for first, last in ((top, min(bottom, half)), (max(top, half), bottom)):
            if first < last:
                plan.append(Slab(0, first, last - first, 96, first - top, slab * SLAB))
    return plan


def out_plan(start, half):
    plan = []
    for first, last in ((start, min(start + 96, half)), (max(start, half), start + 96)):
        if first < last:
            plan.append(Slab(0, first, last - first, LANES, first - start, 0))
    for part in range(2):
        plan.append(Slab(0, start + 96, 48, LANES, part * 48, SLAB, 256, part * 256))
    return plan


GAINS = 288
GAIN_SLAB = Slab(1, GAINS, 16, 16, 0, 0)
FIRST_QKV_PLAN = square_plan(FIRST_HALF) + [GAIN_SLAB]
FIRST_OUT_PLAN = out_plan(GAINS + 16, FIRST_HALF)
QKV_PLAN = square_plan(QKV_HALF) + [GAIN_SLAB]
OUT_PLAN = out_plan(0, OUT_HALF)
FFN_PLAN = [
    Slab(0, 0, 96, 96, 0, 0),
    Slab(0, 96, 96, 96, 0, SLAB),
    Slab(1, 192, 96, 96, 0, 0),
    Slab(1, 288, 96, 96, 0, SLAB),
    Slab(2, 384, 64, 64, 0, 0),
    Slab(2, 448, 64, 64, 0, SLAB),
    Slab(2, 512, 64, 64, 0, 2 * SLAB),
]


def block_index(place_ref, k, dy, dx):
    z, y, x = place_ref[0], place_ref[1], place_ref[2]
    return ((z ^ k) * 2 + (y ^ dy)) * 2 + (x ^ dx)


def fetch(place_ref, pieces, plan, half, matrices, sems):
    for k in range(4):
        for dy in range(2):
            for dx in range(2):
                block = block_index(place_ref, k, dy, dx)
                for slab in plan:
                    at = pl.ds(slab.row, slab.rows)
                    source = pieces[dy * 2 + dx]
                    if dy and dx:
                        part = int(slab.row >= half)
                        at = pl.ds(slab.row - part * half, slab.rows)
                        source = pieces[3 + part]
                    copy = pltpu.make_async_copy(
                        source.at[k, at, slab.lanes()],
                        slab.of(matrices, block),
                        sems.at[slab.matrix],
                    )
                    copy.start()


def send_off(place_ref, k, matrices, stride_base, plan, half, outs, sems):
    to_x, to_y, late_x, late_y, own = range(5)
    for dy in range(2):
        for dx in range(2):
            block = block_index(place_ref, place_ref[0], dy, dx) + stride_base
            for slab in plan:
                part = int(slab.row >= half)
                at = pl.ds(slab.row - part * half, slab.rows)
                if (dy, dx) == (0, 0):
                    which, index = own, (k, part)
                elif dy and dx:
                    which, index = (to_y if part else to_x), (0, k)
                elif part == dy:
                    which, index = (to_y if dy else to_x), (1, k)
                else:
                    which, index = (late_y if dy else late_x), (k,)
                target = outs[which].at[(*index, at, slab.lanes())]
                pltpu.make_async_copy(slab.of(matrices, block), target, sems.at[which]).start()


def fill_spare(source, row, rows, half, outs, sems):
    at = pl.ds(row - half, rows)
    for k in range(4):
        for which, index in ((1, (0, k)), (1, (1, k)), (2, (k,)), (4, (k, 1))):
            target = outs[which].at[(*index, at)]
            pltpu.make_async_copy(source, target, sems.at[which]).start()


def drain(refs, sems):
    for index, ref in enumerate(refs):
        pltpu.make_async_copy(ref, ref, sems.at[index]).wait()


def sent_shapes(half, width):
    shapes = [(2, 4, half, width)] * 2 + [(4, half, width)] * 2 + [(4, 2, half, width)]
    return [(shaped(shape, low), anywhere) for shape in shapes]


def pair_kernel(place_ref, own, far, out, sems):
    copies = [
        pltpu.make_async_copy(ref, out.at[k], sems.at[k]) for k, ref in enumerate((own, far))
    ]
    for copy in copies:
        copy.start()
    for copy in copies:
        copy.wait()


def pair_up(place, own, far, after=()):
    out = shaped((2, *own.shape), low)
    return run(
        pair_kernel,
        "pair",
        place,
        (1,),
        [(own, anywhere), (far, anywhere)],
        [(out, whole(out))],
        [pltpu.SemaphoreType.DMA((2,))],
        after,
        us=2,
    )[0]


def line_kernel(place_ref, pair, near, out, sems):
    copies = []
    for k in range(4):
        ref = near if k % 2 else pair
        copies.append(pltpu.make_async_copy(ref.at[k // 2], out.at[k], sems.at[k]))
        copies[-1].start()
    for copy in copies:
        copy.wait()


def line_up(place, pair, near, after=()):
    _, rows, width = pair.shape
    out = shaped((4, rows, width), low)
    return run(
        line_kernel,
        "line",
        place,
        (1,),
        [(pair, anywhere), (near, anywhere)],
        [(out, whole(out))],
        [pltpu.SemaphoreType.DMA((4,))],
        after,
        us=4,
    )[0]


def halves_kernel(place_ref, from_x, from_y, upper, lower, sems):
    half = upper.shape[1]
    copies = (
        pltpu.make_async_copy(from_x.at[:, pl.ds(0, half)], upper, sems.at[0]),
        pltpu.make_async_copy(from_y.at[:, pl.ds(half, half)], lower, sems.at[1]),
    )
    for copy in copies:
        copy.start()
    for copy in copies:
        copy.wait()


def halves(place, from_x, from_y, after):
    count, rows, width = from_x.shape
    out = shaped((count, rows // 2, width), low)
    return run(
        halves_kernel,
        "halves",
        place,
        (1,),
        [(from_x, anywhere), (from_y, anywhere)],
        [(out, whole(out))] * 2,
        [pltpu.SemaphoreType.DMA((2,))],
        after,
        us=2,
    )


def step_rows(half):
    return next(rows for rows in (96, 80, 48) if half % rows == 0)


def merge_kernel(place_ref, late_x, late_y, got_x, got_y, out_x, out_y):
    out_x[...] = (late_x[...].astype(wide) + got_y[0].astype(wide)).astype(low)
    out_y[...] = (late_y[...].astype(wide) + got_x[0].astype(wide)).astype(low)


def merge(place, late_x, late_y, got_x, got_y, after):
    shape = late_x.shape
    rows = step_rows(shape[1])
    spec = pl.BlockSpec((4, rows, shape[2]), lambda i, place: (0, i, 0))
    got = pl.BlockSpec((1, 4, rows, shape[2]), lambda i, place: (0, 0, i, 0))
    return run(
        merge_kernel,
        "merge",
        place,
        (shape[1] // rows,),
        [(late_x, spec), (late_y, spec), (got_x, got), (got_y, got)],
        [(shaped(shape, low), spec)] * 2,
        after=after,
    )


def sum_kernel(groups, place_ref, *refs):
    ins, (kept, kept_far, sent) = refs[: 5 * groups], refs[5 * groups :]
    row = 0
    for group in range(groups):
        own, got_x, got_y, more_x, more_y = ins[5 * group : 5 * group + 5]
        rows = own.shape[2]
        at = slice(row, row + rows)
        for k in range(4):
            upper = own[k, 0].astype(wide) + got_x[0, k].astype(wide) + more_y[k].astype(wide)
            lower = own[k, 1].astype(wide) + got_y[0, k].astype(wide) + more_x[k].astype(wide)
            if k % 2:
                sent[k // 2, 0, at, :] = upper.astype(low)
                sent[k // 2, 1, at, :] = lower.astype(low)
            else:
                ref = kept_far if k else kept
                ref[0, at, :], ref[1, at, :] = upper, lower
        row += rows


def sum_plane(place, groups, after):
    halves = [group[0].shape[2] for group in groups]
    width = groups[0][0].shape[3]
    steps = halves[0] // step_rows(halves[0]) if len(groups) == 1 else 1
    total, rows = sum(halves), sum(halves) // steps
    operands = []
    for group, half in zip(groups, halves):
        own, got_x, got_y, more_x, more_y = group
        part = half // steps
        got = pl.BlockSpec((1, 4, part, width), lambda i, place: (1, 0, i, 0))
        more = pl.BlockSpec((4, part, width), lambda i, place: (0, i, 0))
        operands += [
            (own, pl.BlockSpec((4, 2, part, width), lambda i, place: (0, 0, i, 0))),
            (got_x, got),
            (got_y, got),
            (more_x, more),
            (more_y, more),
        ]
    out = pl.BlockSpec((2, rows, width), lambda i, place: (0, i, 0))
    both = pl.BlockSpec((2, 2, rows, width), lambda i, place: (0, 0, i, 0))
    return run(
        functools.partial(sum_kernel, len(groups)),
        "sum_plane",
        place,
        (steps,),
        operands,
        [(shaped((2, total, width), wide), out)] * 2
        + [(shaped((2, 2, total, width), low), both)],
        after=after,
        us=5,
    )


def pass_kernel(place_ref, kept_far, near, out):
    out[...] = (kept_far[...] + near[0].astype(wide)).astype(low)


def sum_pass(place, kept_far, near, after):
    _, half, width = kept_far.shape
    rows = step_rows(half)
    spec = pl.BlockSpec((2, rows, width), lambda i, place: (0, i, 0))
    second = pl.BlockSpec((1, 2, rows, width), lambda i, place: (1, 0, i, 0))
    return run(
        pass_kernel,
        "sum_pass",
        place,
        (half // rows,),
        [(kept_far, spec), (near, second)],
        [(shaped(kept_far.shape, low), spec)],
        after=after,
        us=3,
    )[0]


def total_kernel(place_ref, kept, near, far, out, out_low):
    total = kept[...] + near[0].astype(wide) + far[...].astype(wide)
    out[...] = total
    out_low[...] = total.astype(low)


def sum_line(place, kept, near, far, after):
    _, half, width = kept.shape
    rows = step_rows(half)
    spec = pl.BlockSpec((2, rows, width), lambda i, place: (0, i, 0))
    first = pl.BlockSpec((1, 2, rows, width), lambda i, place: (0, 0, i, 0))
    total, total_low = run(
        total_kernel,
        "sum_line",
        place,
        (half // rows,),
        [(kept, spec), (near, first), (far, spec)],
        [(shaped(kept.shape, wide), spec), (shaped(kept.shape, low), spec)],
        after=after,
        us=4,
    )
    return total.reshape(2 * half, width), total_low.reshape(2 * half, width)


def pack_first_kernel(place_ref, query, key, value, square, gain_one, gain_two, out):
    core = place_ref[3]

    def mine(ref):
        columns = ref.shape[1] // 2
        return ref[:, pl.ds(pl.multiple_of(core * columns, LANES), columns)]

    packed = jnp.concatenate([mine(query), mine(key), mine(value)], axis=1)
    rows = packed.shape[0]
    for slab in range(3):
        out[slab * rows : (slab + 1) * rows, :] = packed[:, slab * SLAB : (slab + 1) * SLAB]
    row = lax.broadcasted_iota(jnp.int32, (16, LANES), 0)
    gap = jnp.zeros((16, LANES - rows), wide)
    out[GAINS : GAINS + 16, :] = jnp.zeros((16, SLAB), low)
    for index, gain in enumerate((gain_one, gain_two)):
        spread = jnp.broadcast_to(gain[...].astype(wide), (16, rows))
        spread = jnp.where(row == 0, jnp.concatenate([spread, gap], axis=1), 0.0)
        out[GAINS : GAINS + 16, index * LANES : (index + 1) * LANES] = spread.astype(low)
    at, packed = GAINS + 16, mine(square)
    out[at : at + rows, :] = packed[:, :SLAB]
    for part in range(2):
        out[at + rows :, part * 256 : (part + 1) * 256] = packed[
            part * rows // 2 : (part + 1) * rows // 2, SLAB:
        ]


def pack_first(place, query, key, value, square, gain_one, gain_two):
    operands = [query, key, value, square, gain_one.reshape(1, -1), gain_two.reshape(1, -1)]
    out = shaped((2 * FIRST_HALF, SLAB), low)
    return run(
        pack_first_kernel,
        "pack_first",
        place,
        (1,),
        [(item, whole(item)) for item in operands],
        [(out, whole(out))],
    )[0]


def interleave(even, odd):
    lane = lax.broadcasted_iota(jnp.int32, even.shape, 1)
    left = jnp.where(lane < LANES // 2, even, pltpu.roll(odd, LANES // 2, 1))
    right = jnp.where(lane < LANES // 2, pltpu.roll(even, LANES // 2, 1), odd)
    return left, right


def pack_ffn_kernel(chunk, place_ref, gate, up, down_w, out):
    core = place_ref[3]
    rows = gate.shape[0]
    for matrix, ref in enumerate((gate, up)):
        for pair in range(8):
            windows = [
                ref[:, pl.ds(pl.multiple_of((2 * pair + odd) * 256 + core * LANES, LANES), LANES)]
                for odd in range(2)
            ]
            packed = interleave(windows[0].astype(wide), windows[1].astype(wide))[chunk]
            at = (matrix * 2 + pair // 4) * rows
            column = pair % 4 * LANES
            out[at : at + rows, column : column + LANES] = packed.astype(low)
    units = down_w[pl.ds(pl.multiple_of(core * LANES + chunk * 64, 64), 64), :]
    for slab in range(3):
        at = 4 * rows + slab * 64
        out[at : at + 64, :] = units[:, slab * SLAB : (slab + 1) * SLAB]


def pack_ffn(place, chunk, gate, up, down_w, after):
    out = shaped((2 * FFN_HALF, SLAB), low)
    return run(
        functools.partial(pack_ffn_kernel, chunk),
        "pack_ffn",
        place,
        (1,),
        [(item, whole(item)) for item in (gate, up, down_w)],
        [(out, whole(out))],
        after=after,
    )[0]


def unpack_ffn_kernel(place_ref, mine_0, mine_1, other_0, other_1, gate, up, down_w):
    core = place_ref[3]
    rows = gate.shape[0]
    for owner, chunks in ((core, (mine_0, mine_1)), (1 - core, (other_0, other_1))):
        for matrix, ref in enumerate((gate, up)):
            for pair in range(8):
                at = (matrix * 2 + pair // 4) * rows
                column = pair % 4 * LANES
                parts = [
                    chunk[at : at + rows, column : column + LANES].astype(wide)
                    for chunk in chunks
                ]
                for odd, window in enumerate(interleave(*parts)):
                    place = (2 * pair + odd) * 256 + owner * LANES
                    ref[:, pl.ds(pl.multiple_of(place, LANES), LANES)] = window
        for index, chunk in enumerate(chunks):
            for slab in range(3):
                at = 4 * rows + slab * 64
                place = pl.multiple_of(owner * LANES + index * 64, 64)
                down_w[pl.ds(place, 64), slab * SLAB : (slab + 1) * SLAB] = chunk[
                    at : at + 64, :
                ].astype(wide)


def unpack_ffn(place, mine, other, shapes, after):
    outs = [shaped(shape, wide) for shape in shapes]
    return run(
        unpack_ffn_kernel,
        "unpack_ffn",
        place,
        (1,),
        [(item, whole(item)) for item in (*mine, *other)],
        [(out, whole(out)) for out in outs],
        after=after,
    )


def unpack_first_kernel(place_ref, mine, other, query, key, value, square):
    core = place_ref[3]
    rows = query.shape[0]
    half = QKV_HALF + OUT_HALF

    def put(ref, owner, part):
        columns = ref.shape[1] // 2
        at = pl.ds(pl.multiple_of(owner * columns, LANES), columns)
        ref[:, at] = part.astype(wide)

    for owner, ref in ((core, mine), (1 - core, other)):
        qkv = jnp.concatenate([ref[:QKV_HALF, :], ref[half : half + QKV_HALF, :]], axis=0)
        out = jnp.concatenate([ref[QKV_HALF:half, :], ref[half + QKV_HALF :, :]], axis=0)
        slabs = [qkv[slab * rows : (slab + 1) * rows, :] for slab in range(3)]
        put(query, owner, jnp.concatenate([slabs[0], slabs[1][:, :256]], axis=1))
        put(key, owner, jnp.concatenate([slabs[1][:, 256:], slabs[2][:, :128]], axis=1))
        put(value, owner, slabs[2][:, 128:])
        rest = out[rows : rows + rows // 2, :]
        rest = jnp.concatenate([rest[:, :256], rest[:, 256:]], axis=0)
        put(square, owner, jnp.concatenate([out[:rows, :], rest], axis=1))


def unpack_first(place, mine, other, shapes):
    outs = [shaped(shape, wide) for shape in shapes]
    return run(
        unpack_first_kernel,
        "unpack_first",
        place,
        (1,),
        [(item, whole(item)) for item in (mine, other)],
        [(out, whole(out)) for out in outs],
    )


def turn_table(position):
    frequency = rope_base ** (-jnp.arange(HALF, dtype=wide) * 2.0 / HD)
    angle = position.astype(wide)[:, None] * frequency[None, :]
    gap = jnp.zeros((position.shape[0], LANES // 2 - HALF), wide)
    cosine, sine = jnp.cos(angle), jnp.sin(angle)
    return (
        jnp.concatenate([cosine, gap, cosine, gap], axis=1),
        jnp.concatenate([-sine, gap, sine, gap], axis=1),
    )


def qkv_kernel(tiles, place_ref, own_ref, far_ref, cos_ref, sin_ref, *refs):
    pieces = refs[:5]
    normed_ref, q_ref, k_ref, v_ref, w_ref, gain_ref, gain_rows, x_ref, sems = refs[5:]
    step = pl.program_id(0)

    @pl.when(step < tiles)
    def _():
        x_ref[...] = own_ref[...]

    @pl.when(step >= tiles)
    def _():
        x_ref[...] = far_ref[...]

    @pl.when(pl.program_id(0) == 0)
    def _():
        fetch(place_ref, pieces, FIRST_QKV_PLAN, FIRST_HALF, (w_ref, gain_rows), sems)
        drain((w_ref, gain_rows), sems)
        for index in range(2):
            parts = [
                gain_rows[16 * block : 16 * block + 16, index * LANES : (index + 1) * LANES]
                for block in range(BLOCKS)
            ]
            parts = [part.astype(wide)[:8, :HD] for part in parts]
            gain_ref[8 * index : 8 * index + 8, :] = jnp.concatenate(parts, axis=1)

    hidden = x_ref[...].astype(wide)
    scale = lax.rsqrt(jnp.mean(hidden * hidden, axis=-1, keepdims=True) + epsilon)
    normed = (hidden * scale * gain_ref[0:1, :]).astype(low)
    normed_ref[...] = normed
    gap = jnp.zeros((x_ref.shape[0], LANES // 2 - HALF), wide)
    heads = q_ref.shape[1] // LANES
    groups = k_ref.shape[1] // LANES
    count = 4
    for first in range(0, heads + 2 * groups, count):
        part = project(normed, w_ref[:, first * HD : (first + count) * HD])
        for index in range(first, first + count):
            at = (index - first) * HD
            if index >= heads + groups:
                column = (index - heads - groups) * LANES
                padded = jnp.concatenate([part[:, at : at + HD], gap, gap], axis=1)
                v_ref[:, column : column + LANES] = padded.astype(low)
                continue
            padded = jnp.concatenate(
                [part[:, at : at + HALF], gap, part[:, at + HALF : at + HD], gap], axis=1
            )
            turned = pltpu.roll(padded, LANES // 2, 1)
            padded = (padded * cos_ref[...] + turned * sin_ref[...]).astype(low)
            if index < heads:
                q_ref[:, index * LANES : (index + 1) * LANES] = padded
            else:
                column = (index - heads) * LANES
                k_ref[:, column : column + LANES] = padded


def project_qkv(place, own, far, cosine, sine, pieces, after):
    count, width = own.shape
    tile = 320
    tiles = count // tile
    count = 2 * count
    heads, groups = H // 2 * LANES, KV // 2 * LANES
    weight, gains = shaped((width, width), low), shaped((16, width), wide)
    early = pl.BlockSpec((tile, width), lambda i, place: (jnp.minimum(i, tiles - 1), 0))
    late = pl.BlockSpec((tile, width), lambda i, place: (jnp.maximum(i - tiles, 0), 0))
    return run(
        functools.partial(qkv_kernel, tiles),
        "project_qkv",
        place,
        (count // tile,),
        [
            (own, early),
            (far, late),
            (cosine, rows_of(tile, LANES)),
            (sine, rows_of(tile, LANES)),
        ]
        + [(piece, anywhere) for piece in pieces],
        [
            (shaped((count, width), low), rows_of(tile, width)),
            (shaped((count, heads), low), rows_of(tile, heads)),
            (shaped((count, groups), low), rows_of(tile, groups)),
            (shaped((count, groups), low), rows_of(tile, groups)),
            (weight, whole(weight)),
            (gains, whole(gains)),
        ],
        [
            pltpu.VMEM((BLOCKS * 16, SLAB), low),
            pltpu.VMEM((tile, width), low),
            pltpu.SemaphoreType.DMA((2,)),
        ],
        after,
        us=18,
    )


def fill_bias(bias_ref, column_ref, row_ref):
    size = bias_ref.shape[0]
    for start in range(0, size, TILE):
        shape = (TILE, size)
        slots = lax.broadcasted_iota(jnp.int32, shape, 0) + start
        keys = lax.broadcasted_iota(jnp.int32, shape, 1)
        same = column_ref[start : start + TILE, :] == row_ref[0]
        allowed = same & (keys <= slots)
        bias_ref[start : start + TILE, :] = jnp.where(allowed, 0.0, masked_score)


def attend_kernel(
    place_ref, q_ref, k_ref, v_ref, column_ref, row_ref, out_ref, total_ref, bias_ref
):
    group = pl.program_id(0)
    size = q_ref.shape[0]

    @pl.when(group == 0)
    def _():
        fill_bias(bias_ref, column_ref, row_ref)
        total_ref[...] = jnp.zeros_like(total_ref)

    lane = lax.broadcasted_iota(jnp.int32, (TILE, LANES), 1)
    for start in range(0, size, TILE):
        stop = start + TILE
        for head in range(2):
            columns = slice(head * LANES, (head + 1) * LANES)
            raw = across(q_ref[start:stop, columns], k_ref[:stop, :])
            scores = raw * HD ** (-0.5) + bias_ref[start:stop, :stop]
            top = jnp.max(scores, axis=-1, keepdims=True)
            powers = jnp.exp(scores - top)
            amount = jnp.sum(powers, axis=-1, keepdims=True)
            probs = (powers * (1.0 / amount)).astype(low)
            out_ref[start:stop, columns] = project(probs, v_ref[:stop, :]).astype(low)
            total = top + jnp.log(amount)
            total_ref[start:stop, :] = jnp.where(
                lane == 2 * group + head, total, total_ref[start:stop, :]
            )


def attention_specs(size, block):
    return dict(
        pair=pl.BlockSpec((size, 2 * LANES), lambda g, place: (block, g)),
        one=pl.BlockSpec((size, LANES), lambda g, place: (block, g)),
        pair_alone=pl.BlockSpec((size, 2 * LANES), lambda g, place: (0, g)),
        one_alone=pl.BlockSpec((size, LANES), lambda g, place: (0, g)),
        shared=pl.BlockSpec((size, LANES), lambda g, place: (block, 0)),
        alone=pl.BlockSpec((size, LANES), lambda g, place: (0, 0)),
        column=pl.BlockSpec((size, 1), lambda g, place: (block, 0)),
        row=pl.BlockSpec((1, 1, size), lambda g, place: (block, 0, 0)),
    )


def attend(place, q, k, v, segment, block, after=()):
    blocks, size = segment.shape
    spec = attention_specs(size, block)
    return run(
        attend_kernel,
        "attend",
        place,
        (k.shape[1] // LANES,),
        [
            (q, spec["pair"]),
            (k, spec["one"]),
            (v, spec["one"]),
            (segment.reshape(blocks * size, 1), spec["column"]),
            (segment.reshape(blocks, 1, size), spec["row"]),
        ],
        [
            (shaped((size, q.shape[1]), low), spec["pair_alone"]),
            (shaped((size, LANES), wide), spec["alone"]),
        ],
        [pltpu.VMEM((size, size), wide)],
        after,
        us=17,
    )


def attend_back_kernel(
    place_ref,
    q_ref,
    k_ref,
    v_ref,
    grad_ref,
    total_ref,
    column_ref,
    row_ref,
    cos_ref,
    sin_ref,
    dq_ref,
    dk_ref,
    dv_ref,
    bias_ref,
    dk_sum,
    dv_sum,
):
    group = pl.program_id(0)
    size = q_ref.shape[0]

    @pl.when(group == 0)
    def _():
        fill_bias(bias_ref, column_ref, row_ref)

    def turned_back(grad, rows):
        turned = pltpu.roll(grad, LANES // 2, 1)
        return (grad * cos_ref[rows, :] - turned * sin_ref[rows, :]).astype(low)

    dk_sum[...] = jnp.zeros_like(dk_sum)
    dv_sum[...] = jnp.zeros_like(dv_sum)
    lane = lax.broadcasted_iota(jnp.int32, (TILE, LANES), 1)
    for start in range(0, size, TILE):
        stop = start + TILE
        for head in range(2):
            columns = slice(head * LANES, (head + 1) * LANES)
            queries = q_ref[start:stop, columns]
            grads = grad_ref[start:stop, columns]
            total = jnp.sum(
                jnp.where(lane == 2 * group + head, total_ref[start:stop, :], 0.0),
                axis=-1,
                keepdims=True,
            )
            raw = across(queries, k_ref[:stop, :])
            probs = jnp.exp(raw * HD ** (-0.5) + bias_ref[start:stop, :stop] - total)
            dv_sum[:stop, :] += down(probs.astype(low), grads)
            grad_probs = across(grads, v_ref[:stop, :])
            weighted = probs * grad_probs
            delta = jnp.sum(weighted, axis=-1, keepdims=True)
            grad_raw = ((weighted - probs * delta) * HD ** (-0.5)).astype(low)
            dq = project(grad_raw, k_ref[:stop, :])
            dq_ref[start:stop, columns] = turned_back(dq, slice(start, stop))
            dk_sum[:stop, :] += down(grad_raw, queries)
    dv_ref[...] = dv_sum[...].astype(low)
    dk_ref[...] = turned_back(dk_sum[...], slice(None))


def attend_back(place, q, k, v, grad, total, segment, cosine, sine, block, after=()):
    blocks, size = segment.shape
    spec = attention_specs(size, block)
    return run(
        attend_back_kernel,
        "attend_back",
        place,
        (k.shape[1] // LANES,),
        [
            (q, spec["pair"]),
            (k, spec["one"]),
            (v, spec["one"]),
            (grad, spec["pair_alone"]),
            (total, spec["alone"]),
            (segment.reshape(blocks * size, 1), spec["column"]),
            (segment.reshape(blocks, 1, size), spec["row"]),
            (cosine, spec["shared"]),
            (sine, spec["shared"]),
        ],
        [
            (shaped((size, q.shape[1]), low), spec["pair_alone"]),
            (shaped((size, k.shape[1]), low), spec["one_alone"]),
            (shaped((size, v.shape[1]), low), spec["one_alone"]),
        ],
        [
            pltpu.VMEM((size, size), wide),
            pltpu.VMEM((size, LANES), wide),
            pltpu.VMEM((size, LANES), wide),
        ],
        after,
        us=21,
    )


def out_weight_kernel(place_ref, *refs):
    pieces, weight, sems = refs[:5], refs[5], refs[6]
    fetch(place_ref, pieces, FIRST_OUT_PLAN, FIRST_HALF, (weight,), sems)
    zeros = jnp.zeros((LANES - HD, weight.shape[1]), low)
    for block in range(BLOCKS):
        weight[pl.ds(block * LANES + HD, LANES - HD), :] = zeros
    drain((weight.at[pl.ds(0, BLOCKS * HD)],), sems)


def out_weight(place, pieces, width, after):
    out = shaped((H * LANES, width // 2), low)
    return run(
        out_weight_kernel,
        "out_weight",
        place,
        (1,),
        [(piece, anywhere) for piece in pieces],
        [(out, whole(out))],
        [pltpu.SemaphoreType.DMA((1,))],
        after,
    )[0]


def middle_kernel(
    place_ref, x_ref, mine_ref, other_ref, w_mine, w_other, gain_ref, middle_ref, out_ref, heads
):
    core = place_ref[3]
    span = mine_ref.shape[1]
    heads[:, pl.ds(pl.multiple_of(core * span, LANES), span)] = mine_ref[...]
    heads[:, pl.ds(pl.multiple_of((1 - core) * span, LANES), span)] = other_ref[...]
    columns = w_mine.shape[1]
    for owner, weight in ((core, w_mine), (1 - core, w_other)):
        at = pl.ds(pl.multiple_of(owner * columns, LANES), columns)
        middle_ref[:, at] = x_ref[:, at].astype(wide) + project(heads[...], weight[...])
    hidden = middle_ref[...]
    scale = lax.rsqrt(jnp.mean(hidden * hidden, axis=-1, keepdims=True) + epsilon)
    out_ref[...] = (hidden * scale * gain_ref[8:9, :]).astype(low)


def middle_of(place, x, mine, other, w_mine, w_other, gains, after=()):
    count, width = x.shape
    tile, span = count // 2, mine.shape[1]
    return run(
        middle_kernel,
        "middle",
        place,
        (2,),
        [
            (x, rows_of(tile, width)),
            (mine, rows_of(tile, span)),
            (other, rows_of(tile, span)),
            (w_mine, whole(w_mine)),
            (w_other, whole(w_other)),
            (gains, whole(gains)),
        ],
        [
            (shaped((count, width), wide), rows_of(tile, width)),
            (shaped((count, width), low), rows_of(tile, width)),
        ],
        [pltpu.VMEM((tile, 2 * span), low)],
        after,
        us=11,
    )


def middle_back_kernel(
    place_ref,
    middle_ref,
    mine_0,
    mine_1,
    other_0,
    other_1,
    cotangent_ref,
    gain_ref,
    w_mine,
    w_other,
    grad_ref,
    branch_mine,
    branch_other,
    heads_mine,
    heads_other,
    gain_grad,
    branch,
    heads,
):
    core = place_ref[3]
    hidden = middle_ref[...]
    scale = lax.rsqrt(jnp.mean(hidden * hidden, axis=-1, keepdims=True) + epsilon)
    incoming = mine_0[...] + mine_1[...] + other_0[...].astype(wide) + other_1[...].astype(wide)
    weighted = incoming * gain_ref[8:9, :]
    inner = jnp.mean(weighted * hidden, axis=-1, keepdims=True)
    grad = cotangent_ref[...].astype(wide) + (scale * weighted - hidden * scale**3 * inner)
    grad_ref[...] = grad
    branch[...] = grad.astype(low)

    @pl.when(pl.program_id(0) == 0)
    def _():
        gain_grad[...] = jnp.zeros_like(gain_grad)

    summed = jnp.sum(incoming * hidden * scale, axis=0, keepdims=True)
    gain_grad[...] += jnp.broadcast_to(summed, gain_grad.shape)
    columns, span = w_mine.shape[1], heads_mine.shape[1]

    def part(ref, owner, size):
        return ref[:, pl.ds(pl.multiple_of(owner * size, LANES), size)]

    branch_mine[...] = part(branch, core, columns)
    branch_other[...] = part(branch, 1 - core, columns)
    for at in range(0, 2 * span, SLAB):
        heads[:, at : at + SLAB] = (
            across(branch_mine[...], w_mine[at : at + SLAB, :])
            + across(branch_other[...], w_other[at : at + SLAB, :])
        ).astype(low)
    heads_mine[...] = part(heads, core, span)
    heads_other[...] = part(heads, 1 - core, span)


def middle_back(place, middle, parts, cotangent, gains, w_mine, w_other, after=()):
    count, width = middle.shape
    tile, columns, span = count // 2, w_mine.shape[1], w_mine.shape[0] // 2
    gain_grad = shaped((8, width), wide)
    return run(
        middle_back_kernel,
        "middle_back",
        place,
        (2,),
        [
            *[(item, rows_of(tile, width)) for item in (middle, *parts, cotangent)],
            (gains, whole(gains)),
            (w_mine, whole(w_mine)),
            (w_other, whole(w_other)),
        ],
        [
            (shaped((count, width), wide), rows_of(tile, width)),
            (shaped((count, columns), low), rows_of(tile, columns)),
            (shaped((count, columns), low), rows_of(tile, columns)),
            (shaped((count, span), low), rows_of(tile, span)),
            (shaped((count, span), low), rows_of(tile, span)),
            (gain_grad, whole(gain_grad)),
        ],
        [pltpu.VMEM((tile, width), low), pltpu.VMEM((tile, 2 * span), low)],
        after,
        us=15,
    )


def out_grad_kernel(
    place_ref,
    own_mine,
    own_other,
    far_mine,
    far_other,
    branch_own,
    branch_far,
    *refs,
):
    outs, (grad, sems) = refs[:5], refs[5:]
    core = place_ref[3]
    span = own_mine.shape[1]
    for owner, own, far in ((core, own_mine, far_mine), (1 - core, own_other, far_other)):
        for at in range(0, span, SLAB):
            part = down(own[:, at : at + SLAB], branch_own[...])
            part = part + down(far[:, at : at + SLAB], branch_far[...])
            grad[pl.ds(pl.multiple_of(owner * span + at, LANES), SLAB), :] = part.astype(low)
    for k in range(4):
        base = (place_ref[0] ^ k) * 4
        send_off(place_ref, k, (grad,), base, OUT_PLAN, OUT_HALF, outs, sems)
    fill_spare(grad.at[pl.ds(0, 16), pl.ds(0, SLAB)], 144, 16, OUT_HALF, outs, sems)
    drain(outs, sems)


def out_grad(place, own_mine, own_other, far_mine, far_other, branch_own, branch_far, after=()):
    columns = branch_own.shape[1]
    operands = (own_mine, own_other, far_mine, far_other, branch_own, branch_far)
    return run(
        out_grad_kernel,
        "out_grad",
        place,
        (1,),
        [(item, whole(item)) for item in operands],
        sent_shapes(OUT_HALF, SLAB),
        [pltpu.VMEM((H * LANES, columns), low), pltpu.SemaphoreType.DMA((5,))],
        after,
        us=10,
    )


FFN_TILE = 320
FFN_STEP = 256
FFN_SPAN = 768


def load_tokens(x_ref, c_ref, x_own, x_far, c_own, c_far, sems):
    count = x_far.shape[0]
    for index, (ref, far, own) in enumerate(((x_ref, x_far, x_own), (c_ref, c_far, c_own))):
        for part, source in enumerate((far, own)):
            target = ref.at[pl.ds(part * count, count)]
            pltpu.make_async_copy(source, target, sems.at[index]).start()


def ffn_forward(step, tiles, x_ref, c_ref, weights, sums, middles, at_rows):
    gate_w, up_w, down_w = weights
    inner, grad_gate, grad_up = middles
    units, width = gate_w.shape[1], gate_w.shape[0]
    rows = pl.ds(pl.multiple_of(step * FFN_TILE, FFN_TILE), FFN_TILE)

    @pl.loop(0, units // FFN_STEP)
    def _(index):
        at = pl.ds(pl.multiple_of(index * FFN_STEP, FFN_STEP), FFN_STEP)
        gate = project(x_ref[rows, :], gate_w[:, at])
        upward = project(x_ref[rows, :], up_w[:, at])
        grad_inner = across(c_ref[rows, :], down_w[at, :])
        sigma = 1.0 / (1.0 + jnp.exp(-gate))
        silu = gate * sigma
        inner[at_rows, at] = (silu * upward).astype(low)
        grad_up[at_rows, at] = (grad_inner * silu).astype(low)
        grad_gate[at_rows, at] = (
            grad_inner * upward * sigma * (1.0 + gate * (1.0 - sigma))
        ).astype(low)

    for part in range(2):

        @pl.when((step >= part * tiles // 2) & (step < (part + 1) * tiles // 2))
        def _():
            out_ref, normed_ref = sums[2 * part : 2 * part + 2]

            @pl.loop(0, width // SLAB)
            def _(index):
                at = pl.ds(pl.multiple_of(index * SLAB, SLAB), SLAB)
                out = project(inner[at_rows, :], down_w[:, at])
                normed = across(grad_gate[at_rows, :], gate_w[at, :])
                normed = normed + across(grad_up[at_rows, :], up_w[at, :])
                out_ref[:, at] = out.astype(out_ref.dtype)
                normed_ref[:, at] = normed.astype(normed_ref.dtype)


def ffn_backward(place_ref, k, x_ref, c_ref, middles, stages, turned, turned_units, sent, sems):
    inner, grad_gate, grad_up = middles
    stage_gate, stage_up, stage_down = stages
    width, units = x_ref.shape[1], inner.shape[1]
    depth = place_ref[0] ^ k
    rows, span = width // 4, units // 4
    here = pl.ds(pl.multiple_of(depth * rows, LANES), rows)
    there = pl.ds(pl.multiple_of(depth * span, LANES), span)
    turned[...] = x_ref[:, here].T
    to = pl.ds(pl.multiple_of(k * rows, 16), rows)
    to_units = pl.ds(pl.multiple_of(k * span, 16), span)
    stage_gate[to, :] = project(turned[...], grad_gate[...]).astype(low)
    stage_up[to, :] = project(turned[...], grad_up[...]).astype(low)
    turned_units[...] = inner[:, there].T

    @pl.loop(0, width // FFN_SPAN)
    def _(index):
        at = pl.ds(pl.multiple_of(index * FFN_SPAN, FFN_SPAN), FFN_SPAN)
        stage_down[to_units, at] = project(turned_units[...], c_ref[:, at]).astype(low)

    send_off(place_ref, k, stages, k * 4, FFN_PLAN, FFN_HALF, sent, sems)


def ffn_kernel(tiles, place_ref, *refs):
    tokens, pieces, sums, sent = refs[:4], refs[4:9], refs[9:13], refs[13:18]
    x_ref, c_ref, *rest = refs[18:]
    weights, middles, stages, rest = rest[:3], rest[3:6], rest[6:9], rest[9:]
    turned, turned_units, x_sems, in_sems, out_sems = rest
    step = pl.program_id(0)

    @pl.when(step == 0)
    def _():
        load_tokens(x_ref, c_ref, *tokens, x_sems)
        fetch(place_ref, pieces, FFN_PLAN, FFN_HALF, weights, in_sems)
        drain((x_ref, c_ref), x_sems)
        drain(weights, in_sems)

    @pl.when(step < tiles)
    def _():
        rows = pl.ds(pl.multiple_of(step * FFN_TILE, FFN_TILE), FFN_TILE)
        ffn_forward(step, tiles, x_ref, c_ref, weights, sums, middles, rows)

    @pl.when(step >= tiles)
    def _():
        k = step - tiles
        ffn_backward(
            place_ref, k, x_ref, c_ref, middles, stages, turned, turned_units, sent, out_sems
        )

    @pl.when(step == tiles + 3)
    def _():
        drain(sent, out_sems)


def ffn_forward_kernel(tiles, place_ref, *refs):
    tokens, pieces, sums, middles = refs[:4], refs[4:9], refs[9:13], refs[13:16]
    x_ref, c_ref, *weights, x_sems, in_sems = refs[16:]
    step = pl.program_id(0)

    @pl.when(step == 0)
    def _():
        load_tokens(x_ref, c_ref, *tokens, x_sems)
        fetch(place_ref, pieces, FFN_PLAN, FFN_HALF, weights, in_sems)
        drain((x_ref, c_ref), x_sems)
        drain(weights, in_sems)

    ffn_forward(step, tiles, x_ref, c_ref, weights, sums, middles, slice(None))


def ffn_backward_kernel(place_ref, *refs):
    tokens, sources, sent = refs[:4], refs[4:7], refs[7:12]
    x_ref, c_ref, *rest = refs[12:]
    middles, stages, rest = rest[:3], rest[3:6], rest[6:]
    turned, turned_units, x_sems, in_sems, out_sems = rest
    k = pl.program_id(0)

    @pl.when(k == 0)
    def _():
        load_tokens(x_ref, c_ref, *tokens, x_sems)
        for index in (1, 2, 0):
            pltpu.make_async_copy(sources[index], middles[index], in_sems.at[index]).start()
        drain((x_ref, c_ref), x_sems)
        drain(middles, in_sems)

    ffn_backward(
        place_ref, k, x_ref, c_ref, middles, stages, turned, turned_units, sent, out_sems
    )

    @pl.when(k == 3)
    def _():
        drain(sent, out_sems)


FFN_UNITS = 1024


def ffn_sums(count, width):
    last = count // FFN_TILE - 1
    early = pl.BlockSpec((FFN_TILE, width), lambda i, place: (jnp.minimum(i, last), 0))
    late = pl.BlockSpec(
        (FFN_TILE, width), lambda i, place: (jnp.clip(i - last - 1, 0, last), 0)
    )
    pairs = ((low, early), (low, early), (wide, late), (wide, late))
    return [(shaped((count, width), kind), spec) for kind, spec in pairs]


def ffn_scratch(count, width, weights=True, middles=True, stages=True):
    weight = [pltpu.VMEM((width, FFN_UNITS), low)] * 2 + [pltpu.VMEM((FFN_UNITS, width), low)]
    shapes = [pltpu.VMEM((count, width), low)] * 2
    shapes += weight if weights else []
    shapes += [pltpu.VMEM((count, FFN_UNITS), low)] * 3 if middles else []
    if stages:
        shapes += weight
        shapes += [pltpu.VMEM((width // 4, count), low)]
        shapes += [pltpu.VMEM((FFN_UNITS // 4, count), low)]
    shapes += [pltpu.SemaphoreType.DMA((2,)), pltpu.SemaphoreType.DMA((3,))]
    return shapes + ([pltpu.SemaphoreType.DMA((5,))] if stages else [])


def ffn_chunk(place, tokens, pieces, after=()):
    count, width = tokens[0].shape
    tiles = 2 * count // FFN_TILE
    results = run(
        functools.partial(ffn_kernel, tiles),
        "ffn",
        place,
        (tiles + 4,),
        [(item, anywhere) for item in (*tokens, *pieces)],
        ffn_sums(count, width) + sent_shapes(FFN_HALF, SLAB),
        ffn_scratch(2 * count, width),
        after,
        us=60,
    )
    return results[:4], results[4:]


def ffn_chunk_forward(place, tokens, pieces, after=()):
    count, width = tokens[0].shape
    tiles = 2 * count // FFN_TILE
    middle = pl.BlockSpec((FFN_TILE, FFN_UNITS), lambda i, place: (i, 0))
    results = run(
        functools.partial(ffn_forward_kernel, tiles),
        "ffn_forward",
        place,
        (tiles,),
        [(item, anywhere) for item in (*tokens, *pieces)],
        ffn_sums(count, width) + [(shaped((2 * count, FFN_UNITS), low), middle)] * 3,
        ffn_scratch(2 * count, width, middles=False, stages=False),
        after,
        us=36,
    )
    return results[:4], results[4:]


def ffn_chunk_backward(place, tokens, middles, after=()):
    count, width = tokens[0].shape
    return run(
        ffn_backward_kernel,
        "ffn_backward",
        place,
        (4,),
        [(item, anywhere) for item in (*tokens, *middles)],
        sent_shapes(FFN_HALF, SLAB),
        ffn_scratch(2 * count, width, weights=False),
        after,
        us=22,
    )


def input_back_kernel(
    tiles, place_ref, own_q, own_k, own_v, far_q, far_k, far_v, x_own, x_far, w_ref, *refs
):
    grad_ref, own_ref, far_ref, gain_grad = refs
    step = pl.program_id(0)

    @pl.when(step == 0)
    def _():
        gain_grad[...] = jnp.zeros_like(gain_grad)

    def squeezed(query, key, value):
        parts = []
        for ref in (query, key):
            for at in range(0, ref.shape[1], LANES):
                head = ref[:, at : at + LANES].astype(wide)
                parts.append(head[:, :HALF])
                parts.append(head[:, LANES // 2 : LANES // 2 + HALF])
        for at in range(0, value.shape[1], LANES):
            parts.append(value[:, at : at + LANES].astype(wide)[:, :HD])
        return jnp.concatenate(parts, axis=1).astype(low)

    def rest(x_ref, incoming):
        hidden = x_ref[...].astype(wide)
        scale = lax.rsqrt(jnp.mean(hidden * hidden, axis=-1, keepdims=True) + epsilon)
        summed = jnp.sum(incoming * hidden * scale, axis=0, keepdims=True)
        gain_grad[...] += jnp.broadcast_to(summed, gain_grad.shape)

    @pl.when(step < tiles)
    def _():
        grad_ref[...] = squeezed(far_q, far_k, far_v)
        incoming = across(grad_ref[...], w_ref[...])
        far_ref[...] = incoming.astype(low)
        rest(x_far, incoming)

    @pl.when(step >= tiles)
    def _():
        grad_ref[...] = squeezed(own_q, own_k, own_v)
        incoming = across(grad_ref[...], w_ref[...])
        own_ref[...] = incoming
        rest(x_own, incoming)


def input_back(place, own, far, x_own, x_far, weight, after=()):
    count, width = 2 * x_own.shape[0], x_own.shape[1]
    tile = 320
    tiles = count // 2 // tile
    gain_grad = shaped((8, width), wide)

    def late(columns):
        return pl.BlockSpec((tile, columns), lambda i, place: (jnp.maximum(i - tiles, 0), 0))

    def early(columns):
        return pl.BlockSpec((tile, columns), lambda i, place: (jnp.minimum(i, tiles - 1), 0))

    def both(columns):
        return pl.BlockSpec((tile, columns), lambda i, place: (lax.rem(i + tiles, 2 * tiles), 0))

    return run(
        functools.partial(input_back_kernel, tiles),
        "input_back",
        place,
        (2 * tiles,),
        [(item, late(item.shape[1])) for item in own]
        + [(item, early(item.shape[1])) for item in far]
        + [(x_own, late(width)), (x_far, early(width)), (weight, whole(weight))],
        [
            (shaped((count, width), low), both(width)),
            (shaped((count // 2, width), wide), late(width)),
            (shaped((count // 2, width), low), early(width)),
            (gain_grad, whole(gain_grad)),
        ],
        after=after,
        us=15,
    )


def qkv_grad_kernel(place_ref, x_ref, grad_ref, gain_one, gain_two, *refs):
    outs, (stage, gain_rows, turned, sems) = refs[:5], refs[5:]
    k = pl.program_id(0)
    width = grad_ref.shape[1]

    @pl.when(k == 0)
    def _():
        gap = jnp.zeros((8, LANES - HD), wide)
        row = lax.broadcasted_iota(jnp.int32, (16, LANES), 0)
        gain_rows[...] = jnp.zeros_like(gain_rows)
        for block in range(BLOCKS):
            for index, gain in enumerate((gain_one, gain_two)):
                part = jnp.concatenate([gain[:, block * HD : (block + 1) * HD], gap], axis=1)
                part = jnp.where(row == 0, jnp.concatenate([part, part], axis=0), 0.0)
                gain_rows[
                    16 * block : 16 * block + 16, index * LANES : (index + 1) * LANES
                ] = part.astype(low)

    depth = place_ref[0] ^ k
    rows = width // 4
    turned[...] = x_ref[:, pl.ds(pl.multiple_of(depth * rows, LANES), rows)].T
    to = pl.ds(pl.multiple_of(depth * rows, 16), rows)

    @pl.loop(0, width // SLAB)
    def _(index):
        at = pl.ds(pl.multiple_of(index * SLAB, SLAB), SLAB)
        stage[to, at] = project(turned[...], grad_ref[:, at]).astype(low)

    send_off(place_ref, k, (stage, gain_rows), depth * 4, QKV_PLAN, QKV_HALF, outs, sems)

    @pl.when(k == 3)
    def _():
        fill_spare(gain_rows.at[pl.ds(0, 16)], GAINS + 16, 16, QKV_HALF, outs, sems)
        drain(outs, sems)


def qkv_grad(place, x, grad, gain_one, gain_two, after=()):
    count, width = x.shape
    operands = (x, grad, gain_one, gain_two)
    return run(
        qkv_grad_kernel,
        "qkv_grad",
        place,
        (4,),
        [(item, whole(item)) for item in operands],
        sent_shapes(QKV_HALF, SLAB),
        [
            pltpu.VMEM((width, width), low),
            pltpu.VMEM((BLOCKS * 16, SLAB), low),
            pltpu.VMEM((width // 4, count), low),
            pltpu.SemaphoreType.DMA((5,)),
        ],
        after,
        us=15,
    )


def tokens_grad_kernel(place_ref, x_ref, middle_ref, mine_ref, other_ref, gain_ref, out_ref):
    hidden = x_ref[...].astype(wide)
    scale = lax.rsqrt(jnp.mean(hidden * hidden, axis=-1, keepdims=True) + epsilon)
    weighted = (mine_ref[...] + other_ref[...].astype(wide)) * gain_ref[0:1, :]
    inner = jnp.mean(weighted * hidden, axis=-1, keepdims=True)
    out_ref[...] = middle_ref[...] + (scale * weighted - hidden * scale**3 * inner)


def tokens_grad(place, x, grad_middle, mine, other, gains, after=()):
    count, width = x.shape
    tile = 128
    return run(
        tokens_grad_kernel,
        "tokens_grad",
        place,
        (count // tile,),
        [(item, rows_of(tile, width)) for item in (x, grad_middle, mine, other)]
        + [(gains, whole(gains))],
        [(shaped((count, width), wide), rows_of(tile, width))],
        after=after,
    )[0]


def output_kernel(place_ref, middle_ref, mine_0, mine_1, other_0, other_1, out_ref):
    total = middle_ref[...] + mine_0[...] + mine_1[...]
    total = total + other_0[...].astype(wide) + other_1[...].astype(wide)
    out_ref[...] = total.astype(low)


def output_of(place, middle, parts, after=()):
    count, width = middle.shape
    tile = 128
    return run(
        output_kernel,
        "output",
        place,
        (count // tile,),
        [(item, rows_of(tile, width)) for item in (middle, *parts)],
        [(shaped((count, width), low), rows_of(tile, width))],
        after=after,
    )[0]


def swap(array):
    return lax.ppermute(array, "rep", [(0, 1), (1, 0)])


def hop(array, z_flip, y_flip, x_flip):
    flip = (z_flip * 2 + y_flip) * 2 + x_flip
    return lax.ppermute(array, "fsdp", [(chip, chip ^ flip) for chip in range(BLOCKS)])


def hop_x(array):
    return hop(array, 0, 0, 1)


def hop_y(array):
    return hop(array, 0, 1, 0)


def near(line):
    return hop_x(line), hop_y(line)


def pieces_of(blocks):
    cut = blocks.reshape(4, 2, 2, *blocks.shape[1:])
    half = blocks.shape[1] // 2
    far = cut[:, 1, 1]
    return cut[:, 0, 0], cut[:, 0, 1], cut[:, 1, 0], far[:, :half], far[:, half:]


def blocks_of(sent):
    to_x, to_y, late_x, late_y, own = sent
    near_x = jnp.stack([to_x[1], late_x], axis=1)
    near_y = jnp.stack([late_y, to_y[1]], axis=1)
    far = jnp.stack([to_x[0], to_y[0]], axis=1)
    cut = jnp.stack([jnp.stack([own, near_x], 1), jnp.stack([near_y, far], 1)], 1)
    return cut.reshape(BLOCKS, 2 * own.shape[2], own.shape[3])


def layout(length_row, count):
    ends = jnp.cumsum(length_row)
    slots = jnp.arange(count, dtype=jnp.int32)
    passed = (slots[:, None] >= ends[None, :]).astype(jnp.int32)
    segment = jnp.sum(passed, axis=1)
    position = slots - jnp.sum(passed * length_row[None, :], axis=1)
    return position, segment


class Direct:
    def __init__(self, place, weights):
        self.place = place
        self.weights = weights

    def pack_first(self):
        return pack_first(self.place, *self.weights[:4], *self.weights[7:])

    def pack_ffn(self, chunk, after):
        return pack_ffn(self.place, chunk, *self.weights[4:7], after)

    def step_1(self, shard, after=()):
        return pair_up(self.place, shard, hop(shard, 2, 0, 0), after)

    def step_2(self, pair, after=()):
        return line_up(self.place, pair, hop(pair, 1, 0, 0), after)

    def step_3(self, line):
        return near(line)

    def step_4(self, line, sides, after=()):
        upper, lower = halves(self.place, *sides, after)
        return line, *sides, hop_y(upper), hop_x(lower)

    def scatter_1(self, sent):
        return hop_x(sent[0]), hop_y(sent[1])

    def scatter_2(self, sent, got, after):
        late_x, late_y = merge(self.place, sent[2], sent[3], got[0], got[1], after)
        return late_x, (hop_x(late_x), hop_y(late_y))

    def scatter_3(self, groups, after):
        groups = [(sent[4], *got, *more) for sent, got, more in groups]
        kept, kept_far, part = sum_plane(self.place, groups, after)
        return kept, (kept_far, hop(part, 1, 0, 0))

    def scatter_4(self, kept, parts, after):
        kept_far, near = parts
        token = sum_pass(self.place, kept_far, near, after)
        return token, (near, hop(token, 2, 0, 0))

    def scatter_5(self, kept, parts, after):
        total, total_low = sum_line(self.place, kept, parts[0], parts[1], after)
        return total, swap(total_low)

    def finish_ffn(self, mine, other, shapes, after):
        return unpack_ffn(self.place, mine, other, shapes, after)

    def finish_first(self, mine, other, shapes, owned):
        grads = unpack_first(self.place, mine, other, shapes)
        row = GAINS + OUT_HALF
        both = mine[row, : 2 * LANES] + other[row, : 2 * LANES].astype(wide)
        return grads, (both[:owned], both[LANES : LANES + owned])


def on_device(
    direct,
    tokens,
    lengths,
    attn_gain,
    w_query,
    w_key,
    w_value,
    w_out,
    ffn_gain,
    w_gate,
    w_up,
    w_down,
    cotangent,
):
    count, width = tokens.shape
    owned = attn_gain.shape[0]
    core = lax.axis_index("rep")
    if direct:
        index = lax.axis_index("fsdp")
        spot = (index // 4, (index // 2) % 2, index % 2)
    else:
        spot = (0, 0, 0)
    place = jnp.stack([jnp.int32(item) for item in (*spot, core)])
    weights = (w_query, w_key, w_value, w_out, w_gate, w_up, w_down, attn_gain, ffn_gain)
    routes = Direct(place, weights) if direct else Whole(place, weights)

    first = routes.pack_first()
    far_tokens, far_cotangent = swap(tokens), swap(cotangent)
    laid = [layout(row, count) for row in (lengths[0], swap(lengths)[0])]
    segment = jnp.stack([item[1] for item in laid])
    cosine, sine = turn_table(jnp.concatenate([item[0] for item in laid]))

    pair_first = routes.step_1(first)
    line_first = routes.step_2(pair_first, (far_tokens, far_cotangent, segment, cosine, sine))
    sides_first = routes.step_3(line_first)
    chunk_0 = routes.pack_ffn(0, (line_first,))
    pair_0 = routes.step_1(chunk_0)
    pieces_first = routes.step_4(line_first, sides_first)
    line_0 = routes.step_2(pair_0, (pair_0, *sides_first))
    sides_0 = routes.step_3(line_0)
    w_mine = out_weight(place, pieces_first, tokens.shape[1], (line_0,))
    w_other = swap(w_mine)
    normed_low, queries, keys, values, w_qkv, gains = project_qkv(
        place, tokens, far_tokens, cosine, sine, pieces_first, (w_mine,)
    )
    chunk_1 = routes.pack_ffn(1, (keys,))
    far_mine, far_total = attend(place, queries, keys, values, segment, 1, (chunk_1,))
    own_other = swap(far_mine)
    pair_1 = routes.step_1(chunk_1, (far_mine,))
    pieces_0 = routes.step_4(line_0, sides_0)
    own_mine, own_total = attend(
        place, queries, keys, values, segment, 0, (pair_1, *sides_0)
    )
    far_other = swap(own_mine)
    middle, normed_own = middle_of(
        place, tokens, own_mine, own_other, w_mine, w_other, gains
    )
    normed_far = swap(normed_own)
    line_1 = routes.step_2(pair_1, (normed_own, *pieces_0[3:]))
    sides_1 = routes.step_3(line_1)

    inputs = (normed_own, normed_far, cotangent, far_cotangent)
    sums_0, middles_0 = ffn_chunk_forward(place, inputs, pieces_0, (line_1, far_other))
    out_far_0, norm_far_0 = swap(sums_0[0]), swap(sums_0[1])
    pieces_1 = routes.step_4(line_1, sides_1, (sums_0[0],))
    sent_0 = ffn_chunk_backward(place, inputs, middles_0, (pieces_1[0],))
    got_0 = routes.scatter_1(sent_0)
    sums_1, sent_1 = ffn_chunk(place, inputs, pieces_1)
    out_far_1, norm_far_1 = swap(sums_1[0]), swap(sums_1[1])
    got_1 = routes.scatter_1(sent_1)

    norms = (sums_0[3], sums_1[3], norm_far_0, norm_far_1)
    grad_middle, branch_mine, branch_sent, heads_mine, heads_sent, ffn_gain_grad = middle_back(
        place, middle, norms, cotangent, gains, w_mine, w_other, got_0
    )
    branch_far, heads_far = swap(branch_sent), swap(heads_sent)
    own_grads = attend_back(
        place, queries, keys, values, heads_mine, own_total, segment, cosine, sine, 0
    )
    token, more_0 = routes.scatter_2(sent_0, got_0, (own_grads[0],))
    far_grads = attend_back(
        place,
        queries,
        keys,
        values,
        heads_far,
        far_total,
        segment,
        cosine,
        sine,
        1,
        (token,),
    )
    token, more_1 = routes.scatter_2(sent_1, got_1, (far_grads[0],))
    sent_out = out_grad(
        place,
        own_mine,
        own_other,
        far_mine,
        far_other,
        branch_mine,
        branch_far,
        (token,),
    )
    got_out = routes.scatter_1(sent_out)
    kept_0, parts_0 = routes.scatter_3([(sent_0, got_0, more_0)], (sent_out[4],))
    grad_qkv, own_part, far_part, attn_gain_grad = input_back(
        place, own_grads, far_grads, tokens, far_tokens, w_qkv, (kept_0,)
    )
    own_rest = swap(far_part)
    sent_qkv = qkv_grad(place, normed_low, grad_qkv, attn_gain_grad, ffn_gain_grad)
    got_qkv = routes.scatter_1(sent_qkv)

    token, more_out = routes.scatter_2(sent_out, got_out, (sent_qkv[4],))
    token, parts_0 = routes.scatter_4(kept_0, parts_0, (token,))
    kept_1, parts_1 = routes.scatter_3([(sent_1, got_1, more_1)], (token,))
    token, more_qkv = routes.scatter_2(sent_qkv, got_qkv, (kept_1,))
    owned_0, other_0 = routes.scatter_5(kept_0, parts_0, (token,))
    token, parts_1 = routes.scatter_4(kept_1, parts_1, (owned_0,))
    groups = [(sent_qkv, got_qkv, more_qkv), (sent_out, got_out, more_out)]
    kept_qkv, parts_qkv = routes.scatter_3(groups, (token,))
    outs = (sums_0[2], sums_1[2], out_far_0, out_far_1)
    output = output_of(place, middle, outs, (kept_qkv,))
    owned_1, other_1 = routes.scatter_5(kept_1, parts_1, (output,))
    token, parts_qkv = routes.scatter_4(kept_qkv, parts_qkv, (owned_1,))
    grad_tokens = tokens_grad(place, tokens, grad_middle, own_part, own_rest, gains, (token,))
    shapes = [w_gate.shape, w_up.shape, w_down.shape]
    grad_gate, grad_up, grad_down = routes.finish_ffn(
        (owned_0, owned_1), (other_0, other_1), shapes, (grad_tokens,)
    )
    owned_qkv, other_qkv = routes.scatter_5(kept_qkv, parts_qkv, (grad_gate,))
    shapes = [w_query.shape, w_key.shape, w_value.shape, w_out.shape]
    grads, gain_grads = routes.finish_first(owned_qkv, other_qkv, shapes, owned)
    return (
        output,
        grad_tokens,
        gain_grads[0],
        *grads,
        gain_grads[1],
        grad_gate,
        grad_up,
        grad_down,
    )


class Whole:
    def __init__(self, place, weights):
        self.place = place
        query, key, value, out, gate, up, down_w, gain_one, gain_two = weights
        core = place[3]
        self.core = core
        count = query.shape[1] // query.shape[0]
        self.count = count
        rows = query.shape[1] // BLOCKS

        def full(shard):
            return lax.all_gather(shard, "fsdp", axis=0, tiled=True)

        def mine(weight):
            columns = weight.shape[1] // 2
            return lax.dynamic_slice_in_dim(weight, core * columns, columns, axis=1)

        def slabs(weight):
            blocks = weight.reshape(BLOCKS, -1, weight.shape[1])
            return [blocks[:, :, at : at + SLAB] for at in range(0, weight.shape[1], SLAB)]

        qkv = full(jnp.concatenate([mine(query), mine(key), mine(value)], axis=1))
        gain_rows = jnp.zeros((BLOCKS, 16, SLAB), low)
        for index, gain in enumerate((gain_one, gain_two)):
            part = full(gain).reshape(BLOCKS, rows)
            gain_rows = gain_rows.at[:, 0, index * LANES : index * LANES + rows].set(part)
        square = full(mine(out)).reshape(BLOCKS, rows, -1)
        rest = square[:, :, SLAB:]
        rest = jnp.concatenate([rest[:, : rows // 2], rest[:, rows // 2 :]], axis=2)
        parts = slabs(qkv) + [gain_rows, square[:, :, :SLAB], rest]
        self.first = pieces_of(jnp.concatenate(parts, axis=1))
        quarter = down_w.shape[0] // (2 * CHUNKS)
        self.quarter = quarter

        def units(weight, chunk):
            split = weight.reshape(weight.shape[0], count, 2 * CHUNKS, quarter)
            part = lax.dynamic_index_in_dim(split, CHUNKS * core + chunk, 2, keepdims=False)
            return full(part.reshape(weight.shape[0], count * quarter))

        chunks = []
        for chunk in range(CHUNKS):
            at = (CHUNKS * core + chunk) * quarter
            part = full(lax.dynamic_slice_in_dim(down_w, at, quarter, axis=0))
            parts = slabs(units(gate, chunk)) + slabs(units(up, chunk)) + slabs(part)
            chunks.append(pieces_of(jnp.concatenate(parts, axis=1)))
        self.ffn_0, self.ffn_1 = chunks

    def pack_first(self):
        return self.first

    def pack_ffn(self, chunk, after):
        return (self.ffn_0, self.ffn_1)[chunk]

    def step_1(self, shard, after=()):
        return shard

    def step_2(self, pair, after=()):
        return pair

    def step_3(self, line):
        return ()

    def step_4(self, line, sides, after=()):
        return line

    def scatter_1(self, sent):
        return blocks_of(sent)

    def scatter_2(self, sent, got, after):
        return got, got

    def scatter_3(self, groups, after):
        blocks = jnp.concatenate([got for _, got, _ in groups], axis=1)
        return blocks, blocks

    def scatter_4(self, kept, parts, after):
        return kept, kept

    def scatter_5(self, kept, parts, after):
        return kept, kept

    def split(self, blocks, widths):
        parts, row = [], 0
        for rows, slabs in widths:
            taken = []
            for _ in range(slabs):
                taken.append(blocks[:, row : row + rows])
                row += rows
            part = jnp.concatenate(taken, axis=2)
            part = part.reshape(BLOCKS * rows, part.shape[2])
            parts.append(lax.psum_scatter(part, "fsdp", scatter_dimension=0, tiled=True))
        return parts

    def ordered(self, part):
        other = swap(part).astype(wide)
        part = part.astype(wide)
        first = jnp.where(self.core == 0, part, other)
        return first, jnp.where(self.core == 0, other, part)

    def finish_ffn(self, mine, other, shapes, after):
        gates, ups, downs = [], [], []
        for blocks in mine:
            gate, up, down_w = self.split(blocks, ((96, 2), (96, 2), (64, 3)))
            gates.append(self.ordered(gate))
            ups.append(self.ordered(up))
            downs.append(self.ordered(down_w))

        def columns(pairs):
            parts = [pairs[chunk][owner] for owner in range(2) for chunk in range(CHUNKS)]
            rows = parts[0].shape[0]
            parts = [part.reshape(rows, self.count, self.quarter) for part in parts]
            return jnp.stack(parts, axis=2).reshape(rows, -1)

        grad_down = [downs[chunk][owner] for owner in range(2) for chunk in range(CHUNKS)]
        return columns(gates), columns(ups), jnp.concatenate(grad_down, axis=0)

    def finish_first(self, mine, other, shapes, owned):
        (qkv,) = self.split(mine[:, :GAINS], ((96, 3),))
        blocks = mine[:, 2 * QKV_HALF :]
        rest = blocks[:, 96:144]
        rest = jnp.concatenate([rest[:, :, :256], rest[:, :, 256:]], axis=1)
        (square,) = self.split(jnp.concatenate([blocks[:, :96], rest], axis=2), ((96, 1),))
        pair = self.ordered(qkv)
        grads, at = [], 0
        for shape in shapes[:3]:
            columns = shape[1] // 2
            grads.append(jnp.concatenate([item[:, at : at + columns] for item in pair], axis=1))
            at += columns
        grads.append(jnp.concatenate(self.ordered(square), axis=1))
        rows = mine[:, GAINS, : 2 * LANES].astype(wide)
        rows = rows + swap(rows)
        gains = []
        for index in range(2):
            gain = rows[:, index * LANES : index * LANES + 96].reshape(-1)
            gains.append(lax.psum_scatter(gain, "fsdp", scatter_dimension=0, tiled=True))
        return grads, gains


def solution(mesh):
    rows = P(("rep", "fsdp"), None)
    split = P("fsdp", None)
    gain = P("fsdp")
    return jax.shard_map(
        functools.partial(on_device, mesh.shape["fsdp"] == BLOCKS),
        mesh=mesh,
        in_specs=(rows, rows, gain) + (split,) * 4 + (gain,) + (split,) * 3 + (rows,),
        out_specs=(rows, rows, gain) + (split,) * 4 + (gain,) + (split,) * 3,
        check_vma=False,
    )
```

time: 2640 us -> 675 us (0.26)
  waiting for transfers between devices: 2000 us -> 162 us
  Pallas kernels: 0 us -> 410 us
  matrix products: 353 us -> 0 us
  blocking collectives: 122 us -> 0 us
  other arithmetic: 78.9 us -> 7.94 us
  starting transfers between devices: 0.6 us -> 56.6 us
    reduce_scatter x7 -> x0, waiting for transfers between devices: 1440 us -> none  [the longest x1 364 us: reduce_ffn(): lax.psum_scatter(grad_down, 'fsdp', scatter_dimension=0, tiled=True)]
    all_gather x7 -> x0, waiting for transfers between devices: 551 us -> none  [the longest x1 144 us: on_device(): lax.all_gather(w_up, 'fsdp', axis=0, tiled=True)]
    pallas_call x0 -> x43, Pallas kernels: none -> 410 us  [run(): pl.pallas_call(body, grid_spec=pltpu.PrefetchScalarGridSpec(num_scalar_pr...]
    dot_general x27 -> x0, matrix products: 353 us -> none  [the longest x7 79.5 us: weight_grad(): lax.dot_general(left, right, (((0,), (0,)), ((), ())), preferred_element_...]
    ppermute x0 -> x57, waiting for transfers between devices: none -> 162 us  [the longest x40 153 us: hop(): lax.ppermute(array, 'fsdp', [(chip, chip ^ flip) for chip in range(BLOCKS)])]
    unnamed x2 -> x0, blocking collectives: 119 us -> none
    ppermute x0 -> x57, starting transfers between devices: none -> 56.6 us  [the longest x40 53.9 us: hop(): lax.ppermute(array, 'fsdp', [(chip, chip ^ flip) for chip in range(BLOCKS)])]
    convert_element_type x24 -> x1, other arithmetic: 40.5 us -> 0.01 us  [turn_table(): angle = position.astype(wide)[:, None] * frequency[None, :]]
  transfers between devices with their start and end apart: 15 -> 57, of which waited for: 14 -> 22; matrix products, arithmetic and copies ran while one was open for 14% -> 1% of each run, Pallas kernels for 0% -> 59%
where the time goes in v2:
time: 675 us; the launch traced here: 669 us
  Pallas kernels  410 us (61%)
  waiting for transfers between devices  162 us (24%)
  starting transfers between devices  56.6 us (8%)
  local copies, waits for them, and re-layouts  30.1 us (4%)
  other arithmetic  7.94 us (1%)
    pallas_call x43, Pallas kernels, run(): pl.pallas_call(body, grid_spec=pltpu.PrefetchScalarGridSpec(num_scalar_pr...  410 us
    ppermute x40, waiting for transfers between devices, hop(): lax.ppermute(array, 'fsdp', [(chip, chip ^ flip) for chip in range(BLOCKS)])  153 us
    ppermute x40, starting transfers between devices, hop(): lax.ppermute(array, 'fsdp', [(chip, chip ^ flip) for chip in range(BLOCKS)])  53.9 us
    unnamed x108, local copies, waits for them, and re-layouts  28.9 us
  transfers between devices with their start and end apart: 57, of which 22 were waited for; matrix products, arithmetic and copies ran while one was open for 1% of the time, Pallas kernels for 59%

profile of v2, /device:TPU:0, one launch (start us, length us, event | category | flops | bytes accessed | tf_op | source)
XLA Modules:
  0.0 668.7 jit_solution(2465177281889997205)
XLA Ops:
  10.5 19.2 %collective-permute-done.2.refs_1_ = bf16[448,512]{1,0:T(8,128)(2,1)S(1)} collective-permute-done((bf16[448,512]{1,0:T(8,128)(2,1)}, bf16[448,512]{1,0:T(8,128)(2,1)S(1)}, u32[]{:S(2)}, u32[]{:S(2)}) %collective-permute-start.2) | collective-permute-done | bytes 458784 | tf_op jit(solution)/shard_map/ppermute | solution.py:1409
  39.0 16.6 %collective-permute-done.3.refs_1_ = bf16[2,448,512]{2,1,0:T(8,128)(2,1)S(1)} collective-permute-done((bf16[2,448,512]{2,1,0:T(8,128)(2,1)}, bf16[2,448,512]{2,1,0:T(8,128)(2,1)S(1)}, u32[]{:S(2)}, u32[]{:S(2)}) %collective-permute-start.3) | collective-permute-done | bytes 917536 | tf_op jit(solution)/shard_map/ppermute | solution.py:1409
  69.6 25.3 %collective-permute-done.9.refs_1_ = bf16[576,512]{1,0:T(8,128)(2,1)S(1)} collective-permute-done((bf16[576,512]{1,0:T(8,128)(2,1)}, bf16[576,512]{1,0:T(8,128)(2,1)S(1)}, u32[]{:S(2)}, u32[]{:S(2)}) %collective-permute-start.9) | collective-permute-done | bytes 589856 | tf_op jit(solution)/shard_map/ppermute | solution.py:1409
  110.3 15.6 %collective-permute-done.10.refs_1_ = bf16[2,576,512]{2,1,0:T(8,128)(2,1)S(1)} collective-permute-done((bf16[2,576,512]{2,1,0:T(8,128)(2,1)}, bf16[2,576,512]{2,1,0:T(8,128)(2,1)S(1)}, u32[]{:S(2)}, u32[]{:S(2)}) %collective-permute-start.10) | collective-permute-done | bytes 1179680 | tf_op jit(solution)/shard_map/ppermute | solution.py:1409
  137.6 19.0 %project_qkv.1 = (bf16[1280,1536]{1,0:T(8,128)(2,1)}, bf16[1280,1024]{1,0:T(8,128)(2,1)}, bf16[1280,512]{1,0:T(8,128)(2,1)}, bf16[1280,512]{1,0:T(8,128)(2,1)}, ...) custom-call(s32[4]{0:T(128)} %pad_add_fusion.1.place_ref, bf16[640,1536]{1,0:T(8,128)(2,1)} %refs_0_.11, ...), custom_call_target="tpu_custom_call" | custom-call | bytes 59400 | tf_op jit(solution)/shard_map/project_qkv/pallas_call | solution.py:52
  165.0 17.3 %attend.2 = (bf16[640,1024]{1,0:T(8,128)(2,1)}, f32[640,128]{1,0:T(8,128)}) custom-call(s32[4]{0:T(128)} %pad_add_fusion.1.place_ref, bf16[1280,1024]{1,0:T(8,128)(2,1)} %get-tuple-element.108.refs_0_, bf16[1280,512]{1,0:T(8,128)(2,1)} %get-tuple-element.109.refs_3_.refs_1_, bf16[1280,512]{1,0:T(8,128)(2,1)} %get-tuple-element.110.refs_2_, ...), custom_call_target="tpu_custom_call" | custom-call | bytes 56100 | tf_op jit(solution)/shard_map/attend/pallas_call | solution.py:52
  182.6 7.6 %collective-permute-done.11.refs_1_ = bf16[576,512]{1,0:T(8,128)(2,1)S(1)} collective-permute-done((bf16[576,512]{1,0:T(8,128)(2,1)}, bf16[576,512]{1,0:T(8,128)(2,1)S(1)}, u32[]{:S(2)}, u32[]{:S(2)}) %collective-permute-start.11) | collective-permute-done | bytes 589856 | tf_op jit(solution)/shard_map/ppermute | solution.py:1409
  201.6 17.4 %attend.3 = (bf16[640,1024]{1,0:T(8,128)(2,1)}, f32[640,128]{1,0:T(8,128)}) custom-call(s32[4]{0:T(128)} %pad_add_fusion.1.place_ref, bf16[1280,1024]{1,0:T(8,128)(2,1)} %get-tuple-element.108.refs_0_, bf16[1280,512]{1,0:T(8,128)(2,1)} %get-tuple-element.109.refs_3_.refs_1_, bf16[1280,512]{1,0:T(8,128)(2,1)} %get-tuple-element.110.refs_2_, ...), custom_call_target="tpu_custom_call" | custom-call | bytes 56100 | tf_op jit(solution)/shard_map/attend/pallas_call | solution.py:52
  220.1 11.0 %middle.1 = (f32[640,1536]{1,0:T(8,128)}, bf16[640,1536]{1,0:T(8,128)(2,1)}) custom-call(s32[4]{0:T(128)} %pad_add_fusion.1.place_ref, bf16[640,1536]{1,0:T(8,128)(2,1)} %refs_0_.11, bf16[640,1024]{1,0:T(8,128)(2,1)} %get-tuple-element.112.refs_1_.refs_0_, bf16[640,1024]{1,0:T(8,128)(2,1)} %copy-done.11, ...), custom_call_target="tpu_custom_call" | custom-call | bytes 36300 | tf_op jit(solution)/shard_map/middle/pallas_call | solution.py:52
  238.4 5.2 collective-permute-done.20.refs_10_.refs_3_
  246.0 40.0 %ffn_forward.1 = (bf16[640,1536]{1,0:T(8,128)(2,1)}, bf16[640,1536]{1,0:T(8,128)(2,1)}, f32[640,1536]{1,0:T(8,128)}, f32[640,1536]{1,0:T(8,128)}, bf16[1280,1024...) custom-call(s32[4]{0:T(128)} %pad_add_fusion.1.place_ref, ...), custom_call_target="tpu_custom_call" | custom-call | bytes 118800 | tf_op jit(solution)/shard_map/ffn_forward/pallas_call | solution.py:52
  295.7 22.3 %ffn_backward.1 = (bf16[2,4,288,512]{3,2,1,0:T(8,128)(2,1)}, bf16[2,4,288,512]{3,2,1,0:T(8,128)(2,1)}, bf16[4,288,512]{2,1,0:T(8,128)(2,1)}, bf16[4,288,512]{2,1,0:T(8,128)(2,1)}, bf16[4,2,288,512]{3,2,1,0:T(8,128)(2,1)}) custom-call(s32[4]{0:T(128)} %pad_add_fusion.1.place_ref, bf16[640,1536]{1,0:T(8,128)(2,1)} %get-tuple-element.115.refs_2_.refs_0_, ...), custom_call_target="tpu_custom_call" | custom-call | bytes 72600 | tf_op jit(solution)/shard_map/ffn_backward/pallas_call | solution.py:52
  323.5 55.8 %ffn.1 = (bf16[640,1536]{1,0:T(8,128)(2,1)}, bf16[640,1536]{1,0:T(8,128)(2,1)}, f32[640,1536]{1,0:T(8,128)}, f32[640,1536]{1,0:T(8,128)}, bf16[2,4,288,512]{3,2,...) custom-call(s32[4]{0:T(128)} %pad_add_fusion.1.place_ref, ...), custom_call_target="tpu_custom_call" | custom-call | bytes 198000 | tf_op jit(solution)/shard_map/ffn/pallas_call | solution.py:52
  383.7 16.8 %middle_back.1 = (f32[640,1536]{1,0:T(8,128)}, bf16[640,768]{1,0:T(8,128)(2,1)}, bf16[640,768]{1,0:T(8,128)(2,1)}, bf16[640,1024]{1,0:T(8,128)(2,1)}, bf16[640,1024]{1,0:T(8,128)(2,1)}, /*index=5*/f32[8,1536]{1,0:T(8,128)}) custom-call(s32[4]{0:T(128)} %pad_add_fusion.1.place_ref, f32[640,1536]{1,0:T(8,128)} %get-tuple-element.114.refs_0_, ...), custom_call_target="tpu_custom_call" | custom-call | bytes 49500 | tf_op jit(solution)/shard_map/middle_back/pallas_call | solution.py:52
  400.7 21.1 %attend_back.2 = (bf16[640,1024]{1,0:T(8,128)(2,1)}, bf16[640,512]{1,0:T(8,128)(2,1)}, bf16[640,512]{1,0:T(8,128)(2,1)}) custom-call(s32[4]{0:T(128)} %pad_add_fusion.1.place_ref, bf16[1280,1024]{1,0:T(8,128)(2,1)} %get-tuple-element.108.refs_0_, bf16[1280,512]{1,0:T(8,128)(2,1)} %get-tuple-element.109.refs_3_.refs_1_, ...), custom_call_target="tpu_custom_call" | custom-call | bytes 69300 | tf_op jit(solution)/shard_map/attend_back/pallas_call | solution.py:52
  421.8 5.4 merge.4
  430.9 21.1 %attend_back.3 = (bf16[640,1024]{1,0:T(8,128)(2,1)}, bf16[640,512]{1,0:T(8,128)(2,1)}, bf16[640,512]{1,0:T(8,128)(2,1)}) custom-call(s32[4]{0:T(128)} %pad_add_fusion.1.place_ref, bf16[1280,1024]{1,0:T(8,128)(2,1)} %get-tuple-element.108.refs_0_, bf16[1280,512]{1,0:T(8,128)(2,1)} %get-tuple-element.109.refs_3_.refs_1_, ...), custom_call_target="tpu_custom_call" | custom-call | bytes 69300 | tf_op jit(solution)/shard_map/attend_back/pallas_call | solution.py:52
  452.0 5.5 merge.5
  458.5 10.3 %out_grad.1 = (bf16[2,4,80,512]{3,2,1,0:T(8,128)(2,1)}, bf16[2,4,80,512]{3,2,1,0:T(8,128)(2,1)}, bf16[4,80,512]{2,1,0:T(8,128)(2,1)}, bf16[4,80,512]{2,1,0:T(8,128)(2,1)}, bf16[4,2,80,512]{3,2,1,0:T(8,128)(2,1)}) custom-call(s32[4]{0:T(128)} %pad_add_fusion.1.place_ref, bf16[640,1024]{1,0:T(8,128)(2,1)} %get-tuple-element.112.refs_1_.refs_0_, ...), custom_call_target="tpu_custom_call" | custom-call | bytes 33000 | tf_op jit(solution)/shard_map/out_grad/pallas_call | solution.py:52
  471.8 6.4 sum_plane.3
  481.6 14.5 %input_back.1 = (bf16[1280,1536]{1,0:T(8,128)(2,1)}, f32[640,1536]{1,0:T(8,128)}, bf16[640,1536]{1,0:T(8,128)(2,1)}, f32[8,1536]{1,0:T(8,128)}) custom-call(s32[4]{0:T(128)} %pad_add_fusion.1.place_ref, bf16[640,1024]{1,0:T(8,128)(2,1)} %get-tuple-element.136.refs_4_.refs_0_, bf16[640,512]{1,0:T(8,128)(2,1)} %get-tuple-element.137.refs_1_, ...), custom_call_target="tpu_custom_call" | custom-call | bytes 49500 | tf_op jit(solution)/shard_map/input_back/pallas_call | solution.py:52
  496.1 14.8 %qkv_grad.1 = (bf16[2,4,160,512]{3,2,1,0:T(8,128)(2,1)}, bf16[2,4,160,512]{3,2,1,0:T(8,128)(2,1)}, bf16[4,160,512]{2,1,0:T(8,128)(2,1)}, bf16[4,160,512]{2,1,0:T(8,128)(2,1)}, bf16[4,2,160,512]{3,2,1,0:T(8,128)(2,1)}) custom-call(s32[4]{0:T(128)} %pad_add_fusion.1.place_ref, bf16[1280,1536]{1,0:T(8,128)(2,1)} %get-tuple-element.124.refs_0_, ...), custom_call_target="tpu_custom_call" | custom-call | bytes 49500 | tf_op jit(solution)/shard_map/qkv_grad/pallas_call | solution.py:52
  522.3 6.5 sum_plane.4
  534.5 14.0 %collective-permute-done.47.refs_9_ = bf16[4,80,512]{2,1,0:T(8,128)(2,1)S(1)} collective-permute-done((bf16[4,80,512]{2,1,0:T(8,128)(2,1)S(1)}, bf16[4,80,512]{2,1,0:T(8,128)(2,1)S(1)}, u32[]{:S(2)}, u32[]{:S(2)}) %collective-permute-start.47) | collective-permute-done | bytes 327712 | tf_op jit(solution)/shard_map/ppermute | solution.py:1409
  553.4 5.3 collective-permute-done.46.refs_8_
  559.1 7.3 %collective-permute-done.49.refs_2_ = bf16[2,288,512]{2,1,0:T(8,128)(2,1)S(1)} collective-permute-done((bf16[2,288,512]{2,1,0:T(8,128)(2,1)S(1)}, bf16[2,288,512]{2,1,0:T(8,128)(2,1)S(1)}, u32[]{:S(2)}, u32[]{:S(2)}) %collective-permute-start.49) | collective-permute-done | bytes 589856 | tf_op jit(solution)/shard_map/ppermute | solution.py:1409
  581.2 5.2 sum_plane.5
  590.8 8.3 %output.1.refs_3_ = bf16[640,1536]{1,0:T(8,128)(2,1)} custom-call(s32[4]{0:T(128)} %pad_add_fusion.1.place_ref, f32[640,1536]{1,0:T(8,128)} %get-tuple-element.114.refs_0_, f32[640,1536]{1,0:T(8,128)} %get-tuple-element.118.refs_1_, f32[640,1536]{1,0:T(8,128)} %get-tuple-element.122.refs_2_, bf16[640,1536]{1,0:T(8,128)(2,1)} %collective-permute-done.25.refs_3_, ...), custom_call_target="tpu_custom_call" | custom-call | bytes 13200 | tf_op jit(solution)/shard_map/output/pallas_call | solution.py:52
  599.2 21.8 %collective-permute-done.52.refs_2_ = bf16[2,288,512]{2,1,0:T(8,128)(2,1)S(1)} collective-permute-done((bf16[2,288,512]{2,1,0:T(8,128)(2,1)S(1)}, bf16[2,288,512]{2,1,0:T(8,128)(2,1)S(1)}, u32[]{:S(2)}, u32[]{:S(2)}) %collective-permute-start.52) | collective-permute-done | bytes 589856 | tf_op jit(solution)/shard_map/ppermute | solution.py:1409
  635.4 8.9 %tokens_grad.1.refs_4_ = f32[640,1536]{1,0:T(8,128)} custom-call(s32[4]{0:T(128)} %pad_add_fusion.1.place_ref, bf16[640,1536]{1,0:T(8,128)(2,1)} %refs_0_.11, f32[640,1536]{1,0:T(8,128)} %get-tuple-element.184.refs_1_, f32[640,1536]{1,0:T(8,128)} %get-tuple-element.185.refs_2_, bf16[640,1536]{1,0:T(8,128)(2,1)} %copy-done.23, ...), custom_call_target="tpu_custom_call" | custom-call | bytes 13200 | tf_op jit(solution)/shard_map/tokens_grad/pallas_call | solution.py:52
  646.0 5.4 unpack_ffn.1
  651.4 5.4 collective-permute-done.53.refs_2_
  (250 shorter events, 190.6 us)
Async XLA Ops:
  0.6 55.0 %collective-permute-start = (bf16[640,1536]{1,0:T(8,128)(2,1)}, bf16[640,1536]{1,0:T(8,128)(2,1)}, u32[]{:S(2)}, u32[]{:S(2)}) collective-permute-start(bf16[640,1536]{1,0:T(8,128)(2,1)} %refs_0_.11), channel_id=1, source_target_pairs={{0,16},{16,0},{1,17},{17,1},{2,18},{18,2},{3,19},{19,3},{4,20},{20... | collective-permute-start | bytes 5898248 | tf_op jit(solution)/shard_map/ppermute | solution.py:1404
  1.2 54.5 %collective-permute-start.4 = (bf16[640,1536]{1,0:T(8,128)(2,1)}, bf16[640,1536]{1,0:T(8,128)(2,1)S(1)}, u32[]{:S(2)}, u32[]{:S(2)}) collective-permute-start(bf16[640,1536]{1,0:T(8,128)(2,1)} %refs_5_.1), channel_id=1, source_target_pairs={{0,16},{16,0},{1,17},{17,1},{2,18},{18,2},{3,19},{19,3},{4,20},{20... | collective-permute-start | bytes 5898248 | tf_op jit(solution)/shard_map/ppermute | solution.py:1404
  60.6 41.2 %collective-permute-start.6 = (bf16[4,448,512]{2,1,0:T(8,128)(2,1)}, bf16[4,448,512]{2,1,0:T(8,128)(2,1)S(1)}, u32[]{:S(2)}, u32[]{:S(2)}) collective-permute-start(bf16[4,448,512]{2,1,0:T(8,128)(2,1)} %line.3.refs_3_.refs_0_.refs_4_), channel_id=1, source_target_pairs={{0,2},{1,3},{2,0},{3,1},{4,6},{5,7},{6,4},{7,5},{8,10},{9,11},{10,... | collective-permute-start | bytes 5505032 | tf_op jit(solution)/shard_map/ppermute | solution.py:1409
  62.1 40.6 %collective-permute-start.5 = (bf16[4,448,512]{2,1,0:T(8,128)(2,1)}, bf16[4,448,512]{2,1,0:T(8,128)(2,1)S(1)}, u32[]{:S(2)}, u32[]{:S(2)}) collective-permute-start(bf16[4,448,512]{2,1,0:T(8,128)(2,1)} %line.3.refs_3_.refs_0_.refs_4_), channel_id=1, source_target_pairs={{0,1},{1,0},{2,3},{3,2},{4,5},{5,4},{6,7},{7,6},{8,9},{9,8},{10,11... | collective-permute-start | bytes 5505032 | tf_op jit(solution)/shard_map/ppermute | solution.py:1409
  130.6 64.2 %collective-permute-start.13 = (bf16[4,576,512]{2,1,0:T(8,128)(2,1)}, bf16[4,576,512]{2,1,0:T(8,128)(2,1)}, u32[]{:S(2)}, u32[]{:S(2)}) collective-permute-start(bf16[4,576,512]{2,1,0:T(8,128)(2,1)} %line.4.refs_5_.refs_4_), channel_id=1, source_target_pairs={{0,2},{1,3},{2,0},{3,1},{4,6},{5,7},{6,4},{7,5},{8,10},{9,11},{10,... | collective-permute-start | bytes 7077896 | tf_op jit(solution)/shard_map/ppermute | solution.py:1409
  131.1 63.7 %collective-permute-start.12 = (bf16[4,576,512]{2,1,0:T(8,128)(2,1)}, bf16[4,576,512]{2,1,0:T(8,128)(2,1)}, u32[]{:S(2)}, u32[]{:S(2)}) collective-permute-start(bf16[4,576,512]{2,1,0:T(8,128)(2,1)} %line.4.refs_5_.refs_4_), channel_id=1, source_target_pairs={{0,1},{1,0},{2,3},{3,2},{4,5},{5,4},{6,7},{7,6},{8,9},{9,8},{10,11... | collective-permute-start | bytes 7077896 | tf_op jit(solution)/shard_map/ppermute | solution.py:1409
  137.6 81.4 %collective-permute-start.15 = (bf16[2048,768]{1,0:T(8,128)(2,1)}, bf16[2048,768]{1,0:T(8,128)(2,1)}, u32[]{:S(2)}, u32[]{:S(2)}) collective-permute-start(bf16[2048,768]{1,0:T(8,128)(2,1)} %out_weight.1.refs_9_.refs_3_.refs_7_), channel_id=1, source_target_pairs={{0,16},{16,0},{1,17},{17,1},{2,18},{18,2},{3,19},{19,3},{4,20},{20... | collective-permute-start | bytes 9437192 | tf_op jit(solution)/shard_map/ppermute | solution.py:1404
  182.4 36.6 %collective-permute-start.14 = (bf16[640,1024]{1,0:T(8,128)(2,1)}, bf16[640,1024]{1,0:T(8,128)(2,1)S(1)}, u32[]{:S(2)}, u32[]{:S(2)}) collective-permute-start(bf16[640,1024]{1,0:T(8,128)(2,1)} %get-tuple-element.111.refs_2_), channel_id=1, source_target_pairs={{0,16},{16,0},{1,17},{17,1},{2,18},{18,2},{3,19},{19,3},{4,20},{20... | collective-permute-start | bytes 3932168 | tf_op jit(solution)/shard_map/ppermute | solution.py:1404
  193.9 37.2 %collective-permute-start.19 = (bf16[2,576,512]{2,1,0:T(8,128)(2,1)}, bf16[2,576,512]{2,1,0:T(8,128)(2,1)S(1)}, u32[]{:S(2)}, u32[]{:S(2)}) collective-permute-start(bf16[2,576,512]{2,1,0:T(8,128)(2,1)} %pair.5.refs_5_.refs_0_), channel_id=1, source_target_pairs={{0,4},{1,5},{2,6},{3,7},{4,0},{5,1},{6,2},{7,3},{8,12},{9,13},{10,... | collective-permute-start | bytes 3538952 | tf_op jit(solution)/shard_map/ppermute | solution.py:1409
  236.7 52.7 %collective-permute-start.22 = (bf16[4,576,512]{2,1,0:T(8,128)(2,1)}, bf16[4,576,512]{2,1,0:T(8,128)(2,1)S(1)}, u32[]{:S(2)}, u32[]{:S(2)}) collective-permute-start(bf16[4,576,512]{2,1,0:T(8,128)(2,1)} %line.5.refs_9_.refs_4_.refs_7_), channel_id=1, source_target_pairs={{0,2},{1,3},{2,0},{3,1},{4,6},{5,7},{6,4},{7,5},{8,10},{9,11},{10,... | collective-permute-start | bytes 7077896 | tf_op jit(solution)/shard_map/ppermute | solution.py:1409
  237.3 52.4 %collective-permute-start.21 = (bf16[4,576,512]{2,1,0:T(8,128)(2,1)}, bf16[4,576,512]{2,1,0:T(8,128)(2,1)}, u32[]{:S(2)}, u32[]{:S(2)}) collective-permute-start(bf16[4,576,512]{2,1,0:T(8,128)(2,1)} %line.5.refs_9_.refs_4_.refs_7_), channel_id=1, source_target_pairs={{0,1},{1,0},{2,3},{3,2},{4,5},{5,4},{6,7},{7,6},{8,9},{9,8},{10,11... | collective-permute-start | bytes 7077896 | tf_op jit(solution)/shard_map/ppermute | solution.py:1409
  318.0 63.5 %collective-permute-start.29 = (bf16[2,4,288,512]{3,2,1,0:T(8,128)(2,1)}, bf16[2,4,288,512]{3,2,1,0:T(8,128)(2,1)S(1)}, u32[]{:S(2)}, u32[]{:S(2)}) collective-permute-start(bf16[2,4,288,512]{3,2,1,0:T(8,128)(2,1)} %get-tuple-element.132), channel_id=1, source_target_pairs={{0,1},{1,0},{2,3},{3,2},{4,5},{5,4},{6,7},{7,6},{8,9},{9,8},{10,11... | collective-permute-start | bytes 7077896 | tf_op jit(solution)/shard_map/ppermute | solution.py:1409
  319.6 61.9 %collective-permute-start.30 = (bf16[2,4,288,512]{3,2,1,0:T(8,128)(2,1)}, bf16[2,4,288,512]{3,2,1,0:T(8,128)(2,1)S(1)}, u32[]{:S(2)}, u32[]{:S(2)}) collective-permute-start(bf16[2,4,288,512]{3,2,1,0:T(8,128)(2,1)} %get-tuple-element.133), channel_id=1, source_target_pairs={{0,2},{1,3},{2,0},{3,1},{4,6},{5,7},{6,4},{7,5},{8,10},{9,11},{10,... | collective-permute-start | bytes 7077896 | tf_op jit(solution)/shard_map/ppermute | solution.py:1409
  321.1 59.4 %collective-permute-start.27 = (bf16[640,1536]{1,0:T(8,128)(2,1)}, bf16[640,1536]{1,0:T(8,128)(2,1)S(1)}, u32[]{:S(2)}, u32[]{:S(2)}) collective-permute-start(bf16[640,1536]{1,0:T(8,128)(2,1)} %get-tuple-element.127), channel_id=1, source_target_pairs={{0,16},{16,0},{1,17},{17,1},{2,18},{18,2},{3,19},{19,3},{4,20},{20... | collective-permute-start | bytes 5898248 | tf_op jit(solution)/shard_map/ppermute | solution.py:1404
  379.3 72.7 %collective-permute-start.35 = (bf16[2,4,288,512]{3,2,1,0:T(8,128)(2,1)}, bf16[2,4,288,512]{3,2,1,0:T(8,128)(2,1)}, u32[]{:S(2)}, u32[]{:S(2)}) collective-permute-start(bf16[2,4,288,512]{3,2,1,0:T(8,128)(2,1)} %get-tuple-element.154), channel_id=1, source_target_pairs={{0,1},{1,0},{2,3},{3,2},{4,5},{5,4},{6,7},{7,6},{8,9},{9,8},{10,11... | collective-permute-start | bytes 7077896 | tf_op jit(solution)/shard_map/ppermute | solution.py:1409
  380.5 71.5 %collective-permute-start.36 = (bf16[2,4,288,512]{3,2,1,0:T(8,128)(2,1)}, bf16[2,4,288,512]{3,2,1,0:T(8,128)(2,1)}, u32[]{:S(2)}, u32[]{:S(2)}) collective-permute-start(bf16[2,4,288,512]{3,2,1,0:T(8,128)(2,1)} %get-tuple-element.155), channel_id=1, source_target_pairs={{0,2},{1,3},{2,0},{3,1},{4,6},{5,7},{6,4},{7,5},{8,10},{9,11},{10,... | collective-permute-start | bytes 7077896 | tf_op jit(solution)/shard_map/ppermute | solution.py:1409
  427.2 43.2 %collective-permute-start.33 = (bf16[4,288,512]{2,1,0:T(8,128)(2,1)}, bf16[4,288,512]{2,1,0:T(8,128)(2,1)S(1)}, u32[]{:S(2)}, u32[]{:S(2)}) collective-permute-start(bf16[4,288,512]{2,1,0:T(8,128)(2,1)} %get-tuple-element.149), channel_id=1, source_target_pairs={{0,2},{1,3},{2,0},{3,1},{4,6},{5,7},{6,4},{7,5},{8,10},{9,11},{10,... | collective-permute-start | bytes 3538952 | tf_op jit(solution)/shard_map/ppermute | solution.py:1409
  429.2 41.2 %collective-permute-start.32 = (bf16[4,288,512]{2,1,0:T(8,128)(2,1)}, bf16[4,288,512]{2,1,0:T(8,128)(2,1)S(1)}, u32[]{:S(2)}, u32[]{:S(2)}) collective-permute-start(bf16[4,288,512]{2,1,0:T(8,128)(2,1)} %get-tuple-element.143.refs_9_), channel_id=1, source_target_pairs={{0,1},{1,0},{2,3},{3,2},{4,5},{5,4},{6,7},{7,6},{8,9},{9,8},{10,11... | collective-permute-start | bytes 3538952 | tf_op jit(solution)/shard_map/ppermute | solution.py:1409
  468.8 42.1 %collective-permute-start.42 = (bf16[2,4,80,512]{3,2,1,0:T(8,128)(2,1)}, bf16[2,4,80,512]{3,2,1,0:T(8,128)(2,1)S(1)}, u32[]{:S(2)}, u32[]{:S(2)}) collective-permute-start(bf16[2,4,80,512]{3,2,1,0:T(8,128)(2,1)} %get-tuple-element.173), channel_id=1, source_target_pairs={{0,1},{1,0},{2,3},{3,2},{4,5},{5,4},{6,7},{7,6},{8,9},{9,8},{10,11... | collective-permute-start | bytes 1966088 | tf_op jit(solution)/shard_map/ppermute | solution.py:1409
  470.3 42.1 %collective-permute-start.43 = (bf16[2,4,80,512]{3,2,1,0:T(8,128)(2,1)}, bf16[2,4,80,512]{3,2,1,0:T(8,128)(2,1)S(1)}, u32[]{:S(2)}, u32[]{:S(2)}) collective-permute-start(bf16[2,4,80,512]{3,2,1,0:T(8,128)(2,1)} %get-tuple-element.174), channel_id=1, source_target_pairs={{0,2},{1,3},{2,0},{3,1},{4,6},{5,7},{6,4},{7,5},{8,10},{9,11},{10,... | collective-permute-start | bytes 1966088 | tf_op jit(solution)/shard_map/ppermute | solution.py:1409
  478.2 37.9 %collective-permute-start.41 = (bf16[2,2,288,512]{3,2,1,0:T(8,128)(2,1)}, bf16[2,2,288,512]{3,2,1,0:T(8,128)(2,1)S(1)}, u32[]{:S(2)}, u32[]{:S(2)}) collective-permute-start(bf16[2,2,288,512]{3,2,1,0:T(8,128)(2,1)} %get-tuple-element.170), channel_id=1, source_target_pairs={{0,4},{1,5},{2,6},{3,7},{4,0},{5,1},{6,2},{7,3},{8,12},{9,13},{10,... | collective-permute-start | bytes 3538952 | tf_op jit(solution)/shard_map/ppermute | solution.py:1409
  479.1 41.8 %collective-permute-start.40 = (bf16[4,288,512]{2,1,0:T(8,128)(2,1)}, bf16[4,288,512]{2,1,0:T(8,128)(2,1)S(1)}, u32[]{:S(2)}, u32[]{:S(2)}) collective-permute-start(bf16[4,288,512]{2,1,0:T(8,128)(2,1)} %get-tuple-element.168), channel_id=1, source_target_pairs={{0,2},{1,3},{2,0},{3,1},{4,6},{5,7},{6,4},{7,5},{8,10},{9,11},{10,... | collective-permute-start | bytes 3538952 | tf_op jit(solution)/shard_map/ppermute | solution.py:1409
  481.0 39.9 %collective-permute-start.39 = (bf16[4,288,512]{2,1,0:T(8,128)(2,1)}, bf16[4,288,512]{2,1,0:T(8,128)(2,1)S(1)}, u32[]{:S(2)}, u32[]{:S(2)}) collective-permute-start(bf16[4,288,512]{2,1,0:T(8,128)(2,1)} %get-tuple-element.156.refs_6_), channel_id=1, source_target_pairs={{0,1},{1,0},{2,3},{3,2},{4,5},{5,4},{6,7},{7,6},{8,9},{9,8},{10,11... | collective-permute-start | bytes 3538952 | tf_op jit(solution)/shard_map/ppermute | solution.py:1409
  510.9 37.6 %collective-permute-start.37 = (bf16[2,4,160,512]{3,2,1,0:T(8,128)(2,1)}, bf16[2,4,160,512]{3,2,1,0:T(8,128)(2,1)S(1)}, u32[]{:S(2)}, u32[]{:S(2)}) collective-permute-start(bf16[2,4,160,512]{3,2,1,0:T(8,128)(2,1)} %get-tuple-element.163), channel_id=1, source_target_pairs={{0,1},{1,0},{2,3},{3,2},{4,5},{5,4},{6,7},{7,6},{8,9},{9,8},{10,11... | collective-permute-start | bytes 3932168 | tf_op jit(solution)/shard_map/ppermute | solution.py:1409
  512.4 36.6 %collective-permute-start.38 = (bf16[2,4,160,512]{3,2,1,0:T(8,128)(2,1)}, bf16[2,4,160,512]{3,2,1,0:T(8,128)(2,1)S(1)}, u32[]{:S(2)}, u32[]{:S(2)}) collective-permute-start(bf16[2,4,160,512]{3,2,1,0:T(8,128)(2,1)} %get-tuple-element.164), channel_id=1, source_target_pairs={{0,2},{1,3},{2,0},{3,1},{4,6},{5,7},{6,4},{7,5},{8,10},{9,11},{10,... | collective-permute-start | bytes 3932168 | tf_op jit(solution)/shard_map/ppermute | solution.py:1409
  528.8 38.8 %collective-permute-start.48 = (bf16[2,2,288,512]{3,2,1,0:T(8,128)(2,1)}, bf16[2,2,288,512]{3,2,1,0:T(8,128)(2,1)S(1)}, u32[]{:S(2)}, u32[]{:S(2)}) collective-permute-start(bf16[2,2,288,512]{3,2,1,0:T(8,128)(2,1)} %get-tuple-element.181), channel_id=1, source_target_pairs={{0,4},{1,5},{2,6},{3,7},{4,0},{5,1},{6,2},{7,3},{8,12},{9,13},{10,... | collective-permute-start | bytes 3538952 | tf_op jit(solution)/shard_map/ppermute | solution.py:1409
  531.2 35.2 %collective-permute-start.49 = (bf16[2,288,512]{2,1,0:T(8,128)(2,1)S(1)}, bf16[2,288,512]{2,1,0:T(8,128)(2,1)S(1)}, u32[]{:S(2)}, u32[]{:S(2)}) collective-permute-start(bf16[2,288,512]{2,1,0:T(8,128)(2,1)S(1)} %copy-done.22), channel_id=1, source_target_pairs={{0,8},{1,9},{2,10},{3,11},{4,12},{5,13},{6,14},{7,15},{8,0},{9,1},... | collective-permute-start | bytes 1769480 | tf_op jit(solution)/shard_map/ppermute | solution.py:1409
  548.5 42.3 %collective-permute-start.25 = (bf16[640,1536]{1,0:T(8,128)(2,1)}, bf16[640,1536]{1,0:T(8,128)(2,1)}, u32[]{:S(2)}, u32[]{:S(2)}) collective-permute-start(bf16[640,1536]{1,0:T(8,128)(2,1)} %get-tuple-element.119.refs_2_), channel_id=1, source_target_pairs={{0,16},{16,0},{1,17},{17,1},{2,18},{18,2},{3,19},{19,3},{4,20},{20... | collective-permute-start | bytes 5898248 | tf_op jit(solution)/shard_map/ppermute | solution.py:1404
  548.5 42.3 %collective-permute-start.26 = (bf16[640,1536]{1,0:T(8,128)(2,1)}, bf16[640,1536]{1,0:T(8,128)(2,1)}, u32[]{:S(2)}, u32[]{:S(2)}) collective-permute-start(bf16[640,1536]{1,0:T(8,128)(2,1)} %get-tuple-element.123), channel_id=1, source_target_pairs={{0,16},{16,0},{1,17},{17,1},{2,18},{18,2},{3,19},{19,3},{4,20},{20... | collective-permute-start | bytes 5898248 | tf_op jit(solution)/shard_map/ppermute | solution.py:1404
  567.7 66.5 %collective-permute-start.50 = (bf16[640,1536]{1,0:T(8,128)(2,1)}, bf16[640,1536]{1,0:T(8,128)(2,1)S(1)}, u32[]{:S(2)}, u32[]{:S(2)}) collective-permute-start(bf16[640,1536]{1,0:T(8,128)(2,1)} %get-tuple-element.186), channel_id=1, source_target_pairs={{0,16},{16,0},{1,17},{17,1},{2,18},{18,2},{3,19},{19,3},{4,20},{20... | collective-permute-start | bytes 5898248 | tf_op jit(solution)/shard_map/ppermute | solution.py:1404
  586.4 39.8 %collective-permute-start.51 = (bf16[2,2,240,512]{3,2,1,0:T(8,128)(2,1)}, bf16[2,2,240,512]{3,2,1,0:T(8,128)(2,1)S(1)}, u32[]{:S(2)}, u32[]{:S(2)}) collective-permute-start(bf16[2,2,240,512]{3,2,1,0:T(8,128)(2,1)} %get-tuple-element.188), channel_id=1, source_target_pairs={{0,4},{1,5},{2,6},{3,7},{4,0},{5,1},{6,2},{7,3},{8,12},{9,13},{10,... | collective-permute-start | bytes 2949128 | tf_op jit(solution)/shard_map/ppermute | solution.py:1409
  590.7 53.6 %collective-permute-start.54 = (bf16[576,512]{1,0:T(8,128)(2,1)S(1)}, bf16[576,512]{1,0:T(8,128)(2,1)S(1)}, u32[]{:S(2)}, u32[]{:S(2)}) collective-permute-start(bf16[576,512]{1,0:T(8,128)(2,1)S(1)} %bitcast.46), channel_id=1, source_target_pairs={{0,16},{16,0},{1,17},{17,1},{2,18},{18,2},{3,19},{19,3},{4,20},{20... | collective-permute-start | bytes 1769480 | tf_op jit(solution)/shard_map/ppermute | solution.py:1404
  (78 other events, 717.0 us)

commit v3 on v2

--- a/solution.py
+++ b/solution.py
@@ -131,6 +131,10 @@
     Slab(2, 448, 64, 64, 0, SLAB),
     Slab(2, 512, 64, 64, 0, 2 * SLAB),
 ]
+UPPER_ROWS = 384
+UPPER_PLAN, LOWER_PLAN = FFN_PLAN[:4], [
+    Slab(2, slab * 64, 64, 64, 0, slab * SLAB) for slab in range(3)
+]
 
 
 def block_index(place_ref, k, dy, dx):
@@ -138,24 +142,36 @@
     return ((z ^ k) * 2 + (y ^ dy)) * 2 + (x ^ dx)
 
 
-def fetch(place_ref, pieces, plan, half, matrices, sems):
+def from_pieces(pieces, half):
+    def source(k, dy, dx, slab):
+        at = pl.ds(slab.row, slab.rows)
+        piece = pieces[dy * 2 + dx]
+        if dy and dx:
+            part = int(slab.row >= half)
+            at = pl.ds(slab.row - part * half, slab.rows)
+            piece = pieces[3 + part]
+        return piece.at[k, at, slab.lanes()]
+
+    return source
+
+
+def from_planes(pair, other):
+    def source(k, dy, dx, slab):
+        planes = other if k % 2 else pair
+        return planes.at[k // 2, dy * 2 + dx, pl.ds(slab.row, slab.rows), slab.lanes()]
+
+    return source
+
+
+def fetch(place_ref, source, plan, matrices, sems):
     for k in range(4):
         for dy in range(2):
             for dx in range(2):
                 block = block_index(place_ref, k, dy, dx)
                 for slab in plan:
-                    at = pl.ds(slab.row, slab.rows)
-                    source = pieces[dy * 2 + dx]
-                    if dy and dx:
-                        part = int(slab.row >= half)
-                        at = pl.ds(slab.row - part * half, slab.rows)
-                        source = pieces[3 + part]
-                    copy = pltpu.make_async_copy(
-                        source.at[k, at, slab.lanes()],
-                        slab.of(matrices, block),
-                        sems.at[slab.matrix],
-                    )
-                    copy.start()
+                    pltpu.make_async_copy(
+                        source(k, dy, dx, slab), slab.of(matrices, block), sems.at[slab.matrix]
+                    ).start()
 
 
 def send_off(place_ref, k, matrices, stride_base, plan, half, outs, sems):
@@ -196,6 +212,27 @@
     return [(shaped(shape, low), anywhere) for shape in shapes]
 
 
+def gate_kernel(place_ref, *refs):
+    pass
+
+
+def gate(place, arrays, after):
+    count, extra = len(arrays), len(after)
+    return pl.pallas_call(
+        gate_kernel,
+        grid_spec=pltpu.PrefetchScalarGridSpec(
+            num_scalar_prefetch=1,
+            grid=(1,),
+            in_specs=[anywhere] * (count + extra),
+            out_specs=[anywhere] * count,
+        ),
+        out_shape=[shaped(array.shape, array.dtype) for array in arrays],
+        input_output_aliases={1 + index: index for index in range(count)},
+        cost_estimate=pl.CostEstimate(flops=0, bytes_accessed=0, transcendentals=0),
+        name="gate",
+    )(place, *arrays, *after)
+
+
 def pair_kernel(place_ref, own, far, out, sems):
     copies = [
         pltpu.make_async_copy(ref, out.at[k], sems.at[k]) for k, ref in enumerate((own, far))
@@ -247,6 +284,41 @@
     )[0]
 
 
+def plane_kernel(place_ref, own, from_x, from_y, upper, lower, out, sems):
+    half = upper.shape[1]
+    parts = [
+        (own, out.at[pl.ds(0, 1)]),
+        (from_x, out.at[pl.ds(1, 1)]),
+        (from_y, out.at[pl.ds(2, 1)]),
+        (upper, out.at[pl.ds(3, 1), pl.ds(0, half)]),
+        (lower, out.at[pl.ds(3, 1), pl.ds(half, half)]),
+    ]
+    copies = [
+        pltpu.make_async_copy(source, target, sems.at[index])
+        for index, (source, target) in enumerate(parts)
+    ]
+    for copy in copies:
+        copy.start()
+    for copy in copies:
+        copy.wait()
+
+
+def plane_up(place, parts, after):
+    _, rows, width = parts[0].shape
+    out = shaped((4, rows, width), low)
+    return run(
+        plane_kernel,
+        "plane",
+        place,
+        (1,),
+        [(part, anywhere) for part in parts],
+        [(out, whole(out))],
+        [pltpu.SemaphoreType.DMA((5,))],
+        after,
+        us=2,
+    )[0]
+
+
 def halves_kernel(place_ref, from_x, from_y, upper, lower, sems):
     half = upper.shape[1]
     copies = (
@@ -276,7 +348,7 @@
 
 
 def step_rows(half):
-    return next(rows for rows in (96, 80, 48) if half % rows == 0)
+    return next(rows for rows in (96, 80, 48, 368) if half % rows == 0)
 
 
 def merge_kernel(place_ref, late_x, late_y, got_x, got_y, out_x, out_y):
@@ -300,53 +372,60 @@
     )
 
 
-def sum_kernel(groups, place_ref, *refs):
-    ins, (kept, kept_far, sent) = refs[: 5 * groups], refs[5 * groups :]
-    row = 0
-    for group in range(groups):
-        own, got_x, got_y, more_x, more_y = ins[5 * group : 5 * group + 5]
-        rows = own.shape[2]
-        at = slice(row, row + rows)
-        for k in range(4):
-            upper = own[k, 0].astype(wide) + got_x[0, k].astype(wide) + more_y[k].astype(wide)
-            lower = own[k, 1].astype(wide) + got_y[0, k].astype(wide) + more_x[k].astype(wide)
-            if k % 2:
-                sent[k // 2, 0, at, :] = upper.astype(low)
-                sent[k // 2, 1, at, :] = lower.astype(low)
-            else:
-                ref = kept_far if k else kept
-                ref[0, at, :], ref[1, at, :] = upper, lower
-        row += rows
-
-
-def sum_plane(place, groups, after):
-    halves = [group[0].shape[2] for group in groups]
-    width = groups[0][0].shape[3]
-    steps = halves[0] // step_rows(halves[0]) if len(groups) == 1 else 1
-    total, rows = sum(halves), sum(halves) // steps
+def sum_kernel(direct, groups, place_ref, *refs):
+    ins, (kept, *outs) = refs[: 5 * groups], refs[5 * groups :]
+    step = pl.program_id(0)
+    for k in range(4):
+
+        @pl.when(step == k)
+        def _():
+            row = 0
+            for group in range(groups):
+                own, got_x, got_y, more_x, more_y = ins[5 * group : 5 * group + 5]
+                at = slice(row, row + own.shape[2])
+                row += own.shape[2]
+                upper = own[0, 0].astype(wide) + got_x[0, 0].astype(wide)
+                upper = upper + more_y[0].astype(wide)
+                lower = own[0, 1].astype(wide) + got_y[0, 0].astype(wide)
+                lower = lower + more_x[0].astype(wide)
+                if k == 0:
+                    ref = kept
+                elif direct:
+                    ref = outs[k - 1]
+                else:
+                    ref = outs[1].at[0] if k % 2 else outs[0]
+                ref[0, at, :], ref[1, at, :] = upper.astype(ref.dtype), lower.astype(ref.dtype)
+
+
+def sum_plane(place, groups, direct, after):
     operands = []
-    for group, half in zip(groups, halves):
-        own, got_x, got_y, more_x, more_y = group
-        part = half // steps
-        got = pl.BlockSpec((1, 4, part, width), lambda i, place: (1, 0, i, 0))
-        more = pl.BlockSpec((4, part, width), lambda i, place: (0, i, 0))
+    for own, got_x, got_y, more_x, more_y in groups:
+        _, _, half, width = own.shape
+        got = pl.BlockSpec((1, 1, half, width), lambda k, place: (1, k, 0, 0))
+        more = pl.BlockSpec((1, half, width), lambda k, place: (k, 0, 0))
         operands += [
-            (own, pl.BlockSpec((4, 2, part, width), lambda i, place: (0, 0, i, 0))),
+            (own, pl.BlockSpec((1, 2, half, width), lambda k, place: (k, 0, 0, 0))),
             (got_x, got),
             (got_y, got),
             (more_x, more),
             (more_y, more),
         ]
-    out = pl.BlockSpec((2, rows, width), lambda i, place: (0, i, 0))
-    both = pl.BlockSpec((2, 2, rows, width), lambda i, place: (0, 0, i, 0))
-    return run(
-        functools.partial(sum_kernel, len(groups)),
+    half = sum(group[0].shape[2] for group in groups)
+    out = pl.BlockSpec((2, half, width), lambda k, place: (0, 0, 0))
+    both = pl.BlockSpec((1, 2, half, width), lambda k, place: (k // 2, 0, 0, 0))
+    outs = [(shaped((2, half, width), wide), out)]
+    if direct:
+        outs += [(shaped((2, half, width), low), out)] * 3
+    else:
+        outs += [(shaped((2, half, width), wide), out)]
+        outs += [(shaped((2, 2, half, width), low), both)]
+    return run(
+        functools.partial(sum_kernel, direct, len(groups)),
         "sum_plane",
         place,
-        (steps,),
+        (4,),
         operands,
-        [(shaped((2, total, width), wide), out)] * 2
-        + [(shaped((2, 2, total, width), low), both)],
+        outs,
         after=after,
         us=5,
     )
@@ -373,13 +452,17 @@
     )[0]
 
 
-def total_kernel(place_ref, kept, near, far, out, out_low):
-    total = kept[...] + near[0].astype(wide) + far[...].astype(wide)
+def total_kernel(place_ref, kept, *refs):
+    *received, out, out_low = refs
+    total = kept[...]
+    for ref in received:
+        part = ref[0] if len(ref.shape) > len(kept.shape) else ref[...]
+        total = total + part.astype(wide)
     out[...] = total
     out_low[...] = total.astype(low)
 
 
-def sum_line(place, kept, near, far, after):
+def sum_line(place, kept, received, after):
     _, half, width = kept.shape
     rows = step_rows(half)
     spec = pl.BlockSpec((2, rows, width), lambda i, place: (0, i, 0))
@@ -389,7 +472,7 @@
         "sum_line",
         place,
         (half // rows,),
-        [(kept, spec), (near, first), (far, spec)],
+        [(kept, spec)] + [(item, first if item.ndim == 4 else spec) for item in received],
         [(shaped(kept.shape, wide), spec), (shaped(kept.shape, low), spec)],
         after=after,
         us=4,
@@ -443,9 +526,15 @@
     return left, right
 
 
-def pack_ffn_kernel(chunk, place_ref, gate, up, down_w, out):
+def pack_ffn_kernel(chunk, place_ref, gate, up, down_w, *outs):
     core = place_ref[3]
     rows = gate.shape[0]
+
+    def put(at, size, column, part):
+        span, width = outs[0].shape[0], part.shape[1]
+        out, at = (outs[0], at) if at < span else (outs[1], at - span)
+        out[at : at + size, column : column + width] = part
+
     for matrix, ref in enumerate((gate, up)):
         for pair in range(8):
             windows = [
@@ -455,24 +544,30 @@
             packed = interleave(windows[0].astype(wide), windows[1].astype(wide))[chunk]
             at = (matrix * 2 + pair // 4) * rows
             column = pair % 4 * LANES
-            out[at : at + rows, column : column + LANES] = packed.astype(low)
+            put(at, rows, column, packed.astype(low))
     units = down_w[pl.ds(pl.multiple_of(core * LANES + chunk * 64, 64), 64), :]
     for slab in range(3):
         at = 4 * rows + slab * 64
-        out[at : at + 64, :] = units[:, slab * SLAB : (slab + 1) * SLAB]
-
-
-def pack_ffn(place, chunk, gate, up, down_w, after):
-    out = shaped((2 * FFN_HALF, SLAB), low)
+        put(at, 64, 0, units[:, slab * SLAB : (slab + 1) * SLAB])
+
+
+def pack_ffn(place, chunk, parts, gate, up, down_w, after):
+    outs = [shaped((rows, SLAB), low) for rows in parts]
     return run(
         functools.partial(pack_ffn_kernel, chunk),
         "pack_ffn",
         place,
         (1,),
         [(item, whole(item)) for item in (gate, up, down_w)],
-        [(out, whole(out))],
+        [(out, whole(out)) for out in outs],
         after=after,
-    )[0]
+    )
+
+
+def rows_in(ref, at, rows):
+    if at >= FFN_HALF:
+        at += ref.shape[0] // 2 - FFN_HALF
+    return ref[at : at + rows, :]
 
 
 def unpack_ffn_kernel(place_ref, mine_0, mine_1, other_0, other_1, gate, up, down_w):
@@ -484,7 +579,7 @@
                 at = (matrix * 2 + pair // 4) * rows
                 column = pair % 4 * LANES
                 parts = [
-                    chunk[at : at + rows, column : column + LANES].astype(wide)
+                    rows_in(chunk, at, rows)[:, column : column + LANES].astype(wide)
                     for chunk in chunks
                 ]
                 for odd, window in enumerate(interleave(*parts)):
@@ -494,9 +589,8 @@
             for slab in range(3):
                 at = 4 * rows + slab * 64
                 place = pl.multiple_of(owner * LANES + index * 64, 64)
-                down_w[pl.ds(place, 64), slab * SLAB : (slab + 1) * SLAB] = chunk[
-                    at : at + 64, :
-                ].astype(wide)
+                part = rows_in(chunk, at, 64).astype(wide)
+                down_w[pl.ds(place, 64), slab * SLAB : (slab + 1) * SLAB] = part
 
 
 def unpack_ffn(place, mine, other, shapes, after):
@@ -512,37 +606,40 @@
     )
 
 
-def unpack_first_kernel(place_ref, mine, other, query, key, value, square):
+def unpack_first_kernel(
+    place_ref, mine, other, joint_mine, joint_other, query, key, value, square
+):
     core = place_ref[3]
     rows = query.shape[0]
-    half = QKV_HALF + OUT_HALF
 
     def put(ref, owner, part):
         columns = ref.shape[1] // 2
         at = pl.ds(pl.multiple_of(owner * columns, LANES), columns)
         ref[:, at] = part.astype(wide)
 
-    for owner, ref in ((core, mine), (1 - core, other)):
-        qkv = jnp.concatenate([ref[:QKV_HALF, :], ref[half : half + QKV_HALF, :]], axis=0)
-        out = jnp.concatenate([ref[QKV_HALF:half, :], ref[half + QKV_HALF :, :]], axis=0)
+    for owner, qkv, joint in ((core, mine, joint_mine), (1 - core, other, joint_other)):
         slabs = [qkv[slab * rows : (slab + 1) * rows, :] for slab in range(3)]
         put(query, owner, jnp.concatenate([slabs[0], slabs[1][:, :256]], axis=1))
         put(key, owner, jnp.concatenate([slabs[1][:, 256:], slabs[2][:, :128]], axis=1))
         put(value, owner, slabs[2][:, 128:])
+        half = FFN_HALF + OUT_HALF
+        out = [joint[part * half + FFN_HALF : (part + 1) * half, :] for part in range(2)]
+        out = jnp.concatenate(out, axis=0)
         rest = out[rows : rows + rows // 2, :]
         rest = jnp.concatenate([rest[:, :256], rest[:, 256:]], axis=0)
         put(square, owner, jnp.concatenate([out[:rows, :], rest], axis=1))
 
 
-def unpack_first(place, mine, other, shapes):
+def unpack_first(place, parts, shapes, after):
     outs = [shaped(shape, wide) for shape in shapes]
     return run(
         unpack_first_kernel,
         "unpack_first",
         place,
         (1,),
-        [(item, whole(item)) for item in (mine, other)],
+        [(item, whole(item)) for item in parts],
         [(out, whole(out)) for out in outs],
+        after=after,
     )
 
 
@@ -572,7 +669,9 @@
 
     @pl.when(pl.program_id(0) == 0)
     def _():
-        fetch(place_ref, pieces, FIRST_QKV_PLAN, FIRST_HALF, (w_ref, gain_rows), sems)
+        fetch(
+            place_ref, from_pieces(pieces, FIRST_HALF), FIRST_QKV_PLAN, (w_ref, gain_rows), sems
+        )
         drain((w_ref, gain_rows), sems)
         for index in range(2):
             parts = [
@@ -661,6 +760,14 @@
         bias_ref[start : start + TILE, :] = jnp.where(allowed, 0.0, masked_score)
 
 
+LOG2_E = 1.4426950408889634
+
+
+def both_heads(ref, start):
+    rows = slice(start, start + TILE)
+    return jnp.concatenate([ref[rows, :LANES], ref[rows, LANES:]], axis=0)
+
+
 def attend_kernel(
     place_ref, q_ref, k_ref, v_ref, column_ref, row_ref, out_ref, total_ref, bias_ref
 ):
@@ -675,19 +782,21 @@
     lane = lax.broadcasted_iota(jnp.int32, (TILE, LANES), 1)
     for start in range(0, size, TILE):
         stop = start + TILE
+        raw = across(both_heads(q_ref, start), k_ref[:stop, :])
+        bias = bias_ref[start:stop, :stop]
+        scores = raw * (HD ** (-0.5) * LOG2_E) + jnp.concatenate([bias, bias], axis=0)
+        top = jnp.max(scores, axis=-1, keepdims=True)
+        powers = jnp.exp2(scores - top)
+        amount = jnp.sum(powers, axis=-1, keepdims=True)
+        probs = (powers * (1.0 / amount)).astype(low)
+        mixed = project(probs, v_ref[:stop, :]).astype(low)
+        total = top + jnp.log2(amount)
+        kept = total_ref[start:stop, :]
         for head in range(2):
-            columns = slice(head * LANES, (head + 1) * LANES)
-            raw = across(q_ref[start:stop, columns], k_ref[:stop, :])
-            scores = raw * HD ** (-0.5) + bias_ref[start:stop, :stop]
-            top = jnp.max(scores, axis=-1, keepdims=True)
-            powers = jnp.exp(scores - top)
-            amount = jnp.sum(powers, axis=-1, keepdims=True)
-            probs = (powers * (1.0 / amount)).astype(low)
-            out_ref[start:stop, columns] = project(probs, v_ref[:stop, :]).astype(low)
-            total = top + jnp.log(amount)
-            total_ref[start:stop, :] = jnp.where(
-                lane == 2 * group + head, total, total_ref[start:stop, :]
-            )
+            rows = slice(head * TILE, (head + 1) * TILE)
+            out_ref[start:stop, head * LANES : (head + 1) * LANES] = mixed[rows]
+            kept = jnp.where(lane == 2 * group + head, total[rows], kept)
+        total_ref[start:stop, :] = kept
 
 
 def attention_specs(size, block):
@@ -734,6 +843,7 @@
     k_ref,
     v_ref,
     grad_ref,
+    out_ref,
     total_ref,
     column_ref,
     row_ref,
@@ -760,32 +870,37 @@
     dk_sum[...] = jnp.zeros_like(dk_sum)
     dv_sum[...] = jnp.zeros_like(dv_sum)
     lane = lax.broadcasted_iota(jnp.int32, (TILE, LANES), 1)
+    scale = HD ** (-0.5)
     for start in range(0, size, TILE):
         stop = start + TILE
-        for head in range(2):
-            columns = slice(head * LANES, (head + 1) * LANES)
-            queries = q_ref[start:stop, columns]
-            grads = grad_ref[start:stop, columns]
-            total = jnp.sum(
+        queries, grads = both_heads(q_ref, start), both_heads(grad_ref, start)
+        mixed = both_heads(out_ref, start)
+        delta = jnp.sum(grads.astype(wide) * mixed.astype(wide), axis=-1, keepdims=True)
+        totals = [
+            jnp.sum(
                 jnp.where(lane == 2 * group + head, total_ref[start:stop, :], 0.0),
                 axis=-1,
                 keepdims=True,
             )
-            raw = across(queries, k_ref[:stop, :])
-            probs = jnp.exp(raw * HD ** (-0.5) + bias_ref[start:stop, :stop] - total)
-            dv_sum[:stop, :] += down(probs.astype(low), grads)
-            grad_probs = across(grads, v_ref[:stop, :])
-            weighted = probs * grad_probs
-            delta = jnp.sum(weighted, axis=-1, keepdims=True)
-            grad_raw = ((weighted - probs * delta) * HD ** (-0.5)).astype(low)
-            dq = project(grad_raw, k_ref[:stop, :])
-            dq_ref[start:stop, columns] = turned_back(dq, slice(start, stop))
-            dk_sum[:stop, :] += down(grad_raw, queries)
+            for head in range(2)
+        ]
+        bias = bias_ref[start:stop, :stop]
+        raw = across(queries, k_ref[:stop, :])
+        scores = raw * (scale * LOG2_E) + jnp.concatenate([bias, bias], axis=0)
+        probs = jnp.exp2(scores - jnp.concatenate(totals, axis=0))
+        dv_sum[:stop, :] += down(probs.astype(low), grads)
+        grad_probs = across(grads, v_ref[:stop, :])
+        grad_raw = (probs * (grad_probs - delta)).astype(low)
+        dq = project(grad_raw, k_ref[:stop, :]) * scale
+        for head in range(2):
+            part = turned_back(dq[head * TILE : (head + 1) * TILE], slice(start, stop))
+            dq_ref[start:stop, head * LANES : (head + 1) * LANES] = part
+        dk_sum[:stop, :] += down(grad_raw, queries)
     dv_ref[...] = dv_sum[...].astype(low)
-    dk_ref[...] = turned_back(dk_sum[...], slice(None))
-
-
-def attend_back(place, q, k, v, grad, total, segment, cosine, sine, block, after=()):
+    dk_ref[...] = turned_back(dk_sum[...] * scale, slice(None))
+
+
+def attend_back(place, q, k, v, grad, out, total, segment, cosine, sine, block, after=()):
     blocks, size = segment.shape
     spec = attention_specs(size, block)
     return run(
@@ -798,6 +913,7 @@
             (k, spec["one"]),
             (v, spec["one"]),
             (grad, spec["pair_alone"]),
+            (out, spec["pair_alone"]),
             (total, spec["alone"]),
             (segment.reshape(blocks * size, 1), spec["column"]),
             (segment.reshape(blocks, 1, size), spec["row"]),
@@ -820,39 +936,45 @@
 
 
 def out_weight_kernel(place_ref, *refs):
-    pieces, weight, sems = refs[:5], refs[5], refs[6]
-    fetch(place_ref, pieces, FIRST_OUT_PLAN, FIRST_HALF, (weight,), sems)
-    zeros = jnp.zeros((LANES - HD, weight.shape[1]), low)
+    pieces, weights, whole_weight, sems = refs[:5], refs[5:7], refs[7], refs[8]
+    fetch(place_ref, from_pieces(pieces, FIRST_HALF), FIRST_OUT_PLAN, (whole_weight,), sems)
+    zeros = jnp.zeros((LANES - HD, whole_weight.shape[1]), low)
     for block in range(BLOCKS):
-        weight[pl.ds(block * LANES + HD, LANES - HD), :] = zeros
-    drain((weight.at[pl.ds(0, BLOCKS * HD)],), sems)
+        whole_weight[pl.ds(block * LANES + HD, LANES - HD), :] = zeros
+    drain((whole_weight.at[pl.ds(0, BLOCKS * HD)],), sems)
+    rows = weights[0].shape[0]
+    for part in range(2):
+        weights[part][...] = whole_weight[part * rows : (part + 1) * rows, :]
 
 
 def out_weight(place, pieces, width, after):
-    out = shaped((H * LANES, width // 2), low)
+    out = shaped((H // 2 * LANES, width // 2), low)
     return run(
         out_weight_kernel,
         "out_weight",
         place,
         (1,),
         [(piece, anywhere) for piece in pieces],
-        [(out, whole(out))],
-        [pltpu.SemaphoreType.DMA((1,))],
+        [(out, whole(out))] * 2,
+        [pltpu.VMEM((H * LANES, width // 2), low), pltpu.SemaphoreType.DMA((1,))],
         after,
-    )[0]
+    )
 
 
 def middle_kernel(
-    place_ref, x_ref, mine_ref, other_ref, w_mine, w_other, gain_ref, middle_ref, out_ref, heads
+    place_ref, x_ref, mine_ref, other_ref, *refs
 ):
+    w_mine, w_other, (gain_ref, middle_ref, out_ref, heads) = refs[:2], refs[2:4], refs[4:]
     core = place_ref[3]
     span = mine_ref.shape[1]
     heads[:, pl.ds(pl.multiple_of(core * span, LANES), span)] = mine_ref[...]
     heads[:, pl.ds(pl.multiple_of((1 - core) * span, LANES), span)] = other_ref[...]
-    columns = w_mine.shape[1]
+    columns = w_mine[0].shape[1]
     for owner, weight in ((core, w_mine), (1 - core, w_other)):
         at = pl.ds(pl.multiple_of(owner * columns, LANES), columns)
-        middle_ref[:, at] = x_ref[:, at].astype(wide) + project(heads[...], weight[...])
+        branch = project(heads[:, :span], weight[0][...])
+        branch = branch + project(heads[:, span:], weight[1][...])
+        middle_ref[:, at] = x_ref[:, at].astype(wide) + branch
     hidden = middle_ref[...]
     scale = lax.rsqrt(jnp.mean(hidden * hidden, axis=-1, keepdims=True) + epsilon)
     out_ref[...] = (hidden * scale * gain_ref[8:9, :]).astype(low)
@@ -870,9 +992,7 @@
             (x, rows_of(tile, width)),
             (mine, rows_of(tile, span)),
             (other, rows_of(tile, span)),
-            (w_mine, whole(w_mine)),
-            (w_other, whole(w_other)),
-            (gains, whole(gains)),
+            *[(item, whole(item)) for item in (*w_mine, *w_other, gains)],
         ],
         [
             (shaped((count, width), wide), rows_of(tile, width)),
@@ -893,17 +1013,10 @@
     other_1,
     cotangent_ref,
     gain_ref,
-    w_mine,
-    w_other,
-    grad_ref,
-    branch_mine,
-    branch_other,
-    heads_mine,
-    heads_other,
-    gain_grad,
-    branch,
-    heads,
+    *refs,
 ):
+    w_mine, w_other, refs = refs[:2], refs[2:4], refs[4:]
+    grad_ref, branch_mine, branch_other, heads_mine, heads_other, gain_grad, branch, heads = refs
     core = place_ref[3]
     hidden = middle_ref[...]
     scale = lax.rsqrt(jnp.mean(hidden * hidden, axis=-1, keepdims=True) + epsilon)
@@ -920,7 +1033,7 @@
 
     summed = jnp.sum(incoming * hidden * scale, axis=0, keepdims=True)
     gain_grad[...] += jnp.broadcast_to(summed, gain_grad.shape)
-    columns, span = w_mine.shape[1], heads_mine.shape[1]
+    columns, span = w_mine[0].shape[1], heads_mine.shape[1]
 
     def part(ref, owner, size):
         return ref[:, pl.ds(pl.multiple_of(owner * size, LANES), size)]
@@ -928,9 +1041,10 @@
     branch_mine[...] = part(branch, core, columns)
     branch_other[...] = part(branch, 1 - core, columns)
     for at in range(0, 2 * span, SLAB):
+        index, rows = at // span, slice(at % span, at % span + SLAB)
         heads[:, at : at + SLAB] = (
-            across(branch_mine[...], w_mine[at : at + SLAB, :])
-            + across(branch_other[...], w_other[at : at + SLAB, :])
+            across(branch_mine[...], w_mine[index][rows, :])
+            + across(branch_other[...], w_other[index][rows, :])
         ).astype(low)
     heads_mine[...] = part(heads, core, span)
     heads_other[...] = part(heads, 1 - core, span)
@@ -938,7 +1052,7 @@
 
 def middle_back(place, middle, parts, cotangent, gains, w_mine, w_other, after=()):
     count, width = middle.shape
-    tile, columns, span = count // 2, w_mine.shape[1], w_mine.shape[0] // 2
+    tile, columns, span = count // 2, w_mine[0].shape[1], w_mine[0].shape[0]
     gain_grad = shaped((8, width), wide)
     return run(
         middle_back_kernel,
@@ -947,9 +1061,7 @@
         (2,),
         [
             *[(item, rows_of(tile, width)) for item in (middle, *parts, cotangent)],
-            (gains, whole(gains)),
-            (w_mine, whole(w_mine)),
-            (w_other, whole(w_other)),
+            *[(item, whole(item)) for item in (gains, *w_mine, *w_other)],
         ],
         [
             (shaped((count, width), wide), rows_of(tile, width)),
@@ -1078,46 +1190,21 @@
     send_off(place_ref, k, stages, k * 4, FFN_PLAN, FFN_HALF, sent, sems)
 
 
-def ffn_kernel(tiles, place_ref, *refs):
-    tokens, pieces, sums, sent = refs[:4], refs[4:9], refs[9:13], refs[13:18]
-    x_ref, c_ref, *rest = refs[18:]
-    weights, middles, stages, rest = rest[:3], rest[3:6], rest[6:9], rest[9:]
-    turned, turned_units, x_sems, in_sems, out_sems = rest
+def ffn_forward_kernel(tiles, pieces, place_ref, *refs):
+    tokens, pieces, refs = refs[:4], refs[4 : 4 + pieces], refs[4 + pieces :]
+    sums, middles = refs[:4], refs[4:7]
+    x_ref, c_ref, *weights, x_sems, in_sems = refs[7:]
     step = pl.program_id(0)
 
     @pl.when(step == 0)
     def _():
         load_tokens(x_ref, c_ref, *tokens, x_sems)
-        fetch(place_ref, pieces, FFN_PLAN, FFN_HALF, weights, in_sems)
-        drain((x_ref, c_ref), x_sems)
-        drain(weights, in_sems)
-
-    @pl.when(step < tiles)
-    def _():
-        rows = pl.ds(pl.multiple_of(step * FFN_TILE, FFN_TILE), FFN_TILE)
-        ffn_forward(step, tiles, x_ref, c_ref, weights, sums, middles, rows)
-
-    @pl.when(step >= tiles)
-    def _():
-        k = step - tiles
-        ffn_backward(
-            place_ref, k, x_ref, c_ref, middles, stages, turned, turned_units, sent, out_sems
-        )
-
-    @pl.when(step == tiles + 3)
-    def _():
-        drain(sent, out_sems)
-
-
-def ffn_forward_kernel(tiles, place_ref, *refs):
-    tokens, pieces, sums, middles = refs[:4], refs[4:9], refs[9:13], refs[13:16]
-    x_ref, c_ref, *weights, x_sems, in_sems = refs[16:]
-    step = pl.program_id(0)
-
-    @pl.when(step == 0)
-    def _():
-        load_tokens(x_ref, c_ref, *tokens, x_sems)
-        fetch(place_ref, pieces, FFN_PLAN, FFN_HALF, weights, in_sems)
+        if len(pieces) == 5:
+            fetch(place_ref, from_pieces(pieces, FFN_HALF), FFN_PLAN, weights, in_sems)
+        else:
+            source = from_pieces(pieces[:5], UPPER_ROWS // 2)
+            fetch(place_ref, source, UPPER_PLAN, weights, in_sems)
+            fetch(place_ref, from_planes(*pieces[5:]), LOWER_PLAN, weights, in_sems)
         drain((x_ref, c_ref), x_sems)
         drain(weights, in_sems)
 
@@ -1174,29 +1261,12 @@
     return shapes + ([pltpu.SemaphoreType.DMA((5,))] if stages else [])
 
 
-def ffn_chunk(place, tokens, pieces, after=()):
-    count, width = tokens[0].shape
-    tiles = 2 * count // FFN_TILE
-    results = run(
-        functools.partial(ffn_kernel, tiles),
-        "ffn",
-        place,
-        (tiles + 4,),
-        [(item, anywhere) for item in (*tokens, *pieces)],
-        ffn_sums(count, width) + sent_shapes(FFN_HALF, SLAB),
-        ffn_scratch(2 * count, width),
-        after,
-        us=60,
-    )
-    return results[:4], results[4:]
-
-
 def ffn_chunk_forward(place, tokens, pieces, after=()):
     count, width = tokens[0].shape
     tiles = 2 * count // FFN_TILE
     middle = pl.BlockSpec((FFN_TILE, FFN_UNITS), lambda i, place: (i, 0))
     results = run(
-        functools.partial(ffn_forward_kernel, tiles),
+        functools.partial(ffn_forward_kernel, tiles, len(pieces)),
         "ffn_forward",
         place,
         (tiles,),
@@ -1454,21 +1524,33 @@
     def pack_first(self):
         return pack_first(self.place, *self.weights[:4], *self.weights[7:])
 
-    def pack_ffn(self, chunk, after):
-        return pack_ffn(self.place, chunk, *self.weights[4:7], after)
-
-    def step_1(self, shard, after=()):
-        return pair_up(self.place, shard, hop(shard, 2, 0, 0), after)
-
-    def step_2(self, pair, after=()):
-        return line_up(self.place, pair, hop(pair, 1, 0, 0), after)
-
-    def step_3(self, line):
+    def pack_ffn(self, chunk, parts, after):
+        return pack_ffn(self.place, chunk, parts, *self.weights[4:7], after)
+
+    def step_0(self, shard):
+        return hop(shard, 2, 0, 0)
+
+    def step_1(self, shard, received, after=()):
+        return pair_up(self.place, shard, received, after)
+
+    def step_2(self, pair):
+        return hop(pair, 1, 0, 0)
+
+    def step_3(self, pair, received, after=()):
+        return line_up(self.place, pair, received, after)
+
+    def step_4(self, line):
         return near(line)
 
-    def step_4(self, line, sides, after=()):
+    def step_5(self, line, sides, after=()):
         upper, lower = halves(self.place, *sides, after)
-        return line, *sides, hop_y(upper), hop_x(lower)
+        return (line, *sides, hop_y(upper), hop_x(lower)), upper
+
+    def plane(self, parts, after):
+        return plane_up(self.place, parts, after)
+
+    def gate(self, sent, pieces):
+        return (*gate(self.place, sent[:2], (*pieces[3:5], pieces[6])), *sent[2:])
 
     def scatter_1(self, sent):
         return hop_x(sent[0]), hop_y(sent[1])
@@ -1479,7 +1561,7 @@
 
     def scatter_3(self, groups, after):
         groups = [(sent[4], *got, *more) for sent, got, more in groups]
-        kept, kept_far, part = sum_plane(self.place, groups, after)
+        kept, kept_far, part = sum_plane(self.place, groups, False, after)
         return kept, (kept_far, hop(part, 1, 0, 0))
 
     def scatter_4(self, kept, parts, after):
@@ -1487,17 +1569,24 @@
         token = sum_pass(self.place, kept_far, near, after)
         return token, (near, hop(token, 2, 0, 0))
 
+    def scatter_34(self, sent, got, more, after):
+        kept, *parts = sum_plane(self.place, [(sent[4], *got, *more)], True, after)
+        return kept, tuple(hop(part, k + 1, 0, 0) for k, part in enumerate(parts))
+
     def scatter_5(self, kept, parts, after):
-        total, total_low = sum_line(self.place, kept, parts[0], parts[1], after)
+        total, total_low = sum_line(self.place, kept, parts, after)
         return total, swap(total_low)
 
-    def finish_ffn(self, mine, other, shapes, after):
+    def pins(self, arrays):
+        return tuple(arrays)
+
+    def finish_ffn(self, chunk_0, chunk_1, shapes, after):
+        mine, other = zip(chunk_0, chunk_1)
         return unpack_ffn(self.place, mine, other, shapes, after)
 
-    def finish_first(self, mine, other, shapes, owned):
-        grads = unpack_first(self.place, mine, other, shapes)
-        row = GAINS + OUT_HALF
-        both = mine[row, : 2 * LANES] + other[row, : 2 * LANES].astype(wide)
+    def finish_first(self, first, chunk_1, shapes, owned, after):
+        grads = unpack_first(self.place, (*first, *chunk_1), shapes, after)
+        both = first[0][GAINS, : 2 * LANES] + first[1][GAINS, : 2 * LANES].astype(wide)
         return grads, (both[:owned], both[LANES : LANES + owned])
 
 
@@ -1534,68 +1623,74 @@
     segment = jnp.stack([item[1] for item in laid])
     cosine, sine = turn_table(jnp.concatenate([item[0] for item in laid]))
 
-    pair_first = routes.step_1(first)
-    line_first = routes.step_2(pair_first, (far_tokens, far_cotangent, segment, cosine, sine))
-    sides_first = routes.step_3(line_first)
-    chunk_0 = routes.pack_ffn(0, (line_first,))
-    pair_0 = routes.step_1(chunk_0)
-    pieces_first = routes.step_4(line_first, sides_first)
-    line_0 = routes.step_2(pair_0, (pair_0, *sides_first))
-    sides_0 = routes.step_3(line_0)
+    received_first = routes.step_0(first)
+    whole_rows = 2 * FFN_HALF
+    chunk_a, chunk_b = routes.pack_ffn(1, (UPPER_ROWS, whole_rows - UPPER_ROWS), (first,))
+    if direct:
+        chunk_b = chunk_b.reshape(1, *chunk_b.shape)
+    sides_b = routes.step_4(chunk_b)
+    parts_b, token = routes.step_5(chunk_b, sides_b)
+    pair_first = routes.step_1(first, received_first, (token,))
+    near_first = routes.step_2(pair_first)
+    (chunk_0,) = routes.pack_ffn(0, (whole_rows,), (pair_first,))
+    received_0 = routes.step_0(chunk_0)
+    plane_b = routes.plane(parts_b, (chunk_0,))
+    tables = (far_tokens, far_cotangent, segment, cosine, sine)
+    line_first = routes.step_3(pair_first, near_first, (*tables, plane_b))
+    sides_first = routes.step_4(line_first)
+    pair_0 = routes.step_1(chunk_0, received_0, (line_first,))
+    near_0 = routes.step_2(pair_0)
+    received_a = routes.step_0(chunk_a)
+    received_b = routes.step_0(plane_b)
+    pieces_first, token = routes.step_5(line_first, sides_first, (pair_0,))
+    line_0 = routes.step_3(pair_0, near_0, (token,))
+    sides_0 = routes.step_4(line_0)
     w_mine = out_weight(place, pieces_first, tokens.shape[1], (line_0,))
-    w_other = swap(w_mine)
+    w_other = [swap(part) for part in w_mine]
     normed_low, queries, keys, values, w_qkv, gains = project_qkv(
-        place, tokens, far_tokens, cosine, sine, pieces_first, (w_mine,)
-    )
-    chunk_1 = routes.pack_ffn(1, (keys,))
-    far_mine, far_total = attend(place, queries, keys, values, segment, 1, (chunk_1,))
+        place, tokens, far_tokens, cosine, sine, pieces_first, (w_mine[0],)
+    )
+    far_mine, far_total = attend(place, queries, keys, values, segment, 1, (keys,))
     own_other = swap(far_mine)
-    pair_1 = routes.step_1(chunk_1, (far_mine,))
-    pieces_0 = routes.step_4(line_0, sides_0)
     own_mine, own_total = attend(
-        place, queries, keys, values, segment, 0, (pair_1, *sides_0)
+        place, queries, keys, values, segment, 0, (far_mine, *w_other)
     )
     far_other = swap(own_mine)
+    pair_b = routes.step_1(plane_b, received_b, (own_mine,))
+    near_b = routes.step_2(pair_b)
+    pieces_0, token = routes.step_5(line_0, sides_0, (pair_b, received_a))
+    pair_a = routes.step_1(chunk_a, received_a, (token,))
+    near_a = routes.step_2(pair_a)
     middle, normed_own = middle_of(
-        place, tokens, own_mine, own_other, w_mine, w_other, gains
+        place, tokens, own_mine, own_other, w_mine, w_other, gains, (pair_a,)
     )
     normed_far = swap(normed_own)
-    line_1 = routes.step_2(pair_1, (normed_own, *pieces_0[3:]))
-    sides_1 = routes.step_3(line_1)
+    line_a = routes.step_3(pair_a, near_a, (normed_own, far_other, *pieces_0[3:]))
+    sides_a = routes.step_4(line_a)
 
     inputs = (normed_own, normed_far, cotangent, far_cotangent)
-    sums_0, middles_0 = ffn_chunk_forward(place, inputs, pieces_0, (line_1, far_other))
+    sums_0, middles_0 = ffn_chunk_forward(place, inputs, pieces_0, (line_a,))
     out_far_0, norm_far_0 = swap(sums_0[0]), swap(sums_0[1])
-    pieces_1 = routes.step_4(line_1, sides_1, (sums_0[0],))
-    sent_0 = ffn_chunk_backward(place, inputs, middles_0, (pieces_1[0],))
+    pieces_a, token = routes.step_5(line_a, sides_a, (sums_0[0],))
+    planes_b = (pair_b, near_b) if direct else chunk_b
+    pieces_1 = (*pieces_a, *planes_b)
+    sent_0 = ffn_chunk_backward(place, inputs, middles_0, (token,))
+    sent_0 = routes.gate(sent_0, pieces_1)
     got_0 = routes.scatter_1(sent_0)
-    sums_1, sent_1 = ffn_chunk(place, inputs, pieces_1)
+    sums_1, middles_1 = ffn_chunk_forward(place, inputs, pieces_1, (sent_0[0],))
     out_far_1, norm_far_1 = swap(sums_1[0]), swap(sums_1[1])
+    token, more_0 = routes.scatter_2(sent_0, got_0, (sums_1[0], out_far_0))
+    sent_1 = ffn_chunk_backward(place, inputs, middles_1, (token,))
     got_1 = routes.scatter_1(sent_1)
 
     norms = (sums_0[3], sums_1[3], norm_far_0, norm_far_1)
     grad_middle, branch_mine, branch_sent, heads_mine, heads_sent, ffn_gain_grad = middle_back(
-        place, middle, norms, cotangent, gains, w_mine, w_other, got_0
+        place, middle, norms, cotangent, gains, w_mine, w_other, (sent_1[4], *more_0)
     )
     branch_far, heads_far = swap(branch_sent), swap(heads_sent)
-    own_grads = attend_back(
-        place, queries, keys, values, heads_mine, own_total, segment, cosine, sine, 0
-    )
-    token, more_0 = routes.scatter_2(sent_0, got_0, (own_grads[0],))
-    far_grads = attend_back(
-        place,
-        queries,
-        keys,
-        values,
-        heads_far,
-        far_total,
-        segment,
-        cosine,
-        sine,
-        1,
-        (token,),
-    )
-    token, more_1 = routes.scatter_2(sent_1, got_1, (far_grads[0],))
+    attended = (queries, keys, values)
+    tables = (segment, cosine, sine)
+    own_grads = attend_back(place, *attended, heads_mine, own_mine, own_total, *tables, 0)
     sent_out = out_grad(
         place,
         own_mine,
@@ -1604,37 +1699,39 @@
         far_other,
         branch_mine,
         branch_far,
-        (token,),
+        (own_grads[0],),
     )
     got_out = routes.scatter_1(sent_out)
     kept_0, parts_0 = routes.scatter_3([(sent_0, got_0, more_0)], (sent_out[4],))
+    far_grads = attend_back(
+        place, *attended, heads_far, far_mine, far_total, *tables, 1, (kept_0, out_far_1)
+    )
+    token, more_1 = routes.scatter_2(sent_1, got_1, (far_grads[0], *routes.pins(got_out)))
+    token, more_out = routes.scatter_2(sent_out, got_out, (token,))
+    token, parts_0 = routes.scatter_4(kept_0, parts_0, (token,))
     grad_qkv, own_part, far_part, attn_gain_grad = input_back(
-        place, own_grads, far_grads, tokens, far_tokens, w_qkv, (kept_0,)
+        place, own_grads, far_grads, tokens, far_tokens, w_qkv, (token,)
     )
     own_rest = swap(far_part)
-    sent_qkv = qkv_grad(place, normed_low, grad_qkv, attn_gain_grad, ffn_gain_grad)
+    groups = [(sent_1, got_1, more_1), (sent_out, got_out, more_out)]
+    kept_1, parts_1 = routes.scatter_3(groups, (grad_qkv,))
+    pins = (kept_1, *routes.pins(parts_0[1:]))
+    sent_qkv = qkv_grad(place, normed_low, grad_qkv, attn_gain_grad, ffn_gain_grad, pins)
     got_qkv = routes.scatter_1(sent_qkv)
 
-    token, more_out = routes.scatter_2(sent_out, got_out, (sent_qkv[4],))
-    token, parts_0 = routes.scatter_4(kept_0, parts_0, (token,))
-    kept_1, parts_1 = routes.scatter_3([(sent_1, got_1, more_1)], (token,))
-    token, more_qkv = routes.scatter_2(sent_qkv, got_qkv, (kept_1,))
-    owned_0, other_0 = routes.scatter_5(kept_0, parts_0, (token,))
-    token, parts_1 = routes.scatter_4(kept_1, parts_1, (owned_0,))
-    groups = [(sent_qkv, got_qkv, more_qkv), (sent_out, got_out, more_out)]
-    kept_qkv, parts_qkv = routes.scatter_3(groups, (token,))
+    owned_0 = routes.scatter_5(kept_0, parts_0, (sent_qkv[4],))
     outs = (sums_0[2], sums_1[2], out_far_0, out_far_1)
-    output = output_of(place, middle, outs, (kept_qkv,))
-    owned_1, other_1 = routes.scatter_5(kept_1, parts_1, (output,))
-    token, parts_qkv = routes.scatter_4(kept_qkv, parts_qkv, (owned_1,))
+    output = output_of(place, middle, outs, (owned_0[0],))
+    token, parts_1 = routes.scatter_4(kept_1, parts_1, (output,))
+    token, more_qkv = routes.scatter_2(sent_qkv, got_qkv, (token,))
     grad_tokens = tokens_grad(place, tokens, grad_middle, own_part, own_rest, gains, (token,))
+    kept_qkv, parts_qkv = routes.scatter_34(sent_qkv, got_qkv, more_qkv, (grad_tokens,))
+    owned_1 = routes.scatter_5(kept_1, parts_1, (kept_qkv,))
+    owned_qkv = routes.scatter_5(kept_qkv, parts_qkv, (owned_1[0],))
     shapes = [w_gate.shape, w_up.shape, w_down.shape]
-    grad_gate, grad_up, grad_down = routes.finish_ffn(
-        (owned_0, owned_1), (other_0, other_1), shapes, (grad_tokens,)
-    )
-    owned_qkv, other_qkv = routes.scatter_5(kept_qkv, parts_qkv, (grad_gate,))
+    grad_gate, grad_up, grad_down = routes.finish_ffn(owned_0, owned_1, shapes, (owned_qkv[0],))
     shapes = [w_query.shape, w_key.shape, w_value.shape, w_out.shape]
-    grads, gain_grads = routes.finish_first(owned_qkv, other_qkv, shapes, owned)
+    grads, gain_grads = routes.finish_first(owned_qkv, owned_1, shapes, owned, (grad_gate,))
     return (
         output,
         grad_tokens,
@@ -1691,26 +1788,40 @@
             at = (CHUNKS * core + chunk) * quarter
             part = full(lax.dynamic_slice_in_dim(down_w, at, quarter, axis=0))
             parts = slabs(units(gate, chunk)) + slabs(units(up, chunk)) + slabs(part)
-            chunks.append(pieces_of(jnp.concatenate(parts, axis=1)))
-        self.ffn_0, self.ffn_1 = chunks
+            chunks.append(jnp.concatenate(parts, axis=1))
+        planes = chunks[1][:, UPPER_ROWS:].reshape(4, 4, -1, SLAB)
+        self.ffn_0 = (pieces_of(chunks[0]),)
+        self.ffn_1 = pieces_of(chunks[1][:, :UPPER_ROWS]), (planes[0::2], planes[1::2])
 
     def pack_first(self):
         return self.first
 
-    def pack_ffn(self, chunk, after):
+    def pack_ffn(self, chunk, parts, after):
         return (self.ffn_0, self.ffn_1)[chunk]
 
-    def step_1(self, shard, after=()):
+    def step_0(self, shard):
         return shard
 
-    def step_2(self, pair, after=()):
+    def step_1(self, shard, received, after=()):
+        return shard
+
+    def step_2(self, pair):
         return pair
 
-    def step_3(self, line):
+    def step_3(self, pair, received, after=()):
+        return pair
+
+    def step_4(self, line):
         return ()
 
-    def step_4(self, line, sides, after=()):
-        return line
+    def step_5(self, line, sides, after=()):
+        return line, line
+
+    def plane(self, parts, after):
+        return parts
+
+    def gate(self, sent, pieces):
+        return sent
 
     def scatter_1(self, sent):
         return blocks_of(sent)
@@ -1721,6 +1832,9 @@
     def scatter_3(self, groups, after):
         blocks = jnp.concatenate([got for _, got, _ in groups], axis=1)
         return blocks, blocks
+
+    def scatter_34(self, sent, got, more, after):
+        return got, ()
 
     def scatter_4(self, kept, parts, after):
         return kept, kept
@@ -1746,9 +1860,12 @@
         first = jnp.where(self.core == 0, part, other)
         return first, jnp.where(self.core == 0, other, part)
 
-    def finish_ffn(self, mine, other, shapes, after):
+    def pins(self, arrays):
+        return ()
+
+    def finish_ffn(self, chunk_0, chunk_1, shapes, after):
         gates, ups, downs = [], [], []
-        for blocks in mine:
+        for blocks, _ in (chunk_0, chunk_1):
             gate, up, down_w = self.split(blocks, ((96, 2), (96, 2), (64, 3)))
             gates.append(self.ordered(gate))
             ups.append(self.ordered(up))
@@ -1763,9 +1880,10 @@
         grad_down = [downs[chunk][owner] for owner in range(2) for chunk in range(CHUNKS)]
         return columns(gates), columns(ups), jnp.concatenate(grad_down, axis=0)
 
-    def finish_first(self, mine, other, shapes, owned):
+    def finish_first(self, first, chunk_1, shapes, owned, after):
+        mine = first[0]
         (qkv,) = self.split(mine[:, :GAINS], ((96, 3),))
-        blocks = mine[:, 2 * QKV_HALF :]
+        blocks = chunk_1[0][:, 2 * FFN_HALF :]
         rest = blocks[:, 96:144]
         rest = jnp.concatenate([rest[:, :, :256], rest[:, :, 256:]], axis=1)
         (square,) = self.split(jnp.concatenate([blocks[:, :96], rest], axis=2), ((96, 1),))

time: 675 us -> 648 us (0.960)
  waiting for transfers between devices: 162 us -> 133 us
  Pallas kernels: 410 us -> 396 us
  local copies, waits for them, and re-layouts: 30.1 us -> 39.1 us
    ppermute x40 -> x47, waiting for transfers between devices: 153 us -> 130 us  [hop(): lax.ppermute(array, 'fsdp', [(chip, chip ^ flip) for chip in range(BLOCKS)])]
    pallas_call x43 -> x46, Pallas kernels: 410 us -> 395 us  [run(): pl.pallas_call(body, grid_spec=pltpu.PrefetchScalarGridSpec(num_scalar_pr...]
    unnamed x108 -> x140, local copies, waits for them, and re-layouts: 28.9 us -> 37.9 us
    ppermute x17 -> x18, waiting for transfers between devices: 9.53 us -> 2.6 us  [swap(): return lax.ppermute(array, 'rep', [(0, 1), (1, 0)])]
    ppermute x40 -> x47, starting transfers between devices: 53.9 us -> 58.6 us  [hop(): lax.ppermute(array, 'fsdp', [(chip, chip ^ flip) for chip in range(BLOCKS)])]
  transfers between devices with their start and end apart: 57 -> 65, of which waited for: 22 -> 26; matrix products, arithmetic and copies ran while one was open for 1% -> 1% of each run, Pallas kernels for 59% -> 59%
where the time goes in v3:
time: 648 us; the launch traced here: 638 us
  Pallas kernels  396 us (61%)
  waiting for transfers between devices  133 us (21%)
  starting transfers between devices  61.6 us (10%)
  local copies, waits for them, and re-layouts  39.1 us (6%)
  other arithmetic  6.63 us (1%)
    pallas_call x46, Pallas kernels, run(): pl.pallas_call(body, grid_spec=pltpu.PrefetchScalarGridSpec(num_scalar_pr...  395 us
    ppermute x47, waiting for transfers between devices, hop(): lax.ppermute(array, 'fsdp', [(chip, chip ^ flip) for chip in range(BLOCKS)])  130 us
    ppermute x47, starting transfers between devices, hop(): lax.ppermute(array, 'fsdp', [(chip, chip ^ flip) for chip in range(BLOCKS)])  58.6 us
    unnamed x140, local copies, waits for them, and re-layouts  37.9 us
  transfers between devices with their start and end apart: 65, of which 26 were waited for; matrix products, arithmetic and copies ran while one was open for 1% of the time, Pallas kernels for 59%

profile of v3, /device:TPU:0, one launch (start us, length us, event | category | flops | bytes accessed | tf_op | source)
XLA Modules:
  0.0 638.2 jit_solution(13495396580133200242)
XLA Ops:
  24.6 4.7 collective-permute-done.2.refs_1_
  49.0 5.9 collective-permute-done.5.refs_1_
  66.0 25.1 %collective-permute-done.11.refs_1_ = bf16[576,512]{1,0:T(8,128)(2,1)S(1)} collective-permute-done((bf16[576,512]{1,0:T(8,128)(2,1)S(1)}, bf16[576,512]{1,0:T(8,128)(2,1)S(1)}, u32[]{:S(2)}, u32[]{:S(2)}) %collective-permute-start.11) | collective-permute-done | bytes 589856 | tf_op jit(solution)/shard_map/ppermute | solution.py:1479
  95.6 5.4 collective-permute-done.10.refs_1_.refs_2_.refs_6_
  109.3 12.8 %collective-permute-done.14.refs_1_ = bf16[2,576,512]{2,1,0:T(8,128)(2,1)S(1)} collective-permute-done((bf16[2,576,512]{2,1,0:T(8,128)(2,1)}, bf16[2,576,512]{2,1,0:T(8,128)(2,1)S(1)}, u32[]{:S(2)}, u32[]{:S(2)}) %collective-permute-start.14) | collective-permute-done | bytes 1179680 | tf_op jit(solution)/shard_map/ppermute | solution.py:1479
  140.7 19.0 %project_qkv.1 = (bf16[1280,1536]{1,0:T(8,128)(2,1)}, bf16[1280,1024]{1,0:T(8,128)(2,1)}, bf16[1280,512]{1,0:T(8,128)(2,1)}, bf16[1280,512]{1,0:T(8,128)(2,1)}, ...) custom-call(s32[4]{0:T(128)} %pad_add_fusion.1.place_ref, bf16[640,1536]{1,0:T(8,128)(2,1)} %refs_0_.11, ...), custom_call_target="tpu_custom_call" | custom-call | bytes 59400 | tf_op jit(solution)/shard_map/project_qkv/pallas_call | solution.py:52
  159.7 12.3 %attend.2 = (bf16[640,1024]{1,0:T(8,128)(2,1)}, f32[640,128]{1,0:T(8,128)}) custom-call(s32[4]{0:T(128)} %pad_add_fusion.1.place_ref, bf16[1280,1024]{1,0:T(8,128)(2,1)} %get-tuple-element.124.refs_0_, bf16[1280,512]{1,0:T(8,128)(2,1)} %get-tuple-element.125.refs_1_.refs_5_, bf16[1280,512]{1,0:T(8,128)(2,1)} %get-tuple-element.126.refs_2_, ...), custom_call_target="tpu_custom_call" | custom-call | bytes 56100 | tf_op jit(solution)/shard_map/attend/pallas_call | solution.py:52
  173.6 12.0 %attend.3 = (bf16[640,1024]{1,0:T(8,128)(2,1)}, f32[640,128]{1,0:T(8,128)}) custom-call(s32[4]{0:T(128)} %pad_add_fusion.1.place_ref, bf16[1280,1024]{1,0:T(8,128)(2,1)} %get-tuple-element.124.refs_0_, bf16[1280,512]{1,0:T(8,128)(2,1)} %get-tuple-element.125.refs_1_.refs_5_, bf16[1280,512]{1,0:T(8,128)(2,1)} %get-tuple-element.126.refs_2_, ...), custom_call_target="tpu_custom_call" | custom-call | bytes 56100 | tf_op jit(solution)/shard_map/attend/pallas_call | solution.py:52
  204.2 11.0 %middle.1 = (f32[640,1536]{1,0:T(8,128)}, bf16[640,1536]{1,0:T(8,128)(2,1)}) custom-call(s32[4]{0:T(128)} %pad_add_fusion.1.place_ref, bf16[640,1536]{1,0:T(8,128)(2,1)} %refs_0_.11, bf16[640,1024]{1,0:T(8,128)(2,1)} %get-tuple-element.129.refs_2_.refs_1_.refs_4_.refs_0_, bf16[640,1024]{1,0:T(8,128)(2,1)} %copy-done.22, ...), custom_call_target="tpu_custom_call" | custom-call | bytes 36300 | tf_op jit(solution)/shard_map/middle/pallas_call | solution.py:52
  215.2 6.8 %collective-permute-done.25.refs_1_ = bf16[2,384,512]{2,1,0:T(8,128)(2,1)S(1)} collective-permute-done((bf16[2,384,512]{2,1,0:T(8,128)(2,1)}, bf16[2,384,512]{2,1,0:T(8,128)(2,1)S(1)}, u32[]{:S(2)}, u32[]{:S(2)}) %collective-permute-start.25) | collective-permute-done | bytes 786464 | tf_op jit(solution)/shard_map/ppermute | solution.py:1479
  236.2 39.8 %ffn_forward.2 = (bf16[640,1536]{1,0:T(8,128)(2,1)}, bf16[640,1536]{1,0:T(8,128)(2,1)}, f32[640,1536]{1,0:T(8,128)}, f32[640,1536]{1,0:T(8,128)}, bf16[1280,1024...) custom-call(s32[4]{0:T(128)} %pad_add_fusion.1.place_ref, ...), custom_call_target="tpu_custom_call" | custom-call | bytes 118800 | tf_op jit(solution)/shard_map/ffn_forward/pallas_call | solution.py:52
  281.7 22.5 %ffn_backward.2 = (bf16[2,4,288,512]{3,2,1,0:T(8,128)(2,1)}, bf16[2,4,288,512]{3,2,1,0:T(8,128)(2,1)}, bf16[4,288,512]{2,1,0:T(8,128)(2,1)}, bf16[4,288,512]{2,1,0:T(8,128)(2,1)}, bf16[4,2,288,512]{3,2,1,0:T(8,128)(2,1)}) custom-call(s32[4]{0:T(128)} %pad_add_fusion.1.place_ref, bf16[640,1536]{1,0:T(8,128)(2,1)} %get-tuple-element.134.refs_2_.refs_0_, ...), custom_call_target="tpu_custom_call" | custom-call | bytes 72600 | tf_op jit(solution)/shard_map/ffn_backward/pallas_call | solution.py:52
  310.4 39.9 %ffn_forward.3 = (bf16[640,1536]{1,0:T(8,128)(2,1)}, bf16[640,1536]{1,0:T(8,128)(2,1)}, f32[640,1536]{1,0:T(8,128)}, f32[640,1536]{1,0:T(8,128)}, bf16[1280,1024...) custom-call(s32[4]{0:T(128)} %pad_add_fusion.1.place_ref, ...), custom_call_target="tpu_custom_call" | custom-call | bytes 118800 | tf_op jit(solution)/shard_map/ffn_forward/pallas_call | solution.py:52
  350.4 7.6 %collective-permute-done.34.refs_2_.refs_1_ = bf16[2,4,288,512]{3,2,1,0:T(8,128)(2,1)S(1)} collective-permute-done((bf16[2,4,288,512]{3,2,1,0:T(8,128)(2,1)}, bf16[2,4,288,512]{3,2,1,0:T(8,128)(2,1)S(1)}, u32[]{:S(2)}, u32[]{:S(2)}) %collective-permute-start.34) | collective-permute-done | bytes 2359328 | tf_op jit(solution)/shard_map/ppermute | solution.py:1479
  360.9 5.3 merge.4
  368.3 22.4 %ffn_backward.3 = (bf16[2,4,288,512]{3,2,1,0:T(8,128)(2,1)}, bf16[2,4,288,512]{3,2,1,0:T(8,128)(2,1)}, bf16[4,288,512]{2,1,0:T(8,128)(2,1)}, bf16[4,288,512]{2,1,0:T(8,128)(2,1)}, bf16[4,2,288,512]{3,2,1,0:T(8,128)(2,1)}) custom-call(s32[4]{0:T(128)} %pad_add_fusion.1.place_ref, bf16[640,1536]{1,0:T(8,128)(2,1)} %get-tuple-element.134.refs_2_.refs_0_, ...), custom_call_target="tpu_custom_call" | custom-call | bytes 72600 | tf_op jit(solution)/shard_map/ffn_backward/pallas_call | solution.py:52
  393.8 16.5 %middle_back.1 = (f32[640,1536]{1,0:T(8,128)}, bf16[640,768]{1,0:T(8,128)(2,1)}, bf16[640,768]{1,0:T(8,128)(2,1)}, bf16[640,1024]{1,0:T(8,128)(2,1)}, bf16[640,1024]{1,0:T(8,128)(2,1)}, /*index=5*/f32[8,1536]{1,0:T(8,128)}) custom-call(s32[4]{0:T(128)} %pad_add_fusion.1.place_ref, f32[640,1536]{1,0:T(8,128)} %get-tuple-element.133.refs_0_, ...), custom_call_target="tpu_custom_call" | custom-call | bytes 49500 | tf_op jit(solution)/shard_map/middle_back/pallas_call | solution.py:52
  410.9 14.3 %attend_back.2 = (bf16[640,1024]{1,0:T(8,128)(2,1)}, bf16[640,512]{1,0:T(8,128)(2,1)}, bf16[640,512]{1,0:T(8,128)(2,1)}) custom-call(s32[4]{0:T(128)} %pad_add_fusion.1.place_ref, bf16[1280,1024]{1,0:T(8,128)(2,1)} %get-tuple-element.124.refs_0_, bf16[1280,512]{1,0:T(8,128)(2,1)} %get-tuple-element.125.refs_1_.refs_5_, ...), custom_call_target="tpu_custom_call" | custom-call | bytes 69300 | tf_op jit(solution)/shard_map/attend_back/pallas_call | solution.py:52
  426.1 10.3 %out_grad.1 = (bf16[2,4,80,512]{3,2,1,0:T(8,128)(2,1)}, bf16[2,4,80,512]{3,2,1,0:T(8,128)(2,1)}, bf16[4,80,512]{2,1,0:T(8,128)(2,1)}, bf16[4,80,512]{2,1,0:T(8,128)(2,1)}, bf16[4,2,80,512]{3,2,1,0:T(8,128)(2,1)}) custom-call(s32[4]{0:T(128)} %pad_add_fusion.1.place_ref, bf16[640,1024]{1,0:T(8,128)(2,1)} %get-tuple-element.129.refs_2_.refs_1_.refs_4_.refs_0_, ...), custom_call_target="tpu_custom_call" | custom-call | bytes 33000 | tf_op jit(solution)/shard_map/out_grad/pallas_call | solution.py:52
  438.6 6.4 %sum_plane.3 = (f32[2,288,512]{2,1,0:T(8,128)}, f32[2,288,512]{2,1,0:T(8,128)}, bf16[2,2,288,512]{3,2,1,0:T(8,128)(2,1)}) custom-call(s32[4]{0:T(128)} %pad_add_fusion.1.place_ref, bf16[4,2,288,512]{3,2,1,0:T(8,128)(2,1)} %get-tuple-element.148.refs_0_, bf16[2,4,288,512]{3,2,1,0:T(8,128)(2,1)} %copy-done.9, bf16[2,4,288,512]{3,2,1,0:T(8,128)(2,1)} %copy-done.10, ...), custom_call_target="tpu_custom_call" | custom-call | bytes 16500 | tf_op jit(solution)/shard_map/sum_plane/pallas_call | solution.py:52
  446.8 14.1 %attend_back.3 = (bf16[640,1024]{1,0:T(8,128)(2,1)}, bf16[640,512]{1,0:T(8,128)(2,1)}, bf16[640,512]{1,0:T(8,128)(2,1)}) custom-call(s32[4]{0:T(128)} %pad_add_fusion.1.place_ref, bf16[1280,1024]{1,0:T(8,128)(2,1)} %get-tuple-element.124.refs_0_, bf16[1280,512]{1,0:T(8,128)(2,1)} %get-tuple-element.125.refs_1_.refs_5_, ...), custom_call_target="tpu_custom_call" | custom-call | bytes 69300 | tf_op jit(solution)/shard_map/attend_back/pallas_call | solution.py:52
  463.4 5.3 merge.5
  480.7 14.8 %input_back.1 = (bf16[1280,1536]{1,0:T(8,128)(2,1)}, f32[640,1536]{1,0:T(8,128)}, bf16[640,1536]{1,0:T(8,128)(2,1)}, f32[8,1536]{1,0:T(8,128)}) custom-call(s32[4]{0:T(128)} %pad_add_fusion.1.place_ref, bf16[640,1024]{1,0:T(8,128)(2,1)} %get-tuple-element.166.refs_6_.refs_0_, bf16[640,512]{1,0:T(8,128)(2,1)} %get-tuple-element.185.refs_1_, ...), custom_call_target="tpu_custom_call" | custom-call | bytes 49500 | tf_op jit(solution)/shard_map/input_back/pallas_call | solution.py:52
  495.5 7.6 %collective-permute-done.50.refs_8_ = bf16[4,80,512]{2,1,0:T(8,128)(2,1)S(1)} collective-permute-done((bf16[4,80,512]{2,1,0:T(8,128)(2,1)S(1)}, bf16[4,80,512]{2,1,0:T(8,128)(2,1)S(1)}, u32[]{:S(2)}, u32[]{:S(2)}) %collective-permute-start.50) | collective-permute-done | bytes 327712 | tf_op jit(solution)/shard_map/ppermute | solution.py:1479
  505.3 7.3 %sum_plane.4 = (f32[2,368,512]{2,1,0:T(8,128)}, f32[2,368,512]{2,1,0:T(8,128)}, bf16[2,2,368,512]{3,2,1,0:T(8,128)(2,1)}) custom-call(s32[4]{0:T(128)} %pad_add_fusion.1.place_ref, bf16[4,2,288,512]{3,2,1,0:T(8,128)(2,1)} %get-tuple-element.161.refs_11_.refs_0_, bf16[2,4,288,512]{3,2,1,0:T(8,128)(2,1)} %copy-done.7, bf16[2,4,288,512]{3,2,1,0:T(8,128)(2,1)} %copy-done.8, ...), custom_call_target="tpu_custom_call" | custom-call | bytes 16500 | tf_op jit(solution)/shard_map/sum_plane/pallas_call | solution.py:52
  513.8 14.9 %qkv_grad.1 = (bf16[2,4,160,512]{3,2,1,0:T(8,128)(2,1)}, bf16[2,4,160,512]{3,2,1,0:T(8,128)(2,1)}, bf16[4,160,512]{2,1,0:T(8,128)(2,1)}, bf16[4,160,512]{2,1,0:T(8,128)(2,1)}, bf16[4,2,160,512]{3,2,1,0:T(8,128)(2,1)}) custom-call(s32[4]{0:T(128)} %pad_add_fusion.1.place_ref, bf16[1280,1536]{1,0:T(8,128)(2,1)} %get-tuple-element.184.refs_0_, ...), custom_call_target="tpu_custom_call" | custom-call | bytes 49500 | tf_op jit(solution)/shard_map/qkv_grad/pallas_call | solution.py:52
  535.3 8.3 %output.1.refs_2_ = bf16[640,1536]{1,0:T(8,128)(2,1)} custom-call(s32[4]{0:T(128)} %pad_add_fusion.1.place_ref, f32[640,1536]{1,0:T(8,128)} %get-tuple-element.133.refs_0_, f32[640,1536]{1,0:T(8,128)} %get-tuple-element.136.refs_1_, f32[640,1536]{1,0:T(8,128)} %get-tuple-element.146.refs_2_, bf16[640,1536]{1,0:T(8,128)(2,1)} %copy-done.12, ...), custom_call_target="tpu_custom_call" | custom-call | bytes 13200 | tf_op jit(solution)/shard_map/output/pallas_call | solution.py:52
  550.1 7.4 %collective-permute-done.53.refs_2_.refs_1_ = bf16[2,4,160,512]{3,2,1,0:T(8,128)(2,1)S(1)} collective-permute-done((bf16[2,4,160,512]{3,2,1,0:T(8,128)(2,1)}, bf16[2,4,160,512]{3,2,1,0:T(8,128)(2,1)S(1)}, u32[]{:S(2)}, u32[]{:S(2)}) %collective-permute-start.53) | collective-permute-done | bytes 1310752 | tf_op jit(solution)/shard_map/ppermute | solution.py:1479
  567.3 8.9 %tokens_grad.1.refs_5_ = f32[640,1536]{1,0:T(8,128)} custom-call(s32[4]{0:T(128)} %pad_add_fusion.1.place_ref, bf16[640,1536]{1,0:T(8,128)(2,1)} %refs_0_.11, f32[640,1536]{1,0:T(8,128)} %get-tuple-element.198.refs_1_, f32[640,1536]{1,0:T(8,128)} %get-tuple-element.199.refs_2_, bf16[640,1536]{1,0:T(8,128)(2,1)} %copy-done.35, ...), custom_call_target="tpu_custom_call" | custom-call | bytes 13200 | tf_op jit(solution)/shard_map/tokens_grad/pallas_call | solution.py:52
  578.0 4.9 sum_plane.5
  587.3 24.8 %collective-permute-done.61.refs_2_ = bf16[2,368,512]{2,1,0:T(8,128)(2,1)S(1)} collective-permute-done((bf16[2,368,512]{2,1,0:T(8,128)(2,1)S(1)}, bf16[2,368,512]{2,1,0:T(8,128)(2,1)S(1)}, u32[]{:S(2)}, u32[]{:S(2)}) %collective-permute-start.61) | collective-permute-done | bytes 753696 | tf_op jit(solution)/shard_map/ppermute | solution.py:1479
  628.3 5.6 unpack_ffn.1
  (302 shorter events, 212.4 us)
Async XLA Ops:
  0.6 54.3 %collective-permute-start.6 = (bf16[640,1536]{1,0:T(8,128)(2,1)}, bf16[640,1536]{1,0:T(8,128)(2,1)S(1)}, u32[]{:S(2)}, u32[]{:S(2)}) collective-permute-start(bf16[640,1536]{1,0:T(8,128)(2,1)} %refs_5_.1), channel_id=1, source_target_pairs={{0,16},{16,0},{1,17},{17,1},{2,18},{18,2},{3,19},{19,3},{4,20},{20... | collective-permute-start | bytes 5898248 | tf_op jit(solution)/shard_map/ppermute | solution.py:1474
  1.2 53.8 %collective-permute-start = (bf16[640,1536]{1,0:T(8,128)(2,1)}, bf16[640,1536]{1,0:T(8,128)(2,1)}, u32[]{:S(2)}, u32[]{:S(2)}) collective-permute-start(bf16[640,1536]{1,0:T(8,128)(2,1)} %refs_0_.11), channel_id=1, source_target_pairs={{0,16},{16,0},{1,17},{17,1},{2,18},{18,2},{3,19},{19,3},{4,20},{20... | collective-permute-start | bytes 5898248 | tf_op jit(solution)/shard_map/ppermute | solution.py:1474
  60.1 40.8 %collective-permute-start.10 = (bf16[4,448,512]{2,1,0:T(8,128)(2,1)}, bf16[4,448,512]{2,1,0:T(8,128)(2,1)S(1)}, u32[]{:S(2)}, u32[]{:S(2)}) collective-permute-start(bf16[4,448,512]{2,1,0:T(8,128)(2,1)} %line.3.refs_2_.refs_0_.refs_4_), channel_id=1, source_target_pairs={{0,2},{1,3},{2,0},{3,1},{4,6},{5,7},{6,4},{7,5},{8,10},{9,11},{10,... | collective-permute-start | bytes 5505032 | tf_op jit(solution)/shard_map/ppermute | solution.py:1479
  61.4 40.2 %collective-permute-start.9 = (bf16[4,448,512]{2,1,0:T(8,128)(2,1)}, bf16[4,448,512]{2,1,0:T(8,128)(2,1)S(1)}, u32[]{:S(2)}, u32[]{:S(2)}) collective-permute-start(bf16[4,448,512]{2,1,0:T(8,128)(2,1)} %line.3.refs_2_.refs_0_.refs_4_), channel_id=1, source_target_pairs={{0,1},{1,0},{2,3},{3,2},{4,5},{5,4},{6,7},{7,6},{8,9},{9,8},{10,11... | collective-permute-start | bytes 5505032 | tf_op jit(solution)/shard_map/ppermute | solution.py:1479
  126.9 66.1 %collective-permute-start.19 = (bf16[4,576,512]{2,1,0:T(8,128)(2,1)}, bf16[4,576,512]{2,1,0:T(8,128)(2,1)}, u32[]{:S(2)}, u32[]{:S(2)}) collective-permute-start(bf16[4,576,512]{2,1,0:T(8,128)(2,1)} %line.4.refs_5_.refs_4_), channel_id=1, source_target_pairs={{0,1},{1,0},{2,3},{3,2},{4,5},{5,4},{6,7},{7,6},{8,9},{9,8},{10,11... | collective-permute-start | bytes 7077896 | tf_op jit(solution)/shard_map/ppermute | solution.py:1479
  127.5 65.5 %collective-permute-start.20 = (bf16[4,576,512]{2,1,0:T(8,128)(2,1)}, bf16[4,576,512]{2,1,0:T(8,128)(2,1)}, u32[]{:S(2)}, u32[]{:S(2)}) collective-permute-start(bf16[4,576,512]{2,1,0:T(8,128)(2,1)} %line.4.refs_5_.refs_4_), channel_id=1, source_target_pairs={{0,2},{1,3},{2,0},{3,1},{4,6},{5,7},{6,4},{7,5},{8,10},{9,11},{10,... | collective-permute-start | bytes 7077896 | tf_op jit(solution)/shard_map/ppermute | solution.py:1479
  134.0 38.0 %collective-permute-start.15 = (bf16[1024,768]{1,0:T(8,128)(2,1)}, bf16[1024,768]{1,0:T(8,128)(2,1)S(1)}, u32[]{:S(2)}, u32[]{:S(2)}) collective-permute-start(bf16[1024,768]{1,0:T(8,128)(2,1)} %get-tuple-element.123.refs_9_.refs_3_.refs_7_), channel_id=1, source_target_pairs={{0,16},{16,0},{1,17},{17,1},{2,18},{18,2},{3,19},{19,3},{4,20},{20... | collective-permute-start | bytes 4718600 | tf_op jit(solution)/shard_map/ppermute | solution.py:1474
  134.1 38.0 %collective-permute-start.16 = (bf16[1024,768]{1,0:T(8,128)(2,1)}, bf16[1024,768]{1,0:T(8,128)(2,1)S(1)}, u32[]{:S(2)}, u32[]{:S(2)}) collective-permute-start(bf16[1024,768]{1,0:T(8,128)(2,1)} %get-tuple-element.128.refs_4_.refs_8_), channel_id=1, source_target_pairs={{0,16},{16,0},{1,17},{17,1},{2,18},{18,2},{3,19},{19,3},{4,20},{20... | collective-permute-start | bytes 4718600 | tf_op jit(solution)/shard_map/ppermute | solution.py:1474
  134.6 51.1 %collective-permute-start.21 = (bf16[4,192,512]{2,1,0:T(8,128)(2,1)}, bf16[4,192,512]{2,1,0:T(8,128)(2,1)}, u32[]{:S(2)}, u32[]{:S(2)}) collective-permute-start(bf16[4,192,512]{2,1,0:T(8,128)(2,1)} %plane.1.refs_7_.refs_0_), channel_id=1, source_target_pairs={{0,8},{1,9},{2,10},{3,11},{4,12},{5,13},{6,14},{7,15},{8,0},{9,1},... | collective-permute-start | bytes 2359304 | tf_op jit(solution)/shard_map/ppermute | solution.py:1479
  172.0 31.1 %collective-permute-start.17 = (bf16[640,1024]{1,0:T(8,128)(2,1)}, bf16[640,1024]{1,0:T(8,128)(2,1)S(1)}, u32[]{:S(2)}, u32[]{:S(2)}) collective-permute-start(bf16[640,1024]{1,0:T(8,128)(2,1)} %get-tuple-element.127.refs_5_.refs_2_.refs_4_), channel_id=1, source_target_pairs={{0,16},{16,0},{1,17},{17,1},{2,18},{18,2},{3,19},{19,3},{4,20},{20... | collective-permute-start | bytes 3932168 | tf_op jit(solution)/shard_map/ppermute | solution.py:1474
  185.7 40.5 %collective-permute-start.26 = (bf16[640,1024]{1,0:T(8,128)(2,1)}, bf16[640,1024]{1,0:T(8,128)(2,1)S(1)}, u32[]{:S(2)}, u32[]{:S(2)}) collective-permute-start(bf16[640,1024]{1,0:T(8,128)(2,1)} %get-tuple-element.129.refs_2_.refs_1_.refs_4_.refs_0_), channel_id=1, source_target_pairs={{0,16},{16,0},{1,17},{17,1},{2,18},{18,2},{3,19},{19,3},{4,20},{20... | collective-permute-start | bytes 3932168 | tf_op jit(solution)/shard_map/ppermute | solution.py:1474
  231.6 44.5 %collective-permute-start.27 = (bf16[4,384,512]{2,1,0:T(8,128)(2,1)}, bf16[4,384,512]{2,1,0:T(8,128)(2,1)S(1)}, u32[]{:S(2)}, u32[]{:S(2)}) collective-permute-start(bf16[4,384,512]{2,1,0:T(8,128)(2,1)} %line.5.refs_9_.refs_4_), channel_id=1, source_target_pairs={{0,1},{1,0},{2,3},{3,2},{4,5},{5,4},{6,7},{7,6},{8,9},{9,8},{10,11... | collective-permute-start | bytes 4718600 | tf_op jit(solution)/shard_map/ppermute | solution.py:1479
  233.6 42.5 %collective-permute-start.28 = (bf16[4,384,512]{2,1,0:T(8,128)(2,1)}, bf16[4,384,512]{2,1,0:T(8,128)(2,1)S(1)}, u32[]{:S(2)}, u32[]{:S(2)}) collective-permute-start(bf16[4,384,512]{2,1,0:T(8,128)(2,1)} %line.5.refs_9_.refs_4_), channel_id=1, source_target_pairs={{0,2},{1,3},{2,0},{3,1},{4,6},{5,7},{6,4},{7,5},{8,10},{9,11},{10,... | collective-permute-start | bytes 4718600 | tf_op jit(solution)/shard_map/ppermute | solution.py:1479
  234.9 69.3 %collective-permute-start.31 = (bf16[2,4,192,512]{3,2,1,0:T(8,128)(2,1)S(1)}, bf16[2,4,192,512]{3,2,1,0:T(8,128)(2,1)S(1)}, u32[]{:S(2)}, u32[]{:S(2)}) collective-permute-start(bf16[2,4,192,512]{3,2,1,0:T(8,128)(2,1)S(1)} %copy-done.6), channel_id=1, source_target_pairs={{0,4},{1,5},{2,6},{3,7},{4,0},{5,1},{6,2},{7,3},{8,12},{9,13},{10,... | collective-permute-start | bytes 4718600 | tf_op jit(solution)/shard_map/ppermute | solution.py:1479
  306.5 51.5 %collective-permute-start.34 = (bf16[2,4,288,512]{3,2,1,0:T(8,128)(2,1)}, bf16[2,4,288,512]{3,2,1,0:T(8,128)(2,1)S(1)}, u32[]{:S(2)}, u32[]{:S(2)}) collective-permute-start(bf16[2,4,288,512]{3,2,1,0:T(8,128)(2,1)} %get-tuple-element.145.refs_11_), channel_id=1, source_target_pairs={{0,1},{1,0},{2,3},{3,2},{4,5},{5,4},{6,7},{7,6},{8,9},{9,8},{10,11... | collective-permute-start | bytes 7077896 | tf_op jit(solution)/shard_map/ppermute | solution.py:1479
  308.6 50.9 %collective-permute-start.35 = (bf16[2,4,288,512]{3,2,1,0:T(8,128)(2,1)}, bf16[2,4,288,512]{3,2,1,0:T(8,128)(2,1)S(1)}, u32[]{:S(2)}, u32[]{:S(2)}) collective-permute-start(bf16[2,4,288,512]{3,2,1,0:T(8,128)(2,1)} %get-tuple-element.149), channel_id=1, source_target_pairs={{0,2},{1,3},{2,0},{3,1},{4,6},{5,7},{6,4},{7,5},{8,10},{9,11},{10,... | collective-permute-start | bytes 7077896 | tf_op jit(solution)/shard_map/ppermute | solution.py:1479
  309.9 40.5 %collective-permute-start.32 = (bf16[640,1536]{1,0:T(8,128)(2,1)}, bf16[640,1536]{1,0:T(8,128)(2,1)S(1)}, u32[]{:S(2)}, u32[]{:S(2)}) collective-permute-start(bf16[640,1536]{1,0:T(8,128)(2,1)} %get-tuple-element.137.refs_2_), channel_id=1, source_target_pairs={{0,16},{16,0},{1,17},{17,1},{2,18},{18,2},{3,19},{19,3},{4,20},{20... | collective-permute-start | bytes 5898248 | tf_op jit(solution)/shard_map/ppermute | solution.py:1474
  309.9 80.8 %collective-permute-start.38 = (bf16[640,1536]{1,0:T(8,128)(2,1)}, bf16[640,1536]{1,0:T(8,128)(2,1)}, u32[]{:S(2)}, u32[]{:S(2)}) collective-permute-start(bf16[640,1536]{1,0:T(8,128)(2,1)} %get-tuple-element.156), channel_id=1, source_target_pairs={{0,16},{16,0},{1,17},{17,1},{2,18},{18,2},{3,19},{19,3},{4,20},{20... | collective-permute-start | bytes 5898248 | tf_op jit(solution)/shard_map/ppermute | solution.py:1474
  350.3 41.4 %collective-permute-start.39 = (bf16[640,1536]{1,0:T(8,128)(2,1)}, bf16[640,1536]{1,0:T(8,128)(2,1)}, u32[]{:S(2)}, u32[]{:S(2)}) collective-permute-start(bf16[640,1536]{1,0:T(8,128)(2,1)} %get-tuple-element.157), channel_id=1, source_target_pairs={{0,16},{16,0},{1,17},{17,1},{2,18},{18,2},{3,19},{19,3},{4,20},{20... | collective-permute-start | bytes 5898248 | tf_op jit(solution)/shard_map/ppermute | solution.py:1474
  368.3 69.3 %collective-permute-start.33 = (bf16[640,1536]{1,0:T(8,128)(2,1)}, bf16[640,1536]{1,0:T(8,128)(2,1)S(1)}, u32[]{:S(2)}, u32[]{:S(2)}) collective-permute-start(bf16[640,1536]{1,0:T(8,128)(2,1)} %get-tuple-element.147.refs_4_), channel_id=1, source_target_pairs={{0,16},{16,0},{1,17},{17,1},{2,18},{18,2},{3,19},{19,3},{4,20},{20... | collective-permute-start | bytes 5898248 | tf_op jit(solution)/shard_map/ppermute | solution.py:1474
  390.7 70.2 %collective-permute-start.44 = (bf16[2,4,288,512]{3,2,1,0:T(8,128)(2,1)}, bf16[2,4,288,512]{3,2,1,0:T(8,128)(2,1)S(1)}, u32[]{:S(2)}, u32[]{:S(2)}) collective-permute-start(bf16[2,4,288,512]{3,2,1,0:T(8,128)(2,1)} %get-tuple-element.177), channel_id=1, source_target_pairs={{0,1},{1,0},{2,3},{3,2},{4,5},{5,4},{6,7},{7,6},{8,9},{9,8},{10,11... | collective-permute-start | bytes 7077896 | tf_op jit(solution)/shard_map/ppermute | solution.py:1479
  391.7 69.2 %collective-permute-start.45 = (bf16[2,4,288,512]{3,2,1,0:T(8,128)(2,1)}, bf16[2,4,288,512]{3,2,1,0:T(8,128)(2,1)S(1)}, u32[]{:S(2)}, u32[]{:S(2)}) collective-permute-start(bf16[2,4,288,512]{3,2,1,0:T(8,128)(2,1)} %get-tuple-element.178), channel_id=1, source_target_pairs={{0,2},{1,3},{2,0},{3,1},{4,6},{5,7},{6,4},{7,5},{8,10},{9,11},{10,... | collective-permute-start | bytes 7077896 | tf_op jit(solution)/shard_map/ppermute | solution.py:1479
  410.3 34.7 %collective-permute-start.46 = (bf16[640,1024]{1,0:T(8,128)(2,1)}, bf16[640,1024]{1,0:T(8,128)(2,1)}, u32[]{:S(2)}, u32[]{:S(2)}) collective-permute-start(bf16[640,1024]{1,0:T(8,128)(2,1)} %get-tuple-element.179), channel_id=1, source_target_pairs={{0,16},{16,0},{1,17},{17,1},{2,18},{18,2},{3,19},{19,3},{4,20},{20... | collective-permute-start | bytes 3932168 | tf_op jit(solution)/shard_map/ppermute | solution.py:1474
  468.7 35.0 %collective-permute-start.48 = (bf16[4,288,512]{2,1,0:T(8,128)(2,1)}, bf16[4,288,512]{2,1,0:T(8,128)(2,1)S(1)}, u32[]{:S(2)}, u32[]{:S(2)}) collective-permute-start(bf16[4,288,512]{2,1,0:T(8,128)(2,1)} %get-tuple-element.182.refs_4_), channel_id=1, source_target_pairs={{0,1},{1,0},{2,3},{3,2},{4,5},{5,4},{6,7},{7,6},{8,9},{9,8},{10,11... | collective-permute-start | bytes 3538952 | tf_op jit(solution)/shard_map/ppermute | solution.py:1479
  469.7 34.0 %collective-permute-start.49 = (bf16[4,288,512]{2,1,0:T(8,128)(2,1)}, bf16[4,288,512]{2,1,0:T(8,128)(2,1)S(1)}, u32[]{:S(2)}, u32[]{:S(2)}) collective-permute-start(bf16[4,288,512]{2,1,0:T(8,128)(2,1)} %get-tuple-element.193), channel_id=1, source_target_pairs={{0,2},{1,3},{2,0},{3,1},{4,6},{5,7},{6,4},{7,5},{8,10},{9,11},{10,... | collective-permute-start | bytes 3538952 | tf_op jit(solution)/shard_map/ppermute | solution.py:1479
  478.5 34.6 %collective-permute-start.47 = (bf16[2,288,512]{2,1,0:T(8,128)(2,1)}, bf16[2,288,512]{2,1,0:T(8,128)(2,1)S(1)}, u32[]{:S(2)}, u32[]{:S(2)}) collective-permute-start(bf16[2,288,512]{2,1,0:T(8,128)(2,1)} %sum_pass.2.refs_9_), channel_id=1, source_target_pairs={{0,8},{1,9},{2,10},{3,11},{4,12},{5,13},{6,14},{7,15},{8,0},{9,1},... | collective-permute-start | bytes 1769480 | tf_op jit(solution)/shard_map/ppermute | solution.py:1479
  512.6 33.2 %collective-permute-start.55 = (bf16[2,2,368,512]{3,2,1,0:T(8,128)(2,1)}, bf16[2,2,368,512]{3,2,1,0:T(8,128)(2,1)S(1)}, u32[]{:S(2)}, u32[]{:S(2)}) collective-permute-start(bf16[2,2,368,512]{3,2,1,0:T(8,128)(2,1)} %get-tuple-element.206), channel_id=1, source_target_pairs={{0,4},{1,5},{2,6},{3,7},{4,0},{5,1},{6,2},{7,3},{8,12},{9,13},{10,... | collective-permute-start | bytes 4521992 | tf_op jit(solution)/shard_map/ppermute | solution.py:1479
  530.9 35.1 %collective-permute-start.52 = (bf16[640,1536]{1,0:T(8,128)(2,1)S(1)}, bf16[640,1536]{1,0:T(8,128)(2,1)S(1)}, u32[]{:S(2)}, u32[]{:S(2)}) collective-permute-start(bf16[640,1536]{1,0:T(8,128)(2,1)S(1)} %copy-done.64), channel_id=1, source_target_pairs={{0,16},{16,0},{1,17},{17,1},{2,18},{18,2},{3,19},{19,3},{4,20},{20... | collective-permute-start | bytes 5898248 | tf_op jit(solution)/shard_map/ppermute | solution.py:1474
  564.9 47.2 %collective-permute-start.61 = (bf16[2,368,512]{2,1,0:T(8,128)(2,1)S(1)}, bf16[2,368,512]{2,1,0:T(8,128)(2,1)S(1)}, u32[]{:S(2)}, u32[]{:S(2)}) collective-permute-start(bf16[2,368,512]{2,1,0:T(8,128)(2,1)S(1)} %copy-done.33), channel_id=1, source_target_pairs={{0,8},{1,9},{2,10},{3,11},{4,12},{5,13},{6,14},{7,15},{8,0},{9,1},... | collective-permute-start | bytes 2261000 | tf_op jit(solution)/shard_map/ppermute | solution.py:1479
  582.9 34.2 %collective-permute-start.58 = (bf16[2,160,512]{2,1,0:T(8,128)(2,1)}, bf16[2,160,512]{2,1,0:T(8,128)(2,1)S(1)}, u32[]{:S(2)}, u32[]{:S(2)}) collective-permute-start(bf16[2,160,512]{2,1,0:T(8,128)(2,1)} %get-tuple-element.210), channel_id=1, source_target_pairs={{0,4},{1,5},{2,6},{3,7},{4,0},{5,1},{6,2},{7,3},{8,12},{9,13},{10,... | collective-permute-start | bytes 983048 | tf_op jit(solution)/shard_map/ppermute | solution.py:1479
  584.5 34.6 %collective-permute-start.59 = (bf16[2,160,512]{2,1,0:T(8,128)(2,1)}, bf16[2,160,512]{2,1,0:T(8,128)(2,1)S(1)}, u32[]{:S(2)}, u32[]{:S(2)}) collective-permute-start(bf16[2,160,512]{2,1,0:T(8,128)(2,1)} %get-tuple-element.211), channel_id=1, source_target_pairs={{0,8},{1,9},{2,10},{3,11},{4,12},{5,13},{6,14},{7,15},{8,0},{9,1},... | collective-permute-start | bytes 983048 | tf_op jit(solution)/shard_map/ppermute | solution.py:1479
  586.3 32.8 %collective-permute-start.60 = (bf16[2,160,512]{2,1,0:T(8,128)(2,1)}, bf16[2,160,512]{2,1,0:T(8,128)(2,1)S(1)}, u32[]{:S(2)}, u32[]{:S(2)}) collective-permute-start(bf16[2,160,512]{2,1,0:T(8,128)(2,1)} %get-tuple-element.212), channel_id=1, source_target_pairs={{0,12},{1,13},{2,14},{3,15},{4,8},{5,9},{6,10},{7,11},{8,4},{9,5},... | collective-permute-start | bytes 983048 | tf_op jit(solution)/shard_map/ppermute | solution.py:1479
  (102 other events, 811.1 us)

commit v4 on v3

--- a/solution.py
+++ b/solution.py
@@ -352,8 +352,8 @@
 
 
 def merge_kernel(place_ref, late_x, late_y, got_x, got_y, out_x, out_y):
-    out_x[...] = (late_x[...].astype(wide) + got_y[0].astype(wide)).astype(low)
-    out_y[...] = (late_y[...].astype(wide) + got_x[0].astype(wide)).astype(low)
+    out_x[...] = late_x[...] + got_y[0]
+    out_y[...] = late_y[...] + got_x[0]
 
 
 def merge(place, late_x, late_y, got_x, got_y, after):
@@ -1020,7 +1020,8 @@
     core = place_ref[3]
     hidden = middle_ref[...]
     scale = lax.rsqrt(jnp.mean(hidden * hidden, axis=-1, keepdims=True) + epsilon)
-    incoming = mine_0[...] + mine_1[...] + other_0[...].astype(wide) + other_1[...].astype(wide)
+    parts = (mine_0, mine_1, other_0, other_1)
+    incoming = sum(ref[...].astype(wide) for ref in parts)
     weighted = incoming * gain_ref[8:9, :]
     inner = jnp.mean(weighted * hidden, axis=-1, keepdims=True)
     grad = cotangent_ref[...].astype(wide) + (scale * weighted - hidden * scale**3 * inner)
@@ -1118,17 +1119,15 @@
     )
 
 
-FFN_TILE = 320
+FFN_TILE = 640
 FFN_STEP = 256
 FFN_SPAN = 768
 
 
-def load_tokens(x_ref, c_ref, x_own, x_far, c_own, c_far, sems):
-    count = x_far.shape[0]
-    for index, (ref, far, own) in enumerate(((x_ref, x_far, x_own), (c_ref, c_far, c_own))):
-        for part, source in enumerate((far, own)):
-            target = ref.at[pl.ds(part * count, count)]
-            pltpu.make_async_copy(source, target, sems.at[index]).start()
+def load_tokens(ref, own, far, sem):
+    count = far.shape[0]
+    for part, source in enumerate((far, own)):
+        pltpu.make_async_copy(source, ref.at[pl.ds(part * count, count)], sem).start()
 
 
 def ffn_forward(step, tiles, x_ref, c_ref, weights, sums, middles, at_rows):
@@ -1167,7 +1166,9 @@
                 normed_ref[:, at] = normed.astype(normed_ref.dtype)
 
 
-def ffn_backward(place_ref, k, x_ref, c_ref, middles, stages, turned, turned_units, sent, sems):
+def ffn_backward(
+    place_ref, k, x_ref, c_ref, middles, stages, turned, turned_units, sent, sems, wait
+):
     inner, grad_gate, grad_up = middles
     stage_gate, stage_up, stage_down = stages
     width, units = x_ref.shape[1], inner.shape[1]
@@ -1175,11 +1176,14 @@
     rows, span = width // 4, units // 4
     here = pl.ds(pl.multiple_of(depth * rows, LANES), rows)
     there = pl.ds(pl.multiple_of(depth * span, LANES), span)
+    wait(x_ref, grad_gate)
     turned[...] = x_ref[:, here].T
     to = pl.ds(pl.multiple_of(k * rows, 16), rows)
     to_units = pl.ds(pl.multiple_of(k * span, 16), span)
     stage_gate[to, :] = project(turned[...], grad_gate[...]).astype(low)
+    wait(grad_up)
     stage_up[to, :] = project(turned[...], grad_up[...]).astype(low)
+    wait(inner, c_ref)
     turned_units[...] = inner[:, there].T
 
     @pl.loop(0, width // FFN_SPAN)
@@ -1198,7 +1202,9 @@
 
     @pl.when(step == 0)
     def _():
-        load_tokens(x_ref, c_ref, *tokens, x_sems)
+        x_own, x_far, c_own, c_far = tokens
+        load_tokens(x_ref, x_own, x_far, x_sems.at[0])
+        load_tokens(c_ref, c_own, c_far, x_sems.at[1])
         if len(pieces) == 5:
             fetch(place_ref, from_pieces(pieces, FFN_HALF), FFN_PLAN, weights, in_sems)
         else:
@@ -1218,16 +1224,31 @@
     turned, turned_units, x_sems, in_sems, out_sems = rest
     k = pl.program_id(0)
 
+    x_own, x_far, c_own, c_far = tokens
+
+    def middle(index):
+        pltpu.make_async_copy(sources[index], middles[index], in_sems.at[index]).start()
+
     @pl.when(k == 0)
     def _():
-        load_tokens(x_ref, c_ref, *tokens, x_sems)
-        for index in (1, 2, 0):
-            pltpu.make_async_copy(sources[index], middles[index], in_sems.at[index]).start()
-        drain((x_ref, c_ref), x_sems)
-        drain(middles, in_sems)
+        load_tokens(x_ref, x_own, x_far, x_sems.at[0])
+        middle(1)
+        middle(2)
+        middle(0)
+        load_tokens(c_ref, c_own, c_far, x_sems.at[1])
+
+    arrived = [(x_ref, x_sems.at[0]), (c_ref, x_sems.at[1])]
+    arrived += [(ref, in_sems.at[index]) for index, ref in enumerate(middles)]
+
+    def wait(*refs):
+        @pl.when(k == 0)
+        def _():
+            for ref, sem in arrived:
+                if any(ref is other for other in refs):
+                    pltpu.make_async_copy(ref, ref, sem).wait()
 
     ffn_backward(
-        place_ref, k, x_ref, c_ref, middles, stages, turned, turned_units, sent, out_sems
+        place_ref, k, x_ref, c_ref, middles, stages, turned, turned_units, sent, out_sems, wait
     )
 
     @pl.when(k == 3)
@@ -1244,8 +1265,7 @@
     late = pl.BlockSpec(
         (FFN_TILE, width), lambda i, place: (jnp.clip(i - last - 1, 0, last), 0)
     )
-    pairs = ((low, early), (low, early), (wide, late), (wide, late))
-    return [(shaped((count, width), kind), spec) for kind, spec in pairs]
+    return [(shaped((count, width), low), spec) for spec in (early, early, late, late)]
 
 
 def ffn_scratch(count, width, weights=True, middles=True, stages=True):
@@ -1332,7 +1352,7 @@
     def _():
         grad_ref[...] = squeezed(own_q, own_k, own_v)
         incoming = across(grad_ref[...], w_ref[...])
-        own_ref[...] = incoming
+        own_ref[...] = incoming.astype(low)
         rest(x_own, incoming)
 
 
@@ -1361,7 +1381,7 @@
         + [(x_own, late(width)), (x_far, early(width)), (weight, whole(weight))],
         [
             (shaped((count, width), low), both(width)),
-            (shaped((count // 2, width), wide), late(width)),
+            (shaped((count // 2, width), low), late(width)),
             (shaped((count // 2, width), low), early(width)),
             (gain_grad, whole(gain_grad)),
         ],
@@ -1371,7 +1391,7 @@
 
 
 def qkv_grad_kernel(place_ref, x_ref, grad_ref, gain_one, gain_two, *refs):
-    outs, (stage, gain_rows, turned, sems) = refs[:5], refs[5:]
+    outs, (stage, gain_rows, sems) = refs[:5], refs[5:]
     k = pl.program_id(0)
     width = grad_ref.shape[1]
 
@@ -1390,14 +1410,8 @@
 
     depth = place_ref[0] ^ k
     rows = width // 4
-    turned[...] = x_ref[:, pl.ds(pl.multiple_of(depth * rows, LANES), rows)].T
     to = pl.ds(pl.multiple_of(depth * rows, 16), rows)
-
-    @pl.loop(0, width // SLAB)
-    def _(index):
-        at = pl.ds(pl.multiple_of(index * SLAB, SLAB), SLAB)
-        stage[to, at] = project(turned[...], grad_ref[:, at]).astype(low)
-
+    stage[to, :] = project(x_ref[...].T, grad_ref[...]).astype(low)
     send_off(place_ref, k, (stage, gain_rows), depth * 4, QKV_PLAN, QKV_HALF, outs, sems)
 
     @pl.when(k == 3)
@@ -1408,18 +1422,17 @@
 
 def qkv_grad(place, x, grad, gain_one, gain_two, after=()):
     count, width = x.shape
-    operands = (x, grad, gain_one, gain_two)
+    column = pl.BlockSpec((count, width // 4), lambda k, place: (0, place[0] ^ k))
     return run(
         qkv_grad_kernel,
         "qkv_grad",
         place,
         (4,),
-        [(item, whole(item)) for item in operands],
+        [(x, column)] + [(item, whole(item)) for item in (grad, gain_one, gain_two)],
         sent_shapes(QKV_HALF, SLAB),
         [
             pltpu.VMEM((width, width), low),
             pltpu.VMEM((BLOCKS * 16, SLAB), low),
-            pltpu.VMEM((width // 4, count), low),
             pltpu.SemaphoreType.DMA((5,)),
         ],
         after,
@@ -1430,7 +1443,8 @@
 def tokens_grad_kernel(place_ref, x_ref, middle_ref, mine_ref, other_ref, gain_ref, out_ref):
     hidden = x_ref[...].astype(wide)
     scale = lax.rsqrt(jnp.mean(hidden * hidden, axis=-1, keepdims=True) + epsilon)
-    weighted = (mine_ref[...] + other_ref[...].astype(wide)) * gain_ref[0:1, :]
+    incoming = mine_ref[...].astype(wide) + other_ref[...].astype(wide)
+    weighted = incoming * gain_ref[0:1, :]
     inner = jnp.mean(weighted * hidden, axis=-1, keepdims=True)
     out_ref[...] = middle_ref[...] + (scale * weighted - hidden * scale**3 * inner)
 
@@ -1451,8 +1465,8 @@
 
 
 def output_kernel(place_ref, middle_ref, mine_0, mine_1, other_0, other_1, out_ref):
-    total = middle_ref[...] + mine_0[...] + mine_1[...]
-    total = total + other_0[...].astype(wide) + other_1[...].astype(wide)
+    parts = (mine_0, mine_1, other_0, other_1)
+    total = middle_ref[...] + sum(ref[...].astype(wide) for ref in parts)
     out_ref[...] = total.astype(low)
 
 
@@ -1703,27 +1717,26 @@
     )
     got_out = routes.scatter_1(sent_out)
     kept_0, parts_0 = routes.scatter_3([(sent_0, got_0, more_0)], (sent_out[4],))
+    token, more_1 = routes.scatter_2(sent_1, got_1, (kept_0,))
     far_grads = attend_back(
-        place, *attended, heads_far, far_mine, far_total, *tables, 1, (kept_0, out_far_1)
-    )
-    token, more_1 = routes.scatter_2(sent_1, got_1, (far_grads[0], *routes.pins(got_out)))
-    token, more_out = routes.scatter_2(sent_out, got_out, (token,))
+        place, *attended, heads_far, far_mine, far_total, *tables, 1, (token, out_far_1)
+    )
+    token, more_out = routes.scatter_2(sent_out, got_out, (far_grads[0],))
     token, parts_0 = routes.scatter_4(kept_0, parts_0, (token,))
     grad_qkv, own_part, far_part, attn_gain_grad = input_back(
         place, own_grads, far_grads, tokens, far_tokens, w_qkv, (token,)
     )
     own_rest = swap(far_part)
+    sent_qkv = qkv_grad(place, normed_low, grad_qkv, attn_gain_grad, ffn_gain_grad)
+    got_qkv = routes.scatter_1(sent_qkv)
     groups = [(sent_1, got_1, more_1), (sent_out, got_out, more_out)]
-    kept_1, parts_1 = routes.scatter_3(groups, (grad_qkv,))
-    pins = (kept_1, *routes.pins(parts_0[1:]))
-    sent_qkv = qkv_grad(place, normed_low, grad_qkv, attn_gain_grad, ffn_gain_grad, pins)
-    got_qkv = routes.scatter_1(sent_qkv)
-
-    owned_0 = routes.scatter_5(kept_0, parts_0, (sent_qkv[4],))
+    kept_1, parts_1 = routes.scatter_3(groups, (sent_qkv[4], *routes.pins(parts_0[1:])))
+
+    owned_0 = routes.scatter_5(kept_0, parts_0, (kept_1,))
     outs = (sums_0[2], sums_1[2], out_far_0, out_far_1)
     output = output_of(place, middle, outs, (owned_0[0],))
-    token, parts_1 = routes.scatter_4(kept_1, parts_1, (output,))
-    token, more_qkv = routes.scatter_2(sent_qkv, got_qkv, (token,))
+    token, more_qkv = routes.scatter_2(sent_qkv, got_qkv, (output,))
+    token, parts_1 = routes.scatter_4(kept_1, parts_1, (token,))
     grad_tokens = tokens_grad(place, tokens, grad_middle, own_part, own_rest, gains, (token,))
     kept_qkv, parts_qkv = routes.scatter_34(sent_qkv, got_qkv, more_qkv, (grad_tokens,))
     owned_1 = routes.scatter_5(kept_1, parts_1, (kept_qkv,))

time: 648 us -> 640 us (0.988)
  Pallas kernels: 396 us -> 385 us
    pallas_call x46, Pallas kernels: 395 us -> 385 us  [run(): pl.pallas_call(body, grid_spec=pltpu.PrefetchScalarGridSpec(num_scalar_pr...]
    unnamed x140 -> x130, local copies, waits for them, and re-layouts: 37.9 us -> 35.1 us
  transfers between devices with their start and end apart: 65 -> 65, of which waited for: 26 -> 25; matrix products, arithmetic and copies ran while one was open for 1% -> 1% of each run, Pallas kernels for 59% -> 59%
where the time goes in v4:
time: 640 us; the launch traced here: 628 us
  Pallas kernels  385 us (60%)
  waiting for transfers between devices  135 us (21%)
  starting transfers between devices  63.1 us (10%)
  local copies, waits for them, and re-layouts  36.3 us (6%)
  other arithmetic  6.66 us (1%)
    pallas_call x46, Pallas kernels, run(): pl.pallas_call(body, grid_spec=pltpu.PrefetchScalarGridSpec(num_scalar_pr...  385 us
    ppermute x47, waiting for transfers between devices, hop(): lax.ppermute(array, 'fsdp', [(chip, chip ^ flip) for chip in range(BLOCKS)])  133 us
    ppermute x47, starting transfers between devices, hop(): lax.ppermute(array, 'fsdp', [(chip, chip ^ flip) for chip in range(BLOCKS)])  60 us
    unnamed x130, local copies, waits for them, and re-layouts  35.1 us
  transfers between devices with their start and end apart: 65, of which 25 were waited for; matrix products, arithmetic and copies ran while one was open for 1% of the time, Pallas kernels for 59%

profile of v4, /device:TPU:0, one launch (start us, length us, event | category | flops | bytes accessed | tf_op | source)
XLA Modules:
  0.0 628.2 jit_solution(16233632886377511267)
XLA Ops:
  24.6 4.7 collective-permute-done.2.refs_1_
  49.1 5.9 collective-permute-done.5.refs_1_
  66.0 25.1 %collective-permute-done.11.refs_1_ = bf16[576,512]{1,0:T(8,128)(2,1)S(1)} collective-permute-done((bf16[576,512]{1,0:T(8,128)(2,1)S(1)}, bf16[576,512]{1,0:T(8,128)(2,1)S(1)}, u32[]{:S(2)}, u32[]{:S(2)}) %collective-permute-start.11) | collective-permute-done | bytes 589856 | tf_op jit(solution)/shard_map/ppermute | solution.py:1493
  95.5 5.4 collective-permute-done.10.refs_1_.refs_2_.refs_6_
  109.3 12.7 %collective-permute-done.14.refs_1_ = bf16[2,576,512]{2,1,0:T(8,128)(2,1)S(1)} collective-permute-done((bf16[2,576,512]{2,1,0:T(8,128)(2,1)}, bf16[2,576,512]{2,1,0:T(8,128)(2,1)S(1)}, u32[]{:S(2)}, u32[]{:S(2)}) %collective-permute-start.14) | collective-permute-done | bytes 1179680 | tf_op jit(solution)/shard_map/ppermute | solution.py:1493
  140.8 19.1 %project_qkv.1 = (bf16[1280,1536]{1,0:T(8,128)(2,1)}, bf16[1280,1024]{1,0:T(8,128)(2,1)}, bf16[1280,512]{1,0:T(8,128)(2,1)}, bf16[1280,512]{1,0:T(8,128)(2,1)}, ...) custom-call(s32[4]{0:T(128)} %pad_add_fusion.1.place_ref, bf16[640,1536]{1,0:T(8,128)(2,1)} %refs_0_.11, ...), custom_call_target="tpu_custom_call" | custom-call | bytes 59400 | tf_op jit(solution)/shard_map/project_qkv/pallas_call | solution.py:52
  159.8 12.2 %attend.2 = (bf16[640,1024]{1,0:T(8,128)(2,1)}, f32[640,128]{1,0:T(8,128)}) custom-call(s32[4]{0:T(128)} %pad_add_fusion.1.place_ref, bf16[1280,1024]{1,0:T(8,128)(2,1)} %get-tuple-element.124.refs_0_, bf16[1280,512]{1,0:T(8,128)(2,1)} %get-tuple-element.125.refs_1_.refs_5_, bf16[1280,512]{1,0:T(8,128)(2,1)} %get-tuple-element.126.refs_2_, ...), custom_call_target="tpu_custom_call" | custom-call | bytes 56100 | tf_op jit(solution)/shard_map/attend/pallas_call | solution.py:52
  173.7 12.0 %attend.3 = (bf16[640,1024]{1,0:T(8,128)(2,1)}, f32[640,128]{1,0:T(8,128)}) custom-call(s32[4]{0:T(128)} %pad_add_fusion.1.place_ref, bf16[1280,1024]{1,0:T(8,128)(2,1)} %get-tuple-element.124.refs_0_, bf16[1280,512]{1,0:T(8,128)(2,1)} %get-tuple-element.125.refs_1_.refs_5_, bf16[1280,512]{1,0:T(8,128)(2,1)} %get-tuple-element.126.refs_2_, ...), custom_call_target="tpu_custom_call" | custom-call | bytes 56100 | tf_op jit(solution)/shard_map/attend/pallas_call | solution.py:52
  204.4 10.9 %middle.1 = (f32[640,1536]{1,0:T(8,128)}, bf16[640,1536]{1,0:T(8,128)(2,1)}) custom-call(s32[4]{0:T(128)} %pad_add_fusion.1.place_ref, bf16[640,1536]{1,0:T(8,128)(2,1)} %refs_0_.11, bf16[640,1024]{1,0:T(8,128)(2,1)} %get-tuple-element.129.refs_2_.refs_1_.refs_4_.refs_0_, bf16[640,1024]{1,0:T(8,128)(2,1)} %copy-done.20, ...), custom_call_target="tpu_custom_call" | custom-call | bytes 36300 | tf_op jit(solution)/shard_map/middle/pallas_call | solution.py:52
  215.3 6.8 %collective-permute-done.25.refs_1_ = bf16[2,384,512]{2,1,0:T(8,128)(2,1)S(1)} collective-permute-done((bf16[2,384,512]{2,1,0:T(8,128)(2,1)}, bf16[2,384,512]{2,1,0:T(8,128)(2,1)S(1)}, u32[]{:S(2)}, u32[]{:S(2)}) %collective-permute-start.25) | collective-permute-done | bytes 786464 | tf_op jit(solution)/shard_map/ppermute | solution.py:1493
  236.2 38.5 %ffn_forward.2 = (bf16[640,1536]{1,0:T(8,128)(2,1)}, bf16[640,1536]{1,0:T(8,128)(2,1)}, bf16[640,1536]{1,0:T(8,128)(2,1)}, bf16[640,1536]{1,0:T(8,128)(2,1)}, bf...) custom-call(s32[4]{0:T(128)} %pad_add_fusion.1.place_ref, ...), custom_call_target="tpu_custom_call" | custom-call | bytes 118800 | tf_op jit(solution)/shard_map/ffn_forward/pallas_call | solution.py:52
  280.5 21.4 %ffn_backward.2 = (bf16[2,4,288,512]{3,2,1,0:T(8,128)(2,1)}, bf16[2,4,288,512]{3,2,1,0:T(8,128)(2,1)}, bf16[4,288,512]{2,1,0:T(8,128)(2,1)}, bf16[4,288,512]{2,1,0:T(8,128)(2,1)}, bf16[4,2,288,512]{3,2,1,0:T(8,128)(2,1)}) custom-call(s32[4]{0:T(128)} %pad_add_fusion.1.place_ref, bf16[640,1536]{1,0:T(8,128)(2,1)} %get-tuple-element.134.refs_2_.refs_0_, ...), custom_call_target="tpu_custom_call" | custom-call | bytes 72600 | tf_op jit(solution)/shard_map/ffn_backward/pallas_call | solution.py:52
  308.1 38.3 %ffn_forward.3 = (bf16[640,1536]{1,0:T(8,128)(2,1)}, bf16[640,1536]{1,0:T(8,128)(2,1)}, bf16[640,1536]{1,0:T(8,128)(2,1)}, bf16[640,1536]{1,0:T(8,128)(2,1)}, bf...) custom-call(s32[4]{0:T(128)} %pad_add_fusion.1.place_ref, ...), custom_call_target="tpu_custom_call" | custom-call | bytes 118800 | tf_op jit(solution)/shard_map/ffn_forward/pallas_call | solution.py:52
  346.5 9.2 %collective-permute-done.34.refs_2_.refs_1_ = bf16[2,4,288,512]{3,2,1,0:T(8,128)(2,1)S(1)} collective-permute-done((bf16[2,4,288,512]{3,2,1,0:T(8,128)(2,1)}, bf16[2,4,288,512]{3,2,1,0:T(8,128)(2,1)S(1)}, u32[]{:S(2)}, u32[]{:S(2)}) %collective-permute-start.34) | collective-permute-done | bytes 2359328 | tf_op jit(solution)/shard_map/ppermute | solution.py:1493
  358.5 5.1 merge.4
  365.6 21.7 %ffn_backward.3 = (bf16[2,4,288,512]{3,2,1,0:T(8,128)(2,1)}, bf16[2,4,288,512]{3,2,1,0:T(8,128)(2,1)}, bf16[4,288,512]{2,1,0:T(8,128)(2,1)}, bf16[4,288,512]{2,1,0:T(8,128)(2,1)}, bf16[4,2,288,512]{3,2,1,0:T(8,128)(2,1)}) custom-call(s32[4]{0:T(128)} %pad_add_fusion.1.place_ref, bf16[640,1536]{1,0:T(8,128)(2,1)} %get-tuple-element.134.refs_2_.refs_0_, ...), custom_call_target="tpu_custom_call" | custom-call | bytes 72600 | tf_op jit(solution)/shard_map/ffn_backward/pallas_call | solution.py:52
  391.7 15.9 %middle_back.1 = (f32[640,1536]{1,0:T(8,128)}, bf16[640,768]{1,0:T(8,128)(2,1)}, bf16[640,768]{1,0:T(8,128)(2,1)}, bf16[640,1024]{1,0:T(8,128)(2,1)}, bf16[640,1024]{1,0:T(8,128)(2,1)}, /*index=5*/f32[8,1536]{1,0:T(8,128)}) custom-call(s32[4]{0:T(128)} %pad_add_fusion.1.place_ref, f32[640,1536]{1,0:T(8,128)} %get-tuple-element.133.refs_0_, ...), custom_call_target="tpu_custom_call" | custom-call | bytes 49500 | tf_op jit(solution)/shard_map/middle_back/pallas_call | solution.py:52
  408.2 14.5 %attend_back.2 = (bf16[640,1024]{1,0:T(8,128)(2,1)}, bf16[640,512]{1,0:T(8,128)(2,1)}, bf16[640,512]{1,0:T(8,128)(2,1)}) custom-call(s32[4]{0:T(128)} %pad_add_fusion.1.place_ref, bf16[1280,1024]{1,0:T(8,128)(2,1)} %get-tuple-element.124.refs_0_, bf16[1280,512]{1,0:T(8,128)(2,1)} %get-tuple-element.125.refs_1_.refs_5_, ...), custom_call_target="tpu_custom_call" | custom-call | bytes 69300 | tf_op jit(solution)/shard_map/attend_back/pallas_call | solution.py:52
  423.6 10.3 %out_grad.1 = (bf16[2,4,80,512]{3,2,1,0:T(8,128)(2,1)}, bf16[2,4,80,512]{3,2,1,0:T(8,128)(2,1)}, bf16[4,80,512]{2,1,0:T(8,128)(2,1)}, bf16[4,80,512]{2,1,0:T(8,128)(2,1)}, bf16[4,2,80,512]{3,2,1,0:T(8,128)(2,1)}) custom-call(s32[4]{0:T(128)} %pad_add_fusion.1.place_ref, bf16[640,1024]{1,0:T(8,128)(2,1)} %get-tuple-element.129.refs_2_.refs_1_.refs_4_.refs_0_, ...), custom_call_target="tpu_custom_call" | custom-call | bytes 33000 | tf_op jit(solution)/shard_map/out_grad/pallas_call | solution.py:52
  433.9 6.5 %sum_plane.3 = (f32[2,288,512]{2,1,0:T(8,128)}, f32[2,288,512]{2,1,0:T(8,128)}, bf16[2,2,288,512]{3,2,1,0:T(8,128)(2,1)}) custom-call(s32[4]{0:T(128)} %pad_add_fusion.1.place_ref, bf16[4,2,288,512]{3,2,1,0:T(8,128)(2,1)} %get-tuple-element.148.refs_0_, bf16[2,4,288,512]{3,2,1,0:T(8,128)(2,1)} %copy-done.7, bf16[2,4,288,512]{3,2,1,0:T(8,128)(2,1)} %copy-done.8, ...), custom_call_target="tpu_custom_call" | custom-call | bytes 16500 | tf_op jit(solution)/shard_map/sum_plane/pallas_call | solution.py:52
  444.5 5.1 merge.5
  451.1 14.1 %attend_back.3 = (bf16[640,1024]{1,0:T(8,128)(2,1)}, bf16[640,512]{1,0:T(8,128)(2,1)}, bf16[640,512]{1,0:T(8,128)(2,1)}) custom-call(s32[4]{0:T(128)} %pad_add_fusion.1.place_ref, bf16[1280,1024]{1,0:T(8,128)(2,1)} %get-tuple-element.124.refs_0_, bf16[1280,512]{1,0:T(8,128)(2,1)} %get-tuple-element.125.refs_1_.refs_5_, ...), custom_call_target="tpu_custom_call" | custom-call | bytes 69300 | tf_op jit(solution)/shard_map/attend_back/pallas_call | solution.py:52
  475.9 14.2 %input_back.1 = (bf16[1280,1536]{1,0:T(8,128)(2,1)}, bf16[640,1536]{1,0:T(8,128)(2,1)}, bf16[640,1536]{1,0:T(8,128)(2,1)}, f32[8,1536]{1,0:T(8,128)}) custom-call(s32[4]{0:T(128)} %pad_add_fusion.1.place_ref, bf16[640,1024]{1,0:T(8,128)(2,1)} %get-tuple-element.166.refs_6_.refs_0_, bf16[640,512]{1,0:T(8,128)(2,1)} %get-tuple-element.187.refs_1_, ...), custom_call_target="tpu_custom_call" | custom-call | bytes 49500 | tf_op jit(solution)/shard_map/input_back/pallas_call | solution.py:52
  490.2 11.6 %qkv_grad.1 = (bf16[2,4,160,512]{3,2,1,0:T(8,128)(2,1)}, bf16[2,4,160,512]{3,2,1,0:T(8,128)(2,1)}, bf16[4,160,512]{2,1,0:T(8,128)(2,1)}, bf16[4,160,512]{2,1,0:T(8,128)(2,1)}, bf16[4,2,160,512]{3,2,1,0:T(8,128)(2,1)}) custom-call(s32[4]{0:T(128)} %pad_add_fusion.1.place_ref, bf16[1280,1536]{1,0:T(8,128)(2,1)} %get-tuple-element.186.refs_0_, ...), custom_call_target="tpu_custom_call" | custom-call | bytes 49500 | tf_op jit(solution)/shard_map/qkv_grad/pallas_call | solution.py:52
  505.5 7.3 %sum_plane.4 = (f32[2,368,512]{2,1,0:T(8,128)}, f32[2,368,512]{2,1,0:T(8,128)}, bf16[2,2,368,512]{3,2,1,0:T(8,128)(2,1)}) custom-call(s32[4]{0:T(128)} %pad_add_fusion.1.place_ref, bf16[4,2,288,512]{3,2,1,0:T(8,128)(2,1)} %get-tuple-element.161.refs_11_.refs_0_, bf16[2,4,288,512]{3,2,1,0:T(8,128)(2,1)} %copy-done.9, bf16[2,4,288,512]{3,2,1,0:T(8,128)(2,1)} %copy-done.10, ...), custom_call_target="tpu_custom_call" | custom-call | bytes 16500 | tf_op jit(solution)/shard_map/sum_plane/pallas_call | solution.py:52
  517.9 7.7 %output.1.refs_4_ = bf16[640,1536]{1,0:T(8,128)(2,1)} custom-call(s32[4]{0:T(128)} %pad_add_fusion.1.place_ref, f32[640,1536]{1,0:T(8,128)} %get-tuple-element.133.refs_0_, bf16[640,1536]{1,0:T(8,128)(2,1)} %get-tuple-element.136.refs_1_, bf16[640,1536]{1,0:T(8,128)(2,1)} %get-tuple-element.146.refs_2_, bf16[640,1536]{1,0:T(8,128)(2,1)} %copy-done.12, ...), custom_call_target="tpu_custom_call" | custom-call | bytes 13200 | tf_op jit(solution)/shard_map/output/pallas_call | solution.py:52
  525.6 5.7 collective-permute-done.54.refs_2_.refs_1_
  539.0 9.1 %collective-permute-done.53.refs_1_ = bf16[2,2,368,512]{3,2,1,0:T(8,128)(2,1)S(1)} collective-permute-done((bf16[2,2,368,512]{3,2,1,0:T(8,128)(2,1)}, bf16[2,2,368,512]{3,2,1,0:T(8,128)(2,1)S(1)}, u32[]{:S(2)}, u32[]{:S(2)}) %collective-permute-start.53) | collective-permute-done | bytes 1507360 | tf_op jit(solution)/shard_map/ppermute | solution.py:1493
  555.9 8.6 %tokens_grad.1.refs_5_ = f32[640,1536]{1,0:T(8,128)} custom-call(s32[4]{0:T(128)} %pad_add_fusion.1.place_ref, bf16[640,1536]{1,0:T(8,128)(2,1)} %refs_0_.11, f32[640,1536]{1,0:T(8,128)} %get-tuple-element.198.refs_1_, bf16[640,1536]{1,0:T(8,128)(2,1)} %get-tuple-element.199.refs_2_, bf16[640,1536]{1,0:T(8,128)(2,1)} %copy-done.32, ...), custom_call_target="tpu_custom_call" | custom-call | bytes 13200 | tf_op jit(solution)/shard_map/tokens_grad/pallas_call | solution.py:52
  566.1 4.9 sum_plane.5
  575.4 27.0 %collective-permute-done.61.refs_2_ = bf16[2,368,512]{2,1,0:T(8,128)(2,1)S(1)} collective-permute-done((bf16[2,368,512]{2,1,0:T(8,128)(2,1)}, bf16[2,368,512]{2,1,0:T(8,128)(2,1)S(1)}, u32[]{:S(2)}, u32[]{:S(2)}) %collective-permute-start.61) | collective-permute-done | bytes 753696 | tf_op jit(solution)/shard_map/ppermute | solution.py:1493
  618.6 5.6 unpack_ffn.1
  (292 shorter events, 209.7 us)
Async XLA Ops:
  0.6 54.3 %collective-permute-start.6 = (bf16[640,1536]{1,0:T(8,128)(2,1)}, bf16[640,1536]{1,0:T(8,128)(2,1)S(1)}, u32[]{:S(2)}, u32[]{:S(2)}) collective-permute-start(bf16[640,1536]{1,0:T(8,128)(2,1)} %refs_5_.1), channel_id=1, source_target_pairs={{0,16},{16,0},{1,17},{17,1},{2,18},{18,2},{3,19},{19,3},{4,20},{20... | collective-permute-start | bytes 5898248 | tf_op jit(solution)/shard_map/ppermute | solution.py:1488
  1.2 53.8 %collective-permute-start = (bf16[640,1536]{1,0:T(8,128)(2,1)}, bf16[640,1536]{1,0:T(8,128)(2,1)}, u32[]{:S(2)}, u32[]{:S(2)}) collective-permute-start(bf16[640,1536]{1,0:T(8,128)(2,1)} %refs_0_.11), channel_id=1, source_target_pairs={{0,16},{16,0},{1,17},{17,1},{2,18},{18,2},{3,19},{19,3},{4,20},{20... | collective-permute-start | bytes 5898248 | tf_op jit(solution)/shard_map/ppermute | solution.py:1488
  60.0 40.8 %collective-permute-start.10 = (bf16[4,448,512]{2,1,0:T(8,128)(2,1)}, bf16[4,448,512]{2,1,0:T(8,128)(2,1)S(1)}, u32[]{:S(2)}, u32[]{:S(2)}) collective-permute-start(bf16[4,448,512]{2,1,0:T(8,128)(2,1)} %line.3.refs_2_.refs_0_.refs_4_), channel_id=1, source_target_pairs={{0,2},{1,3},{2,0},{3,1},{4,6},{5,7},{6,4},{7,5},{8,10},{9,11},{10,... | collective-permute-start | bytes 5505032 | tf_op jit(solution)/shard_map/ppermute | solution.py:1493
  61.4 40.2 %collective-permute-start.9 = (bf16[4,448,512]{2,1,0:T(8,128)(2,1)}, bf16[4,448,512]{2,1,0:T(8,128)(2,1)S(1)}, u32[]{:S(2)}, u32[]{:S(2)}) collective-permute-start(bf16[4,448,512]{2,1,0:T(8,128)(2,1)} %line.3.refs_2_.refs_0_.refs_4_), channel_id=1, source_target_pairs={{0,1},{1,0},{2,3},{3,2},{4,5},{5,4},{6,7},{7,6},{8,9},{9,8},{10,11... | collective-permute-start | bytes 5505032 | tf_op jit(solution)/shard_map/ppermute | solution.py:1493
  126.7 66.3 %collective-permute-start.19 = (bf16[4,576,512]{2,1,0:T(8,128)(2,1)}, bf16[4,576,512]{2,1,0:T(8,128)(2,1)}, u32[]{:S(2)}, u32[]{:S(2)}) collective-permute-start(bf16[4,576,512]{2,1,0:T(8,128)(2,1)} %line.4.refs_5_.refs_4_), channel_id=1, source_target_pairs={{0,1},{1,0},{2,3},{3,2},{4,5},{5,4},{6,7},{7,6},{8,9},{9,8},{10,11... | collective-permute-start | bytes 7077896 | tf_op jit(solution)/shard_map/ppermute | solution.py:1493
  127.3 65.7 %collective-permute-start.20 = (bf16[4,576,512]{2,1,0:T(8,128)(2,1)}, bf16[4,576,512]{2,1,0:T(8,128)(2,1)}, u32[]{:S(2)}, u32[]{:S(2)}) collective-permute-start(bf16[4,576,512]{2,1,0:T(8,128)(2,1)} %line.4.refs_5_.refs_4_), channel_id=1, source_target_pairs={{0,2},{1,3},{2,0},{3,1},{4,6},{5,7},{6,4},{7,5},{8,10},{9,11},{10,... | collective-permute-start | bytes 7077896 | tf_op jit(solution)/shard_map/ppermute | solution.py:1493
  133.9 38.2 %collective-permute-start.15 = (bf16[1024,768]{1,0:T(8,128)(2,1)}, bf16[1024,768]{1,0:T(8,128)(2,1)S(1)}, u32[]{:S(2)}, u32[]{:S(2)}) collective-permute-start(bf16[1024,768]{1,0:T(8,128)(2,1)} %get-tuple-element.123.refs_9_.refs_3_.refs_7_), channel_id=1, source_target_pairs={{0,16},{16,0},{1,17},{17,1},{2,18},{18,2},{3,19},{19,3},{4,20},{20... | collective-permute-start | bytes 4718600 | tf_op jit(solution)/shard_map/ppermute | solution.py:1488
  133.9 38.2 %collective-permute-start.16 = (bf16[1024,768]{1,0:T(8,128)(2,1)}, bf16[1024,768]{1,0:T(8,128)(2,1)S(1)}, u32[]{:S(2)}, u32[]{:S(2)}) collective-permute-start(bf16[1024,768]{1,0:T(8,128)(2,1)} %get-tuple-element.128.refs_4_.refs_8_), channel_id=1, source_target_pairs={{0,16},{16,0},{1,17},{17,1},{2,18},{18,2},{3,19},{19,3},{4,20},{20... | collective-permute-start | bytes 4718600 | tf_op jit(solution)/shard_map/ppermute | solution.py:1488
  134.4 51.3 %collective-permute-start.21 = (bf16[4,192,512]{2,1,0:T(8,128)(2,1)}, bf16[4,192,512]{2,1,0:T(8,128)(2,1)}, u32[]{:S(2)}, u32[]{:S(2)}) collective-permute-start(bf16[4,192,512]{2,1,0:T(8,128)(2,1)} %plane.1.refs_7_.refs_0_), channel_id=1, source_target_pairs={{0,8},{1,9},{2,10},{3,11},{4,12},{5,13},{6,14},{7,15},{8,0},{9,1},... | collective-permute-start | bytes 2359304 | tf_op jit(solution)/shard_map/ppermute | solution.py:1493
  172.1 31.2 %collective-permute-start.17 = (bf16[640,1024]{1,0:T(8,128)(2,1)}, bf16[640,1024]{1,0:T(8,128)(2,1)S(1)}, u32[]{:S(2)}, u32[]{:S(2)}) collective-permute-start(bf16[640,1024]{1,0:T(8,128)(2,1)} %get-tuple-element.127.refs_5_.refs_2_.refs_4_), channel_id=1, source_target_pairs={{0,16},{16,0},{1,17},{17,1},{2,18},{18,2},{3,19},{19,3},{4,20},{20... | collective-permute-start | bytes 3932168 | tf_op jit(solution)/shard_map/ppermute | solution.py:1488
  185.8 40.5 %collective-permute-start.26 = (bf16[640,1024]{1,0:T(8,128)(2,1)}, bf16[640,1024]{1,0:T(8,128)(2,1)S(1)}, u32[]{:S(2)}, u32[]{:S(2)}) collective-permute-start(bf16[640,1024]{1,0:T(8,128)(2,1)} %get-tuple-element.129.refs_2_.refs_1_.refs_4_.refs_0_), channel_id=1, source_target_pairs={{0,16},{16,0},{1,17},{17,1},{2,18},{18,2},{3,19},{19,3},{4,20},{20... | collective-permute-start | bytes 3932168 | tf_op jit(solution)/shard_map/ppermute | solution.py:1488
  231.6 43.1 %collective-permute-start.27 = (bf16[4,384,512]{2,1,0:T(8,128)(2,1)}, bf16[4,384,512]{2,1,0:T(8,128)(2,1)S(1)}, u32[]{:S(2)}, u32[]{:S(2)}) collective-permute-start(bf16[4,384,512]{2,1,0:T(8,128)(2,1)} %line.5.refs_9_.refs_4_), channel_id=1, source_target_pairs={{0,1},{1,0},{2,3},{3,2},{4,5},{5,4},{6,7},{7,6},{8,9},{9,8},{10,11... | collective-permute-start | bytes 4718600 | tf_op jit(solution)/shard_map/ppermute | solution.py:1493
  233.5 41.2 %collective-permute-start.28 = (bf16[4,384,512]{2,1,0:T(8,128)(2,1)}, bf16[4,384,512]{2,1,0:T(8,128)(2,1)S(1)}, u32[]{:S(2)}, u32[]{:S(2)}) collective-permute-start(bf16[4,384,512]{2,1,0:T(8,128)(2,1)} %line.5.refs_9_.refs_4_), channel_id=1, source_target_pairs={{0,2},{1,3},{2,0},{3,1},{4,6},{5,7},{6,4},{7,5},{8,10},{9,11},{10,... | collective-permute-start | bytes 4718600 | tf_op jit(solution)/shard_map/ppermute | solution.py:1493
  234.9 67.0 %collective-permute-start.31 = (bf16[2,4,192,512]{3,2,1,0:T(8,128)(2,1)S(1)}, bf16[2,4,192,512]{3,2,1,0:T(8,128)(2,1)S(1)}, u32[]{:S(2)}, u32[]{:S(2)}) collective-permute-start(bf16[2,4,192,512]{3,2,1,0:T(8,128)(2,1)S(1)} %copy-done.4), channel_id=1, source_target_pairs={{0,4},{1,5},{2,6},{3,7},{4,0},{5,1},{6,2},{7,3},{8,12},{9,13},{10,... | collective-permute-start | bytes 4718600 | tf_op jit(solution)/shard_map/ppermute | solution.py:1493
  304.2 51.4 %collective-permute-start.34 = (bf16[2,4,288,512]{3,2,1,0:T(8,128)(2,1)}, bf16[2,4,288,512]{3,2,1,0:T(8,128)(2,1)S(1)}, u32[]{:S(2)}, u32[]{:S(2)}) collective-permute-start(bf16[2,4,288,512]{3,2,1,0:T(8,128)(2,1)} %get-tuple-element.145.refs_11_), channel_id=1, source_target_pairs={{0,1},{1,0},{2,3},{3,2},{4,5},{5,4},{6,7},{7,6},{8,9},{9,8},{10,11... | collective-permute-start | bytes 7077896 | tf_op jit(solution)/shard_map/ppermute | solution.py:1493
  306.2 50.9 %collective-permute-start.35 = (bf16[2,4,288,512]{3,2,1,0:T(8,128)(2,1)}, bf16[2,4,288,512]{3,2,1,0:T(8,128)(2,1)S(1)}, u32[]{:S(2)}, u32[]{:S(2)}) collective-permute-start(bf16[2,4,288,512]{3,2,1,0:T(8,128)(2,1)} %get-tuple-element.149), channel_id=1, source_target_pairs={{0,2},{1,3},{2,0},{3,1},{4,6},{5,7},{6,4},{7,5},{8,10},{9,11},{10,... | collective-permute-start | bytes 7077896 | tf_op jit(solution)/shard_map/ppermute | solution.py:1493
  307.6 38.9 %collective-permute-start.32 = (bf16[640,1536]{1,0:T(8,128)(2,1)}, bf16[640,1536]{1,0:T(8,128)(2,1)S(1)}, u32[]{:S(2)}, u32[]{:S(2)}) collective-permute-start(bf16[640,1536]{1,0:T(8,128)(2,1)} %get-tuple-element.137.refs_2_), channel_id=1, source_target_pairs={{0,16},{16,0},{1,17},{17,1},{2,18},{18,2},{3,19},{19,3},{4,20},{20... | collective-permute-start | bytes 5898248 | tf_op jit(solution)/shard_map/ppermute | solution.py:1488
  307.6 80.8 %collective-permute-start.38 = (bf16[640,1536]{1,0:T(8,128)(2,1)}, bf16[640,1536]{1,0:T(8,128)(2,1)}, u32[]{:S(2)}, u32[]{:S(2)}) collective-permute-start(bf16[640,1536]{1,0:T(8,128)(2,1)} %get-tuple-element.156), channel_id=1, source_target_pairs={{0,16},{16,0},{1,17},{17,1},{2,18},{18,2},{3,19},{19,3},{4,20},{20... | collective-permute-start | bytes 5898248 | tf_op jit(solution)/shard_map/ppermute | solution.py:1488
  346.4 43.0 %collective-permute-start.39 = (bf16[640,1536]{1,0:T(8,128)(2,1)}, bf16[640,1536]{1,0:T(8,128)(2,1)}, u32[]{:S(2)}, u32[]{:S(2)}) collective-permute-start(bf16[640,1536]{1,0:T(8,128)(2,1)} %get-tuple-element.157), channel_id=1, source_target_pairs={{0,16},{16,0},{1,17},{17,1},{2,18},{18,2},{3,19},{19,3},{4,20},{20... | collective-permute-start | bytes 5898248 | tf_op jit(solution)/shard_map/ppermute | solution.py:1488
  387.3 54.5 %collective-permute-start.45 = (bf16[2,4,288,512]{3,2,1,0:T(8,128)(2,1)}, bf16[2,4,288,512]{3,2,1,0:T(8,128)(2,1)S(1)}, u32[]{:S(2)}, u32[]{:S(2)}) collective-permute-start(bf16[2,4,288,512]{3,2,1,0:T(8,128)(2,1)} %get-tuple-element.179), channel_id=1, source_target_pairs={{0,1},{1,0},{2,3},{3,2},{4,5},{5,4},{6,7},{7,6},{8,9},{9,8},{10,11... | collective-permute-start | bytes 7077896 | tf_op jit(solution)/shard_map/ppermute | solution.py:1493
  388.4 54.6 %collective-permute-start.46 = (bf16[2,4,288,512]{3,2,1,0:T(8,128)(2,1)}, bf16[2,4,288,512]{3,2,1,0:T(8,128)(2,1)S(1)}, u32[]{:S(2)}, u32[]{:S(2)}) collective-permute-start(bf16[2,4,288,512]{3,2,1,0:T(8,128)(2,1)} %get-tuple-element.180), channel_id=1, source_target_pairs={{0,2},{1,3},{2,0},{3,1},{4,6},{5,7},{6,4},{7,5},{8,10},{9,11},{10,... | collective-permute-start | bytes 7077896 | tf_op jit(solution)/shard_map/ppermute | solution.py:1493
  389.4 60.2 %collective-permute-start.33 = (bf16[640,1536]{1,0:T(8,128)(2,1)}, bf16[640,1536]{1,0:T(8,128)(2,1)S(1)}, u32[]{:S(2)}, u32[]{:S(2)}) collective-permute-start(bf16[640,1536]{1,0:T(8,128)(2,1)} %get-tuple-element.147.refs_4_), channel_id=1, source_target_pairs={{0,16},{16,0},{1,17},{17,1},{2,18},{18,2},{3,19},{19,3},{4,20},{20... | collective-permute-start | bytes 5898248 | tf_op jit(solution)/shard_map/ppermute | solution.py:1488
  407.7 42.8 %collective-permute-start.44 = (bf16[640,1024]{1,0:T(8,128)(2,1)}, bf16[640,1024]{1,0:T(8,128)(2,1)}, u32[]{:S(2)}, u32[]{:S(2)}) collective-permute-start(bf16[640,1024]{1,0:T(8,128)(2,1)} %get-tuple-element.175), channel_id=1, source_target_pairs={{0,16},{16,0},{1,17},{17,1},{2,18},{18,2},{3,19},{19,3},{4,20},{20... | collective-permute-start | bytes 3932168 | tf_op jit(solution)/shard_map/ppermute | solution.py:1488
  449.6 54.8 %collective-permute-start.48 = (bf16[4,288,512]{2,1,0:T(8,128)(2,1)}, bf16[4,288,512]{2,1,0:T(8,128)(2,1)S(1)}, u32[]{:S(2)}, u32[]{:S(2)}) collective-permute-start(bf16[4,288,512]{2,1,0:T(8,128)(2,1)} %get-tuple-element.181.refs_10_), channel_id=1, source_target_pairs={{0,1},{1,0},{2,3},{3,2},{4,5},{5,4},{6,7},{7,6},{8,9},{9,8},{10,11... | collective-permute-start | bytes 3538952 | tf_op jit(solution)/shard_map/ppermute | solution.py:1493
  450.5 53.9 %collective-permute-start.49 = (bf16[4,288,512]{2,1,0:T(8,128)(2,1)}, bf16[4,288,512]{2,1,0:T(8,128)(2,1)}, u32[]{:S(2)}, u32[]{:S(2)}) collective-permute-start(bf16[4,288,512]{2,1,0:T(8,128)(2,1)} %get-tuple-element.184), channel_id=1, source_target_pairs={{0,2},{1,3},{2,0},{3,1},{4,6},{5,7},{6,4},{7,5},{8,10},{9,11},{10,... | collective-permute-start | bytes 3538952 | tf_op jit(solution)/shard_map/ppermute | solution.py:1493
  473.4 31.0 %collective-permute-start.47 = (bf16[2,288,512]{2,1,0:T(8,128)(2,1)}, bf16[2,288,512]{2,1,0:T(8,128)(2,1)S(1)}, u32[]{:S(2)}, u32[]{:S(2)}) collective-permute-start(bf16[2,288,512]{2,1,0:T(8,128)(2,1)} %sum_pass.2.refs_9_), channel_id=1, source_target_pairs={{0,8},{1,9},{2,10},{3,11},{4,12},{5,13},{6,14},{7,15},{8,0},{9,1},... | collective-permute-start | bytes 1769480 | tf_op jit(solution)/shard_map/ppermute | solution.py:1493
  504.3 50.2 %collective-permute-start.52 = (bf16[640,1536]{1,0:T(8,128)(2,1)}, bf16[640,1536]{1,0:T(8,128)(2,1)S(1)}, u32[]{:S(2)}, u32[]{:S(2)}) collective-permute-start(bf16[640,1536]{1,0:T(8,128)(2,1)} %get-tuple-element.200), channel_id=1, source_target_pairs={{0,16},{16,0},{1,17},{17,1},{2,18},{18,2},{3,19},{19,3},{4,20},{20... | collective-permute-start | bytes 5898248 | tf_op jit(solution)/shard_map/ppermute | solution.py:1488
  512.9 35.3 %collective-permute-start.53 = (bf16[2,2,368,512]{3,2,1,0:T(8,128)(2,1)}, bf16[2,2,368,512]{3,2,1,0:T(8,128)(2,1)S(1)}, u32[]{:S(2)}, u32[]{:S(2)}) collective-permute-start(bf16[2,2,368,512]{3,2,1,0:T(8,128)(2,1)} %get-tuple-element.202), channel_id=1, source_target_pairs={{0,4},{1,5},{2,6},{3,7},{4,0},{5,1},{6,2},{7,3},{8,12},{9,13},{10,... | collective-permute-start | bytes 4521992 | tf_op jit(solution)/shard_map/ppermute | solution.py:1493
  552.6 49.8 %collective-permute-start.61 = (bf16[2,368,512]{2,1,0:T(8,128)(2,1)}, bf16[2,368,512]{2,1,0:T(8,128)(2,1)S(1)}, u32[]{:S(2)}, u32[]{:S(2)}) collective-permute-start(bf16[2,368,512]{2,1,0:T(8,128)(2,1)} %sum_pass.3.refs_5_), channel_id=1, source_target_pairs={{0,8},{1,9},{2,10},{3,11},{4,12},{5,13},{6,14},{7,15},{8,0},{9,1},... | collective-permute-start | bytes 2261000 | tf_op jit(solution)/shard_map/ppermute | solution.py:1493
  571.0 36.3 %collective-permute-start.58 = (bf16[2,160,512]{2,1,0:T(8,128)(2,1)}, bf16[2,160,512]{2,1,0:T(8,128)(2,1)S(1)}, u32[]{:S(2)}, u32[]{:S(2)}) collective-permute-start(bf16[2,160,512]{2,1,0:T(8,128)(2,1)} %get-tuple-element.210), channel_id=1, source_target_pairs={{0,4},{1,5},{2,6},{3,7},{4,0},{5,1},{6,2},{7,3},{8,12},{9,13},{10,... | collective-permute-start | bytes 983048 | tf_op jit(solution)/shard_map/ppermute | solution.py:1493
  572.5 36.9 %collective-permute-start.59 = (bf16[2,160,512]{2,1,0:T(8,128)(2,1)}, bf16[2,160,512]{2,1,0:T(8,128)(2,1)S(1)}, u32[]{:S(2)}, u32[]{:S(2)}) collective-permute-start(bf16[2,160,512]{2,1,0:T(8,128)(2,1)} %get-tuple-element.211), channel_id=1, source_target_pairs={{0,8},{1,9},{2,10},{3,11},{4,12},{5,13},{6,14},{7,15},{8,0},{9,1},... | collective-permute-start | bytes 983048 | tf_op jit(solution)/shard_map/ppermute | solution.py:1493
  572.5 36.9 %collective-permute-start.60 = (bf16[2,160,512]{2,1,0:T(8,128)(2,1)}, bf16[2,160,512]{2,1,0:T(8,128)(2,1)S(1)}, u32[]{:S(2)}, u32[]{:S(2)}) collective-permute-start(bf16[2,160,512]{2,1,0:T(8,128)(2,1)} %get-tuple-element.212), channel_id=1, source_target_pairs={{0,12},{1,13},{2,14},{3,15},{4,8},{5,9},{6,10},{7,11},{8,4},{9,5},... | collective-permute-start | bytes 983048 | tf_op jit(solution)/shard_map/ppermute | solution.py:1493
  (97 other events, 815.7 us)

commit v5 on v4

--- a/solution.py
+++ b/solution.py
@@ -284,6 +284,32 @@
     )[0]
 
 
+def join_kernel(place_ref, *refs):
+    *parts, out, sems = refs
+    copies = [
+        pltpu.make_async_copy(part, out.at[k], sems.at[k]) for k, part in enumerate(parts)
+    ]
+    for copy in copies:
+        copy.start()
+    for copy in copies:
+        copy.wait()
+
+
+def join(place, parts, after=()):
+    out = shaped((4, *parts[0].shape), low)
+    return run(
+        join_kernel,
+        "join",
+        place,
+        (1,),
+        [(part, anywhere) for part in parts],
+        [(out, whole(out))],
+        [pltpu.SemaphoreType.DMA((4,))],
+        after,
+        us=4,
+    )[0]
+
+
 def plane_kernel(place_ref, own, from_x, from_y, upper, lower, out, sems):
     half = upper.shape[1]
     parts = [
@@ -348,7 +374,7 @@
 
 
 def step_rows(half):
-    return next(rows for rows in (96, 80, 48, 368) if half % rows == 0)
+    return next(rows for rows in (144, 80, 96, 48, 368) if half % rows == 0)
 
 
 def merge_kernel(place_ref, late_x, late_y, got_x, got_y, out_x, out_y):
@@ -1544,6 +1570,12 @@
     def step_0(self, shard):
         return hop(shard, 2, 0, 0)
 
+    def all_z(self, shard):
+        return [hop(shard, k, 0, 0) for k in (1, 2, 3)]
+
+    def join(self, shard, received, after):
+        return join(self.place, [shard, *received], after)
+
     def step_1(self, shard, received, after=()):
         return pair_up(self.place, shard, received, after)
 
@@ -1637,20 +1669,20 @@
     segment = jnp.stack([item[1] for item in laid])
     cosine, sine = turn_table(jnp.concatenate([item[0] for item in laid]))
 
-    received_first = routes.step_0(first)
+    received_first = routes.all_z(first)
     whole_rows = 2 * FFN_HALF
-    chunk_a, chunk_b = routes.pack_ffn(1, (UPPER_ROWS, whole_rows - UPPER_ROWS), (first,))
+    chunk_a, chunk_b = routes.pack_ffn(
+        1, (UPPER_ROWS, whole_rows - UPPER_ROWS), (first, far_tokens, far_cotangent)
+    )
     if direct:
         chunk_b = chunk_b.reshape(1, *chunk_b.shape)
     sides_b = routes.step_4(chunk_b)
     parts_b, token = routes.step_5(chunk_b, sides_b)
-    pair_first = routes.step_1(first, received_first, (token,))
-    near_first = routes.step_2(pair_first)
-    (chunk_0,) = routes.pack_ffn(0, (whole_rows,), (pair_first,))
+    (chunk_0,) = routes.pack_ffn(0, (whole_rows,), (token,))
     received_0 = routes.step_0(chunk_0)
     plane_b = routes.plane(parts_b, (chunk_0,))
     tables = (far_tokens, far_cotangent, segment, cosine, sine)
-    line_first = routes.step_3(pair_first, near_first, (*tables, plane_b))
+    line_first = routes.join(first, received_first, (*tables, plane_b))
     sides_first = routes.step_4(line_first)
     pair_0 = routes.step_1(chunk_0, received_0, (line_first,))
     near_0 = routes.step_2(pair_0)
@@ -1815,6 +1847,12 @@
     def step_0(self, shard):
         return shard
 
+    def all_z(self, shard):
+        return ()
+
+    def join(self, shard, received, after):
+        return shard
+
     def step_1(self, shard, received, after=()):
         return shard
 

time: 640 us -> 632 us (0.988)
  waiting for transfers between devices: 135 us -> 125 us
  starting transfers between devices: 63.1 us -> 71.2 us
    ppermute x47 -> x48, waiting for transfers between devices: 133 us -> 124 us  [hop(): lax.ppermute(array, 'fsdp', [(chip, chip ^ flip) for chip in range(BLOCKS)])]
    ppermute x47 -> x48, starting transfers between devices: 60 us -> 68.1 us  [hop(): lax.ppermute(array, 'fsdp', [(chip, chip ^ flip) for chip in range(BLOCKS)])]
    pallas_call x46 -> x45, Pallas kernels: 385 us -> 378 us  [run(): pl.pallas_call(body, grid_spec=pltpu.PrefetchScalarGridSpec(num_scalar_pr...]
    unnamed x130 -> x126, local copies, waits for them, and re-layouts: 35.1 us -> 35 us
  transfers between devices with their start and end apart: 65 -> 66, of which waited for: 25 -> 21; matrix products, arithmetic and copies ran while one was open for 1% -> 2% of each run, Pallas kernels for 59% -> 58%
where the time goes in v5:
time: 632 us; the launch traced here: 621 us
  Pallas kernels  379 us (60%)
  waiting for transfers between devices  125 us (20%)
  starting transfers between devices  71.2 us (11%)
  local copies, waits for them, and re-layouts  36.1 us (6%)
  other arithmetic  7.92 us (1%)
    pallas_call x45, Pallas kernels, run(): pl.pallas_call(body, grid_spec=pltpu.PrefetchScalarGridSpec(num_scalar_pr...  378 us
    ppermute x48, waiting for transfers between devices, hop(): lax.ppermute(array, 'fsdp', [(chip, chip ^ flip) for chip in range(BLOCKS)])  124 us
    ppermute x48, starting transfers between devices, hop(): lax.ppermute(array, 'fsdp', [(chip, chip ^ flip) for chip in range(BLOCKS)])  68.1 us
    unnamed x126, local copies, waits for them, and re-layouts  35 us
  transfers between devices with their start and end apart: 66, of which 21 were waited for; matrix products, arithmetic and copies ran while one was open for 2% of the time, Pallas kernels for 58%

profile of v5, /device:TPU:0, one launch (start us, length us, event | category | flops | bytes accessed | tf_op | source)
XLA Modules:
  0.0 621.0 jit_solution(9070998907998831190)
XLA Ops:
  49.2 10.1 %collective-permute-start.12 = (bf16[576,512]{1,0:T(8,128)(2,1)S(1)}, bf16[576,512]{1,0:T(8,128)(2,1)S(1)}, u32[]{:S(2)}, u32[]{:S(2)}) collective-permute-start(bf16[576,512]{1,0:T(8,128)(2,1)S(1)} %copy-done.17), channel_id=1, source_target_pairs={{0,8},{1,9},{2,10},{3,11},{4,12},{5,13},{6,14},{7,15},{8,0},{9,1},... | collective-permute-start | bytes 1769480 | tf_op jit(solution)/shard_map/ppermute | solution.py:1519
  59.3 24.5 %collective-permute-done.12.refs_1_ = bf16[576,512]{1,0:T(8,128)(2,1)S(1)} collective-permute-done((bf16[576,512]{1,0:T(8,128)(2,1)S(1)}, bf16[576,512]{1,0:T(8,128)(2,1)S(1)}, u32[]{:S(2)}, u32[]{:S(2)}) %collective-permute-start.12) | collective-permute-done | bytes 589856 | tf_op jit(solution)/shard_map/ppermute | solution.py:1519
  95.0 19.5 %collective-permute-done.15.refs_1_ = bf16[2,576,512]{2,1,0:T(8,128)(2,1)S(1)} collective-permute-done((bf16[2,576,512]{2,1,0:T(8,128)(2,1)}, bf16[2,576,512]{2,1,0:T(8,128)(2,1)S(1)}, u32[]{:S(2)}, u32[]{:S(2)}) %collective-permute-start.15) | collective-permute-done | bytes 1179680 | tf_op jit(solution)/shard_map/ppermute | solution.py:1519
  122.3 4.1 out_weight.1
  127.0 7.0 %collective-permute-start.22 = (bf16[4,192,512]{2,1,0:T(8,128)(2,1)}, bf16[4,192,512]{2,1,0:T(8,128)(2,1)}, u32[]{:S(2)}, u32[]{:S(2)}) collective-permute-start(bf16[4,192,512]{2,1,0:T(8,128)(2,1)} %plane.1.refs_9_.refs_0_), channel_id=1, source_target_pairs={{0,8},{1,9},{2,10},{3,11},{4,12},{5,13},{6,14},{7,15},{8,0},{9,1},... | collective-permute-start | bytes 2359304 | tf_op jit(solution)/shard_map/ppermute | solution.py:1519
  135.7 19.0 %project_qkv.1 = (bf16[1280,1536]{1,0:T(8,128)(2,1)}, bf16[1280,1024]{1,0:T(8,128)(2,1)}, bf16[1280,512]{1,0:T(8,128)(2,1)}, bf16[1280,512]{1,0:T(8,128)(2,1)}, ...) custom-call(s32[4]{0:T(128)} %pad_add_fusion.1.place_ref, bf16[640,1536]{1,0:T(8,128)(2,1)} %refs_0_.11, ...), custom_call_target="tpu_custom_call" | custom-call | bytes 59400 | tf_op jit(solution)/shard_map/project_qkv/pallas_call | solution.py:52
  154.8 12.2 %attend.2 = (bf16[640,1024]{1,0:T(8,128)(2,1)}, f32[640,128]{1,0:T(8,128)}) custom-call(s32[4]{0:T(128)} %pad_add_fusion.1.place_ref, bf16[1280,1024]{1,0:T(8,128)(2,1)} %get-tuple-element.124.refs_0_, bf16[1280,512]{1,0:T(8,128)(2,1)} %get-tuple-element.125.refs_1_.refs_5_, bf16[1280,512]{1,0:T(8,128)(2,1)} %get-tuple-element.126.refs_2_, ...), custom_call_target="tpu_custom_call" | custom-call | bytes 56100 | tf_op jit(solution)/shard_map/attend/pallas_call | solution.py:52
  168.7 12.0 %attend.3 = (bf16[640,1024]{1,0:T(8,128)(2,1)}, f32[640,128]{1,0:T(8,128)}) custom-call(s32[4]{0:T(128)} %pad_add_fusion.1.place_ref, bf16[1280,1024]{1,0:T(8,128)(2,1)} %get-tuple-element.124.refs_0_, bf16[1280,512]{1,0:T(8,128)(2,1)} %get-tuple-element.125.refs_1_.refs_5_, bf16[1280,512]{1,0:T(8,128)(2,1)} %get-tuple-element.126.refs_2_, ...), custom_call_target="tpu_custom_call" | custom-call | bytes 56100 | tf_op jit(solution)/shard_map/attend/pallas_call | solution.py:52
  197.7 10.9 %middle.1 = (f32[640,1536]{1,0:T(8,128)}, bf16[640,1536]{1,0:T(8,128)(2,1)}) custom-call(s32[4]{0:T(128)} %pad_add_fusion.1.place_ref, bf16[640,1536]{1,0:T(8,128)(2,1)} %refs_0_.11, bf16[640,1024]{1,0:T(8,128)(2,1)} %get-tuple-element.129.refs_2_.refs_1_.refs_4_.refs_0_, bf16[640,1024]{1,0:T(8,128)(2,1)} %copy-done.20, ...), custom_call_target="tpu_custom_call" | custom-call | bytes 36300 | tf_op jit(solution)/shard_map/middle/pallas_call | solution.py:52
  208.6 7.1 %collective-permute-done.26.refs_1_ = bf16[2,384,512]{2,1,0:T(8,128)(2,1)S(1)} collective-permute-done((bf16[2,384,512]{2,1,0:T(8,128)(2,1)}, bf16[2,384,512]{2,1,0:T(8,128)(2,1)S(1)}, u32[]{:S(2)}, u32[]{:S(2)}) %collective-permute-start.26) | collective-permute-done | bytes 786464 | tf_op jit(solution)/shard_map/ppermute | solution.py:1519
  229.3 38.5 %ffn_forward.2 = (bf16[640,1536]{1,0:T(8,128)(2,1)}, bf16[640,1536]{1,0:T(8,128)(2,1)}, bf16[640,1536]{1,0:T(8,128)(2,1)}, bf16[640,1536]{1,0:T(8,128)(2,1)}, bf...) custom-call(s32[4]{0:T(128)} %pad_add_fusion.1.place_ref, ...), custom_call_target="tpu_custom_call" | custom-call | bytes 118800 | tf_op jit(solution)/shard_map/ffn_forward/pallas_call | solution.py:52
  274.3 21.5 %ffn_backward.2 = (bf16[2,4,288,512]{3,2,1,0:T(8,128)(2,1)}, bf16[2,4,288,512]{3,2,1,0:T(8,128)(2,1)}, bf16[4,288,512]{2,1,0:T(8,128)(2,1)}, bf16[4,288,512]{2,1,0:T(8,128)(2,1)}, bf16[4,2,288,512]{3,2,1,0:T(8,128)(2,1)}) custom-call(s32[4]{0:T(128)} %pad_add_fusion.1.place_ref, bf16[640,1536]{1,0:T(8,128)(2,1)} %get-tuple-element.134.refs_2_.refs_0_, ...), custom_call_target="tpu_custom_call" | custom-call | bytes 72600 | tf_op jit(solution)/shard_map/ffn_backward/pallas_call | solution.py:52
  301.3 38.3 %ffn_forward.3 = (bf16[640,1536]{1,0:T(8,128)(2,1)}, bf16[640,1536]{1,0:T(8,128)(2,1)}, bf16[640,1536]{1,0:T(8,128)(2,1)}, bf16[640,1536]{1,0:T(8,128)(2,1)}, bf...) custom-call(s32[4]{0:T(128)} %pad_add_fusion.1.place_ref, ...), custom_call_target="tpu_custom_call" | custom-call | bytes 118800 | tf_op jit(solution)/shard_map/ffn_forward/pallas_call | solution.py:52
  339.7 9.6 %collective-permute-done.35.refs_2_.refs_1_ = bf16[2,4,288,512]{3,2,1,0:T(8,128)(2,1)S(1)} collective-permute-done((bf16[2,4,288,512]{3,2,1,0:T(8,128)(2,1)}, bf16[2,4,288,512]{3,2,1,0:T(8,128)(2,1)S(1)}, u32[]{:S(2)}, u32[]{:S(2)}) %collective-permute-start.35) | collective-permute-done | bytes 2359328 | tf_op jit(solution)/shard_map/ppermute | solution.py:1519
  352.0 4.1 merge.4
  358.2 21.7 %ffn_backward.3 = (bf16[2,4,288,512]{3,2,1,0:T(8,128)(2,1)}, bf16[2,4,288,512]{3,2,1,0:T(8,128)(2,1)}, bf16[4,288,512]{2,1,0:T(8,128)(2,1)}, bf16[4,288,512]{2,1,0:T(8,128)(2,1)}, bf16[4,2,288,512]{3,2,1,0:T(8,128)(2,1)}) custom-call(s32[4]{0:T(128)} %pad_add_fusion.1.place_ref, bf16[640,1536]{1,0:T(8,128)(2,1)} %get-tuple-element.134.refs_2_.refs_0_, ...), custom_call_target="tpu_custom_call" | custom-call | bytes 72600 | tf_op jit(solution)/shard_map/ffn_backward/pallas_call | solution.py:52
  384.2 15.9 %middle_back.1 = (f32[640,1536]{1,0:T(8,128)}, bf16[640,768]{1,0:T(8,128)(2,1)}, bf16[640,768]{1,0:T(8,128)(2,1)}, bf16[640,1024]{1,0:T(8,128)(2,1)}, bf16[640,1024]{1,0:T(8,128)(2,1)}, /*index=5*/f32[8,1536]{1,0:T(8,128)}) custom-call(s32[4]{0:T(128)} %pad_add_fusion.1.place_ref, f32[640,1536]{1,0:T(8,128)} %get-tuple-element.133.refs_0_, ...), custom_call_target="tpu_custom_call" | custom-call | bytes 49500 | tf_op jit(solution)/shard_map/middle_back/pallas_call | solution.py:52
  400.7 14.5 %attend_back.2 = (bf16[640,1024]{1,0:T(8,128)(2,1)}, bf16[640,512]{1,0:T(8,128)(2,1)}, bf16[640,512]{1,0:T(8,128)(2,1)}) custom-call(s32[4]{0:T(128)} %pad_add_fusion.1.place_ref, bf16[1280,1024]{1,0:T(8,128)(2,1)} %get-tuple-element.124.refs_0_, bf16[1280,512]{1,0:T(8,128)(2,1)} %get-tuple-element.125.refs_1_.refs_5_, ...), custom_call_target="tpu_custom_call" | custom-call | bytes 69300 | tf_op jit(solution)/shard_map/attend_back/pallas_call | solution.py:52
  416.1 10.3 %out_grad.1 = (bf16[2,4,80,512]{3,2,1,0:T(8,128)(2,1)}, bf16[2,4,80,512]{3,2,1,0:T(8,128)(2,1)}, bf16[4,80,512]{2,1,0:T(8,128)(2,1)}, bf16[4,80,512]{2,1,0:T(8,128)(2,1)}, bf16[4,2,80,512]{3,2,1,0:T(8,128)(2,1)}) custom-call(s32[4]{0:T(128)} %pad_add_fusion.1.place_ref, bf16[640,1024]{1,0:T(8,128)(2,1)} %get-tuple-element.129.refs_2_.refs_1_.refs_4_.refs_0_, ...), custom_call_target="tpu_custom_call" | custom-call | bytes 33000 | tf_op jit(solution)/shard_map/out_grad/pallas_call | solution.py:52
  426.4 6.5 %sum_plane.3 = (f32[2,288,512]{2,1,0:T(8,128)}, f32[2,288,512]{2,1,0:T(8,128)}, bf16[2,2,288,512]{3,2,1,0:T(8,128)(2,1)}) custom-call(s32[4]{0:T(128)} %pad_add_fusion.1.place_ref, bf16[4,2,288,512]{3,2,1,0:T(8,128)(2,1)} %get-tuple-element.148.refs_0_, bf16[2,4,288,512]{3,2,1,0:T(8,128)(2,1)} %copy-done.7, bf16[2,4,288,512]{3,2,1,0:T(8,128)(2,1)} %copy-done.8, ...), custom_call_target="tpu_custom_call" | custom-call | bytes 16500 | tf_op jit(solution)/shard_map/sum_plane/pallas_call | solution.py:52
  436.9 4.2 merge.5
  443.0 14.1 %attend_back.3 = (bf16[640,1024]{1,0:T(8,128)(2,1)}, bf16[640,512]{1,0:T(8,128)(2,1)}, bf16[640,512]{1,0:T(8,128)(2,1)}) custom-call(s32[4]{0:T(128)} %pad_add_fusion.1.place_ref, bf16[1280,1024]{1,0:T(8,128)(2,1)} %get-tuple-element.124.refs_0_, bf16[1280,512]{1,0:T(8,128)(2,1)} %get-tuple-element.125.refs_1_.refs_5_, ...), custom_call_target="tpu_custom_call" | custom-call | bytes 69300 | tf_op jit(solution)/shard_map/attend_back/pallas_call | solution.py:52
  469.7 14.2 %input_back.1 = (bf16[1280,1536]{1,0:T(8,128)(2,1)}, bf16[640,1536]{1,0:T(8,128)(2,1)}, bf16[640,1536]{1,0:T(8,128)(2,1)}, f32[8,1536]{1,0:T(8,128)}) custom-call(s32[4]{0:T(128)} %pad_add_fusion.1.place_ref, bf16[640,1024]{1,0:T(8,128)(2,1)} %get-tuple-element.166.refs_6_.refs_0_, bf16[640,512]{1,0:T(8,128)(2,1)} %get-tuple-element.187.refs_1_, ...), custom_call_target="tpu_custom_call" | custom-call | bytes 49500 | tf_op jit(solution)/shard_map/input_back/pallas_call | solution.py:52
  483.9 11.6 %qkv_grad.1 = (bf16[2,4,160,512]{3,2,1,0:T(8,128)(2,1)}, bf16[2,4,160,512]{3,2,1,0:T(8,128)(2,1)}, bf16[4,160,512]{2,1,0:T(8,128)(2,1)}, bf16[4,160,512]{2,1,0:T(8,128)(2,1)}, bf16[4,2,160,512]{3,2,1,0:T(8,128)(2,1)}) custom-call(s32[4]{0:T(128)} %pad_add_fusion.1.place_ref, bf16[1280,1536]{1,0:T(8,128)(2,1)} %get-tuple-element.186.refs_0_, ...), custom_call_target="tpu_custom_call" | custom-call | bytes 49500 | tf_op jit(solution)/shard_map/qkv_grad/pallas_call | solution.py:52
  498.7 7.3 %sum_plane.4 = (f32[2,368,512]{2,1,0:T(8,128)}, f32[2,368,512]{2,1,0:T(8,128)}, bf16[2,2,368,512]{3,2,1,0:T(8,128)(2,1)}) custom-call(s32[4]{0:T(128)} %pad_add_fusion.1.place_ref, bf16[4,2,288,512]{3,2,1,0:T(8,128)(2,1)} %get-tuple-element.161.refs_11_.refs_0_, bf16[2,4,288,512]{3,2,1,0:T(8,128)(2,1)} %copy-done.9, bf16[2,4,288,512]{3,2,1,0:T(8,128)(2,1)} %copy-done.10, ...), custom_call_target="tpu_custom_call" | custom-call | bytes 16500 | tf_op jit(solution)/shard_map/sum_plane/pallas_call | solution.py:52
  509.9 7.7 %output.1.refs_4_ = bf16[640,1536]{1,0:T(8,128)(2,1)} custom-call(s32[4]{0:T(128)} %pad_add_fusion.1.place_ref, f32[640,1536]{1,0:T(8,128)} %get-tuple-element.133.refs_0_, bf16[640,1536]{1,0:T(8,128)(2,1)} %get-tuple-element.136.refs_1_, bf16[640,1536]{1,0:T(8,128)(2,1)} %get-tuple-element.146.refs_2_, bf16[640,1536]{1,0:T(8,128)(2,1)} %copy-done.12, ...), custom_call_target="tpu_custom_call" | custom-call | bytes 13200 | tf_op jit(solution)/shard_map/output/pallas_call | solution.py:52
  517.6 7.4 %collective-permute-done.55.refs_2_.refs_1_ = bf16[2,4,160,512]{3,2,1,0:T(8,128)(2,1)S(1)} collective-permute-done((bf16[2,4,160,512]{3,2,1,0:T(8,128)(2,1)}, bf16[2,4,160,512]{3,2,1,0:T(8,128)(2,1)S(1)}, u32[]{:S(2)}, u32[]{:S(2)}) %collective-permute-start.55) | collective-permute-done | bytes 1310752 | tf_op jit(solution)/shard_map/ppermute | solution.py:1519
  532.1 9.2 %collective-permute-done.54.refs_1_ = bf16[2,2,368,512]{3,2,1,0:T(8,128)(2,1)S(1)} collective-permute-done((bf16[2,2,368,512]{3,2,1,0:T(8,128)(2,1)}, bf16[2,2,368,512]{3,2,1,0:T(8,128)(2,1)S(1)}, u32[]{:S(2)}, u32[]{:S(2)}) %collective-permute-start.54) | collective-permute-done | bytes 1507360 | tf_op jit(solution)/shard_map/ppermute | solution.py:1519
  547.5 8.6 %tokens_grad.1.refs_5_ = f32[640,1536]{1,0:T(8,128)} custom-call(s32[4]{0:T(128)} %pad_add_fusion.1.place_ref, bf16[640,1536]{1,0:T(8,128)(2,1)} %refs_0_.11, f32[640,1536]{1,0:T(8,128)} %get-tuple-element.198.refs_1_, bf16[640,1536]{1,0:T(8,128)(2,1)} %get-tuple-element.199.refs_2_, bf16[640,1536]{1,0:T(8,128)(2,1)} %copy-done.32, ...), custom_call_target="tpu_custom_call" | custom-call | bytes 13200 | tf_op jit(solution)/shard_map/tokens_grad/pallas_call | solution.py:52
  557.8 4.9 sum_plane.5
  567.0 28.2 %collective-permute-done.62.refs_2_ = bf16[2,368,512]{2,1,0:T(8,128)(2,1)S(1)} collective-permute-done((bf16[2,368,512]{2,1,0:T(8,128)(2,1)}, bf16[2,368,512]{2,1,0:T(8,128)(2,1)S(1)}, u32[]{:S(2)}, u32[]{:S(2)}) %collective-permute-start.62) | collective-permute-done | bytes 753696 | tf_op jit(solution)/shard_map/ppermute | solution.py:1519
  611.4 5.6 unpack_ffn.1
  (289 shorter events, 189.0 us)
Async XLA Ops:
  4.5 36.9 %collective-permute-start.2 = (bf16[448,512]{1,0:T(8,128)(2,1)}, bf16[448,512]{1,0:T(8,128)(2,1)S(1)}, u32[]{:S(2)}, u32[]{:S(2)}) collective-permute-start(bf16[448,512]{1,0:T(8,128)(2,1)} %pack_first.1.refs_3_.refs_0_), channel_id=1, source_target_pairs={{0,4},{1,5},{2,6},{3,7},{4,0},{5,1},{6,2},{7,3},{8,12},{9,13},{10,... | collective-permute-start | bytes 1376264 | tf_op jit(solution)/shard_map/ppermute | solution.py:1519
  7.5 34.2 %collective-permute-start.3 = (bf16[448,512]{1,0:T(8,128)(2,1)}, bf16[448,512]{1,0:T(8,128)(2,1)S(1)}, u32[]{:S(2)}, u32[]{:S(2)}) collective-permute-start(bf16[448,512]{1,0:T(8,128)(2,1)} %pack_first.1.refs_3_.refs_0_), channel_id=1, source_target_pairs={{0,8},{1,9},{2,10},{3,11},{4,12},{5,13},{6,14},{7,15},{8,0},{9,1},... | collective-permute-start | bytes 1376264 | tf_op jit(solution)/shard_map/ppermute | solution.py:1519
  46.1 41.6 %collective-permute-start.10 = (bf16[4,448,512]{2,1,0:T(8,128)(2,1)}, bf16[4,448,512]{2,1,0:T(8,128)(2,1)S(1)}, u32[]{:S(2)}, u32[]{:S(2)}) collective-permute-start(bf16[4,448,512]{2,1,0:T(8,128)(2,1)} %join.1.refs_2_.refs_0_.refs_4_), channel_id=1, source_target_pairs={{0,1},{1,0},{2,3},{3,2},{4,5},{5,4},{6,7},{7,6},{8,9},{9,8},{10,11... | collective-permute-start | bytes 5505032 | tf_op jit(solution)/shard_map/ppermute | solution.py:1519
  47.7 40.0 %collective-permute-start.11 = (bf16[4,448,512]{2,1,0:T(8,128)(2,1)}, bf16[4,448,512]{2,1,0:T(8,128)(2,1)S(1)}, u32[]{:S(2)}, u32[]{:S(2)}) collective-permute-start(bf16[4,448,512]{2,1,0:T(8,128)(2,1)} %join.1.refs_2_.refs_0_.refs_4_), channel_id=1, source_target_pairs={{0,2},{1,3},{2,0},{3,1},{4,6},{5,7},{6,4},{7,5},{8,10},{9,11},{10,... | collective-permute-start | bytes 5505032 | tf_op jit(solution)/shard_map/ppermute | solution.py:1519
  49.2 34.7 %collective-permute-start.12 = (bf16[576,512]{1,0:T(8,128)(2,1)S(1)}, bf16[576,512]{1,0:T(8,128)(2,1)S(1)}, u32[]{:S(2)}, u32[]{:S(2)}) collective-permute-start(bf16[576,512]{1,0:T(8,128)(2,1)S(1)} %copy-done.17), channel_id=1, source_target_pairs={{0,8},{1,9},{2,10},{3,11},{4,12},{5,13},{6,14},{7,15},{8,0},{9,1},... | collective-permute-start | bytes 1769480 | tf_op jit(solution)/shard_map/ppermute | solution.py:1519
  119.3 67.5 %collective-permute-start.20 = (bf16[4,576,512]{2,1,0:T(8,128)(2,1)}, bf16[4,576,512]{2,1,0:T(8,128)(2,1)}, u32[]{:S(2)}, u32[]{:S(2)}) collective-permute-start(bf16[4,576,512]{2,1,0:T(8,128)(2,1)} %line.2.refs_5_.refs_4_), channel_id=1, source_target_pairs={{0,1},{1,0},{2,3},{3,2},{4,5},{5,4},{6,7},{7,6},{8,9},{9,8},{10,11... | collective-permute-start | bytes 7077896 | tf_op jit(solution)/shard_map/ppermute | solution.py:1519
  119.9 66.9 %collective-permute-start.21 = (bf16[4,576,512]{2,1,0:T(8,128)(2,1)}, bf16[4,576,512]{2,1,0:T(8,128)(2,1)}, u32[]{:S(2)}, u32[]{:S(2)}) collective-permute-start(bf16[4,576,512]{2,1,0:T(8,128)(2,1)} %line.2.refs_5_.refs_4_), channel_id=1, source_target_pairs={{0,2},{1,3},{2,0},{3,1},{4,6},{5,7},{6,4},{7,5},{8,10},{9,11},{10,... | collective-permute-start | bytes 7077896 | tf_op jit(solution)/shard_map/ppermute | solution.py:1519
  126.4 40.6 %collective-permute-start.16 = (bf16[1024,768]{1,0:T(8,128)(2,1)}, bf16[1024,768]{1,0:T(8,128)(2,1)S(1)}, u32[]{:S(2)}, u32[]{:S(2)}) collective-permute-start(bf16[1024,768]{1,0:T(8,128)(2,1)} %get-tuple-element.123.refs_9_.refs_3_.refs_7_), channel_id=1, source_target_pairs={{0,16},{16,0},{1,17},{17,1},{2,18},{18,2},{3,19},{19,3},{4,20},{20... | collective-permute-start | bytes 4718600 | tf_op jit(solution)/shard_map/ppermute | solution.py:1514
  126.5 40.6 %collective-permute-start.17 = (bf16[1024,768]{1,0:T(8,128)(2,1)}, bf16[1024,768]{1,0:T(8,128)(2,1)S(1)}, u32[]{:S(2)}, u32[]{:S(2)}) collective-permute-start(bf16[1024,768]{1,0:T(8,128)(2,1)} %get-tuple-element.128.refs_4_.refs_8_), channel_id=1, source_target_pairs={{0,16},{16,0},{1,17},{17,1},{2,18},{18,2},{3,19},{19,3},{4,20},{20... | collective-permute-start | bytes 4718600 | tf_op jit(solution)/shard_map/ppermute | solution.py:1514
  127.0 53.7 %collective-permute-start.22 = (bf16[4,192,512]{2,1,0:T(8,128)(2,1)}, bf16[4,192,512]{2,1,0:T(8,128)(2,1)}, u32[]{:S(2)}, u32[]{:S(2)}) collective-permute-start(bf16[4,192,512]{2,1,0:T(8,128)(2,1)} %plane.1.refs_9_.refs_0_), channel_id=1, source_target_pairs={{0,8},{1,9},{2,10},{3,11},{4,12},{5,13},{6,14},{7,15},{8,0},{9,1},... | collective-permute-start | bytes 2359304 | tf_op jit(solution)/shard_map/ppermute | solution.py:1519
  180.7 39.3 %collective-permute-start.27 = (bf16[640,1024]{1,0:T(8,128)(2,1)}, bf16[640,1024]{1,0:T(8,128)(2,1)S(1)}, u32[]{:S(2)}, u32[]{:S(2)}) collective-permute-start(bf16[640,1024]{1,0:T(8,128)(2,1)} %get-tuple-element.129.refs_2_.refs_1_.refs_4_.refs_0_), channel_id=1, source_target_pairs={{0,16},{16,0},{1,17},{17,1},{2,18},{18,2},{3,19},{19,3},{4,20},{20... | collective-permute-start | bytes 3932168 | tf_op jit(solution)/shard_map/ppermute | solution.py:1514
  225.3 42.4 %collective-permute-start.28 = (bf16[4,384,512]{2,1,0:T(8,128)(2,1)}, bf16[4,384,512]{2,1,0:T(8,128)(2,1)S(1)}, u32[]{:S(2)}, u32[]{:S(2)}) collective-permute-start(bf16[4,384,512]{2,1,0:T(8,128)(2,1)} %line.3.refs_9_.refs_4_), channel_id=1, source_target_pairs={{0,1},{1,0},{2,3},{3,2},{4,5},{5,4},{6,7},{7,6},{8,9},{9,8},{10,11... | collective-permute-start | bytes 4718600 | tf_op jit(solution)/shard_map/ppermute | solution.py:1519
  226.9 40.9 %collective-permute-start.29 = (bf16[4,384,512]{2,1,0:T(8,128)(2,1)}, bf16[4,384,512]{2,1,0:T(8,128)(2,1)S(1)}, u32[]{:S(2)}, u32[]{:S(2)}) collective-permute-start(bf16[4,384,512]{2,1,0:T(8,128)(2,1)} %line.3.refs_9_.refs_4_), channel_id=1, source_target_pairs={{0,2},{1,3},{2,0},{3,1},{4,6},{5,7},{6,4},{7,5},{8,10},{9,11},{10,... | collective-permute-start | bytes 4718600 | tf_op jit(solution)/shard_map/ppermute | solution.py:1519
  228.0 67.8 %collective-permute-start.32 = (bf16[2,4,192,512]{3,2,1,0:T(8,128)(2,1)S(1)}, bf16[2,4,192,512]{3,2,1,0:T(8,128)(2,1)S(1)}, u32[]{:S(2)}, u32[]{:S(2)}) collective-permute-start(bf16[2,4,192,512]{3,2,1,0:T(8,128)(2,1)S(1)} %copy-done.4), channel_id=1, source_target_pairs={{0,4},{1,5},{2,6},{3,7},{4,0},{5,1},{6,2},{7,3},{8,12},{9,13},{10,... | collective-permute-start | bytes 4718600 | tf_op jit(solution)/shard_map/ppermute | solution.py:1519
  298.1 51.3 %collective-permute-start.35 = (bf16[2,4,288,512]{3,2,1,0:T(8,128)(2,1)}, bf16[2,4,288,512]{3,2,1,0:T(8,128)(2,1)S(1)}, u32[]{:S(2)}, u32[]{:S(2)}) collective-permute-start(bf16[2,4,288,512]{3,2,1,0:T(8,128)(2,1)} %get-tuple-element.145.refs_11_), channel_id=1, source_target_pairs={{0,1},{1,0},{2,3},{3,2},{4,5},{5,4},{6,7},{7,6},{8,9},{9,8},{10,11... | collective-permute-start | bytes 7077896 | tf_op jit(solution)/shard_map/ppermute | solution.py:1519
  299.7 50.9 %collective-permute-start.36 = (bf16[2,4,288,512]{3,2,1,0:T(8,128)(2,1)}, bf16[2,4,288,512]{3,2,1,0:T(8,128)(2,1)S(1)}, u32[]{:S(2)}, u32[]{:S(2)}) collective-permute-start(bf16[2,4,288,512]{3,2,1,0:T(8,128)(2,1)} %get-tuple-element.149), channel_id=1, source_target_pairs={{0,2},{1,3},{2,0},{3,1},{4,6},{5,7},{6,4},{7,5},{8,10},{9,11},{10,... | collective-permute-start | bytes 7077896 | tf_op jit(solution)/shard_map/ppermute | solution.py:1519
  300.8 38.9 %collective-permute-start.33 = (bf16[640,1536]{1,0:T(8,128)(2,1)}, bf16[640,1536]{1,0:T(8,128)(2,1)S(1)}, u32[]{:S(2)}, u32[]{:S(2)}) collective-permute-start(bf16[640,1536]{1,0:T(8,128)(2,1)} %get-tuple-element.137.refs_2_), channel_id=1, source_target_pairs={{0,16},{16,0},{1,17},{17,1},{2,18},{18,2},{3,19},{19,3},{4,20},{20... | collective-permute-start | bytes 5898248 | tf_op jit(solution)/shard_map/ppermute | solution.py:1514
  300.8 80.2 %collective-permute-start.39 = (bf16[640,1536]{1,0:T(8,128)(2,1)}, bf16[640,1536]{1,0:T(8,128)(2,1)}, u32[]{:S(2)}, u32[]{:S(2)}) collective-permute-start(bf16[640,1536]{1,0:T(8,128)(2,1)} %get-tuple-element.156), channel_id=1, source_target_pairs={{0,16},{16,0},{1,17},{17,1},{2,18},{18,2},{3,19},{19,3},{4,20},{20... | collective-permute-start | bytes 5898248 | tf_op jit(solution)/shard_map/ppermute | solution.py:1514
  339.6 42.3 %collective-permute-start.40 = (bf16[640,1536]{1,0:T(8,128)(2,1)}, bf16[640,1536]{1,0:T(8,128)(2,1)}, u32[]{:S(2)}, u32[]{:S(2)}) collective-permute-start(bf16[640,1536]{1,0:T(8,128)(2,1)} %get-tuple-element.157), channel_id=1, source_target_pairs={{0,16},{16,0},{1,17},{17,1},{2,18},{18,2},{3,19},{19,3},{4,20},{20... | collective-permute-start | bytes 5898248 | tf_op jit(solution)/shard_map/ppermute | solution.py:1514
  379.9 54.4 %collective-permute-start.46 = (bf16[2,4,288,512]{3,2,1,0:T(8,128)(2,1)}, bf16[2,4,288,512]{3,2,1,0:T(8,128)(2,1)S(1)}, u32[]{:S(2)}, u32[]{:S(2)}) collective-permute-start(bf16[2,4,288,512]{3,2,1,0:T(8,128)(2,1)} %get-tuple-element.179), channel_id=1, source_target_pairs={{0,1},{1,0},{2,3},{3,2},{4,5},{5,4},{6,7},{7,6},{8,9},{9,8},{10,11... | collective-permute-start | bytes 7077896 | tf_op jit(solution)/shard_map/ppermute | solution.py:1519
  381.0 54.5 %collective-permute-start.47 = (bf16[2,4,288,512]{3,2,1,0:T(8,128)(2,1)}, bf16[2,4,288,512]{3,2,1,0:T(8,128)(2,1)S(1)}, u32[]{:S(2)}, u32[]{:S(2)}) collective-permute-start(bf16[2,4,288,512]{3,2,1,0:T(8,128)(2,1)} %get-tuple-element.180), channel_id=1, source_target_pairs={{0,2},{1,3},{2,0},{3,1},{4,6},{5,7},{6,4},{7,5},{8,10},{9,11},{10,... | collective-permute-start | bytes 7077896 | tf_op jit(solution)/shard_map/ppermute | solution.py:1519
  381.9 59.1 %collective-permute-start.34 = (bf16[640,1536]{1,0:T(8,128)(2,1)}, bf16[640,1536]{1,0:T(8,128)(2,1)S(1)}, u32[]{:S(2)}, u32[]{:S(2)}) collective-permute-start(bf16[640,1536]{1,0:T(8,128)(2,1)} %get-tuple-element.147.refs_4_), channel_id=1, source_target_pairs={{0,16},{16,0},{1,17},{17,1},{2,18},{18,2},{3,19},{19,3},{4,20},{20... | collective-permute-start | bytes 5898248 | tf_op jit(solution)/shard_map/ppermute | solution.py:1514
  400.2 41.8 %collective-permute-start.45 = (bf16[640,1024]{1,0:T(8,128)(2,1)}, bf16[640,1024]{1,0:T(8,128)(2,1)}, u32[]{:S(2)}, u32[]{:S(2)}) collective-permute-start(bf16[640,1024]{1,0:T(8,128)(2,1)} %get-tuple-element.175), channel_id=1, source_target_pairs={{0,16},{16,0},{1,17},{17,1},{2,18},{18,2},{3,19},{19,3},{4,20},{20... | collective-permute-start | bytes 3932168 | tf_op jit(solution)/shard_map/ppermute | solution.py:1514
  441.1 56.4 %collective-permute-start.49 = (bf16[4,288,512]{2,1,0:T(8,128)(2,1)}, bf16[4,288,512]{2,1,0:T(8,128)(2,1)S(1)}, u32[]{:S(2)}, u32[]{:S(2)}) collective-permute-start(bf16[4,288,512]{2,1,0:T(8,128)(2,1)} %get-tuple-element.181.refs_10_), channel_id=1, source_target_pairs={{0,1},{1,0},{2,3},{3,2},{4,5},{5,4},{6,7},{7,6},{8,9},{9,8},{10,11... | collective-permute-start | bytes 3538952 | tf_op jit(solution)/shard_map/ppermute | solution.py:1519
  442.0 55.5 %collective-permute-start.50 = (bf16[4,288,512]{2,1,0:T(8,128)(2,1)}, bf16[4,288,512]{2,1,0:T(8,128)(2,1)}, u32[]{:S(2)}, u32[]{:S(2)}) collective-permute-start(bf16[4,288,512]{2,1,0:T(8,128)(2,1)} %get-tuple-element.184), channel_id=1, source_target_pairs={{0,2},{1,3},{2,0},{3,1},{4,6},{5,7},{6,4},{7,5},{8,10},{9,11},{10,... | collective-permute-start | bytes 3538952 | tf_op jit(solution)/shard_map/ppermute | solution.py:1519
  465.0 32.5 %collective-permute-start.48 = (bf16[2,288,512]{2,1,0:T(8,128)(2,1)}, bf16[2,288,512]{2,1,0:T(8,128)(2,1)S(1)}, u32[]{:S(2)}, u32[]{:S(2)}) collective-permute-start(bf16[2,288,512]{2,1,0:T(8,128)(2,1)} %sum_pass.2.refs_9_), channel_id=1, source_target_pairs={{0,8},{1,9},{2,10},{3,11},{4,12},{5,13},{6,14},{7,15},{8,0},{9,1},... | collective-permute-start | bytes 1769480 | tf_op jit(solution)/shard_map/ppermute | solution.py:1519
  497.5 48.7 %collective-permute-start.53 = (bf16[640,1536]{1,0:T(8,128)(2,1)}, bf16[640,1536]{1,0:T(8,128)(2,1)S(1)}, u32[]{:S(2)}, u32[]{:S(2)}) collective-permute-start(bf16[640,1536]{1,0:T(8,128)(2,1)} %get-tuple-element.200), channel_id=1, source_target_pairs={{0,16},{16,0},{1,17},{17,1},{2,18},{18,2},{3,19},{19,3},{4,20},{20... | collective-permute-start | bytes 5898248 | tf_op jit(solution)/shard_map/ppermute | solution.py:1514
  506.0 35.3 %collective-permute-start.54 = (bf16[2,2,368,512]{3,2,1,0:T(8,128)(2,1)}, bf16[2,2,368,512]{3,2,1,0:T(8,128)(2,1)S(1)}, u32[]{:S(2)}, u32[]{:S(2)}) collective-permute-start(bf16[2,2,368,512]{3,2,1,0:T(8,128)(2,1)} %get-tuple-element.202), channel_id=1, source_target_pairs={{0,4},{1,5},{2,6},{3,7},{4,0},{5,1},{6,2},{7,3},{8,12},{9,13},{10,... | collective-permute-start | bytes 4521992 | tf_op jit(solution)/shard_map/ppermute | solution.py:1519
  545.7 49.5 %collective-permute-start.62 = (bf16[2,368,512]{2,1,0:T(8,128)(2,1)}, bf16[2,368,512]{2,1,0:T(8,128)(2,1)S(1)}, u32[]{:S(2)}, u32[]{:S(2)}) collective-permute-start(bf16[2,368,512]{2,1,0:T(8,128)(2,1)} %sum_pass.3.refs_5_), channel_id=1, source_target_pairs={{0,8},{1,9},{2,10},{3,11},{4,12},{5,13},{6,14},{7,15},{8,0},{9,1},... | collective-permute-start | bytes 2261000 | tf_op jit(solution)/shard_map/ppermute | solution.py:1519
  562.7 37.4 %collective-permute-start.59 = (bf16[2,160,512]{2,1,0:T(8,128)(2,1)}, bf16[2,160,512]{2,1,0:T(8,128)(2,1)S(1)}, u32[]{:S(2)}, u32[]{:S(2)}) collective-permute-start(bf16[2,160,512]{2,1,0:T(8,128)(2,1)} %get-tuple-element.210), channel_id=1, source_target_pairs={{0,4},{1,5},{2,6},{3,7},{4,0},{5,1},{6,2},{7,3},{8,12},{9,13},{10,... | collective-permute-start | bytes 983048 | tf_op jit(solution)/shard_map/ppermute | solution.py:1519
  564.1 38.1 %collective-permute-start.60 = (bf16[2,160,512]{2,1,0:T(8,128)(2,1)}, bf16[2,160,512]{2,1,0:T(8,128)(2,1)S(1)}, u32[]{:S(2)}, u32[]{:S(2)}) collective-permute-start(bf16[2,160,512]{2,1,0:T(8,128)(2,1)} %get-tuple-element.211), channel_id=1, source_target_pairs={{0,8},{1,9},{2,10},{3,11},{4,12},{5,13},{6,14},{7,15},{8,0},{9,1},... | collective-permute-start | bytes 983048 | tf_op jit(solution)/shard_map/ppermute | solution.py:1519
  565.7 36.6 %collective-permute-start.61 = (bf16[2,160,512]{2,1,0:T(8,128)(2,1)}, bf16[2,160,512]{2,1,0:T(8,128)(2,1)S(1)}, u32[]{:S(2)}, u32[]{:S(2)}) collective-permute-start(bf16[2,160,512]{2,1,0:T(8,128)(2,1)} %get-tuple-element.212), channel_id=1, source_target_pairs={{0,12},{1,13},{2,14},{3,15},{4,8},{5,9},{6,10},{7,11},{8,4},{9,5},... | collective-permute-start | bytes 983048 | tf_op jit(solution)/shard_map/ppermute | solution.py:1519
  (96 other events, 824.4 us)

commit v6 on v5

--- a/solution.py
+++ b/solution.py
@@ -1615,8 +1615,9 @@
         token = sum_pass(self.place, kept_far, near, after)
         return token, (near, hop(token, 2, 0, 0))
 
-    def scatter_34(self, sent, got, more, after):
-        kept, *parts = sum_plane(self.place, [(sent[4], *got, *more)], True, after)
+    def scatter_34(self, groups, after):
+        groups = [(sent[4], *got, *more) for sent, got, more in groups]
+        kept, *parts = sum_plane(self.place, groups, True, after)
         return kept, tuple(hop(part, k + 1, 0, 0) for k, part in enumerate(parts))
 
     def scatter_5(self, kept, parts, after):
@@ -1762,15 +1763,14 @@
     sent_qkv = qkv_grad(place, normed_low, grad_qkv, attn_gain_grad, ffn_gain_grad)
     got_qkv = routes.scatter_1(sent_qkv)
     groups = [(sent_1, got_1, more_1), (sent_out, got_out, more_out)]
-    kept_1, parts_1 = routes.scatter_3(groups, (sent_qkv[4], *routes.pins(parts_0[1:])))
+    kept_1, parts_1 = routes.scatter_34(groups, (sent_qkv[4], *routes.pins(parts_0[1:])))
 
     owned_0 = routes.scatter_5(kept_0, parts_0, (kept_1,))
     outs = (sums_0[2], sums_1[2], out_far_0, out_far_1)
     output = output_of(place, middle, outs, (owned_0[0],))
     token, more_qkv = routes.scatter_2(sent_qkv, got_qkv, (output,))
-    token, parts_1 = routes.scatter_4(kept_1, parts_1, (token,))
     grad_tokens = tokens_grad(place, tokens, grad_middle, own_part, own_rest, gains, (token,))
-    kept_qkv, parts_qkv = routes.scatter_34(sent_qkv, got_qkv, more_qkv, (grad_tokens,))
+    kept_qkv, parts_qkv = routes.scatter_34([(sent_qkv, got_qkv, more_qkv)], (grad_tokens,))
     owned_1 = routes.scatter_5(kept_1, parts_1, (kept_qkv,))
     owned_qkv = routes.scatter_5(kept_qkv, parts_qkv, (owned_1[0],))
     shapes = [w_gate.shape, w_up.shape, w_down.shape]
@@ -1884,8 +1884,8 @@
         blocks = jnp.concatenate([got for _, got, _ in groups], axis=1)
         return blocks, blocks
 
-    def scatter_34(self, sent, got, more, after):
-        return got, ()
+    def scatter_34(self, groups, after):
+        return self.scatter_3(groups, after)[0], ()
 
     def scatter_4(self, kept, parts, after):
         return kept, kept

time: 632 us -> 695 us (1.100)
  waiting for transfers between devices: 125 us -> 190 us
    ppermute x48 -> x49, waiting for transfers between devices: 124 us -> 188 us  [hop(): lax.ppermute(array, 'fsdp', [(chip, chip ^ flip) for chip in range(BLOCKS)])]
    pallas_call x45 -> x44, Pallas kernels: 378 us -> 375 us  [run(): pl.pallas_call(body, grid_spec=pltpu.PrefetchScalarGridSpec(num_scalar_pr...]
    ppermute x48 -> x49, starting transfers between devices: 68.1 us -> 70.8 us  [hop(): lax.ppermute(array, 'fsdp', [(chip, chip ^ flip) for chip in range(BLOCKS)])]
    unnamed x126 -> x136, local copies, waits for them, and re-layouts: 35 us -> 34 us
  transfers between devices with their start and end apart: 66 -> 67, of which waited for: 21 -> 21; matrix products, arithmetic and copies ran while one was open for 2% -> 1% of each run, Pallas kernels for 58% -> 52%
where the time goes in v6:
time: 695 us; the launch traced here: 684 us
  Pallas kernels  376 us (54%)
  waiting for transfers between devices  190 us (27%)
  starting transfers between devices  74 us (11%)
  local copies, waits for them, and re-layouts  35.2 us (5%)
  other arithmetic  7.9 us (1%)
    pallas_call x44, Pallas kernels, run(): pl.pallas_call(body, grid_spec=pltpu.PrefetchScalarGridSpec(num_scalar_pr...  375 us
    ppermute x49, waiting for transfers between devices, hop(): lax.ppermute(array, 'fsdp', [(chip, chip ^ flip) for chip in range(BLOCKS)])  188 us
    ppermute x49, starting transfers between devices, hop(): lax.ppermute(array, 'fsdp', [(chip, chip ^ flip) for chip in range(BLOCKS)])  70.8 us
    unnamed x136, local copies, waits for them, and re-layouts  34 us
  transfers between devices with their start and end apart: 67, of which 21 were waited for; matrix products, arithmetic and copies ran while one was open for 1% of the time, Pallas kernels for 52%

profile of v6, /device:TPU:0, one launch (start us, length us, event | category | flops | bytes accessed | tf_op | source)
XLA Modules:
  0.0 684.3 jit_solution(15858340175649325728)
XLA Ops:
  49.2 10.1 %collective-permute-start.12 = (bf16[576,512]{1,0:T(8,128)(2,1)S(1)}, bf16[576,512]{1,0:T(8,128)(2,1)S(1)}, u32[]{:S(2)}, u32[]{:S(2)}) collective-permute-start(bf16[576,512]{1,0:T(8,128)(2,1)S(1)} %copy-done.16), channel_id=1, source_target_pairs={{0,8},{1,9},{2,10},{3,11},{4,12},{5,13},{6,14},{7,15},{8,0},{9,1},... | collective-permute-start | bytes 1769480 | tf_op jit(solution)/shard_map/ppermute | solution.py:1519
  59.3 24.5 %collective-permute-done.12.refs_1_ = bf16[576,512]{1,0:T(8,128)(2,1)S(1)} collective-permute-done((bf16[576,512]{1,0:T(8,128)(2,1)S(1)}, bf16[576,512]{1,0:T(8,128)(2,1)S(1)}, u32[]{:S(2)}, u32[]{:S(2)}) %collective-permute-start.12) | collective-permute-done | bytes 589856 | tf_op jit(solution)/shard_map/ppermute | solution.py:1519
  95.0 19.6 %collective-permute-done.15.refs_1_ = bf16[2,576,512]{2,1,0:T(8,128)(2,1)S(1)} collective-permute-done((bf16[2,576,512]{2,1,0:T(8,128)(2,1)}, bf16[2,576,512]{2,1,0:T(8,128)(2,1)S(1)}, u32[]{:S(2)}, u32[]{:S(2)}) %collective-permute-start.15) | collective-permute-done | bytes 1179680 | tf_op jit(solution)/shard_map/ppermute | solution.py:1519
  127.0 7.0 %collective-permute-start.22 = (bf16[4,192,512]{2,1,0:T(8,128)(2,1)}, bf16[4,192,512]{2,1,0:T(8,128)(2,1)}, u32[]{:S(2)}, u32[]{:S(2)}) collective-permute-start(bf16[4,192,512]{2,1,0:T(8,128)(2,1)} %plane.1.refs_9_.refs_0_), channel_id=1, source_target_pairs={{0,8},{1,9},{2,10},{3,11},{4,12},{5,13},{6,14},{7,15},{8,0},{9,1},... | collective-permute-start | bytes 2359304 | tf_op jit(solution)/shard_map/ppermute | solution.py:1519
  135.7 19.0 %project_qkv.1 = (bf16[1280,1536]{1,0:T(8,128)(2,1)}, bf16[1280,1024]{1,0:T(8,128)(2,1)}, bf16[1280,512]{1,0:T(8,128)(2,1)}, bf16[1280,512]{1,0:T(8,128)(2,1)}, ...) custom-call(s32[4]{0:T(128)} %pad_add_fusion.1.place_ref, bf16[640,1536]{1,0:T(8,128)(2,1)} %refs_0_.11, ...), custom_call_target="tpu_custom_call" | custom-call | bytes 59400 | tf_op jit(solution)/shard_map/project_qkv/pallas_call | solution.py:52
  154.7 12.2 %attend.2 = (bf16[640,1024]{1,0:T(8,128)(2,1)}, f32[640,128]{1,0:T(8,128)}) custom-call(s32[4]{0:T(128)} %pad_add_fusion.1.place_ref, bf16[1280,1024]{1,0:T(8,128)(2,1)} %get-tuple-element.125.refs_0_, bf16[1280,512]{1,0:T(8,128)(2,1)} %get-tuple-element.126.refs_1_.refs_5_, bf16[1280,512]{1,0:T(8,128)(2,1)} %get-tuple-element.127.refs_2_, ...), custom_call_target="tpu_custom_call" | custom-call | bytes 56100 | tf_op jit(solution)/shard_map/attend/pallas_call | solution.py:52
  168.6 12.0 %attend.3 = (bf16[640,1024]{1,0:T(8,128)(2,1)}, f32[640,128]{1,0:T(8,128)}) custom-call(s32[4]{0:T(128)} %pad_add_fusion.1.place_ref, bf16[1280,1024]{1,0:T(8,128)(2,1)} %get-tuple-element.125.refs_0_, bf16[1280,512]{1,0:T(8,128)(2,1)} %get-tuple-element.126.refs_1_.refs_5_, bf16[1280,512]{1,0:T(8,128)(2,1)} %get-tuple-element.127.refs_2_, ...), custom_call_target="tpu_custom_call" | custom-call | bytes 56100 | tf_op jit(solution)/shard_map/attend/pallas_call | solution.py:52
  197.6 10.9 %middle.1 = (f32[640,1536]{1,0:T(8,128)}, bf16[640,1536]{1,0:T(8,128)(2,1)}) custom-call(s32[4]{0:T(128)} %pad_add_fusion.1.place_ref, bf16[640,1536]{1,0:T(8,128)(2,1)} %refs_0_.11, bf16[640,1024]{1,0:T(8,128)(2,1)} %get-tuple-element.130.refs_2_.refs_1_.refs_4_.refs_0_, bf16[640,1024]{1,0:T(8,128)(2,1)} %copy-done.19, ...), custom_call_target="tpu_custom_call" | custom-call | bytes 36300 | tf_op jit(solution)/shard_map/middle/pallas_call | solution.py:52
  208.5 7.1 %collective-permute-done.26.refs_1_ = bf16[2,384,512]{2,1,0:T(8,128)(2,1)S(1)} collective-permute-done((bf16[2,384,512]{2,1,0:T(8,128)(2,1)}, bf16[2,384,512]{2,1,0:T(8,128)(2,1)S(1)}, u32[]{:S(2)}, u32[]{:S(2)}) %collective-permute-start.26) | collective-permute-done | bytes 786464 | tf_op jit(solution)/shard_map/ppermute | solution.py:1519
  229.2 38.5 %ffn_forward.2 = (bf16[640,1536]{1,0:T(8,128)(2,1)}, bf16[640,1536]{1,0:T(8,128)(2,1)}, bf16[640,1536]{1,0:T(8,128)(2,1)}, bf16[640,1536]{1,0:T(8,128)(2,1)}, bf...) custom-call(s32[4]{0:T(128)} %pad_add_fusion.1.place_ref, ...), custom_call_target="tpu_custom_call" | custom-call | bytes 118800 | tf_op jit(solution)/shard_map/ffn_forward/pallas_call | solution.py:52
  274.0 21.4 %ffn_backward.2 = (bf16[2,4,288,512]{3,2,1,0:T(8,128)(2,1)}, bf16[2,4,288,512]{3,2,1,0:T(8,128)(2,1)}, bf16[4,288,512]{2,1,0:T(8,128)(2,1)}, bf16[4,288,512]{2,1,0:T(8,128)(2,1)}, bf16[4,2,288,512]{3,2,1,0:T(8,128)(2,1)}) custom-call(s32[4]{0:T(128)} %pad_add_fusion.1.place_ref, bf16[640,1536]{1,0:T(8,128)(2,1)} %get-tuple-element.135.refs_2_.refs_0_, ...), custom_call_target="tpu_custom_call" | custom-call | bytes 72600 | tf_op jit(solution)/shard_map/ffn_backward/pallas_call | solution.py:52
  301.0 38.3 %ffn_forward.3 = (bf16[640,1536]{1,0:T(8,128)(2,1)}, bf16[640,1536]{1,0:T(8,128)(2,1)}, bf16[640,1536]{1,0:T(8,128)(2,1)}, bf16[640,1536]{1,0:T(8,128)(2,1)}, bf...) custom-call(s32[4]{0:T(128)} %pad_add_fusion.1.place_ref, ...), custom_call_target="tpu_custom_call" | custom-call | bytes 118800 | tf_op jit(solution)/shard_map/ffn_forward/pallas_call | solution.py:52
  339.4 9.6 %collective-permute-done.35.refs_2_.refs_1_ = bf16[2,4,288,512]{3,2,1,0:T(8,128)(2,1)S(1)} collective-permute-done((bf16[2,4,288,512]{3,2,1,0:T(8,128)(2,1)}, bf16[2,4,288,512]{3,2,1,0:T(8,128)(2,1)S(1)}, u32[]{:S(2)}, u32[]{:S(2)}) %collective-permute-start.35) | collective-permute-done | bytes 2359328 | tf_op jit(solution)/shard_map/ppermute | solution.py:1519
  351.7 4.2 merge.4
  357.9 21.7 %ffn_backward.3 = (bf16[2,4,288,512]{3,2,1,0:T(8,128)(2,1)}, bf16[2,4,288,512]{3,2,1,0:T(8,128)(2,1)}, bf16[4,288,512]{2,1,0:T(8,128)(2,1)}, bf16[4,288,512]{2,1,0:T(8,128)(2,1)}, bf16[4,2,288,512]{3,2,1,0:T(8,128)(2,1)}) custom-call(s32[4]{0:T(128)} %pad_add_fusion.1.place_ref, bf16[640,1536]{1,0:T(8,128)(2,1)} %get-tuple-element.135.refs_2_.refs_0_, ...), custom_call_target="tpu_custom_call" | custom-call | bytes 72600 | tf_op jit(solution)/shard_map/ffn_backward/pallas_call | solution.py:52
  385.0 15.9 %middle_back.1 = (f32[640,1536]{1,0:T(8,128)}, bf16[640,768]{1,0:T(8,128)(2,1)}, bf16[640,768]{1,0:T(8,128)(2,1)}, bf16[640,1024]{1,0:T(8,128)(2,1)}, bf16[640,1024]{1,0:T(8,128)(2,1)}, /*index=5*/f32[8,1536]{1,0:T(8,128)}) custom-call(s32[4]{0:T(128)} %pad_add_fusion.1.place_ref, f32[640,1536]{1,0:T(8,128)} %get-tuple-element.134.refs_0_, ...), custom_call_target="tpu_custom_call" | custom-call | bytes 49500 | tf_op jit(solution)/shard_map/middle_back/pallas_call | solution.py:52
  401.5 14.5 %attend_back.2 = (bf16[640,1024]{1,0:T(8,128)(2,1)}, bf16[640,512]{1,0:T(8,128)(2,1)}, bf16[640,512]{1,0:T(8,128)(2,1)}) custom-call(s32[4]{0:T(128)} %pad_add_fusion.1.place_ref, bf16[1280,1024]{1,0:T(8,128)(2,1)} %get-tuple-element.125.refs_0_, bf16[1280,512]{1,0:T(8,128)(2,1)} %get-tuple-element.126.refs_1_.refs_5_, ...), custom_call_target="tpu_custom_call" | custom-call | bytes 69300 | tf_op jit(solution)/shard_map/attend_back/pallas_call | solution.py:52
  417.0 10.3 %out_grad.1 = (bf16[2,4,80,512]{3,2,1,0:T(8,128)(2,1)}, bf16[2,4,80,512]{3,2,1,0:T(8,128)(2,1)}, bf16[4,80,512]{2,1,0:T(8,128)(2,1)}, bf16[4,80,512]{2,1,0:T(8,128)(2,1)}, bf16[4,2,80,512]{3,2,1,0:T(8,128)(2,1)}) custom-call(s32[4]{0:T(128)} %pad_add_fusion.1.place_ref, bf16[640,1024]{1,0:T(8,128)(2,1)} %get-tuple-element.130.refs_2_.refs_1_.refs_4_.refs_0_, ...), custom_call_target="tpu_custom_call" | custom-call | bytes 33000 | tf_op jit(solution)/shard_map/out_grad/pallas_call | solution.py:52
  427.3 6.4 sum_plane.3
  437.3 4.2 merge.5
  442.8 14.1 %attend_back.3 = (bf16[640,1024]{1,0:T(8,128)(2,1)}, bf16[640,512]{1,0:T(8,128)(2,1)}, bf16[640,512]{1,0:T(8,128)(2,1)}) custom-call(s32[4]{0:T(128)} %pad_add_fusion.1.place_ref, bf16[1280,1024]{1,0:T(8,128)(2,1)} %get-tuple-element.125.refs_0_, bf16[1280,512]{1,0:T(8,128)(2,1)} %get-tuple-element.126.refs_1_.refs_5_, ...), custom_call_target="tpu_custom_call" | custom-call | bytes 69300 | tf_op jit(solution)/shard_map/attend_back/pallas_call | solution.py:52
  466.1 14.3 %input_back.1 = (bf16[1280,1536]{1,0:T(8,128)(2,1)}, bf16[640,1536]{1,0:T(8,128)(2,1)}, bf16[640,1536]{1,0:T(8,128)(2,1)}, f32[8,1536]{1,0:T(8,128)}) custom-call(s32[4]{0:T(128)} %pad_add_fusion.1.place_ref, bf16[640,1024]{1,0:T(8,128)(2,1)} %get-tuple-element.167.refs_6_.refs_0_, bf16[640,512]{1,0:T(8,128)(2,1)} %get-tuple-element.188.refs_1_, ...), custom_call_target="tpu_custom_call" | custom-call | bytes 49500 | tf_op jit(solution)/shard_map/input_back/pallas_call | solution.py:52
  482.1 11.7 %qkv_grad.1 = (bf16[2,4,160,512]{3,2,1,0:T(8,128)(2,1)}, bf16[2,4,160,512]{3,2,1,0:T(8,128)(2,1)}, bf16[4,160,512]{2,1,0:T(8,128)(2,1)}, bf16[4,160,512]{2,1,0:T(8,128)(2,1)}, bf16[4,2,160,512]{3,2,1,0:T(8,128)(2,1)}) custom-call(s32[4]{0:T(128)} %pad_add_fusion.1.place_ref, bf16[1280,1536]{1,0:T(8,128)(2,1)} %get-tuple-element.187.refs_0_, ...), custom_call_target="tpu_custom_call" | custom-call | bytes 49500 | tf_op jit(solution)/shard_map/qkv_grad/pallas_call | solution.py:52
  499.8 51.3 %collective-permute-done.50.refs_4_ = bf16[4,288,512]{2,1,0:T(8,128)(2,1)S(1)} collective-permute-done((bf16[4,288,512]{2,1,0:T(8,128)(2,1)}, bf16[4,288,512]{2,1,0:T(8,128)(2,1)S(1)}, u32[]{:S(2)}, u32[]{:S(2)}) %collective-permute-start.50) | collective-permute-done | bytes 1179680 | tf_op jit(solution)/shard_map/ppermute | solution.py:1519
  552.3 7.1 %sum_plane.4 = (f32[2,368,512]{2,1,0:T(8,128)}, bf16[2,368,512]{2,1,0:T(8,128)(2,1)}, bf16[2,368,512]{2,1,0:T(8,128)(2,1)}, bf16[2,368,512]{2,1,0:T(8,128)(2,1)}) custom-call(s32[4]{0:T(128)} %pad_add_fusion.1.place_ref, bf16[4,2,288,512]{3,2,1,0:T(8,128)(2,1)} %get-tuple-element.162.refs_11_.refs_0_, bf16[2,4,288,512]{3,2,1,0:T(8,128)(2,1)} %copy-done.9, ...), custom_call_target="tpu_custom_call" | custom-call | bytes 16500 | tf_op jit(solution)/shard_map/sum_plane/pallas_call | solution.py:52
  564.1 7.7 %output.1.refs_4_ = bf16[640,1536]{1,0:T(8,128)(2,1)} custom-call(s32[4]{0:T(128)} %pad_add_fusion.1.place_ref, f32[640,1536]{1,0:T(8,128)} %get-tuple-element.134.refs_0_, bf16[640,1536]{1,0:T(8,128)(2,1)} %get-tuple-element.137.refs_1_, bf16[640,1536]{1,0:T(8,128)(2,1)} %get-tuple-element.147.refs_2_, bf16[640,1536]{1,0:T(8,128)(2,1)} %copy-done.12, ...), custom_call_target="tpu_custom_call" | custom-call | bytes 13200 | tf_op jit(solution)/shard_map/output/pallas_call | solution.py:52
  581.5 8.6 %tokens_grad.1.refs_5_ = f32[640,1536]{1,0:T(8,128)} custom-call(s32[4]{0:T(128)} %pad_add_fusion.1.place_ref, bf16[640,1536]{1,0:T(8,128)(2,1)} %refs_0_.11, f32[640,1536]{1,0:T(8,128)} %get-tuple-element.199.refs_1_, bf16[640,1536]{1,0:T(8,128)(2,1)} %get-tuple-element.200.refs_2_, bf16[640,1536]{1,0:T(8,128)(2,1)} %copy-done.33, ...), custom_call_target="tpu_custom_call" | custom-call | bytes 13200 | tf_op jit(solution)/shard_map/tokens_grad/pallas_call | solution.py:52
  593.7 4.9 sum_plane.5
  602.9 39.5 %collective-permute-done.62.refs_2_ = bf16[2,368,512]{2,1,0:T(8,128)(2,1)S(1)} collective-permute-done((bf16[2,368,512]{2,1,0:T(8,128)(2,1)S(1)}, bf16[2,368,512]{2,1,0:T(8,128)(2,1)S(1)}, u32[]{:S(2)}, u32[]{:S(2)}) %collective-permute-start.62) | collective-permute-done | bytes 753696 | tf_op jit(solution)/shard_map/ppermute | solution.py:1519
  643.6 4.4 sum_line.4
  648.0 17.6 %collective-permute-done.59.refs_2_ = bf16[2,160,512]{2,1,0:T(8,128)(2,1)S(1)} collective-permute-done((bf16[2,160,512]{2,1,0:T(8,128)(2,1)}, bf16[2,160,512]{2,1,0:T(8,128)(2,1)S(1)}, u32[]{:S(2)}, u32[]{:S(2)}) %collective-permute-start.59) | collective-permute-done | bytes 327712 | tf_op jit(solution)/shard_map/ppermute | solution.py:1519
  674.7 5.6 unpack_ffn.1
  (300 shorter events, 188.6 us)
Async XLA Ops:
  46.1 41.6 %collective-permute-start.10 = (bf16[4,448,512]{2,1,0:T(8,128)(2,1)}, bf16[4,448,512]{2,1,0:T(8,128)(2,1)S(1)}, u32[]{:S(2)}, u32[]{:S(2)}) collective-permute-start(bf16[4,448,512]{2,1,0:T(8,128)(2,1)} %join.1.refs_2_.refs_0_.refs_4_), channel_id=1, source_target_pairs={{0,1},{1,0},{2,3},{3,2},{4,5},{5,4},{6,7},{7,6},{8,9},{9,8},{10,11... | collective-permute-start | bytes 5505032 | tf_op jit(solution)/shard_map/ppermute | solution.py:1519
  47.6 40.0 %collective-permute-start.11 = (bf16[4,448,512]{2,1,0:T(8,128)(2,1)}, bf16[4,448,512]{2,1,0:T(8,128)(2,1)S(1)}, u32[]{:S(2)}, u32[]{:S(2)}) collective-permute-start(bf16[4,448,512]{2,1,0:T(8,128)(2,1)} %join.1.refs_2_.refs_0_.refs_4_), channel_id=1, source_target_pairs={{0,2},{1,3},{2,0},{3,1},{4,6},{5,7},{6,4},{7,5},{8,10},{9,11},{10,... | collective-permute-start | bytes 5505032 | tf_op jit(solution)/shard_map/ppermute | solution.py:1519
  119.3 67.4 %collective-permute-start.20 = (bf16[4,576,512]{2,1,0:T(8,128)(2,1)}, bf16[4,576,512]{2,1,0:T(8,128)(2,1)}, u32[]{:S(2)}, u32[]{:S(2)}) collective-permute-start(bf16[4,576,512]{2,1,0:T(8,128)(2,1)} %line.2.refs_5_.refs_4_), channel_id=1, source_target_pairs={{0,1},{1,0},{2,3},{3,2},{4,5},{5,4},{6,7},{7,6},{8,9},{9,8},{10,11... | collective-permute-start | bytes 7077896 | tf_op jit(solution)/shard_map/ppermute | solution.py:1519
  119.9 66.8 %collective-permute-start.21 = (bf16[4,576,512]{2,1,0:T(8,128)(2,1)}, bf16[4,576,512]{2,1,0:T(8,128)(2,1)}, u32[]{:S(2)}, u32[]{:S(2)}) collective-permute-start(bf16[4,576,512]{2,1,0:T(8,128)(2,1)} %line.2.refs_5_.refs_4_), channel_id=1, source_target_pairs={{0,2},{1,3},{2,0},{3,1},{4,6},{5,7},{6,4},{7,5},{8,10},{9,11},{10,... | collective-permute-start | bytes 7077896 | tf_op jit(solution)/shard_map/ppermute | solution.py:1519
  126.4 40.6 %collective-permute-start.16 = (bf16[1024,768]{1,0:T(8,128)(2,1)}, bf16[1024,768]{1,0:T(8,128)(2,1)S(1)}, u32[]{:S(2)}, u32[]{:S(2)}) collective-permute-start(bf16[1024,768]{1,0:T(8,128)(2,1)} %get-tuple-element.124.refs_9_.refs_3_.refs_7_), channel_id=1, source_target_pairs={{0,16},{16,0},{1,17},{17,1},{2,18},{18,2},{3,19},{19,3},{4,20},{20... | collective-permute-start | bytes 4718600 | tf_op jit(solution)/shard_map/ppermute | solution.py:1514
  126.5 40.6 %collective-permute-start.17 = (bf16[1024,768]{1,0:T(8,128)(2,1)}, bf16[1024,768]{1,0:T(8,128)(2,1)S(1)}, u32[]{:S(2)}, u32[]{:S(2)}) collective-permute-start(bf16[1024,768]{1,0:T(8,128)(2,1)} %get-tuple-element.129.refs_4_.refs_8_), channel_id=1, source_target_pairs={{0,16},{16,0},{1,17},{17,1},{2,18},{18,2},{3,19},{19,3},{4,20},{20... | collective-permute-start | bytes 4718600 | tf_op jit(solution)/shard_map/ppermute | solution.py:1514
  127.0 53.7 %collective-permute-start.22 = (bf16[4,192,512]{2,1,0:T(8,128)(2,1)}, bf16[4,192,512]{2,1,0:T(8,128)(2,1)}, u32[]{:S(2)}, u32[]{:S(2)}) collective-permute-start(bf16[4,192,512]{2,1,0:T(8,128)(2,1)} %plane.1.refs_9_.refs_0_), channel_id=1, source_target_pairs={{0,8},{1,9},{2,10},{3,11},{4,12},{5,13},{6,14},{7,15},{8,0},{9,1},... | collective-permute-start | bytes 2359304 | tf_op jit(solution)/shard_map/ppermute | solution.py:1519
  180.6 39.4 %collective-permute-start.27 = (bf16[640,1024]{1,0:T(8,128)(2,1)}, bf16[640,1024]{1,0:T(8,128)(2,1)S(1)}, u32[]{:S(2)}, u32[]{:S(2)}) collective-permute-start(bf16[640,1024]{1,0:T(8,128)(2,1)} %get-tuple-element.130.refs_2_.refs_1_.refs_4_.refs_0_), channel_id=1, source_target_pairs={{0,16},{16,0},{1,17},{17,1},{2,18},{18,2},{3,19},{19,3},{4,20},{20... | collective-permute-start | bytes 3932168 | tf_op jit(solution)/shard_map/ppermute | solution.py:1514
  225.3 42.4 %collective-permute-start.28 = (bf16[4,384,512]{2,1,0:T(8,128)(2,1)}, bf16[4,384,512]{2,1,0:T(8,128)(2,1)S(1)}, u32[]{:S(2)}, u32[]{:S(2)}) collective-permute-start(bf16[4,384,512]{2,1,0:T(8,128)(2,1)} %line.3.refs_9_.refs_4_), channel_id=1, source_target_pairs={{0,1},{1,0},{2,3},{3,2},{4,5},{5,4},{6,7},{7,6},{8,9},{9,8},{10,11... | collective-permute-start | bytes 4718600 | tf_op jit(solution)/shard_map/ppermute | solution.py:1519
  226.8 40.9 %collective-permute-start.29 = (bf16[4,384,512]{2,1,0:T(8,128)(2,1)}, bf16[4,384,512]{2,1,0:T(8,128)(2,1)S(1)}, u32[]{:S(2)}, u32[]{:S(2)}) collective-permute-start(bf16[4,384,512]{2,1,0:T(8,128)(2,1)} %line.3.refs_9_.refs_4_), channel_id=1, source_target_pairs={{0,2},{1,3},{2,0},{3,1},{4,6},{5,7},{6,4},{7,5},{8,10},{9,11},{10,... | collective-permute-start | bytes 4718600 | tf_op jit(solution)/shard_map/ppermute | solution.py:1519
  227.9 67.5 %collective-permute-start.32 = (bf16[2,4,192,512]{3,2,1,0:T(8,128)(2,1)S(1)}, bf16[2,4,192,512]{3,2,1,0:T(8,128)(2,1)S(1)}, u32[]{:S(2)}, u32[]{:S(2)}) collective-permute-start(bf16[2,4,192,512]{3,2,1,0:T(8,128)(2,1)S(1)} %copy-done.4), channel_id=1, source_target_pairs={{0,4},{1,5},{2,6},{3,7},{4,0},{5,1},{6,2},{7,3},{8,12},{9,13},{10,... | collective-permute-start | bytes 4718600 | tf_op jit(solution)/shard_map/ppermute | solution.py:1519
  297.8 51.3 %collective-permute-start.35 = (bf16[2,4,288,512]{3,2,1,0:T(8,128)(2,1)}, bf16[2,4,288,512]{3,2,1,0:T(8,128)(2,1)S(1)}, u32[]{:S(2)}, u32[]{:S(2)}) collective-permute-start(bf16[2,4,288,512]{3,2,1,0:T(8,128)(2,1)} %get-tuple-element.146.refs_11_), channel_id=1, source_target_pairs={{0,1},{1,0},{2,3},{3,2},{4,5},{5,4},{6,7},{7,6},{8,9},{9,8},{10,11... | collective-permute-start | bytes 7077896 | tf_op jit(solution)/shard_map/ppermute | solution.py:1519
  299.4 50.9 %collective-permute-start.36 = (bf16[2,4,288,512]{3,2,1,0:T(8,128)(2,1)}, bf16[2,4,288,512]{3,2,1,0:T(8,128)(2,1)S(1)}, u32[]{:S(2)}, u32[]{:S(2)}) collective-permute-start(bf16[2,4,288,512]{3,2,1,0:T(8,128)(2,1)} %get-tuple-element.150), channel_id=1, source_target_pairs={{0,2},{1,3},{2,0},{3,1},{4,6},{5,7},{6,4},{7,5},{8,10},{9,11},{10,... | collective-permute-start | bytes 7077896 | tf_op jit(solution)/shard_map/ppermute | solution.py:1519
  300.5 39.0 %collective-permute-start.33 = (bf16[640,1536]{1,0:T(8,128)(2,1)}, bf16[640,1536]{1,0:T(8,128)(2,1)S(1)}, u32[]{:S(2)}, u32[]{:S(2)}) collective-permute-start(bf16[640,1536]{1,0:T(8,128)(2,1)} %get-tuple-element.138.refs_2_), channel_id=1, source_target_pairs={{0,16},{16,0},{1,17},{17,1},{2,18},{18,2},{3,19},{19,3},{4,20},{20... | collective-permute-start | bytes 5898248 | tf_op jit(solution)/shard_map/ppermute | solution.py:1514
  300.5 80.2 %collective-permute-start.39 = (bf16[640,1536]{1,0:T(8,128)(2,1)}, bf16[640,1536]{1,0:T(8,128)(2,1)}, u32[]{:S(2)}, u32[]{:S(2)}) collective-permute-start(bf16[640,1536]{1,0:T(8,128)(2,1)} %get-tuple-element.157), channel_id=1, source_target_pairs={{0,16},{16,0},{1,17},{17,1},{2,18},{18,2},{3,19},{19,3},{4,20},{20... | collective-permute-start | bytes 5898248 | tf_op jit(solution)/shard_map/ppermute | solution.py:1514
  339.3 42.3 %collective-permute-start.40 = (bf16[640,1536]{1,0:T(8,128)(2,1)}, bf16[640,1536]{1,0:T(8,128)(2,1)}, u32[]{:S(2)}, u32[]{:S(2)}) collective-permute-start(bf16[640,1536]{1,0:T(8,128)(2,1)} %get-tuple-element.158), channel_id=1, source_target_pairs={{0,16},{16,0},{1,17},{17,1},{2,18},{18,2},{3,19},{19,3},{4,20},{20... | collective-permute-start | bytes 5898248 | tf_op jit(solution)/shard_map/ppermute | solution.py:1514
  379.6 55.5 %collective-permute-start.46 = (bf16[2,4,288,512]{3,2,1,0:T(8,128)(2,1)}, bf16[2,4,288,512]{3,2,1,0:T(8,128)(2,1)S(1)}, u32[]{:S(2)}, u32[]{:S(2)}) collective-permute-start(bf16[2,4,288,512]{3,2,1,0:T(8,128)(2,1)} %get-tuple-element.180), channel_id=1, source_target_pairs={{0,1},{1,0},{2,3},{3,2},{4,5},{5,4},{6,7},{7,6},{8,9},{9,8},{10,11... | collective-permute-start | bytes 7077896 | tf_op jit(solution)/shard_map/ppermute | solution.py:1519
  380.7 55.1 %collective-permute-start.47 = (bf16[2,4,288,512]{3,2,1,0:T(8,128)(2,1)}, bf16[2,4,288,512]{3,2,1,0:T(8,128)(2,1)S(1)}, u32[]{:S(2)}, u32[]{:S(2)}) collective-permute-start(bf16[2,4,288,512]{3,2,1,0:T(8,128)(2,1)} %get-tuple-element.181), channel_id=1, source_target_pairs={{0,2},{1,3},{2,0},{3,1},{4,6},{5,7},{6,4},{7,5},{8,10},{9,11},{10,... | collective-permute-start | bytes 7077896 | tf_op jit(solution)/shard_map/ppermute | solution.py:1519
  401.0 40.5 %collective-permute-start.34 = (bf16[640,1536]{1,0:T(8,128)(2,1)}, bf16[640,1536]{1,0:T(8,128)(2,1)S(1)}, u32[]{:S(2)}, u32[]{:S(2)}) collective-permute-start(bf16[640,1536]{1,0:T(8,128)(2,1)} %get-tuple-element.148.refs_4_), channel_id=1, source_target_pairs={{0,16},{16,0},{1,17},{17,1},{2,18},{18,2},{3,19},{19,3},{4,20},{20... | collective-permute-start | bytes 5898248 | tf_op jit(solution)/shard_map/ppermute | solution.py:1514
  401.5 41.4 %collective-permute-start.45 = (bf16[640,1024]{1,0:T(8,128)(2,1)}, bf16[640,1024]{1,0:T(8,128)(2,1)}, u32[]{:S(2)}, u32[]{:S(2)}) collective-permute-start(bf16[640,1024]{1,0:T(8,128)(2,1)} %get-tuple-element.176), channel_id=1, source_target_pairs={{0,16},{16,0},{1,17},{17,1},{2,18},{18,2},{3,19},{19,3},{4,20},{20... | collective-permute-start | bytes 3932168 | tf_op jit(solution)/shard_map/ppermute | solution.py:1514
  441.5 55.8 %collective-permute-start.49 = (bf16[4,288,512]{2,1,0:T(8,128)(2,1)}, bf16[4,288,512]{2,1,0:T(8,128)(2,1)}, u32[]{:S(2)}, u32[]{:S(2)}) collective-permute-start(bf16[4,288,512]{2,1,0:T(8,128)(2,1)} %get-tuple-element.182.refs_10_), channel_id=1, source_target_pairs={{0,1},{1,0},{2,3},{3,2},{4,5},{5,4},{6,7},{7,6},{8,9},{9,8},{10,11... | collective-permute-start | bytes 3538952 | tf_op jit(solution)/shard_map/ppermute | solution.py:1519
  480.4 99.5 %collective-permute-start.53 = (bf16[640,1536]{1,0:T(8,128)(2,1)}, bf16[640,1536]{1,0:T(8,128)(2,1)S(1)}, u32[]{:S(2)}, u32[]{:S(2)}) collective-permute-start(bf16[640,1536]{1,0:T(8,128)(2,1)} %get-tuple-element.201), channel_id=1, source_target_pairs={{0,16},{16,0},{1,17},{17,1},{2,18},{18,2},{3,19},{19,3},{4,20},{20... | collective-permute-start | bytes 5898248 | tf_op jit(solution)/shard_map/ppermute | solution.py:1514
  493.8 78.0 %collective-permute-start.54 = (bf16[2,4,160,512]{3,2,1,0:T(8,128)(2,1)}, bf16[2,4,160,512]{3,2,1,0:T(8,128)(2,1)S(1)}, u32[]{:S(2)}, u32[]{:S(2)}) collective-permute-start(bf16[2,4,160,512]{3,2,1,0:T(8,128)(2,1)} %get-tuple-element.204), channel_id=1, source_target_pairs={{0,1},{1,0},{2,3},{3,2},{4,5},{5,4},{6,7},{7,6},{8,9},{9,8},{10,11... | collective-permute-start | bytes 3932168 | tf_op jit(solution)/shard_map/ppermute | solution.py:1519
  495.3 76.5 %collective-permute-start.55 = (bf16[2,4,160,512]{3,2,1,0:T(8,128)(2,1)}, bf16[2,4,160,512]{3,2,1,0:T(8,128)(2,1)S(1)}, u32[]{:S(2)}, u32[]{:S(2)}) collective-permute-start(bf16[2,4,160,512]{3,2,1,0:T(8,128)(2,1)} %get-tuple-element.205), channel_id=1, source_target_pairs={{0,2},{1,3},{2,0},{3,1},{4,6},{5,7},{6,4},{7,5},{8,10},{9,11},{10,... | collective-permute-start | bytes 3932168 | tf_op jit(solution)/shard_map/ppermute | solution.py:1519
  496.4 54.6 %collective-permute-start.50 = (bf16[4,288,512]{2,1,0:T(8,128)(2,1)}, bf16[4,288,512]{2,1,0:T(8,128)(2,1)S(1)}, u32[]{:S(2)}, u32[]{:S(2)}) collective-permute-start(bf16[4,288,512]{2,1,0:T(8,128)(2,1)} %get-tuple-element.185), channel_id=1, source_target_pairs={{0,2},{1,3},{2,0},{3,1},{4,6},{5,7},{6,4},{7,5},{8,10},{9,11},{10,... | collective-permute-start | bytes 3538952 | tf_op jit(solution)/shard_map/ppermute | solution.py:1519
  497.3 53.7 %collective-permute-start.48 = (bf16[2,288,512]{2,1,0:T(8,128)(2,1)S(1)}, bf16[2,288,512]{2,1,0:T(8,128)(2,1)S(1)}, u32[]{:S(2)}, u32[]{:S(2)}) collective-permute-start(bf16[2,288,512]{2,1,0:T(8,128)(2,1)S(1)} %copy-done.32), channel_id=1, source_target_pairs={{0,8},{1,9},{2,10},{3,11},{4,12},{5,13},{6,14},{7,15},{8,0},{9,1},... | collective-permute-start | bytes 1769480 | tf_op jit(solution)/shard_map/ppermute | solution.py:1519
  559.3 42.2 %collective-permute-start.61 = (bf16[2,368,512]{2,1,0:T(8,128)(2,1)}, bf16[2,368,512]{2,1,0:T(8,128)(2,1)S(1)}, u32[]{:S(2)}, u32[]{:S(2)}) collective-permute-start(bf16[2,368,512]{2,1,0:T(8,128)(2,1)} %get-tuple-element.212), channel_id=1, source_target_pairs={{0,4},{1,5},{2,6},{3,7},{4,0},{5,1},{6,2},{7,3},{8,12},{9,13},{10,... | collective-permute-start | bytes 2261000 | tf_op jit(solution)/shard_map/ppermute | solution.py:1519
  578.4 64.0 %collective-permute-start.62 = (bf16[2,368,512]{2,1,0:T(8,128)(2,1)S(1)}, bf16[2,368,512]{2,1,0:T(8,128)(2,1)S(1)}, u32[]{:S(2)}, u32[]{:S(2)}) collective-permute-start(bf16[2,368,512]{2,1,0:T(8,128)(2,1)S(1)} %copy-done.63), channel_id=1, source_target_pairs={{0,8},{1,9},{2,10},{3,11},{4,12},{5,13},{6,14},{7,15},{8,0},{9,1},... | collective-permute-start | bytes 2261000 | tf_op jit(solution)/shard_map/ppermute | solution.py:1519
  580.0 62.5 %collective-permute-start.63 = (bf16[2,368,512]{2,1,0:T(8,128)(2,1)S(1)}, bf16[2,368,512]{2,1,0:T(8,128)(2,1)S(1)}, u32[]{:S(2)}, u32[]{:S(2)}) collective-permute-start(bf16[2,368,512]{2,1,0:T(8,128)(2,1)S(1)} %copy-done.62), channel_id=1, source_target_pairs={{0,12},{1,13},{2,14},{3,15},{4,8},{5,9},{6,10},{7,11},{8,4},{9,5},... | collective-permute-start | bytes 2261000 | tf_op jit(solution)/shard_map/ppermute | solution.py:1519
  598.6 49.5 %collective-permute-start.58 = (bf16[2,160,512]{2,1,0:T(8,128)(2,1)}, bf16[2,160,512]{2,1,0:T(8,128)(2,1)S(1)}, u32[]{:S(2)}, u32[]{:S(2)}) collective-permute-start(bf16[2,160,512]{2,1,0:T(8,128)(2,1)} %get-tuple-element.209), channel_id=1, source_target_pairs={{0,4},{1,5},{2,6},{3,7},{4,0},{5,1},{6,2},{7,3},{8,12},{9,13},{10,... | collective-permute-start | bytes 983048 | tf_op jit(solution)/shard_map/ppermute | solution.py:1519
  599.1 66.5 %collective-permute-start.59 = (bf16[2,160,512]{2,1,0:T(8,128)(2,1)}, bf16[2,160,512]{2,1,0:T(8,128)(2,1)S(1)}, u32[]{:S(2)}, u32[]{:S(2)}) collective-permute-start(bf16[2,160,512]{2,1,0:T(8,128)(2,1)} %get-tuple-element.210), channel_id=1, source_target_pairs={{0,8},{1,9},{2,10},{3,11},{4,12},{5,13},{6,14},{7,15},{8,0},{9,1},... | collective-permute-start | bytes 983048 | tf_op jit(solution)/shard_map/ppermute | solution.py:1519
  601.5 64.1 %collective-permute-start.60 = (bf16[2,160,512]{2,1,0:T(8,128)(2,1)}, bf16[2,160,512]{2,1,0:T(8,128)(2,1)S(1)}, u32[]{:S(2)}, u32[]{:S(2)}) collective-permute-start(bf16[2,160,512]{2,1,0:T(8,128)(2,1)} %get-tuple-element.211), channel_id=1, source_target_pairs={{0,12},{1,13},{2,14},{3,15},{4,8},{5,9},{6,10},{7,11},{8,4},{9,5},... | collective-permute-start | bytes 983048 | tf_op jit(solution)/shard_map/ppermute | solution.py:1519
  (102 other events, 1068.9 us)
